TPU v7x, 128 devices: a whole 4x4x4 slice. The times are simulated.
128 devices in a mesh: row: 16 (over x, y_lo, core), col: 8 (over z, y_hi).
Axes of the slice: x: 4, y: 4 (y_hi: 2, y_lo: 2; y = y_hi * 2 + y_lo), z: 4, core: 2. Of those that a mesh axis runs over, the one named last changes fastest.
Arguments:
- covariance: float32 [16384, 16384], P('row', 'col'), as said below
- innovations: float32 [1024, 16, 1024], P('row', None, 'col'), may hold values from -6 to 6
- block_owner: int32 [64], replicated, may hold values from 0 to 63, as said below
- panel_index: int32 [1], replicated, may hold values from 0 to 31
Outputs:
- factor: float32 [16384, 16384], P('row', 'col')
- solved: float32 [1024, 16384], P('col', 'row')
Inputs may be any that keep to these rules, and one draw needn't show every extreme that they name: Storage block s holds global block block_owner[s]; every global block appears once; the storage blocks s with one value of s // 4 hold the blocks of one residue modulo 16, rising with s. `covariance`: symmetric positive definite.
All inputs are finite; a program needn't handle non-finite values.
Results may differ from a plain program's by a relative error of at most 0.0016.
Values may be sent and summed in bfloat16 or wider, within the bound.
No kernel may reach another device: no remote copies, remote signals or barrier semaphores. Data moves between devices by JAX's collectives and lax.ppermute only.
A program may use at most 128 MiB of HBM per device.

v0:
```python
import jax
import jax.numpy as jnp
from jax import lax
from jax.sharding import PartitionSpec as P

B = 256
PANELS = 2


CONTRACT_LAST = (((1,), (1,)), ((), ()))


def spread(value, axis, source):
    kept = jnp.where(lax.axis_index(axis) == source, value, 0).astype(value.dtype)
    return lax.psum(kept, axis)


def lower_solve(factor, right_side):
    return jax.scipy.linalg.solve_triangular(factor, right_side, lower=True)


def outer_rows(left, right):
    return lax.dot_general(left, right, CONTRACT_LAST, preferred_element_type=jnp.float32)


def locate(block_owner, target):
    positions = jnp.arange(block_owner.shape[0], dtype=jnp.int32)
    return jnp.sum(jnp.where(block_owner == target, positions, 0))


def per_device(covariance, innovations, block_owner, panel_index):
    panel_width = B
    local_rows, local_cols = covariance.shape
    row_blocks = local_rows // panel_width
    column_blocks = local_cols // panel_width
    row_here = lax.axis_index("row")
    column_here = lax.axis_index("col")
    relaid = lax.all_to_all(
        lax.all_to_all(innovations, "row", split_axis=1, concat_axis=0, tiled=True),
        "col",
        split_axis=0,
        concat_axis=2,
        tiled=True,
    )
    solved = relaid.reshape(relaid.shape[0], local_rows)
    owner_rows = jnp.repeat(
        lax.dynamic_slice_in_dim(block_owner, row_here * row_blocks, row_blocks), panel_width
    )
    owner_columns = jnp.repeat(
        lax.dynamic_slice_in_dim(block_owner, column_here * column_blocks, column_blocks),
        panel_width,
    )
    matrix = covariance
    ahead_column = None
    for panel_turn in range(PANELS):
        target = panel_index[0] + panel_turn
        slot_index = locate(block_owner, target)
        row_root = slot_index // row_blocks
        column_root = slot_index // column_blocks
        row_start = slot_index % row_blocks * panel_width
        column_start = slot_index % column_blocks * panel_width
        column_local = lax.dynamic_slice_in_dim(matrix, column_start, panel_width, 1)
        ahead_column = None
        live_rows = owner_rows > target
        live_columns = owner_columns > target
        column = spread(column_local, "col", column_root)
        diagonal_local = lax.dynamic_slice_in_dim(column, row_start, panel_width, 0)
        innovation_local = lax.dynamic_slice_in_dim(solved, row_start, panel_width, 1)
        diagonal, innovation_block = (
            spread(diagonal_local, "row", row_root),
            spread(innovation_local, "row", row_root),
        )
        factor = jnp.linalg.cholesky(diagonal)
        panel_rows = jnp.where(live_rows[:, None], lower_solve(factor, column.T).T, 0.0)
        rows_half = panel_rows.astype(jnp.bfloat16)
        everything = lax.all_gather(rows_half, "row", axis=0, tiled=True)
        columns_half = lax.dynamic_slice_in_dim(everything, column_here * local_cols, local_cols, 0)
        matrix = matrix - outer_rows(rows_half, columns_half)
        whitened = lower_solve(factor, innovation_block.T).T
        solved = solved - outer_rows(whitened.astype(jnp.bfloat16), rows_half)
        spot_old = lax.dynamic_slice_in_dim(solved, row_start, panel_width, 1)
        spot_new = jnp.where(row_here == row_root, whitened, spot_old)
        solved = lax.dynamic_update_slice_in_dim(solved, spot_new, row_start, 1)
        row_old = lax.dynamic_slice_in_dim(matrix, row_start, panel_width, 0)
        row_new = jnp.where((row_here == row_root) & live_columns[None, :], 0.0, row_old)
        matrix = lax.dynamic_update_slice_in_dim(matrix, row_new, row_start, 0)
        column_old = lax.dynamic_slice_in_dim(matrix, column_start, panel_width, 1)
        column_new = jnp.where(live_rows[:, None], panel_rows, column_old)
        diagonal_spot = lax.dynamic_update_slice_in_dim(column_new, factor, row_start, 0)
        column_new = jnp.where(row_here == row_root, diagonal_spot, column_new)
        column_new = jnp.where(column_here == column_root, column_new, column_old)
        matrix = lax.dynamic_update_slice_in_dim(matrix, column_new, column_start, 1)
    return (matrix, solved)


def solution(mesh):
    placed = (P("row", "col"), P("row", None, "col"), P(), P())
    return jax.shard_map(
        per_device,
        mesh=mesh,
        in_specs=placed,
        out_specs=(P("row", "col"), P("col", "row")),
        check_vma=False,
    )
```

profile of v0, /device:TPU:0, one launch (start us, length us, event | category | flops | bytes accessed | tf_op | source)
XLA Modules:
  0.0 740.0 jit_solution(2396850284032272871)
XLA Ops:
  9.2 5.6 all-to-all-start
  19.4 9.3 %copy.54 = f32[1024,2048]{0,1:T(8,128)} copy(f32[1024,2048]{1,0:T(8,128)} %param.9) | data formatting | bytes 16777216 | tf_op args[0]
  31.1 7.7 %all-to-all-start.1 = ((f32[1024,1,128]{2,1,0:T(1,128)}), f32[1024,1,128]{2,1,0:T(1,128)S(1)}, u32[]{:S(2)}, u32[]{:S(2)}) async-start(f32[1024,1,128]{2,1,0:T(1,128)} %bitcast.18), calls=%async_computation.1 | async-start | bytes 1048576 | tf_op jit(solution)/shard_map/all_to_all | solution.py:38
  38.8 15.6 %all-to-all-done.1 = f32[1024,1,128]{2,1,0:T(1,128)S(1)} async-done(((f32[1024,1,128]{2,1,0:T(1,128)}), f32[1024,1,128]{2,1,0:T(1,128)S(1)}, u32[]{:S(2)}, u32[]{:S(2)}) %all-to-all-start.1) | async-done | bytes 524320 | tf_op jit(solution)/shard_map/all_to_all | solution.py:38
  55.3 71.9 %all-reduce.8.cloned.1.call-done = f32[1024,256]{0,1:T(8,128)} async-done(((f32[1024,256]{0,1:T(8,128)}), f32[1024,256]{0,1:T(8,128)}) %all-reduce.8.cloned.1.call-update) | async-done | bytes 1048592 | tf_op jit(solution)/shard_map/psum | solution.py:15
  129.1 116.0 %all-reduce.14.cloned.1.call-done = (f32[256,256]{0,1:T(8,128)}, f32[256,128]{1,0:T(8,128)}) async-done(((f32[256,256]{0,1:T(8,128)}, f32[256,128]{1,0:T(8,128)}), (f32[256,256]{0,1:T(8,128)}, f32[256,128]{1,0:T(8,128)})) %all-reduce.14.cloned.1.call-update) | async-done | bytes 393232 | tf_op jit(solution)/shard_map/psum | solution.py:15
  247.3 11.7 %cholesky.130 = f32[128,128]{1,0:T(8,128)S(1)} custom-call(f32[128,128]{1,0:T(8,128)S(1)} %cholesky.194), custom_call_target="Cholesky" | custom-call | tf_op jit(solution)/shard_map/jit(cholesky)/cholesky | solution.py:73
  259.0 9.8 %custom-call.17 = f32[1,128,128]{1,2,0:T(8,128)S(1)} custom-call(f32[1,128,128]{2,1,0:T(8,128)S(1)} %get-tuple-element.120), custom_call_target="InvertDiagBlocksLowerTriangular" | custom-call | tf_op jit(solution)/shard_map/jit(cholesky)/cholesky | solution.py:73
  269.3 11.7 %cholesky.147 = f32[128,128]{1,0:T(8,128)S(1)} custom-call(f32[128,128]{1,0:T(8,128)S(1)} %convolution_subtract_fusion.9), custom_call_target="Cholesky" | custom-call | tf_op jit(solution)/shard_map/jit(cholesky)/cholesky | solution.py:73
  283.6 4.5 while.8
  288.1 19.7 %custom-call.18 = f32[2,128,128]{1,2,0:T(8,128)S(1)} custom-call(f32[2,128,128]{2,1,0:T(8,128)S(1)} %get-tuple-element.33), custom_call_target="InvertDiagBlocksLowerTriangular" | custom-call | tf_op jit(solution)/shard_map/jit(_solve_triangular)/triangular_solve | solution.py:19
  315.8 50.1 %all-gather.3.cloned.1.call-done = bf16[16384,256]{0,1:T(8,128)(2,1)} async-done(((bf16[1024,256]{0,1:T(8,128)(2,1)}), bf16[16384,256]{0,1:T(8,128)(2,1)}) %all-gather.3.cloned.1.call-update) | async-done | bytes 8388624 | tf_op jit(solution)/shard_map/all_gather | solution.py:76
  365.8 5.2 convolution_subtract_fusion.1
  372.1 3.4 copy-done
  378.6 90.0 %all-reduce.10.cloned.1.call-done = f32[1024,256]{0,1:T(8,128)} async-done(((f32[1024,256]{0,1:T(8,128)}), f32[1024,256]{0,1:T(8,128)}) %all-reduce.10.cloned.1.call-update) | async-done | bytes 1048592 | tf_op jit(solution)/shard_map/psum | solution.py:15
  470.7 116.0 %all-reduce.12.cloned.1.call-done = (f32[256,256]{0,1:T(8,128)}, f32[256,128]{1,0:T(8,128)}) async-done(((f32[256,256]{0,1:T(8,128)}, f32[256,128]{1,0:T(8,128)}), (f32[256,256]{0,1:T(8,128)}, f32[256,128]{1,0:T(8,128)})) %all-reduce.12.cloned.1.call-update) | async-done | bytes 393232 | tf_op jit(solution)/shard_map/psum | solution.py:15
  588.8 11.7 %cholesky.164 = f32[128,128]{1,0:T(8,128)S(1)} custom-call(f32[128,128]{1,0:T(8,128)S(1)} %cholesky.197), custom_call_target="Cholesky" | custom-call | tf_op jit(solution)/shard_map/jit(cholesky)/cholesky | solution.py:73
  600.5 9.8 %custom-call.19 = f32[1,128,128]{1,2,0:T(8,128)S(1)} custom-call(f32[1,128,128]{2,1,0:T(8,128)S(1)} %get-tuple-element.118), custom_call_target="InvertDiagBlocksLowerTriangular" | custom-call | tf_op jit(solution)/shard_map/jit(cholesky)/cholesky | solution.py:73
  610.8 11.7 %cholesky.181 = f32[128,128]{1,0:T(8,128)S(1)} custom-call(f32[128,128]{1,0:T(8,128)S(1)} %convolution_subtract_fusion.8), custom_call_target="Cholesky" | custom-call | tf_op jit(solution)/shard_map/jit(cholesky)/cholesky | solution.py:73
  625.7 4.6 while.9
  630.3 19.7 %custom-call.20 = f32[2,128,128]{1,2,0:T(8,128)S(1)} custom-call(f32[2,128,128]{2,1,0:T(8,128)S(1)} %get-tuple-element.34), custom_call_target="InvertDiagBlocksLowerTriangular" | custom-call | tf_op jit(solution)/shard_map/jit(_solve_triangular)/triangular_solve | solution.py:19
  658.3 49.7 %all-gather.5.cloned.1.call-done = bf16[16384,256]{0,1:T(8,128)(2,1)} async-done(((bf16[1024,256]{0,1:T(8,128)(2,1)}), bf16[16384,256]{0,1:T(8,128)(2,1)}) %all-gather.5.cloned.1.call-update) | async-done | bytes 8388624 | tf_op jit(solution)/shard_map/all_gather | solution.py:76
  708.0 8.4 %convolution_subtract_fusion = f32[1024,2048]{0,1:T(8,128)} fusion(f32[1024,2048]{0,1:T(8,128)} %copy-done, bf16[1024,256]{0,1:T(8,128)(2,1)} %fusion.4, bf16[16384,256]{0,1:T(8,128)(2,1)} %all-gather.5.cloned.1.call-done, s32[]{:T(128)S(6)} %select_n.199), kind=kOutput, calls=%fused_computation.4 | convolution fusion | flops 1075838976 | bytes 18350084 | tf_op jit(solution)/shard_map/dot_general | solution.py:23
  723.6 9.1 %copy.69 = f32[1024,2048]{1,0:T(8,128)} copy(f32[1024,2048]{0,1:T(8,128)} %select_dynamic-update-slice_fusion.2) | data formatting | bytes 16777216
  (123 shorter events, 51.9 us)
Async XLA Ops:
  9.2 21.9 %all-to-all-start = ((f32[64,16,128]{2,0,1:T(8,128)}), f32[64,16,128]{2,0,1:T(8,128)}, u32[]{:S(2)}, u32[]{:S(2)}) async-start(f32[64,16,128]{2,0,1:T(8,128)} %copy.62), calls=%async_computation | async-start | bytes 1048576 | tf_op jit(solution)/shard_map/all_to_all | solution.py:39
  14.7 112.5 %all-reduce.8.cloned.1.call-start = ((), (), s32[]{:S(2)}) async-start(), calls=%async_computation.2 | async-start | bytes 2097152 | tf_op jit(solution)/shard_map/psum | solution.py:15
  19.4 109.6 %copy-start.4 = (s32[64]{0:T(128)S(1)}, s32[64]{0:T(128)}, u32[]{:S(2)}) copy-start(s32[64]{0:T(128)} %param.11) | copy-start | bytes 772
  31.1 23.3 %all-to-all-start.1 = ((f32[1024,1,128]{2,1,0:T(1,128)}), f32[1024,1,128]{2,1,0:T(1,128)S(1)}, u32[]{:S(2)}, u32[]{:S(2)}) async-start(f32[1024,1,128]{2,1,0:T(1,128)} %bitcast.18), calls=%async_computation.1 | async-start | bytes 1048576 | tf_op jit(solution)/shard_map/all_to_all | solution.py:38
  38.7 206.5 %all-reduce.14.cloned.1.call-start = ((), (), s32[]{:S(2)}) async-start(), calls=%async_computation.7 | async-start | bytes 786432 | tf_op jit(solution)/shard_map/psum | solution.py:15
  128.9 236.9 %all-gather.3.cloned.1.call-start = ((), (), s32[]{:S(2)}) async-start(), calls=%async_computation.3 | async-start | bytes 8912896 | tf_op jit(solution)/shard_map/all_gather | solution.py:76
  312.7 155.9 %all-reduce.10.cloned.1.call-start = ((), (), s32[]{:S(2)}) async-start(), calls=%async_computation.4 | async-start | bytes 2097152 | tf_op jit(solution)/shard_map/psum | solution.py:15
  371.0 5.7 copy-start.2
  371.0 6.5 copy-start.1
  372.1 3.4 copy-start
  376.6 210.0 %all-reduce.12.cloned.1.call-start = ((), (), s32[]{:S(2)}) async-start(), calls=%async_computation.6 | async-start | bytes 786432 | tf_op jit(solution)/shard_map/psum | solution.py:15
  470.3 237.6 %all-gather.5.cloned.1.call-start = ((), (), s32[]{:S(2)}) async-start(), calls=%async_computation.5 | async-start | bytes 8912896 | tf_op jit(solution)/shard_map/all_gather | solution.py:76
  586.7 68.3 %copy-start.3 = (f32[256,128]{1,0:T(8,128)S(1)}, f32[256,128]{1,0:T(8,128)}, u32[]{:S(2)}) copy-start(f32[256,128]{1,0:T(8,128)} %get-tuple-element.110) | copy-start | bytes 393220
Sparse Core Ops, SparseCore 0:
  31.2 95.9 all-reduce.7
  130.3 114.8 all-reduce.13
  312.9 52.9 all-gather.2
  376.8 91.8 all-reduce.9
  471.8 114.8 all-reduce.11
  655.0 52.9 all-gather.4
where the time goes:
time: 751 us; the launch traced here: 740 us
  waiting for transfers between devices  509 us (68%)
  other arithmetic  130 us (17%)
  local copies, waits for them, and re-layouts  36.8 us (5%)
  matrix products  25.9 us (3%)
  between operations  23.8 us (3%)
  starting transfers between devices  13.7 us (2%)
    psum x4, waiting for transfers between devices, spread(): return lax.psum(kept, axis)  394 us
    all_gather x2, waiting for transfers between devices, per_device(): everything = lax.all_gather(rows_half, 'row', axis=0, tiled=True)  99.8 us
    another operation x13, other arithmetic, per_device(): factor = jnp.linalg.cholesky(diagonal)  68.7 us
    another operation x5, other arithmetic, lower_solve(): return jax.scipy.linalg.solve_triangular(factor, right_side, lower=True)  39.4 us
    unnamed x14, local copies, waits for them, and re-layouts  24.8 us
    all_to_all x1, waiting for transfers between devices, per_device(): lax.all_to_all(lax.all_to_all(innovations, 'row', split_axis=1, concat_ax...  15.6 us
    dot_general x4, matrix products, outer_rows(): lax.dot_general(left, right, CONTRACT_LAST, preferred_element_type=jnp.fl...  15.3 us
  transfers between devices with their start and end apart: 8, of which 7 were waited for; matrix products, arithmetic and copies ran while one was open for 3% of the time, Pallas kernels for 0%

commit v1 on v0

v1 whole, which is shorter than its diff:
```python
import functools

import jax
import jax.numpy as jnp
from jax import lax
from jax.experimental import pallas as pl
from jax.experimental.pallas import tpu as pltpu
from jax.sharding import PartitionSpec as P

B = 256
S = 64
F32 = jnp.float32
BF16 = jnp.bfloat16
HIGH = lax.Precision.HIGHEST
VMEM_SPEC = pl.BlockSpec(memory_space=pltpu.VMEM)
SMEM_SPEC = pl.BlockSpec(memory_space=pltpu.SMEM)


def dot(a, b, dims, precision=None):
    return lax.dot_general(a, b, (dims, ((), ())), precision=precision, preferred_element_type=F32)


NN = ((1,), (0,))
NT = ((1,), (1,))
TN = ((0,), (0,))


def pick_kernel(slots, cov_ref, out_ref):
    out_ref[...] = cov_ref[...].reshape(out_ref.shape)


def pick_columns(slots, covariance, parts):
    rows = covariance.shape[0]
    blocks = rows // B
    part = B // parts
    return pl.pallas_call(
        pick_kernel,
        grid_spec=pltpu.PrefetchScalarGridSpec(
            num_scalar_prefetch=1,
            grid=(blocks, 2),
            in_specs=[pl.BlockSpec((B, B), lambda b, j, slots: (b, slots[j]))],
            out_specs=pl.BlockSpec((parts, 1, part, B), lambda b, j, slots: (0, b, 0, j)),
        ),
        out_shape=jax.ShapeDtypeStruct((parts, blocks, part, 2 * B), F32),
    )(slots, covariance)


def lanes(tile, j):
    return jnp.broadcast_to(tile[:, j : j + 1], (8, 128))


def eliminate(tiles):
    sub = lax.broadcasted_iota(jnp.int32, (8, 128), 0)
    scales = []
    for t in range(8):
        own = tiles[t]
        cols = [lanes(own, 8 * t + j) for j in range(8)]
        inv, cross = [], {}
        pivots = jnp.ones((8, 128), F32)
        for j in range(8):
            pivot = jnp.broadcast_to(cols[j][j : j + 1, :], (8, 128))
            pivots = jnp.where(sub == j, pivot, pivots)
            r = 1.0 / pivot
            inv.append(r)
            if j == 7:
                break
            m = jnp.where(sub > j, cols[j] * r, 0.0)
            for k in range(j + 1, 8):
                cross[j, k] = jnp.broadcast_to(cols[k][j : j + 1, :], (8, 128))
                cols[k] = cols[k] - m * cross[j, k]
            own = own - m * jnp.broadcast_to(own[j : j + 1, :], (8, 128))
        tiles[t] = own
        scales.append(lax.rsqrt(pivots))
        rows = [jnp.broadcast_to(own[j : j + 1, :], (8, 128)) for j in range(8)]
        for i in range(t + 1, 8):
            low = tiles[i]
            cols = [lanes(low, 8 * t + j) for j in range(8)]
            for j in range(8):
                m = cols[j] * inv[j]
                for k in range(j + 1, 8):
                    cols[k] = cols[k] - m * cross[j, k]
                low = low - m * rows[j]
            tiles[i] = low
    return tiles, scales


def factor_block(work, small, inverse_small):
    for b in range(B // S):
        lo, hi = b * S, (b + 1) * S
        small[:, 0:S] = work[lo:hi, lo:hi]
        row = lax.broadcasted_iota(jnp.int32, (S, S), 0)
        col = lax.broadcasted_iota(jnp.int32, (S, S), 1)
        small[:, S : 2 * S] = jnp.where(row == col, 1.0, 0.0)
        tiles, scales = eliminate([small[8 * i : 8 * i + 8, :] for i in range(8)])
        for i in range(8):
            small[8 * i : 8 * i + 8, :] = tiles[i] * scales[i]
        inverse_small[...] = small[:, S : 2 * S]
        top = dot(inverse_small[...], work[lo:hi, :], NN, HIGH)
        work[lo:hi, :] = top
        if hi < B:
            work[hi:B, :] = work[hi:B, :] - dot(top[:, hi:B], top, TN, HIGH)


def factor_kernel(diag_ref, x0_ref, x1_ref, l10t_ref, l00_ref, l11_ref, work, small, inverse_small):
    row = lax.broadcasted_iota(jnp.int32, (B, B), 0)
    col = lax.broadcasted_iota(jnp.int32, (B, B), 1)
    eye = jnp.where(row == col, 1.0, 0.0)
    work[:, 0:B] = diag_ref[:, 0:B]
    work[:, B : 2 * B] = eye
    factor_block(work, small, inverse_small)
    x0 = work[:, B : 2 * B]
    x0_ref[...] = x0
    l00_ref[...] = jnp.where(row <= col, work[:, 0:B], 0.0).T
    l10t = dot(x0, diag_ref[:, B : 2 * B], NN, HIGH).astype(BF16)
    l10t_ref[...] = l10t
    work[:, 0:B] = diag_ref[:, 2 * B : 3 * B] - dot(l10t, l10t, TN)
    work[:, B : 2 * B] = eye
    factor_block(work, small, inverse_small)
    x1_ref[...] = work[:, B : 2 * B]
    l11_ref[...] = jnp.where(row <= col, work[:, 0:B], 0.0).T


def factor_diagonal(diag):
    square = jax.ShapeDtypeStruct((B, B), F32)
    return pl.pallas_call(
        factor_kernel,
        in_specs=[VMEM_SPEC],
        out_specs=[VMEM_SPEC] * 5,
        out_shape=[square, square, jax.ShapeDtypeStruct((B, B), BF16), square, square],
        scratch_shapes=[pltpu.VMEM((B, 2 * B), F32), pltpu.VMEM((S, 2 * S), F32), pltpu.VMEM((S, S), F32)],
        cost_estimate=pl.CostEstimate(flops=2 * 10**10, bytes_accessed=80_000_000, transcendentals=0),
    )(diag)


def solve_rows(first, second, x0, x1, l10t):
    p0 = dot(first, x0, NT, HIGH)
    p1 = dot(second - dot(p0.astype(BF16), l10t, NN), x1, NT, HIGH)
    return p0, p1


def update_kernel(
    flags, cov_ref, across_ref, along_ref, x0_ref, x1_ref, l10t_ref, l00_ref, l11_ref, out_ref, rows_ref, pc
):
    i = pl.program_id(0)
    parts, part = along_ref.shape[0], along_ref.shape[2]
    column_blocks = pc.shape[0] // B
    blocks = column_blocks // 2

    @pl.when(i == 0)
    def _():
        @pl.loop(0, parts)
        def _(q):
            raw = [across_ref[pl.ds(2 * q, 2), j].reshape(2 * 128, 128) for j in range(4)]
            p0, p1 = solve_rows(
                jnp.concatenate(raw[:2], axis=1),
                jnp.concatenate(raw[2:], axis=1),
                x0_ref[...],
                x1_ref[...],
                l10t_ref[...],
            )
            p0, p1 = p0.astype(BF16), p1.astype(BF16)
            for n in range(column_blocks):
                place = pl.ds(pl.multiple_of(n * B + q * part, part), part)
                here = slice(n * part, (n + 1) * part)
                pc[place, 0:B] = jnp.where(flags[8 + n] > 0, p0[here], jnp.zeros_like(p0[here]))
                pc[place, B : 2 * B] = jnp.where(flags[8 + n] > 1, p1[here], jnp.zeros_like(p1[here]))

    level = flags[16 + i]
    raw = along_ref[:, 0].reshape(parts * part, 2 * B)
    p0, p1 = solve_rows(raw[:, 0:B], raw[:, B : 2 * B], x0_ref[...], x1_ref[...], l10t_ref[...])
    p0 = jnp.where(level > 0, p0, 0.0)
    p1 = jnp.where(level > 1, p1, 0.0)
    rows_ref[:, 0:B] = p0.astype(BF16)
    rows_ref[:, B : 2 * B] = p1.astype(BF16)
    for n in range(column_blocks):
        cut = slice(n * B, (n + 1) * B)
        out_ref[:, cut] = cov_ref[:, cut] - dot(rows_ref[...], pc[cut, :], NT)

    for panel, factor_ref, solved in ((0, l00_ref, p0), (1, l11_ref, p1)):
        is_row = i == flags[2 + panel]
        for n in range(column_blocks):

            @pl.when(is_row & (flags[8 + n] > panel))
            def _():
                out_ref[:, n * B : (n + 1) * B] = jnp.zeros((B, B), F32)

        column = flags[4 + panel]
        place = pl.ds(pl.multiple_of(jnp.maximum(column, 0) * B, B), B)

        @pl.when((column >= 0) & (level > panel))
        def _():
            out_ref[:, place] = solved

        @pl.when((column >= 0) & is_row)
        def _():
            out_ref[:, place] = factor_ref[...]


def update(flags, covariance, across, along, factors):
    rows, columns = covariance.shape
    blocks = rows // B
    parts = along.shape[0]
    part = B // parts
    whole = lambda *shape: pl.BlockSpec(shape, lambda i, flags: (0,) * len(shape))
    return pl.pallas_call(
        update_kernel,
        grid_spec=pltpu.PrefetchScalarGridSpec(
            num_scalar_prefetch=1,
            grid=(blocks,),
            in_specs=[
                pl.BlockSpec((B, columns), lambda i, flags: (i, 0)),
                whole(*across.shape),
                pl.BlockSpec((parts, 1, part, 2 * B), lambda i, flags: (0, i, 0, 0)),
            ]
            + [whole(B, B)] * 5,
            out_specs=[
                pl.BlockSpec((B, columns), lambda i, flags: (i, 0)),
                pl.BlockSpec((B, 2 * B), lambda i, flags: (i, 0)),
            ],
            scratch_shapes=[pltpu.VMEM((columns, 2 * B), BF16)],
        ),
        out_shape=[jax.ShapeDtypeStruct((rows, columns), F32), jax.ShapeDtypeStruct((rows, 2 * B), BF16)],
        compiler_params=pltpu.CompilerParams(vmem_limit_bytes=48 * 1024 * 1024),
        cost_estimate=pl.CostEstimate(flops=10**10, bytes_accessed=24_000_000, transcendentals=0),
    )(flags, covariance, across, along, *factors)


def forward_kernel(flags, relaid_ref, across_ref, rows_ref, x0_ref, x1_ref, l10t_ref, out_ref, white):
    half = relaid_ref.shape[1]
    width = relaid_ref.shape[2]
    raw = []
    for panel in range(2):
        first = flags[6 + panel]
        for h in range(2):
            for parity in range(2):
                piece = across_ref[first + 2 * h + parity, 4, panel * half : (panel + 1) * half, :]
                white[parity * half : (parity + 1) * half, panel * B + h * width : panel * B + (h + 1) * width] = piece
    w0, w1 = solve_rows(white[:, 0:B], white[:, B : 2 * B], x0_ref[...], x1_ref[...], l10t_ref[...])
    white[:, 0:B] = w0
    white[:, B : 2 * B] = w1
    product = dot(white[...].astype(BF16), rows_ref[...], NT)
    for n in range(relaid_ref.shape[0]):
        q, parity = n // 2, n % 2
        there = (slice(parity * half, (parity + 1) * half), slice(q * width, (q + 1) * width))
        out_ref[there] = relaid_ref[n] - product[there]
    for panel in range(2):
        block = flags[2 + panel]

        @pl.when(block >= 0)
        def _():
            place = pl.ds(pl.multiple_of(jnp.maximum(block, 0) * B, B), B)
            out_ref[:, place] = white[:, panel * B : (panel + 1) * B]


def forward(flags, relaid, across, rows, factors):
    particles = 2 * relaid.shape[1]
    return pl.pallas_call(
        forward_kernel,
        in_specs=[SMEM_SPEC] + [VMEM_SPEC] * 6,
        out_specs=VMEM_SPEC,
        out_shape=jax.ShapeDtypeStruct((particles, rows.shape[0]), F32),
        scratch_shapes=[pltpu.VMEM((particles, 2 * B), F32)],
        compiler_params=pltpu.CompilerParams(vmem_limit_bytes=32 * 1024 * 1024),
        cost_estimate=pl.CostEstimate(flops=10**9, bytes_accessed=8_000_000, transcendentals=0),
    )(flags, relaid, across, rows, *factors[:3])


def per_device(covariance, innovations, block_owner, panel_index, *, n_row, n_col):
    local_rows, local_cols = covariance.shape
    row_blocks, column_blocks = local_rows // B, local_cols // B
    r, c = lax.axis_index("row"), lax.axis_index("col")
    targets = panel_index[0] + jnp.arange(2, dtype=jnp.int32)
    positions = jnp.arange(block_owner.shape[0], dtype=jnp.int32)
    slot = jnp.sum(jnp.where(block_owner[None, :] == targets[:, None], positions[None, :], 0), axis=1)
    row_root, column_root = slot // row_blocks, slot // column_blocks
    row_slot, column_slot = slot % row_blocks, slot % column_blocks
    levels = jnp.sum((block_owner[:, None] > targets[None, :]).astype(jnp.int32), axis=1)
    flags = jnp.concatenate(
        [
            jnp.zeros((2,), jnp.int32),
            jnp.where(row_root == r, row_slot, -1),
            jnp.where(column_root == c, column_slot, -1),
            row_slot * 4,
            lax.dynamic_slice_in_dim(levels, c * column_blocks, column_blocks),
            lax.dynamic_slice_in_dim(levels, r * row_blocks, row_blocks),
        ]
    ).astype(jnp.int32)
    across_axes = [
        (a * n_col + b, (2 * b + a % 2) * n_col + a // 2) for a in range(n_row) for b in range(n_col)
    ]

    turned = lax.ppermute(jnp.transpose(innovations, (1, 0, 2)), ("row", "col"), across_axes)

    picked = pick_columns(column_slot.astype(jnp.int32), covariance, n_col)
    parts = lax.all_to_all(picked, "col", split_axis=0, concat_axis=0, tiled=True)
    piece = jnp.concatenate(
        [
            lax.dynamic_index_in_dim(parts[..., :B], column_root[0], 0, keepdims=False),
            lax.dynamic_index_in_dim(parts[..., B:], column_root[1], 0, keepdims=False),
        ],
        axis=-1,
    )
    part = piece.shape[1]

    chosen = jnp.where(r == row_root[0], row_slot[0], row_slot[1])
    mine = lax.dynamic_index_in_dim(piece, chosen, 0, keepdims=False)
    spread = lax.all_to_all(
        jnp.broadcast_to(mine[None], (n_row,) + mine.shape), "row", split_axis=0, concat_axis=0, tiled=True
    )
    upper = lax.dynamic_index_in_dim(spread, row_root[0], 0, keepdims=False)
    lower = lax.dynamic_index_in_dim(spread[..., B:], row_root[1], 0, keepdims=False)
    strip = jnp.concatenate([upper, lower], axis=-1)
    diag = lax.all_to_all(
        jnp.broadcast_to(strip[None], (n_col,) + strip.shape), "col", split_axis=0, concat_axis=0, tiled=True
    ).reshape(B, 3 * B)

    tiled = jnp.transpose(piece.reshape(row_blocks * part, 4, 128), (1, 0, 2))
    tiled = lax.ppermute(tiled, ("row", "col"), across_axes)
    wanted = jnp.concatenate(
        [
            lax.dynamic_index_in_dim(turned, row_root[0], 0, keepdims=False),
            lax.dynamic_index_in_dim(turned, row_root[1], 0, keepdims=False),
        ],
        axis=0,
    )
    across = lax.all_gather(jnp.concatenate([tiled, wanted[None]], axis=0), "row", axis=0)

    factors = factor_diagonal(diag)

    along = lax.all_to_all(
        jnp.broadcast_to(piece[None], (n_col,) + piece.shape), "col", split_axis=0, concat_axis=0, tiled=True
    )
    relaid = lax.all_to_all(turned, "row", split_axis=0, concat_axis=0, tiled=True)

    matrix, rows = update(flags, covariance, across, along, factors)
    solved = forward(flags, relaid, across, rows, factors)
    return matrix, solved


def solution(mesh):
    placed = (P("row", "col"), P("row", None, "col"), P(), P())
    return jax.shard_map(
        functools.partial(per_device, n_row=mesh.shape["row"], n_col=mesh.shape["col"]),
        mesh=mesh,
        in_specs=placed,
        out_specs=(P("row", "col"), P("col", "row")),
        check_vma=False,
    )
```

time: 751 us -> 256 us (0.34); the launches traced: 740 us -> 254 us
  waiting for transfers between devices: 509 us -> 80.1 us
  other arithmetic: 130 us -> 1.62 us
  Pallas kernels: 0 us -> 53.7 us
  blocking collectives: 0 us -> 51.3 us
  matrix products: 25.9 us -> 0 us
  local copies, waits for them, and re-layouts: 36.8 us -> 15.6 us
  starting transfers between devices: 13.7 us -> 27.1 us
    psum x4 -> x0, waiting for transfers between devices: 394 us -> none  [spread(): return lax.psum(kept, axis)]
    another operation x18 -> x0, other arithmetic: 108 us -> none  [the longest x13 68.7 us: per_device(): factor = jnp.linalg.cholesky(diagonal)]
    all_gather x2 -> x1, waiting for transfers between devices: 99.8 us -> 0.02 us  [per_device(): lax.all_gather(jnp.concatenate([tiled, wanted[None]], axis=0), 'row', axi...]
    all_to_all x2 -> x4, waiting for transfers between devices: 15.6 us -> 80.1 us  [the longest x1 53.2 us: per_device(): lax.all_to_all(picked, 'col', split_axis=0, concat_axis=0, tiled=True)]
    pallas_call x0 -> x4, Pallas kernels: none -> 53.7 us  [the longest x1 22.6 us: update(): pl.pallas_call(update_kernel, grid_spec=pltpu.PrefetchScalarGridSpec(num_...]
    all_to_all x0 -> x1, blocking collectives: none -> 51.3 us  [per_device(): lax.all_to_all(jnp.broadcast_to(mine[None], (n_row,) + mine.shape), 'row'...]
    dot_general x4 -> x0, matrix products: 15.3 us -> none  [outer_rows(): lax.dot_general(left, right, CONTRACT_LAST, preferred_element_type=jnp.fl...]
    unnamed x14 -> x29, local copies, waits for them, and re-layouts: 24.8 us -> 9.57 us
  transfers between devices with their start and end apart: 8 -> 7, of which waited for: 7 -> 3; matrix products, arithmetic and copies ran while one was open for 3% -> 2% of each run, Pallas kernels for 0% -> 18%
where the time goes in v1:
time: 256 us; the launch traced here: 254 us
  waiting for transfers between devices  80.1 us (31%)
  Pallas kernels  53.7 us (21%)
  blocking collectives  51.3 us (20%)
  starting transfers between devices  27.1 us (11%)
  between operations  24.7 us (10%)
  local copies, waits for them, and re-layouts  15.6 us (6%)
    all_to_all x1, waiting for transfers between devices, per_device(): lax.all_to_all(picked, 'col', split_axis=0, concat_axis=0, tiled=True)  53.2 us
    all_to_all x1, blocking collectives, per_device(): lax.all_to_all(jnp.broadcast_to(mine[None], (n_row,) + mine.shape), 'row'...  51.3 us
    pallas_call x1, Pallas kernels, update(): pl.pallas_call(update_kernel, grid_spec=pltpu.PrefetchScalarGridSpec(num_...  22.6 us
    pallas_call x1, Pallas kernels, factor_diagonal(): pl.pallas_call(factor_kernel, in_specs=[VMEM_SPEC], out_specs=[VMEM_SPEC]...  22 us
    all_to_all x1, waiting for transfers between devices, per_device(): lax.all_to_all(jnp.broadcast_to(strip[None], (n_col,) + strip.shape), 'co...  20.1 us
    unnamed x29, local copies, waits for them, and re-layouts  9.57 us
    all_to_all x1, starting transfers between devices, per_device(): lax.all_to_all(jnp.broadcast_to(strip[None], (n_col,) + strip.shape), 'co...  8.33 us
    all_to_all x1, starting transfers between devices, per_device(): lax.all_to_all(picked, 'col', split_axis=0, concat_axis=0, tiled=True)  8.16 us
  transfers between devices with their start and end apart: 7, of which 3 were waited for; matrix products, arithmetic and copies ran while one was open for 2% of the time, Pallas kernels for 18%

profile of v1, /device:TPU:0, one launch (start us, length us, event | category | flops | bytes accessed | tf_op | source)
XLA Modules:
  0.0 254.1 jit_solution(11829506758653656497)
XLA Ops:
  7.8 0.8 fusion.2
  9.2 6.3 %shard_map.59 = f32[8,4,32,512]{3,2,1,0:T(8,128)} custom-call(s32[2]{0:T(128)} %get-tuple-element.20.slots, f32[1024,2048]{1,0:T(8,128)} %cov_ref.3), custom_call_target="tpu_custom_call" | custom-call | tf_op jit(solution)/shard_map/pallas_call | solution.py:36
  15.5 8.2 %all-to-all-start = ((f32[8,4,32,512]{3,2,1,0:T(8,128)}), f32[8,4,32,512]{3,2,1,0:T(8,128)S(1)}, u32[]{:S(2)}, u32[]{:S(2)}) async-start(f32[8,4,32,512]{3,2,1,0:T(8,128)} %shard_map.59), calls=%async_computation | async-start | bytes 4194304 | tf_op jit(solution)/shard_map/all_to_all | solution.py:295
  23.9 1.5 collective-permute-start.1
  30.0 53.2 %all-to-all-done = f32[8,4,32,512]{3,2,1,0:T(8,128)S(1)} async-done(((f32[8,4,32,512]{3,2,1,0:T(8,128)}), f32[8,4,32,512]{3,2,1,0:T(8,128)S(1)}, u32[]{:S(2)}, u32[]{:S(2)}) %all-to-all-start) | async-done | bytes 2097184 | tf_op jit(solution)/shard_map/all_to_all | solution.py:295
  92.5 51.3 %all_to_all.25 = f32[16,32,512]{2,1,0:T(8,128)S(1)} all-to-all(f32[16,32,512]{2,1,0:T(8,128)S(1)} %broadcast_in_dim.48), channel_id=1, replica_groups=mesh['row'=16,'col'=8] {'row'}, dimensions={0} | all-to-all | bytes 2097152 | tf_op jit(solution)/shard_map/all_to_all | solution.py:307
  143.9 0.9 broadcast_in_dim.49
  144.9 8.3 %all-to-all-start.3 = ((f32[8,32,768]{2,1,0:T(8,128)}), f32[8,32,768]{2,1,0:T(8,128)S(1)}, u32[]{:S(2)}, u32[]{:S(2)}) async-start(f32[8,32,768]{2,1,0:T(8,128)} %broadcast_in_dim.49), calls=%async_computation.3 | async-start | bytes 1572864 | tf_op jit(solution)/shard_map/all_to_all | solution.py:313
  153.5 20.1 %all-to-all-done.3 = f32[8,32,768]{2,1,0:T(8,128)S(1)} async-done(((f32[8,32,768]{2,1,0:T(8,128)}), f32[8,32,768]{2,1,0:T(8,128)S(1)}, u32[]{:S(2)}, u32[]{:S(2)}) %all-to-all-start.3) | async-done | bytes 786464 | tf_op jit(solution)/shard_map/all_to_all | solution.py:313
  173.7 1.6 broadcast_in_dim.46
  175.3 4.6 %all-to-all-start.1 = ((f32[8,4,32,512]{3,2,1,0:T(8,128)}), f32[8,4,32,512]{3,2,1,0:T(8,128)S(1)}, u32[]{:S(2)}, u32[]{:S(2)}) async-start(f32[8,4,32,512]{3,2,1,0:T(8,128)} %broadcast_in_dim.46), calls=%async_computation.1 | async-start | bytes 4194304 | tf_op jit(solution)/shard_map/all_to_all | solution.py:330
  179.9 22.0 %shard_map.60 = (f32[256,256]{1,0:T(8,128)}, f32[256,256]{1,0:T(8,128)}, bf16[256,256]{1,0:T(8,128)(2,1)}, f32[256,256]{1,0:T(8,128)}, f32[256,256]{1,0:T(8,128)}) custom-call(f32[256,768]{1,0:T(8,128)} %bitcast.31), custom_call_target="tpu_custom_call" | custom-call | flops 20000000000 | bytes 80000000 | tf_op jit(solution)/shard_map/pallas_call | solution.py:125
  201.9 6.8 %all-to-all-done.1.along_ref = f32[8,4,32,512]{3,2,1,0:T(8,128)S(1)} async-done(((f32[8,4,32,512]{3,2,1,0:T(8,128)}), f32[8,4,32,512]{3,2,1,0:T(8,128)S(1)}, u32[]{:S(2)}, u32[]{:S(2)}) %all-to-all-start.1) | async-done | bytes 2097184 | tf_op jit(solution)/shard_map/all_to_all | solution.py:330
  208.6 3.8 %all-to-all-start.4 = ((f32[16,64,128]{2,1,0:T(8,128)}), f32[16,64,128]{2,1,0:T(8,128)S(1)}, u32[]{:S(2)}, u32[]{:S(2)}) async-start(f32[16,64,128]{2,1,0:T(8,128)} %collective-permute-done.1), calls=%async_computation.4 | async-start | bytes 1048576 | tf_op jit(solution)/shard_map/all_to_all | solution.py:333
  212.5 0.9 copy-done.3
  213.4 0.9 copy-done.5
  214.4 0.9 copy-done.7
  215.3 0.9 copy-done.9
  216.2 0.9 copy-done.10
  217.2 22.6 %shard_map.61 = (f32[1024,2048]{1,0:T(8,128)}, bf16[1024,512]{1,0:T(8,128)(2,1)S(1)}) custom-call(s32[20]{0:T(128)S(1)} %concatenate.15.flags, f32[1024,2048]{1,0:T(8,128)} %cov_ref.3, f32[16,5,128,128]{3,2,1,0:T(8,128)} %bitcast.29, f32[8,4,32,512]{3,2,1,0:T(8,128)S(1)} %all-to-all-done.1.along_ref, f32[256,256]{1,0:T(8,128)S(1)} %copy-done.3, ...), custom_call_target="tpu_custom_call" | custom-call | flops 10000000000 | bytes 24000000 | tf_op jit(solution)/shard_map/pallas_call | solution.py:205
  239.7 1.0 copy-done.1
  240.7 2.5 copy-done
  243.2 1.2 copy-done.2
  244.5 2.8 %shard_map.62 = f32[128,1024]{1,0:T(8,128)} custom-call(s32[20]{0:T(128)S(1)} %concatenate.15.flags, f32[16,64,128]{2,1,0:T(8,128)S(1)} %all-to-all-done.4.relaid_ref, f32[16,5,128,128]{3,2,1,0:T(8,128)S(1)} %bitcast.30, bf16[1024,512]{1,0:T(8,128)(2,1)S(1)} %copy-done.2, f32[256,256]{1,0:T(8,128)S(1)} %copy-done.4, f32[256,256]{1,0:T(8,128)S(1)} %copy-done.6, ...), custom_call_target="tpu_custom_call" | custom-call | flops 1000000000 | bytes 8000000 | tf_op jit(solution)/shard_map/pallas_call | solution.py:257
  (53 shorter events, 5.3 us)
Async XLA Ops:
  15.5 8.2 %copy-start.12 = (f32[64,16,128]{2,1,0:T(8,128)S(1)}, f32[64,16,128]{2,1,0:T(8,128)}, u32[]{:S(2)}) copy-start(f32[64,16,128]{2,1,0:T(8,128)} %param.5) | copy-start | bytes 1572868
  15.5 67.7 %all-to-all-start = ((f32[8,4,32,512]{3,2,1,0:T(8,128)}), f32[8,4,32,512]{3,2,1,0:T(8,128)S(1)}, u32[]{:S(2)}, u32[]{:S(2)}) async-start(f32[8,4,32,512]{3,2,1,0:T(8,128)} %shard_map.59), calls=%async_computation | async-start | bytes 4194304 | tf_op jit(solution)/shard_map/all_to_all | solution.py:295
  23.7 188.8 %all-gather.3.cloned.1.call-start = ((), (), s32[]{:S(2)}) async-start(), calls=%async_computation.5 | async-start | bytes 5570560 | tf_op jit(solution)/shard_map/all_gather | solution.py:326
  23.9 64.9 %collective-permute-start.1 = (f32[16,64,128]{2,1,0:T(8,128)S(1)}, f32[16,64,128]{2,1,0:T(8,128)}, u32[]{:S(2)}, u32[]{:S(2)}) collective-permute-start(f32[16,64,128]{2,1,0:T(8,128)S(1)} %bitcast.32), channel_id=1, source_target_pairs={{0,0},{1,16},{2,32},{3,48},{4,64},{5,80},{6,96},{7,112},{8,8},{9,2... | collective-permute-start | bytes 1572872 | tf_op jit(solution)/shard_map/ppermute | solution.py:292
  83.6 6.0 %collective-permute-start = (f32[4,128,128]{2,0,1:T(4,128)S(1)}, f32[4,128,128]{2,0,1:T(4,128)S(1)}, u32[]{:S(2)}, u32[]{:S(2)}) collective-permute-start(f32[4,128,128]{2,0,1:T(4,128)S(1)} %bitcast.33), channel_id=1, source_target_pairs={{0,0},{1,16},{2,32},{3,48},{4,64},{5,80},{6,96},{7,112},{8,8},{9,2... | collective-permute-start | bytes 786440 | tf_op jit(solution)/shard_map/ppermute | solution.py:318
  143.8 9.4 %copy-start.13 = (s32[64]{0:T(128)S(1)}, s32[64]{0:T(128)}, u32[]{:S(2)}) copy-start(s32[64]{0:T(128)} %param.6) | copy-start | bytes 772
  144.9 28.8 %all-to-all-start.3 = ((f32[8,32,768]{2,1,0:T(8,128)}), f32[8,32,768]{2,1,0:T(8,128)S(1)}, u32[]{:S(2)}, u32[]{:S(2)}) async-start(f32[8,32,768]{2,1,0:T(8,128)} %broadcast_in_dim.49), calls=%async_computation.3 | async-start | bytes 1572864 | tf_op jit(solution)/shard_map/all_to_all | solution.py:313
  173.7 1.6 copy-start.11
  175.3 33.3 %all-to-all-start.1 = ((f32[8,4,32,512]{3,2,1,0:T(8,128)}), f32[8,4,32,512]{3,2,1,0:T(8,128)S(1)}, u32[]{:S(2)}, u32[]{:S(2)}) async-start(f32[8,4,32,512]{3,2,1,0:T(8,128)} %broadcast_in_dim.46), calls=%async_computation.1 | async-start | bytes 4194304 | tf_op jit(solution)/shard_map/all_to_all | solution.py:330
  208.6 32.1 %all-to-all-start.4 = ((f32[16,64,128]{2,1,0:T(8,128)}), f32[16,64,128]{2,1,0:T(8,128)S(1)}, u32[]{:S(2)}, u32[]{:S(2)}) async-start(f32[16,64,128]{2,1,0:T(8,128)} %collective-permute-done.1), calls=%async_computation.4 | async-start | bytes 1048576 | tf_op jit(solution)/shard_map/all_to_all | solution.py:333
  212.5 1.0 copy-start.3
  213.4 0.9 copy-start.5
  214.4 0.9 copy-start.7
  215.3 0.9 copy-start.9
  216.2 0.9 copy-start.10
  217.2 23.6 %copy-start.4 = (f32[256,256]{1,0:T(8,128)S(1)}, f32[256,256]{1,0:T(8,128)}, u32[]{:S(2)}) copy-start(f32[256,256]{1,0:T(8,128)} %get-tuple-element.9.x0_ref) | copy-start | bytes 786436
  217.2 23.6 %copy-start.6 = (f32[256,256]{1,0:T(8,128)S(1)}, f32[256,256]{1,0:T(8,128)}, u32[]{:S(2)}) copy-start(f32[256,256]{1,0:T(8,128)} %get-tuple-element.10.x1_ref) | copy-start | bytes 786436
  217.2 23.6 %copy-start.8 = (bf16[256,256]{1,0:T(8,128)(2,1)S(1)}, bf16[256,256]{1,0:T(8,128)(2,1)}, u32[]{:S(2)}) copy-start(bf16[256,256]{1,0:T(8,128)(2,1)} %get-tuple-element.11.l10t_ref) | copy-start | bytes 393220
  239.7 1.0 copy-start.1
  240.7 2.5 copy-start
  243.2 1.2 copy-start.2
Sparse Core Ops, SparseCore 0:
  90.7 77.9 all-gather.2

commit v2 on v1

v2 whole, which is shorter than its diff:
```python
import functools

import jax
import jax.numpy as jnp
from jax import lax
from jax.experimental import pallas as pl
from jax.experimental.pallas import tpu as pltpu
from jax.sharding import PartitionSpec as P

B = 256
S = 64
VMEM_BYTES = 60 * 1024 * 1024
F32 = jnp.float32
BF16 = jnp.bfloat16
HIGH = lax.Precision.HIGHEST
VMEM_SPEC = pl.BlockSpec(memory_space=pltpu.VMEM)
SMEM_SPEC = pl.BlockSpec(memory_space=pltpu.SMEM)


def dot(a, b, dims, precision=None):
    return lax.dot_general(a, b, (dims, ((), ())), precision=precision, preferred_element_type=F32)


NN = ((1,), (0,))
NT = ((1,), (1,))
TN = ((0,), (0,))


def pick_kernel(slots, cov_ref, out_ref):
    parts, blocks, part, width = out_ref.shape
    for b in range(blocks):
        out_ref[:, b] = cov_ref[b * B : (b + 1) * B, :].reshape(parts, part, width)


def pick_columns(slots, covariance, parts):
    rows = covariance.shape[0]
    blocks = rows // B
    part = B // parts
    return pl.pallas_call(
        pick_kernel,
        grid_spec=pltpu.PrefetchScalarGridSpec(
            num_scalar_prefetch=1,
            grid=(2, blocks // 2),
            in_specs=[pl.BlockSpec((2 * B, B), lambda j, b, slots: (b, slots[j]))],
            out_specs=pl.BlockSpec((parts, 2, part, B), lambda j, b, slots: (0, b, 0, j)),
        ),
        out_shape=jax.ShapeDtypeStruct((parts, blocks, part, 2 * B), F32),
    )(slots, covariance)


def lanes(tile, j):
    return jnp.broadcast_to(tile[:, j : j + 1], (8, 128))


def eliminate(tiles):
    sub = lax.broadcasted_iota(jnp.int32, (8, 128), 0)
    scales = []
    for t in range(8):
        own = tiles[t]
        cols = [lanes(own, 8 * t + j) for j in range(8)]
        inv, cross = [], {}
        pivots = jnp.ones((8, 128), F32)
        for j in range(8):
            pivot = jnp.broadcast_to(cols[j][j : j + 1, :], (8, 128))
            pivots = jnp.where(sub == j, pivot, pivots)
            r = 1.0 / pivot
            inv.append(r)
            if j == 7:
                break
            m = jnp.where(sub > j, cols[j] * r, 0.0)
            for k in range(j + 1, 8):
                cross[j, k] = jnp.broadcast_to(cols[k][j : j + 1, :], (8, 128))
                cols[k] = cols[k] - m * cross[j, k]
            own = own - m * jnp.broadcast_to(own[j : j + 1, :], (8, 128))
        tiles[t] = own
        scales.append(lax.rsqrt(pivots))
        rows = [jnp.broadcast_to(own[j : j + 1, :], (8, 128)) for j in range(8)]
        for i in range(t + 1, 8):
            low = tiles[i]
            cols = [lanes(low, 8 * t + j) for j in range(8)]
            for j in range(8):
                m = cols[j] * inv[j]
                for k in range(j + 1, 8):
                    cols[k] = cols[k] - m * cross[j, k]
                low = low - m * rows[j]
            tiles[i] = low
    return tiles, scales


def factor_block(work, small, inverse_small):
    for b in range(B // S):
        lo, hi = b * S, (b + 1) * S
        small[:, 0:S] = work[lo:hi, lo:hi]
        row = lax.broadcasted_iota(jnp.int32, (S, S), 0)
        col = lax.broadcasted_iota(jnp.int32, (S, S), 1)
        small[:, S : 2 * S] = jnp.where(row == col, 1.0, 0.0)
        tiles, scales = eliminate([small[8 * i : 8 * i + 8, :] for i in range(8)])
        for i in range(8):
            small[8 * i : 8 * i + 8, :] = tiles[i] * scales[i]
        inverse_small[...] = small[:, S : 2 * S]
        top = dot(inverse_small[...], work[lo:hi, :], NN, HIGH)
        work[lo:hi, :] = top
        if hi < B:
            work[hi:B, :] = work[hi:B, :] - dot(top[:, hi:B], top, TN, HIGH)


def factor_kernel(diag_ref, packed_ref, l10t_ref, work, small, inverse_small):
    row = lax.broadcasted_iota(jnp.int32, (B, B), 0)
    col = lax.broadcasted_iota(jnp.int32, (B, B), 1)
    eye = jnp.where(row == col, 1.0, 0.0)
    work[:, 0:B] = diag_ref[:, 0:B]
    work[:, B : 2 * B] = eye
    factor_block(work, small, inverse_small)
    x0 = work[:, B : 2 * B]
    packed_ref[:, 0:B] = x0
    packed_ref[:, 2 * B : 3 * B] = jnp.where(row <= col, work[:, 0:B], 0.0).T
    l10t = dot(x0, diag_ref[:, B : 2 * B], NN, HIGH).astype(BF16)
    l10t_ref[...] = l10t
    work[:, 0:B] = diag_ref[:, 2 * B : 3 * B] - dot(l10t, l10t, TN)
    work[:, B : 2 * B] = eye
    factor_block(work, small, inverse_small)
    packed_ref[:, B : 2 * B] = work[:, B : 2 * B]
    packed_ref[:, 3 * B : 4 * B] = jnp.where(row <= col, work[:, 0:B], 0.0).T


def factor_diagonal(diag):
    return pl.pallas_call(
        factor_kernel,
        in_specs=[VMEM_SPEC],
        out_specs=[VMEM_SPEC] * 2,
        out_shape=[jax.ShapeDtypeStruct((B, 4 * B), F32), jax.ShapeDtypeStruct((B, B), BF16)],
        scratch_shapes=[pltpu.VMEM((B, 2 * B), F32), pltpu.VMEM((S, 2 * S), F32), pltpu.VMEM((S, S), F32)],
        compiler_params=pltpu.CompilerParams(vmem_limit_bytes=VMEM_BYTES),
        cost_estimate=pl.CostEstimate(flops=2 * 10**10, bytes_accessed=80_000_000, transcendentals=0),
    )(diag)


def solve_rows(first, second, packed_ref, l10t_ref):
    p0 = dot(first, packed_ref[:, 0:B], NT, HIGH)
    p1 = dot(second - dot(p0.astype(BF16), l10t_ref[...], NN), packed_ref[:, B : 2 * B], NT, HIGH)
    return p0, p1


def across_kernel(flags, across_ref, packed_ref, l10t_ref, pc_ref, white_ref, raw):
    k = pl.program_id(0)
    pairs, part = pc_ref.shape[2], pc_ref.shape[3]
    blocks = pc_ref.shape[1]
    held = blocks * part
    half = raw.shape[0] // 2
    fold = half // 2

    p0, p1 = solve_rows(
        across_ref[:, 0:held, 0:B].reshape(4 * held, B),
        across_ref[:, 0:held, B : 2 * B].reshape(4 * held, B),
        packed_ref,
        l10t_ref,
    )
    p0, p1 = p0.astype(BF16), p1.astype(BF16)
    for n in range(4):
        h, parity = n // 2, n % 2
        for b in range(blocks):
            here = slice(n * held + b * part, n * held + (b + 1) * part)
            level = flags[8 + parity * blocks + b]
            pc_ref[parity, b, h, :, 0:B] = jnp.where(level > 0, p0[here], jnp.zeros_like(p0[here]))
            pc_ref[parity, b, h, :, B : 2 * B] = jnp.where(level > 1, p1[here], jnp.zeros_like(p1[here]))

    for panel in range(2):

        @pl.when(k == flags[6 + panel])
        def _():
            for n in range(4):
                h, parity = n // 2, n % 2
                for f in range(2):
                    lane = (2 * f + panel) * 128
                    raw[
                        parity * half + f * fold : parity * half + (f + 1) * fold,
                        panel * B + h * 128 : panel * B + (h + 1) * 128,
                    ] = across_ref[n, held : held + fold, lane : lane + 128]

    @pl.when(k == pl.num_programs(0) - 1)
    def _():
        w0, w1 = solve_rows(raw[:, 0:B], raw[:, B : 2 * B], packed_ref, l10t_ref)
        white_ref[:, 0:B] = w0
        white_ref[:, B : 2 * B] = w1


def whole(*shape):
    return pl.BlockSpec(shape, lambda i, flags: (0,) * len(shape))


def solve_across(flags, across, packed, l10t, blocks, parts, particles):
    part = B // parts
    steps = across.shape[0] // 4
    return pl.pallas_call(
        across_kernel,
        grid_spec=pltpu.PrefetchScalarGridSpec(
            num_scalar_prefetch=1,
            grid=(steps,),
            in_specs=[
                pl.BlockSpec((4,) + across.shape[1:], lambda k, flags: (k, 0, 0)),
                whole(*packed.shape),
                whole(*l10t.shape),
            ],
            out_specs=[
                pl.BlockSpec(
                    (2, blocks, 2, part, 2 * B), lambda k, flags: (0, 0, lax.rem(k + steps - flags[0], steps), 0, 0)
                ),
                whole(particles, 2 * B),
            ],
            scratch_shapes=[pltpu.VMEM((particles, 2 * B), F32)],
        ),
        out_shape=[
            jax.ShapeDtypeStruct((2, blocks, parts, part, 2 * B), BF16),
            jax.ShapeDtypeStruct((particles, 2 * B), F32),
        ],
        compiler_params=pltpu.CompilerParams(vmem_limit_bytes=VMEM_BYTES),
        cost_estimate=pl.CostEstimate(flops=6 * 10**9, bytes_accessed=8_000_000, transcendentals=0),
    )(flags, across, packed, l10t)


def update_kernel(flags, cov_ref, along_ref, pc_ref, white_ref, packed_ref, l10t_ref, out_ref, product_ref):
    i = pl.program_id(0)
    parts, part = along_ref.shape[0], along_ref.shape[2]
    column_blocks = pc_ref.shape[0] // B

    level = flags[16 + i]
    raw = along_ref[:, 0].reshape(parts * part, 2 * B)
    p0, p1 = solve_rows(raw[:, 0:B], raw[:, B : 2 * B], packed_ref, l10t_ref)
    p0 = jnp.where(level > 0, p0, 0.0)
    p1 = jnp.where(level > 1, p1, 0.0)
    rows = jnp.concatenate([p0.astype(BF16), p1.astype(BF16)], axis=1)
    for n in range(column_blocks):
        cut = slice(n * B, (n + 1) * B)
        out_ref[:, cut] = cov_ref[:, cut] - dot(rows, pc_ref[cut, :], NT)
    product_ref[...] = dot(white_ref[...].astype(BF16), rows, NT)

    for panel, solved in ((0, p0), (1, p1)):
        is_row = i == flags[2 + panel]
        for n in range(column_blocks):

            @pl.when(is_row & (flags[8 + n] > panel))
            def _():
                out_ref[:, n * B : (n + 1) * B] = jnp.zeros((B, B), F32)

        column = flags[4 + panel]
        place = pl.ds(pl.multiple_of(jnp.maximum(column, 0) * B, B), B)

        @pl.when((column >= 0) & (level > panel))
        def _():
            out_ref[:, place] = solved

        @pl.when((column >= 0) & is_row)
        def _():
            out_ref[:, place] = packed_ref[:, (2 + panel) * B : (3 + panel) * B]


def update(flags, covariance, along, pc, white, packed, l10t):
    rows, columns = covariance.shape
    blocks = rows // B
    parts = along.shape[0]
    part = B // parts
    particles = white.shape[0]
    return pl.pallas_call(
        update_kernel,
        grid_spec=pltpu.PrefetchScalarGridSpec(
            num_scalar_prefetch=1,
            grid=(blocks,),
            in_specs=[
                pl.BlockSpec((B, columns), lambda i, flags: (i, 0)),
                pl.BlockSpec((parts, 1, part, 2 * B), lambda i, flags: (0, i, 0, 0)),
                whole(*pc.shape),
                whole(*white.shape),
                whole(*packed.shape),
                whole(*l10t.shape),
            ],
            out_specs=[
                pl.BlockSpec((B, columns), lambda i, flags: (i, 0)),
                pl.BlockSpec((particles, B), lambda i, flags: (0, i)),
            ],
        ),
        out_shape=[jax.ShapeDtypeStruct((rows, columns), F32), jax.ShapeDtypeStruct((particles, rows), F32)],
        compiler_params=pltpu.CompilerParams(vmem_limit_bytes=VMEM_BYTES),
        cost_estimate=pl.CostEstimate(flops=5 * 10**9, bytes_accessed=20_000_000, transcendentals=0),
    )(flags, covariance, along, pc, white, packed, l10t)


def forward_kernel(flags, relaid_ref, product_ref, white_ref, out_ref):
    half, width = relaid_ref.shape[1:]
    steps = relaid_ref.shape[0] // 4
    for q in range(relaid_ref.shape[0] // 2):
        first = lax.rem(q // 2 + flags[0], steps) * 4 + q % 2 * 2
        for parity in range(2):
            there = (slice(parity * half, (parity + 1) * half), slice(q * width, (q + 1) * width))
            out_ref[there] = relaid_ref[first + parity] - product_ref[there]
    for panel in range(2):
        block = flags[2 + panel]

        @pl.when(block >= 0)
        def _():
            place = pl.ds(pl.multiple_of(jnp.maximum(block, 0) * B, B), B)
            out_ref[:, place] = white_ref[:, panel * B : (panel + 1) * B]


def forward(flags, relaid, product, white):
    return pl.pallas_call(
        forward_kernel,
        in_specs=[SMEM_SPEC] + [VMEM_SPEC] * 3,
        out_specs=VMEM_SPEC,
        out_shape=jax.ShapeDtypeStruct(product.shape, F32),
        compiler_params=pltpu.CompilerParams(vmem_limit_bytes=VMEM_BYTES),
        cost_estimate=pl.CostEstimate(flops=10**6, bytes_accessed=2_000_000, transcendentals=0),
    )(flags, relaid, product, white)


def per_device(covariance, innovations, block_owner, panel_index, *, n_row, n_col):
    local_rows, local_cols = covariance.shape
    row_blocks, column_blocks = local_rows // B, local_cols // B
    r, c = lax.axis_index("row"), lax.axis_index("col")
    targets = panel_index[0] + jnp.arange(2, dtype=jnp.int32)
    positions = jnp.arange(block_owner.shape[0], dtype=jnp.int32)
    slot = jnp.sum(jnp.where(block_owner[None, :] == targets[:, None], positions[None, :], 0), axis=1)
    row_root, column_root = slot // row_blocks, slot // column_blocks
    row_slot, column_slot = slot % row_blocks, slot % column_blocks
    levels = jnp.sum((block_owner[:, None] > targets[None, :]).astype(jnp.int32), axis=1)
    steps = n_row // 4
    shift = c // 2
    flags = jnp.concatenate(
        [
            jnp.full((2,), shift, jnp.int32),
            jnp.where(row_root == r, row_slot, -1),
            jnp.where(column_root == c, column_slot, -1),
            (row_slot + shift) % steps,
            lax.dynamic_slice_in_dim(levels, c * column_blocks, column_blocks),
            lax.dynamic_slice_in_dim(levels, r * row_blocks, row_blocks),
        ]
    ).astype(jnp.int32)
    across_axes = [
        (a * n_col + b, ((b // 2 + a // 4) % steps * 4 + b % 2 * 2 + a % 2) * n_col + a // 2)
        for a in range(n_row)
        for b in range(n_col)
    ]

    turned = lax.ppermute(jnp.transpose(innovations, (1, 0, 2)), ("row", "col"), across_axes)

    picked = pick_columns(column_slot.astype(jnp.int32), covariance, n_col)
    parts = lax.all_to_all(picked, "col", split_axis=0, concat_axis=0, tiled=True)
    part = parts.shape[2]
    piece = jnp.concatenate(
        [
            lax.dynamic_slice(parts, (column_root[n], 0, 0, n * B), (1, row_blocks, part, B))[0]
            for n in range(2)
        ],
        axis=-1,
    )

    chosen = jnp.where(r == row_root[0], row_slot[0], row_slot[1])
    mine = lax.dynamic_index_in_dim(piece, chosen, 0, keepdims=False)
    spread = lax.all_to_all(
        jnp.broadcast_to(mine[None], (n_row,) + mine.shape), "row", split_axis=0, concat_axis=0, tiled=True
    )
    upper = lax.dynamic_slice(spread, (row_root[0], 0, 0), (1, part, 2 * B))[0]
    lower = lax.dynamic_slice(spread, (row_root[1], 0, B), (1, part, B))[0]
    strip = jnp.concatenate([upper, lower], axis=-1)
    diag = lax.all_to_all(
        jnp.broadcast_to(strip[None], (n_col,) + strip.shape), "col", split_axis=0, concat_axis=0, tiled=True
    ).reshape(B, 3 * B)

    tiled = lax.ppermute(piece.reshape(row_blocks * part, 2 * B), ("row", "col"), across_axes)
    wanted = [lax.dynamic_index_in_dim(turned, row_root[n], 0, keepdims=False) for n in range(2)]
    fold = wanted[0].shape[0] // 2
    wanted = jnp.concatenate([wanted[0][:fold], wanted[1][:fold], wanted[0][fold:], wanted[1][fold:]], axis=1)
    payload, _ = lax.optimization_barrier((jnp.concatenate([tiled, wanted], axis=0), spread))
    across = lax.all_gather(payload, "row", axis=0)

    packed, l10t = factor_diagonal(diag)

    along = lax.all_to_all(
        jnp.broadcast_to(piece[None], (n_col,) + piece.shape), "col", split_axis=0, concat_axis=0, tiled=True
    )
    relaid = lax.all_to_all(turned, "row", split_axis=0, concat_axis=0, tiled=True)

    pc, white = solve_across(flags, across, packed, l10t, row_blocks, n_col, 2 * turned.shape[1])
    matrix, product = update(flags, covariance, along, pc.reshape(local_cols, 2 * B), white, packed, l10t)
    solved = forward(flags, relaid, product, white)
    return matrix, solved


def solution(mesh):
    placed = (P("row", "col"), P("row", None, "col"), P(), P())
    return jax.shard_map(
        functools.partial(per_device, n_row=mesh.shape["row"], n_col=mesh.shape["col"]),
        mesh=mesh,
        in_specs=placed,
        out_specs=(P("row", "col"), P("col", "row")),
        check_vma=False,
    )
```

time: 256 us -> 198 us (0.77)
  blocking collectives: 51.3 us -> 0 us
  starting transfers between devices: 27.1 us -> 44.8 us
  waiting for transfers between devices: 80.1 us -> 63.2 us
  local copies, waits for them, and re-layouts: 15.6 us -> 7.43 us
    all_to_all x1 -> x0, blocking collectives: 51.3 us -> none  [per_device(): lax.all_to_all(jnp.broadcast_to(mine[None], (n_row,) + mine.shape), 'row'...]
    all_to_all x1, waiting for transfers between devices: 53.2 us -> 21.6 us  [per_device(): lax.all_to_all(picked, 'col', split_axis=0, concat_axis=0, tiled=True)]
    all_to_all x1, starting transfers between devices: 8.33 us -> 22.8 us  [per_device(): lax.all_to_all(jnp.broadcast_to(strip[None], (n_col,) + strip.shape), 'co...]
    pallas_call x1 -> x2, Pallas kernels: 2.78 us -> 14.4 us  [the longest x1 12.3 us: solve_across(): pl.pallas_call(across_kernel, grid_spec=pltpu.PrefetchScalarGridSpec(num_...]
    pallas_call x1, Pallas kernels: 22.6 us -> 13.2 us  [update(): pl.pallas_call(update_kernel, grid_spec=pltpu.PrefetchScalarGridSpec(num_...]
    all_to_all x0 -> x1, waiting for transfers between devices: none -> 8.77 us  [per_device(): lax.all_to_all(jnp.broadcast_to(mine[None], (n_row,) + mine.shape), 'row'...]
    unnamed x29 -> x11, local copies, waits for them, and re-layouts: 9.57 us -> 0.97 us
    all_to_all x0 -> x1, starting transfers between devices: none -> 4.52 us  [per_device(): lax.all_to_all(jnp.broadcast_to(mine[None], (n_row,) + mine.shape), 'row'...]
  transfers between devices with their start and end apart: 7 -> 8, of which waited for: 3 -> 4; matrix products, arithmetic and copies ran while one was open for 2% -> 3% of each run, Pallas kernels for 18% -> 24%
where the time goes in v2:
time: 198 us; the launch traced here: 196 us
  waiting for transfers between devices  63.2 us (32%)
  Pallas kernels  54.4 us (27%)
  starting transfers between devices  44.8 us (23%)
  between operations  24.3 us (12%)
  local copies, waits for them, and re-layouts  7.43 us (4%)
  other arithmetic  2.28 us (1%)
    all_to_all x1, starting transfers between devices, per_device(): lax.all_to_all(jnp.broadcast_to(strip[None], (n_col,) + strip.shape), 'co...  22.8 us
    all_to_all x1, waiting for transfers between devices, per_device(): lax.all_to_all(jnp.broadcast_to(strip[None], (n_col,) + strip.shape), 'co...  22.3 us
    pallas_call x1, Pallas kernels, factor_diagonal(): pl.pallas_call(factor_kernel, in_specs=[VMEM_SPEC], out_specs=[VMEM_SPEC]...  22.2 us
    all_to_all x1, waiting for transfers between devices, per_device(): lax.all_to_all(picked, 'col', split_axis=0, concat_axis=0, tiled=True)  21.6 us
    pallas_call x1, Pallas kernels, update(): pl.pallas_call(update_kernel, grid_spec=pltpu.PrefetchScalarGridSpec(num_...  13.2 us
    pallas_call x1, Pallas kernels, solve_across(): pl.pallas_call(across_kernel, grid_spec=pltpu.PrefetchScalarGridSpec(num_...  12.3 us
    all_to_all x1, waiting for transfers between devices, per_device(): lax.all_to_all(jnp.broadcast_to(piece[None], (n_col,) + piece.shape), 'co...  10.6 us
    all_to_all x1, waiting for transfers between devices, per_device(): lax.all_to_all(jnp.broadcast_to(mine[None], (n_row,) + mine.shape), 'row'...  8.77 us
  transfers between devices with their start and end apart: 8, of which 4 were waited for; matrix products, arithmetic and copies ran while one was open for 3% of the time, Pallas kernels for 24%

profile of v2, /device:TPU:0, one launch (start us, length us, event | category | flops | bytes accessed | tf_op | source)
XLA Modules:
  0.0 196.5 jit_solution(4336800694323107002)
XLA Ops:
  7.8 0.8 fusion.2
  9.2 4.5 %shard_map.59 = f32[8,4,32,512]{3,2,1,0:T(8,128)} custom-call(s32[2]{0:T(128)} %get-tuple-element.20.slots, f32[1024,2048]{1,0:T(8,128)} %cov_ref.3), custom_call_target="tpu_custom_call" | custom-call | tf_op jit(solution)/shard_map/pallas_call | solution.py:39
  13.7 8.0 %all-to-all-start = ((f32[8,4,32,512]{3,2,1,0:T(8,128)}), f32[8,4,32,512]{3,2,1,0:T(8,128)S(1)}, u32[]{:S(2)}, u32[]{:S(2)}) async-start(f32[8,4,32,512]{3,2,1,0:T(8,128)} %shard_map.59), calls=%async_computation | async-start | bytes 4194304 | tf_op jit(solution)/shard_map/all_to_all | solution.py:346
  28.6 21.6 %all-to-all-done = f32[8,4,32,512]{3,2,1,0:T(8,128)S(1)} async-done(((f32[8,4,32,512]{3,2,1,0:T(8,128)}), f32[8,4,32,512]{3,2,1,0:T(8,128)S(1)}, u32[]{:S(2)}, u32[]{:S(2)}) %all-to-all-start) | async-done | bytes 2097184 | tf_op jit(solution)/shard_map/all_to_all | solution.py:346
  50.2 1.1 broadcast_in_dim.48
  51.3 4.5 %all-to-all-start.2 = ((f32[16,32,512]{2,1,0:T(8,128)}), f32[16,32,512]{2,1,0:T(8,128)S(1)}, u32[]{:S(2)}, u32[]{:S(2)}) async-start(f32[16,32,512]{2,1,0:T(8,128)} %broadcast_in_dim.48), calls=%async_computation.2 | async-start | bytes 2097152 | tf_op jit(solution)/shard_map/all_to_all | solution.py:358
  56.1 1.5 collective-permute-start.1
  57.6 0.7 collective-permute-start
  62.0 0.8 dynamic-slice_bitcast_fusion.5
  62.8 0.8 maximum_maximum_fusion
  63.6 8.8 %all-to-all-done.2 = f32[16,32,512]{2,1,0:T(8,128)S(1)} async-done(((f32[16,32,512]{2,1,0:T(8,128)}), f32[16,32,512]{2,1,0:T(8,128)S(1)}, u32[]{:S(2)}, u32[]{:S(2)}) %all-to-all-start.2) | async-done | bytes 1048608 | tf_op jit(solution)/shard_map/all_to_all | solution.py:358
  72.4 0.9 broadcast_in_dim.49
  73.3 22.8 %all-to-all-start.3 = ((f32[8,32,768]{2,1,0:T(8,128)}), f32[8,32,768]{2,1,0:T(8,128)S(1)}, u32[]{:S(2)}, u32[]{:S(2)}) async-start(f32[8,32,768]{2,1,0:T(8,128)} %broadcast_in_dim.49), calls=%async_computation.3 | async-start | bytes 1572864 | tf_op jit(solution)/shard_map/all_to_all | solution.py:364
  96.3 0.7 concatenate.22.flags
  97.0 22.3 %all-to-all-done.3 = f32[8,32,768]{2,1,0:T(8,128)S(1)} async-done(((f32[8,32,768]{2,1,0:T(8,128)}), f32[8,32,768]{2,1,0:T(8,128)S(1)}, u32[]{:S(2)}, u32[]{:S(2)}) %all-to-all-start.3) | async-done | bytes 786464 | tf_op jit(solution)/shard_map/all_to_all | solution.py:364
  119.3 1.6 broadcast_in_dim.46
  120.9 3.6 %all-to-all-start.1 = ((f32[8,4,32,512]{3,2,1,0:T(8,128)}), f32[8,4,32,512]{3,2,1,0:T(8,128)S(1)}, u32[]{:S(2)}, u32[]{:S(2)}) async-start(f32[8,4,32,512]{3,2,1,0:T(8,128)} %broadcast_in_dim.46), calls=%async_computation.1 | async-start | bytes 4194304 | tf_op jit(solution)/shard_map/all_to_all | solution.py:377
  124.5 22.2 %shard_map.60 = (f32[256,1024]{1,0:T(8,128)}, bf16[256,256]{1,0:T(8,128)(2,1)}) custom-call(f32[256,768]{1,0:T(8,128)} %bitcast.38), custom_call_target="tpu_custom_call" | custom-call | flops 20000000000 | bytes 80000000 | tf_op jit(solution)/shard_map/pallas_call | solution.py:127
  146.7 10.6 %all-to-all-done.1.along_ref = f32[8,4,32,512]{3,2,1,0:T(8,128)S(1)} async-done(((f32[8,4,32,512]{3,2,1,0:T(8,128)}), f32[8,4,32,512]{3,2,1,0:T(8,128)S(1)}, u32[]{:S(2)}, u32[]{:S(2)}) %all-to-all-start.1) | async-done | bytes 2097184 | tf_op jit(solution)/shard_map/all_to_all | solution.py:377
  157.3 3.8 %all-to-all-start.4 = ((f32[16,64,128]{2,1,0:T(8,128)}), f32[16,64,128]{2,1,0:T(8,128)S(1)}, u32[]{:S(2)}, u32[]{:S(2)}) async-start(f32[16,64,128]{2,1,0:T(8,128)} %collective-permute-done.1), calls=%async_computation.4 | async-start | bytes 1048576 | tf_op jit(solution)/shard_map/all_to_all | solution.py:380
  161.1 12.3 %shard_map.61 = (bf16[2,4,8,32,512]{4,3,2,1,0:T(8,128)(2,1)}, f32[128,512]{1,0:T(8,128)}) custom-call(s32[20]{0:T(128)} %concatenate.22.flags, f32[16,160,512]{2,1,0:T(8,128)} %bitcast.40, f32[256,1024]{1,0:T(8,128)} %get-tuple-element.10.packed_ref, bf16[256,256]{1,0:T(8,128)(2,1)} %get-tuple-element.11.l10t_ref), custom_call_target="tpu_custom_call" | custom-call | flops 6000000000 | bytes 8000000 | tf_op jit(solution)/shard_map/pallas_call | solution.py:194
  173.4 13.2 %shard_map.62 = (f32[1024,2048]{1,0:T(8,128)}, f32[128,1024]{1,0:T(8,128)}) custom-call(s32[20]{0:T(128)} %concatenate.22.flags, f32[1024,2048]{1,0:T(8,128)} %cov_ref.3, f32[8,4,32,512]{3,2,1,0:T(8,128)} %copy-done, bf16[2048,512]{1,0:T(8,128)(2,1)} %bitcast.41, f32[128,512]{1,0:T(8,128)} %get-tuple-element.13.white_ref, ...), custom_call_target="tpu_custom_call" | custom-call | flops 5000000000 | bytes 20000000 | tf_op jit(solution)/shard_map/pallas_call | solution.py:263
  186.7 0.8 copy-done.1
  187.5 2.1 %shard_map.63 = f32[128,1024]{1,0:T(8,128)} custom-call(s32[20]{0:T(128)} %concatenate.22.flags, f32[16,64,128]{2,1,0:T(8,128)} %copy-done.1, f32[128,1024]{1,0:T(8,128)} %get-tuple-element.15.product_ref, f32[128,512]{1,0:T(8,128)} %get-tuple-element.13.white_ref), custom_call_target="tpu_custom_call" | custom-call | flops 1000000 | bytes 2000000 | tf_op jit(solution)/shard_map/pallas_call | solution.py:305
  (32 shorter events, 2.3 us)
Async XLA Ops:
  13.7 36.5 %all-to-all-start = ((f32[8,4,32,512]{3,2,1,0:T(8,128)}), f32[8,4,32,512]{3,2,1,0:T(8,128)S(1)}, u32[]{:S(2)}, u32[]{:S(2)}) async-start(f32[8,4,32,512]{3,2,1,0:T(8,128)} %shard_map.59), calls=%async_computation | async-start | bytes 4194304 | tf_op jit(solution)/shard_map/all_to_all | solution.py:346
  21.7 34.2 %copy-start.3 = (f32[64,16,128]{2,1,0:T(8,128)S(1)}, f32[64,16,128]{2,1,0:T(8,128)}, u32[]{:S(2)}) copy-start(f32[64,16,128]{2,1,0:T(8,128)} %param.5) | copy-start | bytes 1572868
  51.3 21.0 %all-to-all-start.2 = ((f32[16,32,512]{2,1,0:T(8,128)}), f32[16,32,512]{2,1,0:T(8,128)S(1)}, u32[]{:S(2)}, u32[]{:S(2)}) async-start(f32[16,32,512]{2,1,0:T(8,128)} %broadcast_in_dim.48), calls=%async_computation.2 | async-start | bytes 2097152 | tf_op jit(solution)/shard_map/all_to_all | solution.py:358
  55.8 105.3 %all-gather.3.cloned.1.call-start = ((), (), s32[]{:S(2)}) async-start(), calls=%async_computation.5 | async-start | bytes 5570560 | tf_op jit(solution)/shard_map/all_gather | solution.py:373
  56.1 5.9 %collective-permute-start.1 = (f32[16,64,128]{2,1,0:T(8,128)S(1)}, f32[16,64,128]{2,1,0:T(8,128)}, u32[]{:S(2)}, u32[]{:S(2)}) collective-permute-start(f32[16,64,128]{2,1,0:T(8,128)S(1)} %bitcast.39), channel_id=1, source_target_pairs={{0,0},{1,16},{2,32},{3,48},{4,64},{5,80},{6,96},{7,112},{8,8},{9,2... | collective-permute-start | bytes 1572872 | tf_op jit(solution)/shard_map/ppermute | solution.py:343
  57.6 38.5 %copy-start.4 = (s32[64]{0:T(128)S(1)}, s32[64]{0:T(128)}, u32[]{:S(2)}) copy-start(s32[64]{0:T(128)} %param.6) | copy-start | bytes 772
  57.6 5.2 %collective-permute-start = (f32[128,512]{1,0:T(8,128)S(1)}, f32[128,512]{1,0:T(8,128)S(1)}, u32[]{:S(2)}, u32[]{:S(2)}) collective-permute-start(f32[128,512]{1,0:T(8,128)S(1)} %pad_maximum_fusion.1), channel_id=1, source_target_pairs={{0,0},{1,16},{2,32},{3,48},{4,64},{5,80},{6,96},{7,112},{8,8},{9,2... | collective-permute-start | bytes 786440 | tf_op jit(solution)/shard_map/ppermute | solution.py:368
  73.3 45.9 %all-to-all-start.3 = ((f32[8,32,768]{2,1,0:T(8,128)}), f32[8,32,768]{2,1,0:T(8,128)S(1)}, u32[]{:S(2)}, u32[]{:S(2)}) async-start(f32[8,32,768]{2,1,0:T(8,128)} %broadcast_in_dim.49), calls=%async_computation.3 | async-start | bytes 1572864 | tf_op jit(solution)/shard_map/all_to_all | solution.py:364
  119.3 1.6 copy-start.2
  120.9 36.5 %all-to-all-start.1 = ((f32[8,4,32,512]{3,2,1,0:T(8,128)}), f32[8,4,32,512]{3,2,1,0:T(8,128)S(1)}, u32[]{:S(2)}, u32[]{:S(2)}) async-start(f32[8,4,32,512]{3,2,1,0:T(8,128)} %broadcast_in_dim.46), calls=%async_computation.1 | async-start | bytes 4194304 | tf_op jit(solution)/shard_map/all_to_all | solution.py:377
  157.3 16.1 %copy-start = (f32[8,4,32,512]{3,2,1,0:T(8,128)}, f32[8,4,32,512]{3,2,1,0:T(8,128)S(1)}, u32[]{:S(2)}) copy-start(f32[8,4,32,512]{3,2,1,0:T(8,128)S(1)} %all-to-all-done.1.along_ref) | copy-start | bytes 6291460
  157.3 29.3 %all-to-all-start.4 = ((f32[16,64,128]{2,1,0:T(8,128)}), f32[16,64,128]{2,1,0:T(8,128)S(1)}, u32[]{:S(2)}, u32[]{:S(2)}) async-start(f32[16,64,128]{2,1,0:T(8,128)} %collective-permute-done.1), calls=%async_computation.4 | async-start | bytes 1048576 | tf_op jit(solution)/shard_map/all_to_all | solution.py:380
  186.7 0.8 copy-start.1
Sparse Core Ops, SparseCore 0:
  72.5 67.2 all-gather.2

commit v3 on v2

--- a/solution.py
+++ b/solution.py
@@ -104,7 +104,26 @@
             work[hi:B, :] = work[hi:B, :] - dot(top[:, hi:B], top, TN, HIGH)
 
 
-def factor_kernel(diag_ref, packed_ref, l10t_ref, work, small, inverse_small):
+def split(a):
+    high = a.astype(BF16)
+    rest = a - high.astype(F32)
+    middle = rest.astype(BF16)
+    return high, middle, (rest - middle.astype(F32)).astype(BF16)
+
+
+def write_left(ref, a):
+    high, middle, low = split(a)
+    for n, term in enumerate((high, high, middle, high, low, middle)):
+        ref[:, n * B : (n + 1) * B] = term
+
+
+def write_right(ref, start, a):
+    high, middle, low = split(a)
+    for n, term in enumerate((high, middle, high, low, high, middle)):
+        ref[:, start + n * B : start + (n + 1) * B] = term
+
+
+def factor_kernel(diag_ref, inverse_ref, l10t_ref, lower_ref, work, small, inverse_small):
     row = lax.broadcasted_iota(jnp.int32, (B, B), 0)
     col = lax.broadcasted_iota(jnp.int32, (B, B), 1)
     eye = jnp.where(row == col, 1.0, 0.0)
@@ -112,38 +131,44 @@
     work[:, B : 2 * B] = eye
     factor_block(work, small, inverse_small)
     x0 = work[:, B : 2 * B]
-    packed_ref[:, 0:B] = x0
-    packed_ref[:, 2 * B : 3 * B] = jnp.where(row <= col, work[:, 0:B], 0.0).T
+    write_right(inverse_ref, 0, x0)
+    lower_ref[:, 0:B] = jnp.where(row <= col, work[:, 0:B], 0.0).T
     l10t = dot(x0, diag_ref[:, B : 2 * B], NN, HIGH).astype(BF16)
     l10t_ref[...] = l10t
     work[:, 0:B] = diag_ref[:, 2 * B : 3 * B] - dot(l10t, l10t, TN)
     work[:, B : 2 * B] = eye
     factor_block(work, small, inverse_small)
-    packed_ref[:, B : 2 * B] = work[:, B : 2 * B]
-    packed_ref[:, 3 * B : 4 * B] = jnp.where(row <= col, work[:, 0:B], 0.0).T
+    write_right(inverse_ref, 6 * B, work[:, B : 2 * B])
+    lower_ref[:, B : 2 * B] = jnp.where(row <= col, work[:, 0:B], 0.0).T
 
 
 def factor_diagonal(diag):
     return pl.pallas_call(
         factor_kernel,
         in_specs=[VMEM_SPEC],
-        out_specs=[VMEM_SPEC] * 2,
-        out_shape=[jax.ShapeDtypeStruct((B, 4 * B), F32), jax.ShapeDtypeStruct((B, B), BF16)],
+        out_specs=[VMEM_SPEC] * 3,
+        out_shape=[
+            jax.ShapeDtypeStruct((B, 12 * B), BF16),
+            jax.ShapeDtypeStruct((B, B), BF16),
+            jax.ShapeDtypeStruct((B, 2 * B), F32),
+        ],
         scratch_shapes=[pltpu.VMEM((B, 2 * B), F32), pltpu.VMEM((S, 2 * S), F32), pltpu.VMEM((S, S), F32)],
         compiler_params=pltpu.CompilerParams(vmem_limit_bytes=VMEM_BYTES),
         cost_estimate=pl.CostEstimate(flops=2 * 10**10, bytes_accessed=80_000_000, transcendentals=0),
     )(diag)
 
 
-def solve_rows(first, second, packed_ref, l10t_ref):
-    p0 = dot(first, packed_ref[:, 0:B], NT, HIGH)
-    p1 = dot(second - dot(p0.astype(BF16), l10t_ref[...], NN), packed_ref[:, B : 2 * B], NT, HIGH)
+def solve_rows(first, second, wide, inverse_ref, l10t_ref):
+    write_left(wide, first)
+    p0 = dot(wide[...], inverse_ref[:, 0 : 6 * B], NT)
+    write_left(wide, second - dot(p0.astype(BF16), l10t_ref[...], NN))
+    p1 = dot(wide[...], inverse_ref[:, 6 * B : 12 * B], NT)
     return p0, p1
 
 
-def across_kernel(flags, across_ref, packed_ref, l10t_ref, pc_ref, white_ref, raw):
+def across_kernel(flags, across_ref, inverse_ref, l10t_ref, pc_ref, white_ref, raw, wide, wide_white):
     k = pl.program_id(0)
-    pairs, part = pc_ref.shape[2], pc_ref.shape[3]
+    part = pc_ref.shape[3]
     blocks = pc_ref.shape[1]
     held = blocks * part
     half = raw.shape[0] // 2
@@ -152,7 +177,8 @@
     p0, p1 = solve_rows(
         across_ref[:, 0:held, 0:B].reshape(4 * held, B),
         across_ref[:, 0:held, B : 2 * B].reshape(4 * held, B),
-        packed_ref,
+        wide,
+        inverse_ref,
         l10t_ref,
     )
     p0, p1 = p0.astype(BF16), p1.astype(BF16)
@@ -179,7 +205,7 @@
 
     @pl.when(k == pl.num_programs(0) - 1)
     def _():
-        w0, w1 = solve_rows(raw[:, 0:B], raw[:, B : 2 * B], packed_ref, l10t_ref)
+        w0, w1 = solve_rows(raw[:, 0:B], raw[:, B : 2 * B], wide_white, inverse_ref, l10t_ref)
         white_ref[:, 0:B] = w0
         white_ref[:, B : 2 * B] = w1
 
@@ -188,7 +214,7 @@
     return pl.BlockSpec(shape, lambda i, flags: (0,) * len(shape))
 
 
-def solve_across(flags, across, packed, l10t, blocks, parts, particles):
+def solve_across(flags, across, inverse, l10t, blocks, parts, particles):
     part = B // parts
     steps = across.shape[0] // 4
     return pl.pallas_call(
@@ -198,7 +224,7 @@
             grid=(steps,),
             in_specs=[
                 pl.BlockSpec((4,) + across.shape[1:], lambda k, flags: (k, 0, 0)),
-                whole(*packed.shape),
+                whole(*inverse.shape),
                 whole(*l10t.shape),
             ],
             out_specs=[
@@ -207,7 +233,11 @@
                 ),
                 whole(particles, 2 * B),
             ],
-            scratch_shapes=[pltpu.VMEM((particles, 2 * B), F32)],
+            scratch_shapes=[
+                pltpu.VMEM((particles, 2 * B), F32),
+                pltpu.VMEM((4 * blocks * part, 6 * B), BF16),
+                pltpu.VMEM((particles, 6 * B), BF16),
+            ],
         ),
         out_shape=[
             jax.ShapeDtypeStruct((2, blocks, parts, part, 2 * B), BF16),
@@ -215,24 +245,26 @@
         ],
         compiler_params=pltpu.CompilerParams(vmem_limit_bytes=VMEM_BYTES),
         cost_estimate=pl.CostEstimate(flops=6 * 10**9, bytes_accessed=8_000_000, transcendentals=0),
-    )(flags, across, packed, l10t)
-
-
-def update_kernel(flags, cov_ref, along_ref, pc_ref, white_ref, packed_ref, l10t_ref, out_ref, product_ref):
+    )(flags, across, inverse, l10t)
+
+
+def update_kernel(
+    flags, cov_ref, along_ref, pc_ref, relaid_ref, white_ref, inverse_ref, l10t_ref, lower_ref, out_ref, solved_ref, wide
+):
     i = pl.program_id(0)
     parts, part = along_ref.shape[0], along_ref.shape[2]
     column_blocks = pc_ref.shape[0] // B
+    fold = relaid_ref.shape[1]
 
     level = flags[16 + i]
     raw = along_ref[:, 0].reshape(parts * part, 2 * B)
-    p0, p1 = solve_rows(raw[:, 0:B], raw[:, B : 2 * B], packed_ref, l10t_ref)
+    p0, p1 = solve_rows(raw[:, 0:B], raw[:, B : 2 * B], wide, inverse_ref, l10t_ref)
     p0 = jnp.where(level > 0, p0, 0.0)
     p1 = jnp.where(level > 1, p1, 0.0)
     rows = jnp.concatenate([p0.astype(BF16), p1.astype(BF16)], axis=1)
     for n in range(column_blocks):
         cut = slice(n * B, (n + 1) * B)
         out_ref[:, cut] = cov_ref[:, cut] - dot(rows, pc_ref[cut, :], NT)
-    product_ref[...] = dot(white_ref[...].astype(BF16), rows, NT)
 
     for panel, solved in ((0, p0), (1, p1)):
         is_row = i == flags[2 + panel]
@@ -251,15 +283,30 @@
 
         @pl.when((column >= 0) & is_row)
         def _():
-            out_ref[:, place] = packed_ref[:, (2 + panel) * B : (3 + panel) * B]
-
-
-def update(flags, covariance, along, pc, white, packed, l10t):
+            out_ref[:, place] = lower_ref[:, panel * B : (panel + 1) * B]
+
+    product = dot(white_ref[...].astype(BF16), rows, NT)
+    for n in range(4):
+        h, parity = n // 2, n % 2
+        for f in range(4):
+            top = parity * 4 * fold + f * fold
+            there = (slice(top, top + fold), slice(h * 128, (h + 1) * 128))
+            solved_ref[there] = relaid_ref[n, :, f * 128 : (f + 1) * 128] - product[there]
+    for panel in range(2):
+
+        @pl.when(i == flags[2 + panel])
+        def _():
+            solved_ref[...] = white_ref[:, panel * B : (panel + 1) * B]
+
+
+def update(flags, covariance, along, pc, exchanged, white, inverse, l10t, lower):
     rows, columns = covariance.shape
     blocks = rows // B
     parts = along.shape[0]
     part = B // parts
     particles = white.shape[0]
+    fold = particles // 8
+    below = exchanged.shape[1] // fold - 1
     return pl.pallas_call(
         update_kernel,
         grid_spec=pltpu.PrefetchScalarGridSpec(
@@ -269,47 +316,22 @@
                 pl.BlockSpec((B, columns), lambda i, flags: (i, 0)),
                 pl.BlockSpec((parts, 1, part, 2 * B), lambda i, flags: (0, i, 0, 0)),
                 whole(*pc.shape),
+                pl.BlockSpec((4, fold, 2 * B), lambda i, flags: (lax.rem(i + flags[0], blocks), below, 0)),
                 whole(*white.shape),
-                whole(*packed.shape),
+                whole(*inverse.shape),
                 whole(*l10t.shape),
+                whole(*lower.shape),
             ],
             out_specs=[
                 pl.BlockSpec((B, columns), lambda i, flags: (i, 0)),
                 pl.BlockSpec((particles, B), lambda i, flags: (0, i)),
             ],
+            scratch_shapes=[pltpu.VMEM((B, 6 * B), BF16)],
         ),
         out_shape=[jax.ShapeDtypeStruct((rows, columns), F32), jax.ShapeDtypeStruct((particles, rows), F32)],
         compiler_params=pltpu.CompilerParams(vmem_limit_bytes=VMEM_BYTES),
         cost_estimate=pl.CostEstimate(flops=5 * 10**9, bytes_accessed=20_000_000, transcendentals=0),
-    )(flags, covariance, along, pc, white, packed, l10t)
-
-
-def forward_kernel(flags, relaid_ref, product_ref, white_ref, out_ref):
-    half, width = relaid_ref.shape[1:]
-    steps = relaid_ref.shape[0] // 4
-    for q in range(relaid_ref.shape[0] // 2):
-        first = lax.rem(q // 2 + flags[0], steps) * 4 + q % 2 * 2
-        for parity in range(2):
-            there = (slice(parity * half, (parity + 1) * half), slice(q * width, (q + 1) * width))
-            out_ref[there] = relaid_ref[first + parity] - product_ref[there]
-    for panel in range(2):
-        block = flags[2 + panel]
-
-        @pl.when(block >= 0)
-        def _():
-            place = pl.ds(pl.multiple_of(jnp.maximum(block, 0) * B, B), B)
-            out_ref[:, place] = white_ref[:, panel * B : (panel + 1) * B]
-
-
-def forward(flags, relaid, product, white):
-    return pl.pallas_call(
-        forward_kernel,
-        in_specs=[SMEM_SPEC] + [VMEM_SPEC] * 3,
-        out_specs=VMEM_SPEC,
-        out_shape=jax.ShapeDtypeStruct(product.shape, F32),
-        compiler_params=pltpu.CompilerParams(vmem_limit_bytes=VMEM_BYTES),
-        cost_estimate=pl.CostEstimate(flops=10**6, bytes_accessed=2_000_000, transcendentals=0),
-    )(flags, relaid, product, white)
+    )(flags, covariance, along, pc, exchanged, white, inverse, l10t, lower)
 
 
 def per_device(covariance, innovations, block_owner, panel_index, *, n_row, n_col):
@@ -355,11 +377,12 @@
 
     chosen = jnp.where(r == row_root[0], row_slot[0], row_slot[1])
     mine = lax.dynamic_index_in_dim(piece, chosen, 0, keepdims=False)
-    spread = lax.all_to_all(
-        jnp.broadcast_to(mine[None], (n_row,) + mine.shape), "row", split_axis=0, concat_axis=0, tiled=True
-    )
-    upper = lax.dynamic_slice(spread, (row_root[0], 0, 0), (1, part, 2 * B))[0]
-    lower = lax.dynamic_slice(spread, (row_root[1], 0, B), (1, part, B))[0]
+    fold = turned.shape[1] // 4
+    groups = jnp.concatenate([turned[:, f * fold : (f + 1) * fold] for f in range(4)], axis=2)
+    sent = jnp.concatenate([jnp.broadcast_to(mine[None], (n_row,) + mine.shape), groups], axis=1)
+    exchanged = lax.all_to_all(sent, "row", split_axis=0, concat_axis=0, tiled=True)
+    upper = lax.dynamic_slice(exchanged, (row_root[0], 0, 0), (1, part, 2 * B))[0]
+    lower = lax.dynamic_slice(exchanged, (row_root[1], 0, B), (1, part, B))[0]
     strip = jnp.concatenate([upper, lower], axis=-1)
     diag = lax.all_to_all(
         jnp.broadcast_to(strip[None], (n_col,) + strip.shape), "col", split_axis=0, concat_axis=0, tiled=True
@@ -367,22 +390,22 @@
 
     tiled = lax.ppermute(piece.reshape(row_blocks * part, 2 * B), ("row", "col"), across_axes)
     wanted = [lax.dynamic_index_in_dim(turned, row_root[n], 0, keepdims=False) for n in range(2)]
-    fold = wanted[0].shape[0] // 2
-    wanted = jnp.concatenate([wanted[0][:fold], wanted[1][:fold], wanted[0][fold:], wanted[1][fold:]], axis=1)
-    payload, _ = lax.optimization_barrier((jnp.concatenate([tiled, wanted], axis=0), spread))
+    wanted = jnp.concatenate(
+        [w[h * 2 * fold : (h + 1) * 2 * fold] for h in range(2) for w in wanted], axis=1
+    )
+    payload, _ = lax.optimization_barrier((jnp.concatenate([tiled, wanted], axis=0), exchanged))
     across = lax.all_gather(payload, "row", axis=0)
 
-    packed, l10t = factor_diagonal(diag)
+    inverse, l10t, lower = factor_diagonal(diag)
 
     along = lax.all_to_all(
         jnp.broadcast_to(piece[None], (n_col,) + piece.shape), "col", split_axis=0, concat_axis=0, tiled=True
     )
-    relaid = lax.all_to_all(turned, "row", split_axis=0, concat_axis=0, tiled=True)
-
-    pc, white = solve_across(flags, across, packed, l10t, row_blocks, n_col, 2 * turned.shape[1])
-    matrix, product = update(flags, covariance, along, pc.reshape(local_cols, 2 * B), white, packed, l10t)
-    solved = forward(flags, relaid, product, white)
-    return matrix, solved
+
+    pc, white = solve_across(flags, across, inverse, l10t, row_blocks, n_col, 2 * turned.shape[1])
+    return update(
+        flags, covariance, along, pc.reshape(local_cols, 2 * B), exchanged, white, inverse, l10t, lower
+    )
 
 
 def solution(mesh):

time: 198 us -> 194 us (0.980)
  starting transfers between devices: 44.8 us -> 38.6 us
  waiting for transfers between devices: 63.2 us -> 65.5 us
    all_to_all x1, waiting for transfers between devices: 10.6 us -> 0.01 us  [per_device(): lax.all_to_all(jnp.broadcast_to(piece[None], (n_col,) + piece.shape), 'co...]
    all_to_all x2 -> x1, waiting for transfers between devices: 8.77 us -> 16.6 us  [per_device(): lax.all_to_all(sent, 'row', split_axis=0, concat_axis=0, tiled=True)]
    all_to_all x1, starting transfers between devices: 22.8 us -> 15.9 us  [per_device(): lax.all_to_all(jnp.broadcast_to(strip[None], (n_col,) + strip.shape), 'co...]
    all_to_all x1, waiting for transfers between devices: 21.6 us -> 27.1 us  [per_device(): lax.all_to_all(picked, 'col', split_axis=0, concat_axis=0, tiled=True)]
    pallas_call x1 -> x0, Pallas kernels: 2.14 us -> none  [forward(): pl.pallas_call(forward_kernel, in_specs=[SMEM_SPEC] + [VMEM_SPEC] * 3, ou...]
    all_to_all x2 -> x1, starting transfers between devices: 8.27 us -> 9.37 us  [per_device(): lax.all_to_all(sent, 'row', split_axis=0, concat_axis=0, tiled=True)]
  transfers between devices with their start and end apart: 8 -> 7, of which waited for: 4 -> 3; matrix products, arithmetic and copies ran while one was open for 3% -> 3% of each run, Pallas kernels for 24% -> 18%
where the time goes in v3:
time: 194 us; the launch traced here: 193 us
  waiting for transfers between devices  65.5 us (34%)
  Pallas kernels  53.8 us (28%)
  starting transfers between devices  38.6 us (20%)
  between operations  24.5 us (13%)
  local copies, waits for them, and re-layouts  6.78 us (3%)
  other arithmetic  3.58 us (2%)
    all_to_all x1, waiting for transfers between devices, per_device(): lax.all_to_all(picked, 'col', split_axis=0, concat_axis=0, tiled=True)  27.1 us
    pallas_call x1, Pallas kernels, factor_diagonal(): pl.pallas_call(factor_kernel, in_specs=[VMEM_SPEC], out_specs=[VMEM_SPEC]...  22.5 us
    all_to_all x1, waiting for transfers between devices, per_device(): lax.all_to_all(jnp.broadcast_to(strip[None], (n_col,) + strip.shape), 'co...  21.7 us
    all_to_all x1, waiting for transfers between devices, per_device(): lax.all_to_all(sent, 'row', split_axis=0, concat_axis=0, tiled=True)  16.6 us
    all_to_all x1, starting transfers between devices, per_device(): lax.all_to_all(jnp.broadcast_to(strip[None], (n_col,) + strip.shape), 'co...  15.9 us
    pallas_call x1, Pallas kernels, update(): pl.pallas_call(update_kernel, grid_spec=pltpu.PrefetchScalarGridSpec(num_...  14.1 us
    pallas_call x1, Pallas kernels, solve_across(): pl.pallas_call(across_kernel, grid_spec=pltpu.PrefetchScalarGridSpec(num_...  12.7 us
    all_to_all x1, starting transfers between devices, per_device(): lax.all_to_all(sent, 'row', split_axis=0, concat_axis=0, tiled=True)  9.37 us
  transfers between devices with their start and end apart: 7, of which 3 were waited for; matrix products, arithmetic and copies ran while one was open for 3% of the time, Pallas kernels for 18%

profile of v3, /device:TPU:0, one launch (start us, length us, event | category | flops | bytes accessed | tf_op | source)
XLA Modules:
  0.0 192.7 jit_solution(3129450310064728997)
XLA Ops:
  7.8 0.8 fusion.2
  8.7 0.5 compare_select_fusion.2
  9.2 4.5 %shard_map.59 = f32[8,4,32,512]{3,2,1,0:T(8,128)} custom-call(s32[2]{0:T(128)} %get-tuple-element.18.slots, f32[1024,2048]{1,0:T(8,128)} %cov_ref.3), custom_call_target="tpu_custom_call" | custom-call | tf_op jit(solution)/shard_map/pallas_call | solution.py:39
  13.7 8.2 %all-to-all-start = ((f32[8,4,32,512]{3,2,1,0:T(8,128)}), f32[8,4,32,512]{3,2,1,0:T(8,128)S(1)}, u32[]{:S(2)}, u32[]{:S(2)}) async-start(f32[8,4,32,512]{3,2,1,0:T(8,128)} %shard_map.59), calls=%async_computation | async-start | bytes 4194304 | tf_op jit(solution)/shard_map/all_to_all | solution.py:368
  22.0 0.7 collective-permute-start.1
  22.7 0.6 fusion.6
  25.9 0.7 fusion.7
  29.7 27.1 %all-to-all-done = f32[8,4,32,512]{3,2,1,0:T(8,128)S(1)} async-done(((f32[8,4,32,512]{3,2,1,0:T(8,128)}), f32[8,4,32,512]{3,2,1,0:T(8,128)S(1)}, u32[]{:S(2)}, u32[]{:S(2)}) %all-to-all-start) | async-done | bytes 2097184 | tf_op jit(solution)/shard_map/all_to_all | solution.py:368
  57.1 1.3 maximum_maximum_fusion
  58.4 9.4 %all-to-all-start.2 = ((f32[16,48,512]{2,1,0:T(8,128)}), f32[16,48,512]{2,1,0:T(8,128)S(1)}, u32[]{:S(2)}, u32[]{:S(2)}) async-start(f32[16,48,512]{2,1,0:T(8,128)} %maximum_maximum_fusion), calls=%async_computation.2 | async-start | bytes 3145728 | tf_op jit(solution)/shard_map/all_to_all | solution.py:383
  67.8 0.7 collective-permute-start
  72.5 0.8 maximum_maximum_fusion.1
  73.2 16.6 %all-to-all-done.2.relaid_ref = f32[16,48,512]{2,1,0:T(8,128)S(1)} async-done(((f32[16,48,512]{2,1,0:T(8,128)}), f32[16,48,512]{2,1,0:T(8,128)S(1)}, u32[]{:S(2)}, u32[]{:S(2)}) %all-to-all-start.2) | async-done | bytes 1572896 | tf_op jit(solution)/shard_map/all_to_all | solution.py:383
  89.9 1.1 broadcast_in_dim.49
  91.0 0.3 copy-done.1
  91.3 15.9 %all-to-all-start.3 = ((f32[8,32,768]{2,1,0:T(8,128)}), f32[8,32,768]{2,1,0:T(8,128)S(1)}, u32[]{:S(2)}, u32[]{:S(2)}) async-start(f32[8,32,768]{2,1,0:T(8,128)} %broadcast_in_dim.49), calls=%async_computation.3 | async-start | bytes 1572864 | tf_op jit(solution)/shard_map/all_to_all | solution.py:387
  107.4 0.6 concatenate.28.flags
  108.1 21.7 %all-to-all-done.3 = f32[8,32,768]{2,1,0:T(8,128)S(1)} async-done(((f32[8,32,768]{2,1,0:T(8,128)}), f32[8,32,768]{2,1,0:T(8,128)S(1)}, u32[]{:S(2)}, u32[]{:S(2)}) %all-to-all-start.3) | async-done | bytes 786464 | tf_op jit(solution)/shard_map/all_to_all | solution.py:387
  129.8 1.6 broadcast_in_dim.46
  131.4 3.8 %all-to-all-start.1 = ((f32[8,4,32,512]{3,2,1,0:T(8,128)}), f32[8,4,32,512]{3,2,1,0:T(8,128)S(1)}, u32[]{:S(2)}, u32[]{:S(2)}) async-start(f32[8,4,32,512]{3,2,1,0:T(8,128)} %broadcast_in_dim.46), calls=%async_computation.1 | async-start | bytes 4194304 | tf_op jit(solution)/shard_map/all_to_all | solution.py:401
  135.2 22.5 %shard_map.60 = (bf16[256,3072]{1,0:T(8,128)(2,1)}, bf16[256,256]{1,0:T(8,128)(2,1)}, f32[256,512]{1,0:T(8,128)}) custom-call(f32[256,768]{1,0:T(8,128)} %bitcast.38), custom_call_target="tpu_custom_call" | custom-call | flops 20000000000 | bytes 80000000 | tf_op jit(solution)/shard_map/pallas_call | solution.py:146
  157.7 12.7 %shard_map.61 = (bf16[2,4,8,32,512]{4,3,2,1,0:T(8,128)(2,1)}, f32[128,512]{1,0:T(8,128)}) custom-call(s32[20]{0:T(128)} %concatenate.28.flags, f32[16,160,512]{2,1,0:T(8,128)} %bitcast.40, bf16[256,3072]{1,0:T(8,128)(2,1)} %get-tuple-element.9.inverse_ref, bf16[256,256]{1,0:T(8,128)(2,1)} %get-tuple-element.10.l10t_ref), custom_call_target="tpu_custom_call" | custom-call | flops 6000000000 | bytes 8000000 | tf_op jit(solution)/shard_map/pallas_call | solution.py:220
  170.4 1.3 copy-done
  171.7 14.1 %shard_map.62 = (f32[1024,2048]{1,0:T(8,128)}, f32[128,1024]{1,0:T(8,128)}) custom-call(s32[20]{0:T(128)} %concatenate.28.flags, f32[1024,2048]{1,0:T(8,128)} %cov_ref.3, f32[8,4,32,512]{3,2,1,0:T(8,128)} %copy-done, bf16[2048,512]{1,0:T(8,128)(2,1)} %bitcast.41, f32[16,48,512]{2,1,0:T(8,128)} %copy-done.1, f32[128,512]{1,0:T(8,128)} %get-tuple-element.12.white_ref, ...), custom_call_target="tpu_custom_call" | custom-call | flops 5000000000 | bytes 20000000 | tf_op jit(solution)/shard_map/pallas_call | solution.py:310
  (31 shorter events, 0.8 us)
Async XLA Ops:
  13.7 8.2 %copy-start.3 = (f32[64,16,128]{2,1,0:T(8,128)S(1)}, f32[64,16,128]{2,1,0:T(8,128)}, u32[]{:S(2)}) copy-start(f32[64,16,128]{2,1,0:T(8,128)} %param.5) | copy-start | bytes 1572868
  13.7 43.2 %all-to-all-start = ((f32[8,4,32,512]{3,2,1,0:T(8,128)}), f32[8,4,32,512]{3,2,1,0:T(8,128)S(1)}, u32[]{:S(2)}, u32[]{:S(2)}) async-start(f32[8,4,32,512]{3,2,1,0:T(8,128)} %shard_map.59), calls=%async_computation | async-start | bytes 4194304 | tf_op jit(solution)/shard_map/all_to_all | solution.py:368
  22.0 7.7 %collective-permute-start.1 = (f32[16,64,128]{2,1,0:T(8,128)S(1)}, f32[16,64,128]{2,1,0:T(8,128)S(1)}, u32[]{:S(2)}, u32[]{:S(2)}) collective-permute-start(f32[16,64,128]{2,1,0:T(8,128)S(1)} %bitcast.39), channel_id=1, source_target_pairs={{0,0},{1,16},{2,32},{3,48},{4,64},{5,80},{6,96},{7,112},{8,8},{9,2... | collective-permute-start | bytes 1572872 | tf_op jit(solution)/shard_map/ppermute | solution.py:365
  58.4 31.5 %all-to-all-start.2 = ((f32[16,48,512]{2,1,0:T(8,128)}), f32[16,48,512]{2,1,0:T(8,128)S(1)}, u32[]{:S(2)}, u32[]{:S(2)}) async-start(f32[16,48,512]{2,1,0:T(8,128)} %maximum_maximum_fusion), calls=%async_computation.2 | async-start | bytes 3145728 | tf_op jit(solution)/shard_map/all_to_all | solution.py:383
  67.7 90.0 %all-gather.3.cloned.1.call-start = ((), (), s32[]{:S(2)}) async-start(), calls=%async_computation.4 | async-start | bytes 5570560 | tf_op jit(solution)/shard_map/all_gather | solution.py:397
  67.8 4.6 %collective-permute-start = (f32[128,512]{1,0:T(8,128)S(1)}, f32[128,512]{1,0:T(8,128)S(1)}, u32[]{:S(2)}, u32[]{:S(2)}) collective-permute-start(f32[128,512]{1,0:T(8,128)S(1)} %pad_maximum_fusion.1), channel_id=1, source_target_pairs={{0,0},{1,16},{2,32},{3,48},{4,64},{5,80},{6,96},{7,112},{8,8},{9,2... | collective-permute-start | bytes 786440 | tf_op jit(solution)/shard_map/ppermute | solution.py:391
  73.2 33.9 %copy-start.4 = (s32[64]{0:T(128)S(1)}, s32[64]{0:T(128)}, u32[]{:S(2)}) copy-start(s32[64]{0:T(128)} %param.6) | copy-start | bytes 772
  89.8 1.5 copy-start.1
  91.3 38.5 %all-to-all-start.3 = ((f32[8,32,768]{2,1,0:T(8,128)}), f32[8,32,768]{2,1,0:T(8,128)S(1)}, u32[]{:S(2)}, u32[]{:S(2)}) async-start(f32[8,32,768]{2,1,0:T(8,128)} %broadcast_in_dim.49), calls=%async_computation.3 | async-start | bytes 1572864 | tf_op jit(solution)/shard_map/all_to_all | solution.py:387
  129.8 1.6 copy-start.2
  131.4 39.0 %all-to-all-start.1 = ((f32[8,4,32,512]{3,2,1,0:T(8,128)}), f32[8,4,32,512]{3,2,1,0:T(8,128)S(1)}, u32[]{:S(2)}, u32[]{:S(2)}) async-start(f32[8,4,32,512]{3,2,1,0:T(8,128)} %broadcast_in_dim.46), calls=%async_computation.1 | async-start | bytes 4194304 | tf_op jit(solution)/shard_map/all_to_all | solution.py:401
  170.4 1.3 copy-start
Sparse Core Ops, SparseCore 0:
  90.0 64.5 all-gather.2

commit v4 on v3

v4 whole, which is shorter than its diff:
```python
import functools

import jax
import jax.numpy as jnp
from jax import lax
from jax.experimental import pallas as pl
from jax.experimental.pallas import tpu as pltpu
from jax.sharding import PartitionSpec as P

B = 256
S = 64
VMEM_BYTES = 60 * 1024 * 1024
F32 = jnp.float32
BF16 = jnp.bfloat16
HIGH = lax.Precision.HIGHEST
VMEM_SPEC = pl.BlockSpec(memory_space=pltpu.VMEM)
SMEM_SPEC = pl.BlockSpec(memory_space=pltpu.SMEM)


def dot(a, b, dims, precision=None):
    return lax.dot_general(a, b, (dims, ((), ())), precision=precision, preferred_element_type=F32)


NN = ((1,), (0,))
NT = ((1,), (1,))
TN = ((0,), (0,))


def pick_kernel(slots, cov_ref, out_ref):
    parts, blocks, part, width = out_ref.shape
    for b in range(blocks):
        out_ref[:, b] = cov_ref[b * B : (b + 1) * B, :].reshape(parts, part, width)


def pick_columns(slots, covariance, parts):
    rows = covariance.shape[0]
    blocks = rows // B
    part = B // parts
    return pl.pallas_call(
        pick_kernel,
        grid_spec=pltpu.PrefetchScalarGridSpec(
            num_scalar_prefetch=1,
            grid=(2, blocks // 2),
            in_specs=[pl.BlockSpec((2 * B, B), lambda j, b, slots: (b, slots[j]))],
            out_specs=pl.BlockSpec((parts, 2, part, B), lambda j, b, slots: (0, b, 0, j)),
        ),
        out_shape=jax.ShapeDtypeStruct((parts, blocks, part, 2 * B), F32),
    )(slots, covariance)


def lanes(tile, j):
    return jnp.broadcast_to(tile[:, j : j + 1], (8, 128))


def eliminate(tiles):
    sub = lax.broadcasted_iota(jnp.int32, (8, 128), 0)
    scales = []
    for t in range(8):
        own = tiles[t]
        cols = [lanes(own, 8 * t + j) for j in range(8)]
        inv, cross = [], {}
        pivots = jnp.ones((8, 128), F32)
        for j in range(8):
            pivot = jnp.broadcast_to(cols[j][j : j + 1, :], (8, 128))
            pivots = jnp.where(sub == j, pivot, pivots)
            r = 1.0 / pivot
            inv.append(r)
            if j == 7:
                break
            m = jnp.where(sub > j, cols[j] * r, 0.0)
            for k in range(j + 1, 8):
                cross[j, k] = jnp.broadcast_to(cols[k][j : j + 1, :], (8, 128))
                cols[k] = cols[k] - m * cross[j, k]
            own = own - m * jnp.broadcast_to(own[j : j + 1, :], (8, 128))
        tiles[t] = own
        scales.append(lax.rsqrt(pivots))
        rows = [jnp.broadcast_to(own[j : j + 1, :], (8, 128)) for j in range(8)]
        for i in range(t + 1, 8):
            low = tiles[i]
            cols = [lanes(low, 8 * t + j) for j in range(8)]
            for j in range(8):
                m = cols[j] * inv[j]
                for k in range(j + 1, 8):
                    cols[k] = cols[k] - m * cross[j, k]
                low = low - m * rows[j]
            tiles[i] = low
    return tiles, scales


def factor_block(work, small, inverse_small):
    for b in range(B // S):
        lo, hi = b * S, (b + 1) * S
        small[:, 0:S] = work[lo:hi, lo:hi]
        row = lax.broadcasted_iota(jnp.int32, (S, S), 0)
        col = lax.broadcasted_iota(jnp.int32, (S, S), 1)
        small[:, S : 2 * S] = jnp.where(row == col, 1.0, 0.0)
        tiles, scales = eliminate([small[8 * i : 8 * i + 8, :] for i in range(8)])
        for i in range(8):
            small[8 * i : 8 * i + 8, :] = tiles[i] * scales[i]
        inverse_small[...] = small[:, S : 2 * S]
        top = dot(inverse_small[...], work[lo:hi, :], NN, HIGH)
        work[lo:hi, :] = top
        if hi < B:
            work[hi:B, :] = work[hi:B, :] - dot(top[:, hi:B], top, TN, HIGH)


def split(a):
    high = a.astype(BF16)
    rest = a - high.astype(F32)
    middle = rest.astype(BF16)
    return high, middle, (rest - middle.astype(F32)).astype(BF16)


def write_left(ref, a):
    high, middle, low = split(a)
    for n, term in enumerate((high, high, middle, high, low, middle)):
        ref[:, n * B : (n + 1) * B] = term


def write_right(ref, start, a):
    high, middle, low = split(a)
    for n, term in enumerate((high, middle, high, low, high, middle)):
        ref[:, start + n * B : start + (n + 1) * B] = term


def factor_kernel(flags, near_ref, far_ref, inverse_ref, l10t_ref, lower_ref, diag_ref, work, small, inverse_small):
    parts, part = near_ref.shape[:2]
    for ref, first in ((near_ref, flags[1] * part), (far_ref, (1 - flags[1]) * part)):
        for q in range(parts):
            diag_ref[pl.ds(pl.multiple_of(q * 2 * part + first, part), part), :] = ref[q]
    row = lax.broadcasted_iota(jnp.int32, (B, B), 0)
    col = lax.broadcasted_iota(jnp.int32, (B, B), 1)
    eye = jnp.where(row == col, 1.0, 0.0)
    work[:, 0:B] = diag_ref[:, 0:B]
    work[:, B : 2 * B] = eye
    factor_block(work, small, inverse_small)
    x0 = work[:, B : 2 * B]
    write_right(inverse_ref, 0, x0)
    lower_ref[:, 0:B] = jnp.where(row <= col, work[:, 0:B], 0.0).T
    l10t = dot(x0, diag_ref[:, B : 2 * B], NN, HIGH).astype(BF16)
    l10t_ref[...] = l10t
    work[:, 0:B] = diag_ref[:, 2 * B : 3 * B] - dot(l10t, l10t, TN)
    work[:, B : 2 * B] = eye
    factor_block(work, small, inverse_small)
    write_right(inverse_ref, 6 * B, work[:, B : 2 * B])
    lower_ref[:, B : 2 * B] = jnp.where(row <= col, work[:, 0:B], 0.0).T


def factor_diagonal(flags, near, far):
    return pl.pallas_call(
        factor_kernel,
        in_specs=[SMEM_SPEC] + [VMEM_SPEC] * 2,
        out_specs=[VMEM_SPEC] * 3,
        out_shape=[
            jax.ShapeDtypeStruct((B, 12 * B), BF16),
            jax.ShapeDtypeStruct((B, B), BF16),
            jax.ShapeDtypeStruct((B, 2 * B), F32),
        ],
        scratch_shapes=[
            pltpu.VMEM((B, 3 * B), F32),
            pltpu.VMEM((B, 2 * B), F32),
            pltpu.VMEM((S, 2 * S), F32),
            pltpu.VMEM((S, S), F32),
        ],
        compiler_params=pltpu.CompilerParams(vmem_limit_bytes=VMEM_BYTES),
        cost_estimate=pl.CostEstimate(flops=2 * 10**10, bytes_accessed=80_000_000, transcendentals=0),
    )(flags, near, far)


def solve_rows(first, second, wide, inverse_ref, l10t_ref):
    write_left(wide, first)
    p0 = dot(wide[...], inverse_ref[:, 0 : 6 * B], NT)
    write_left(wide, second - dot(p0.astype(BF16), l10t_ref[...], NN))
    p1 = dot(wide[...], inverse_ref[:, 6 * B : 12 * B], NT)
    return p0, p1


def across_kernel(flags, across_ref, inverse_ref, l10t_ref, pc_ref, white_ref, raw, wide, wide_white):
    blocks, parts, part = pc_ref.shape[:3]
    held = blocks * part
    half = raw.shape[0]
    fold = half // 2
    steps = parts // 2

    for k in range(steps):
        two = slice(2 * k, 2 * k + 2)
        p0, p1 = solve_rows(
            across_ref[two, 0:held, 0:B].reshape(2 * held, B),
            across_ref[two, 0:held, B : 2 * B].reshape(2 * held, B),
            wide.at[k],
            inverse_ref,
            l10t_ref,
        )
        p0, p1 = p0.astype(BF16), p1.astype(BF16)
        for h in range(2):
            q = lax.rem(k + steps - flags[0], steps) * 2 + h
            for b in range(blocks):
                here = slice(h * held + b * part, h * held + (b + 1) * part)
                level = flags[8 + flags[1] * blocks + b]
                pc_ref[b, q, :, 0:B] = jnp.where(level > 0, p0[here], jnp.zeros_like(p0[here]))
                pc_ref[b, q, :, B : 2 * B] = jnp.where(level > 1, p1[here], jnp.zeros_like(p1[here]))

    for panel in range(2):
        for h in range(2):
            for f in range(2):
                lane = (2 * f + panel) * 128
                raw[f * fold : (f + 1) * fold, panel * B + h * 128 : panel * B + (h + 1) * 128] = across_ref[
                    2 * flags[6 + panel] + h, held : held + fold, lane : lane + 128
                ]
    w0, w1 = solve_rows(raw[:, 0:B], raw[:, B : 2 * B], wide_white, inverse_ref, l10t_ref)
    white_ref[:, 0:B] = w0
    white_ref[:, B : 2 * B] = w1


def solve_across(flags, across, inverse, l10t, blocks, particles):
    parts = across.shape[0]
    part = B // parts
    return pl.pallas_call(
        across_kernel,
        in_specs=[SMEM_SPEC] + [VMEM_SPEC] * 3,
        out_specs=[VMEM_SPEC] * 2,
        scratch_shapes=[
            pltpu.VMEM((particles, 2 * B), F32),
            pltpu.VMEM((parts // 2, 2 * blocks * part, 6 * B), BF16),
            pltpu.VMEM((particles, 6 * B), BF16),
        ],
        out_shape=[
            jax.ShapeDtypeStruct((blocks, parts, part, 2 * B), BF16),
            jax.ShapeDtypeStruct((particles, 2 * B), F32),
        ],
        compiler_params=pltpu.CompilerParams(vmem_limit_bytes=VMEM_BYTES),
        cost_estimate=pl.CostEstimate(flops=3 * 10**9, bytes_accessed=4_000_000, transcendentals=0),
    )(flags, across, inverse, l10t)


def whole(*shape):
    return pl.BlockSpec(shape, lambda i, flags: (0,) * len(shape))


def update_kernel(
    flags,
    cov_ref,
    along_ref,
    near_ref,
    far_ref,
    relaid_ref,
    near_white_ref,
    far_white_ref,
    inverse_ref,
    l10t_ref,
    lower_ref,
    out_ref,
    solved_ref,
    panels,
    rows,
    wide,
):
    i = pl.program_id(0)
    parts, blocks, part = along_ref.shape[:3]
    column_blocks = 2 * near_ref.shape[0] // B
    half = relaid_ref.shape[1]

    @pl.when(i == 0)
    def _():
        for b in range(blocks):
            raw = along_ref[:, b].reshape(parts * part, 2 * B)
            p0, p1 = solve_rows(raw[:, 0:B], raw[:, B : 2 * B], wide.at[b], inverse_ref, l10t_ref)
            for panel, p in ((0, p0), (1, p1)):
                p = jnp.where(flags[16 + b] > panel, p, 0.0)
                panels[b, :, panel * B : (panel + 1) * B] = p
                rows[b, :, panel * B : (panel + 1) * B] = p.astype(BF16)

    level = flags[16 + i]
    own = rows[i]
    for side, ref in ((flags[1], near_ref), (1 - flags[1], far_ref)):
        for n in range(column_blocks // 2):
            place = pl.ds(pl.multiple_of((side * (column_blocks // 2) + n) * B, B), B)
            out_ref[:, place] = cov_ref[:, place] - dot(own, ref[n * B : (n + 1) * B, :], NT)

    for panel in range(2):
        is_row = i == flags[2 + panel]
        for n in range(column_blocks):

            @pl.when(is_row & (flags[8 + n] > panel))
            def _():
                out_ref[:, n * B : (n + 1) * B] = jnp.zeros((B, B), F32)

        column = flags[4 + panel]
        place = pl.ds(pl.multiple_of(jnp.maximum(column, 0) * B, B), B)

        @pl.when((column >= 0) & (level > panel))
        def _():
            out_ref[:, place] = panels[i, :, panel * B : (panel + 1) * B]

        @pl.when((column >= 0) & is_row)
        def _():
            out_ref[:, place] = lower_ref[:, panel * B : (panel + 1) * B]

    for side, ref in ((flags[1], near_white_ref), (1 - flags[1], far_white_ref)):
        place = pl.ds(pl.multiple_of(side * half, half), half)
        product = dot(ref[...].astype(BF16), own, NT)
        for h in range(2):
            cut = slice(h * 128, (h + 1) * 128)
            solved_ref[place, cut] = relaid_ref[2 * h + side] - product[:, cut]
        for panel in range(2):

            @pl.when(i == flags[2 + panel])
            def _():
                solved_ref[place, :] = ref[:, panel * B : (panel + 1) * B]


def update(flags, covariance, along, near, far, relaid, near_white, far_white, inverse, l10t, lower):
    rows, columns = covariance.shape
    blocks = rows // B
    half = relaid.shape[1]
    return pl.pallas_call(
        update_kernel,
        grid_spec=pltpu.PrefetchScalarGridSpec(
            num_scalar_prefetch=1,
            grid=(blocks,),
            in_specs=[
                pl.BlockSpec((B, columns), lambda i, flags: (i, 0)),
                whole(*along.shape),
                whole(*near.shape),
                whole(*far.shape),
                pl.BlockSpec((4, half, 128), lambda i, flags: (lax.rem(i + flags[0], blocks), 0, 0)),
                whole(*near_white.shape),
                whole(*far_white.shape),
                whole(*inverse.shape),
                whole(*l10t.shape),
                whole(*lower.shape),
            ],
            out_specs=[
                pl.BlockSpec((B, columns), lambda i, flags: (i, 0)),
                pl.BlockSpec((2 * half, B), lambda i, flags: (0, i)),
            ],
            scratch_shapes=[
                pltpu.VMEM((blocks, B, 2 * B), F32),
                pltpu.VMEM((blocks, B, 2 * B), BF16),
                pltpu.VMEM((blocks, B, 6 * B), BF16),
            ],
        ),
        out_shape=[jax.ShapeDtypeStruct((rows, columns), F32), jax.ShapeDtypeStruct((2 * half, rows), F32)],
        compiler_params=pltpu.CompilerParams(vmem_limit_bytes=VMEM_BYTES),
        cost_estimate=pl.CostEstimate(flops=5 * 10**9, bytes_accessed=20_000_000, transcendentals=0),
    )(flags, covariance, along, near, far, relaid, near_white, far_white, inverse, l10t, lower)


def per_device(covariance, innovations, block_owner, panel_index, *, n_row, n_col):
    local_rows, local_cols = covariance.shape
    row_blocks, column_blocks = local_rows // B, local_cols // B
    r, c = lax.axis_index("row"), lax.axis_index("col")
    targets = panel_index[0] + jnp.arange(2, dtype=jnp.int32)
    positions = jnp.arange(block_owner.shape[0], dtype=jnp.int32)
    slot = jnp.sum(jnp.where(block_owner[None, :] == targets[:, None], positions[None, :], 0), axis=1)
    row_root, column_root = slot // row_blocks, slot // column_blocks
    row_slot, column_slot = slot % row_blocks, slot % column_blocks
    levels = jnp.sum((block_owner[:, None] > targets[None, :]).astype(jnp.int32), axis=1)
    steps = n_row // 4
    shift, core = c // 2, r % 2
    pairs = [(a, a ^ 1) for a in range(n_row)]
    same_core = [[a for a in range(n_row) if a % 2 == k] for k in range(2)]
    flags = jnp.concatenate(
        [
            shift[None],
            core[None],
            jnp.where(row_root == r, row_slot, -1),
            jnp.where(column_root == c, column_slot, -1),
            (row_slot + shift) % steps,
            lax.dynamic_slice_in_dim(levels, c * column_blocks, column_blocks),
            lax.dynamic_slice_in_dim(levels, r * row_blocks, row_blocks),
        ]
    ).astype(jnp.int32)
    across_axes = [
        (a * n_col + b, ((b // 2 + a // 4) % steps * 4 + b % 2 * 2 + a % 2) * n_col + a // 2)
        for a in range(n_row)
        for b in range(n_col)
    ]

    picked = pick_columns(column_slot.astype(jnp.int32), covariance, n_col)
    parts = lax.all_to_all(picked, "col", split_axis=0, concat_axis=0, tiled=True)
    part = parts.shape[2]
    piece = jnp.concatenate(
        [
            lax.dynamic_slice(parts, (column_root[n], 0, 0, n * B), (1, row_blocks, part, B))[0]
            for n in range(2)
        ],
        axis=-1,
    )

    chosen = jnp.where(r == row_root[0], row_slot[0], row_slot[1])
    mine = lax.dynamic_index_in_dim(piece, chosen, 0, keepdims=False)
    half = part // 2
    kept = lax.dynamic_slice_in_dim(mine, core * half, half, 0)
    given = lax.ppermute(lax.dynamic_slice_in_dim(mine, (1 - core) * half, half, 0), "row", pairs)
    both = jnp.concatenate([jnp.where(core == 0, kept, given), jnp.where(core == 0, given, kept)], axis=0)

    fold = innovations.shape[0] // 2
    wanted = [lax.dynamic_index_in_dim(innovations, row_root[n], 1, keepdims=False) for n in range(2)]
    wanted = jnp.concatenate([w[h * fold : (h + 1) * fold] for h in range(2) for w in wanted], axis=1)
    payload = jnp.concatenate([piece.reshape(row_blocks * part, 2 * B), wanted], axis=0)
    payload, both = lax.optimization_barrier((payload, both))
    payload = lax.ppermute(payload, ("row", "col"), across_axes)

    spread = lax.all_to_all(
        jnp.broadcast_to(both[None], (n_row // 2,) + both.shape),
        "row",
        split_axis=0,
        concat_axis=0,
        tiled=True,
        axis_index_groups=same_core,
    )
    upper = lax.dynamic_slice(spread, (row_root[0] // 2, row_root[0] % 2 * half, 0), (1, half, 2 * B))[0]
    lower = lax.dynamic_slice(spread, (row_root[1] // 2, row_root[1] % 2 * half, B), (1, half, B))[0]
    strip = jnp.concatenate([upper, lower], axis=-1)
    near = lax.all_to_all(
        jnp.broadcast_to(strip[None], (n_col,) + strip.shape), "col", split_axis=0, concat_axis=0, tiled=True
    )
    far = lax.ppermute(near, "row", pairs)

    payload, _ = lax.optimization_barrier((payload, spread))
    across = lax.all_gather(payload, "row", axis=0, axis_index_groups=same_core)

    inverse, l10t, lower = factor_diagonal(flags, near, far)

    along = lax.all_to_all(
        jnp.broadcast_to(piece[None], (n_col,) + piece.shape), "col", split_axis=0, concat_axis=0, tiled=True
    )

    groups, _ = lax.optimization_barrier((jnp.transpose(innovations, (1, 0, 2)), near))
    turned = lax.ppermute(groups, ("row", "col"), across_axes)
    across, turned = lax.optimization_barrier((across, turned))
    turned, _ = lax.optimization_barrier((turned, along))
    relaid = lax.all_to_all(turned, "row", split_axis=0, concat_axis=0, tiled=True)

    near_rows, near_white = solve_across(flags, across, inverse, l10t, row_blocks, innovations.shape[0])
    near_rows = near_rows.reshape(local_cols // 2, 2 * B)
    far_rows, far_white = lax.ppermute(near_rows, "row", pairs), lax.ppermute(near_white, "row", pairs)
    return update(
        flags, covariance, along, near_rows, far_rows, relaid, near_white, far_white, inverse, l10t, lower
    )


def solution(mesh):
    placed = (P("row", "col"), P("row", None, "col"), P(), P())
    return jax.shard_map(
        functools.partial(per_device, n_row=mesh.shape["row"], n_col=mesh.shape["col"]),
        mesh=mesh,
        in_specs=placed,
        out_specs=(P("row", "col"), P("col", "row")),
        check_vma=False,
    )
```

time: 194 us -> 202 us (1.041)
  blocking collectives: 0 us -> 31.7 us
  starting transfers between devices: 38.6 us -> 23.2 us
  waiting for transfers between devices: 65.5 us -> 60.7 us
  Pallas kernels: 53.8 us -> 49.3 us
  between operations: 24.5 us -> 28.3 us
  other arithmetic: 3.58 us -> 1.55 us
    all_to_all x0 -> x1, blocking collectives: none -> 31.7 us  [per_device(): lax.all_to_all(jnp.broadcast_to(strip[None], (n_col,) + strip.shape), 'co...]
    all_to_all x2, waiting for transfers between devices: 38.3 us -> 18.3 us  [the longest x1 9.22 us: per_device(): lax.all_to_all(turned, 'row', split_axis=0, concat_axis=0, tiled=True)]
    all_to_all x2, starting transfers between devices: 25.2 us -> 8.62 us  [the longest x1 4.42 us: per_device(): lax.all_to_all(jnp.broadcast_to(both[None], (n_row // 2,) + both.shape),...]
    all_gather x1, waiting for transfers between devices: 0.01 us -> 16.2 us  [per_device(): across = lax.all_gather(payload, 'row', axis=0, axis_index_groups=same_core)]
    all_to_all x1, waiting for transfers between devices: 27.1 us -> 17.4 us  [per_device(): lax.all_to_all(picked, 'col', split_axis=0, concat_axis=0, tiled=True)]
    all_to_all x1, waiting for transfers between devices: 0.01 us -> 6.51 us  [per_device(): lax.all_to_all(jnp.broadcast_to(piece[None], (n_col,) + piece.shape), 'co...]
    pallas_call x2, Pallas kernels: 35.2 us -> 29.1 us  [the longest x1 22.5 us: factor_diagonal(): pl.pallas_call(factor_kernel, in_specs=[SMEM_SPEC] + [VMEM_SPEC] * 2, out...]
    ppermute x2 -> x6, waiting for transfers between devices: 0.01 us -> 2.39 us  [the longest x1 1.23 us: per_device(): lax.ppermute(near_white, 'row', pairs)]
  transfers between devices with their start and end apart: 7 -> 11, of which waited for: 3 -> 7; matrix products, arithmetic and copies ran while one was open for 3% -> 2% of each run, Pallas kernels for 18% -> 14%
where the time goes in v4:
time: 202 us; the launch traced here: 201 us
  waiting for transfers between devices  60.7 us (30%)
  Pallas kernels  49.3 us (24%)
  blocking collectives  31.7 us (16%)
  between operations  28.3 us (14%)
  starting transfers between devices  23.2 us (11%)
  local copies, waits for them, and re-layouts  6.37 us (3%)
    all_to_all x1, blocking collectives, per_device(): lax.all_to_all(jnp.broadcast_to(strip[None], (n_col,) + strip.shape), 'co...  31.7 us
    pallas_call x1, Pallas kernels, factor_diagonal(): pl.pallas_call(factor_kernel, in_specs=[SMEM_SPEC] + [VMEM_SPEC] * 2, out...  22.5 us
    all_to_all x1, waiting for transfers between devices, per_device(): lax.all_to_all(picked, 'col', split_axis=0, concat_axis=0, tiled=True)  17.4 us
    all_gather x1, waiting for transfers between devices, per_device(): across = lax.all_gather(payload, 'row', axis=0, axis_index_groups=same_core)  16.2 us
    pallas_call x1, Pallas kernels, update(): pl.pallas_call(update_kernel, grid_spec=pltpu.PrefetchScalarGridSpec(num_...  15.7 us
    all_to_all x1, waiting for transfers between devices, per_device(): lax.all_to_all(turned, 'row', split_axis=0, concat_axis=0, tiled=True)  9.22 us
    all_to_all x1, waiting for transfers between devices, per_device(): lax.all_to_all(jnp.broadcast_to(both[None], (n_row // 2,) + both.shape),...  9.05 us
    all_to_all x1, starting transfers between devices, per_device(): lax.all_to_all(picked, 'col', split_axis=0, concat_axis=0, tiled=True)  8.16 us
  transfers between devices with their start and end apart: 11, of which 7 were waited for; matrix products, arithmetic and copies ran while one was open for 2% of the time, Pallas kernels for 14%

profile of v4, /device:TPU:0, one launch (start us, length us, event | category | flops | bytes accessed | tf_op | source)
XLA Modules:
  0.0 201.1 jit_solution(9999968986832798896)
XLA Ops:
  7.8 0.8 fusion.4
  9.2 4.5 %shard_map.59 = f32[8,4,32,512]{3,2,1,0:T(8,128)} custom-call(s32[2]{0:T(128)} %get-tuple-element.30.slots, f32[1024,2048]{1,0:T(8,128)} %cov_ref.3), custom_call_target="tpu_custom_call" | custom-call | tf_op jit(solution)/shard_map/pallas_call | solution.py:39
  13.7 8.2 %all-to-all-start = ((f32[8,4,32,512]{3,2,1,0:T(8,128)}), f32[8,4,32,512]{3,2,1,0:T(8,128)S(1)}, u32[]{:S(2)}, u32[]{:S(2)}) async-start(f32[8,4,32,512]{3,2,1,0:T(8,128)} %shard_map.59), calls=%async_computation | async-start | bytes 4194304 | tf_op jit(solution)/shard_map/all_to_all | solution.py:381
  33.0 17.4 %all-to-all-done = f32[8,4,32,512]{3,2,1,0:T(8,128)S(1)} async-done(((f32[8,4,32,512]{3,2,1,0:T(8,128)}), f32[8,4,32,512]{3,2,1,0:T(8,128)S(1)}, u32[]{:S(2)}, u32[]{:S(2)}) %all-to-all-start) | async-done | bytes 2097184 | tf_op jit(solution)/shard_map/all_to_all | solution.py:381
  50.5 1.1 collective-permute-done
  51.7 0.9 broadcast_in_dim.49
  52.5 4.4 %all-to-all-start.2 = ((f32[8,32,512]{2,1,0:T(8,128)}), f32[8,32,512]{2,1,0:T(8,128)S(1)}, u32[]{:S(2)}, u32[]{:S(2)}) async-start(f32[8,32,512]{2,1,0:T(8,128)} %broadcast_in_dim.49), calls=%async_computation.2 | async-start | bytes 1048576 | tf_op jit(solution)/shard_map/all_to_all | solution.py:405
  57.0 0.7 collective-permute-start.1
  57.7 9.0 %all-to-all-done.2 = f32[8,32,512]{2,1,0:T(8,128)S(1)} async-done(((f32[8,32,512]{2,1,0:T(8,128)}), f32[8,32,512]{2,1,0:T(8,128)S(1)}, u32[]{:S(2)}, u32[]{:S(2)}) %all-to-all-start.2) | async-done | bytes 524320 | tf_op jit(solution)/shard_map/all_to_all | solution.py:405
  70.6 31.7 %all_to_all.25.near_ref = f32[8,16,768]{2,1,0:T(8,128)S(1)} all-to-all(f32[8,16,768]{2,1,0:T(8,128)S(1)} %broadcast_in_dim.50), channel_id=1, replica_groups=mesh['row'=16,'col'=8] {'col'}, dimensions={0} | all-to-all | bytes 786432 | tf_op jit(solution)/shard_map/all_to_all | solution.py:416
  102.7 0.7 concatenate.25.flags
  103.4 1.6 broadcast_in_dim.48
  105.0 3.6 %all-to-all-start.1 = ((f32[8,4,32,512]{3,2,1,0:T(8,128)}), f32[8,4,32,512]{3,2,1,0:T(8,128)S(1)}, u32[]{:S(2)}, u32[]{:S(2)}) async-start(f32[8,4,32,512]{3,2,1,0:T(8,128)} %broadcast_in_dim.48), calls=%async_computation.1 | async-start | bytes 4194304 | tf_op jit(solution)/shard_map/all_to_all | solution.py:426
  108.6 1.5 collective-permute-start.2
  110.1 0.8 copy-done.5
  110.8 22.5 %shard_map.60 = (bf16[256,3072]{1,0:T(8,128)(2,1)}, bf16[256,256]{1,0:T(8,128)(2,1)}, f32[256,512]{1,0:T(8,128)}) custom-call(s32[20]{0:T(128)} %concatenate.25.flags, f32[8,16,768]{2,1,0:T(8,128)} %copy-done.3, f32[8,16,768]{2,1,0:T(8,128)} %copy-done.5), custom_call_target="tpu_custom_call" | custom-call | flops 20000000000 | bytes 80000000 | tf_op jit(solution)/shard_map/pallas_call | solution.py:150
  133.4 16.2 %all-gather.3.cloned.1.call-done = f32[1280,512]{1,0:T(8,128)} async-done(((f32[160,512]{1,0:T(8,128)}), f32[1280,512]{1,0:T(8,128)}) %all-gather.3.cloned.1.call-update) | async-done | bytes 2621456 | tf_op jit(solution)/shard_map/all_gather | solution.py:422
  149.5 6.6 %shard_map.61 = (bf16[4,8,32,512]{3,2,1,0:T(8,128)(2,1)}, f32[64,512]{1,0:T(8,128)}) custom-call(s32[20]{0:T(128)} %concatenate.25.flags, f32[8,160,512]{2,1,0:T(8,128)} %bitcast.50, bf16[256,3072]{1,0:T(8,128)(2,1)} %get-tuple-element.19.inverse_ref, bf16[256,256]{1,0:T(8,128)(2,1)} %get-tuple-element.20.l10t_ref), custom_call_target="tpu_custom_call" | custom-call | flops 3000000000 | bytes 4000000 | tf_op jit(solution)/shard_map/pallas_call | solution.py:218
  156.1 6.5 %all-to-all-done.1.along_ref = f32[8,4,32,512]{3,2,1,0:T(8,128)S(1)} async-done(((f32[8,4,32,512]{3,2,1,0:T(8,128)}), f32[8,4,32,512]{3,2,1,0:T(8,128)S(1)}, u32[]{:S(2)}, u32[]{:S(2)}) %all-to-all-start.1) | async-done | bytes 2097184 | tf_op jit(solution)/shard_map/all_to_all | solution.py:426
  162.6 4.2 %all-to-all-start.4 = ((f32[16,64,128]{2,1,0:T(8,128)}), f32[16,64,128]{2,1,0:T(8,128)S(1)}, u32[]{:S(2)}, u32[]{:S(2)}) async-start(f32[16,64,128]{2,1,0:T(8,128)} %collective-permute-done.2), calls=%async_computation.4 | async-start | bytes 1048576 | tf_op jit(solution)/shard_map/all_to_all | solution.py:434
  167.3 1.2 collective-permute-done.5.far_white_ref
  168.5 9.2 %all-to-all-done.4.relaid_ref = f32[16,64,128]{2,1,0:T(8,128)S(1)} async-done(((f32[16,64,128]{2,1,0:T(8,128)}), f32[16,64,128]{2,1,0:T(8,128)S(1)}, u32[]{:S(2)}, u32[]{:S(2)}) %all-to-all-start.4) | async-done | bytes 524320 | tf_op jit(solution)/shard_map/all_to_all | solution.py:434
  177.7 0.8 copy-done.2
  178.5 15.7 %shard_map.62 = (f32[1024,2048]{1,0:T(8,128)}, f32[128,1024]{1,0:T(8,128)}) custom-call(s32[20]{0:T(128)} %concatenate.25.flags, f32[1024,2048]{1,0:T(8,128)} %cov_ref.3, f32[8,4,32,512]{3,2,1,0:T(8,128)} %copy-done, bf16[1024,512]{1,0:T(8,128)(2,1)} %bitcast.52, bf16[1024,512]{1,0:T(8,128)(2,1)} %collective-permute-done.4.far_ref, ...), custom_call_target="tpu_custom_call" | custom-call | flops 5000000000 | bytes 20000000 | tf_op jit(solution)/shard_map/pallas_call | solution.py:316
  (47 shorter events, 3.1 us)
Async XLA Ops:
  13.7 16.5 %copy-start.1 = (f32[64,16,128]{2,1,0:T(8,128)S(1)}, f32[64,16,128]{2,1,0:T(8,128)}, u32[]{:S(2)}) copy-start(f32[64,16,128]{2,1,0:T(8,128)} %param.5) | copy-start | bytes 1572868
  13.7 36.6 %all-to-all-start = ((f32[8,4,32,512]{3,2,1,0:T(8,128)}), f32[8,4,32,512]{3,2,1,0:T(8,128)S(1)}, u32[]{:S(2)}, u32[]{:S(2)}) async-start(f32[8,4,32,512]{3,2,1,0:T(8,128)} %shard_map.59), calls=%async_computation | async-start | bytes 4194304 | tf_op jit(solution)/shard_map/all_to_all | solution.py:381
  50.4 1.3 collective-permute-start
  50.5 52.0 %copy-start.7 = (s32[64]{0:T(128)S(1)}, s32[64]{0:T(128)}, u32[]{:S(2)}) copy-start(s32[64]{0:T(128)} %param.6) | copy-start | bytes 772
  52.5 14.2 %all-to-all-start.2 = ((f32[8,32,512]{2,1,0:T(8,128)}), f32[8,32,512]{2,1,0:T(8,128)S(1)}, u32[]{:S(2)}, u32[]{:S(2)}) async-start(f32[8,32,512]{2,1,0:T(8,128)} %broadcast_in_dim.49), calls=%async_computation.2 | async-start | bytes 1048576 | tf_op jit(solution)/shard_map/all_to_all | solution.py:405
  56.9 92.6 %all-gather.3.cloned.1.call-start = ((), (), s32[]{:S(2)}) async-start(), calls=%async_computation.5 | async-start | bytes 2949120 | tf_op jit(solution)/shard_map/all_gather | solution.py:422
  57.0 0.7 collective-permute-start.1
  57.7 9.1 %copy-start.4 = (f32[160,512]{1,0:T(8,128)}, f32[160,512]{1,0:T(8,128)S(1)}, u32[]{:S(2)}) copy-start(f32[160,512]{1,0:T(8,128)S(1)} %collective-permute-done.1) | copy-start | bytes 983044
  102.3 2.6 %copy-start.3 = (f32[8,16,768]{2,1,0:T(8,128)}, f32[8,16,768]{2,1,0:T(8,128)S(1)}, u32[]{:S(2)}) copy-start(f32[8,16,768]{2,1,0:T(8,128)S(1)} %all_to_all.25.near_ref) | copy-start | bytes 1179652
  102.3 7.7 %collective-permute-start.3 = (f32[8,16,768]{2,1,0:T(8,128)S(1)}, f32[8,16,768]{2,1,0:T(8,128)S(1)}, u32[]{:S(2)}, u32[]{:S(2)}) collective-permute-start(f32[8,16,768]{2,1,0:T(8,128)S(1)} %all_to_all.25.near_ref), channel_id=1, source_target_pairs={{0,8},{8,0},{16,24},{24,16},{32,40},{40,32},{48,56},{56,48},{64,72... | collective-permute-start | bytes 1179656 | tf_op jit(solution)/shard_map/ppermute | solution.py:419
  105.0 57.6 %all-to-all-start.1 = ((f32[8,4,32,512]{3,2,1,0:T(8,128)}), f32[8,4,32,512]{3,2,1,0:T(8,128)S(1)}, u32[]{:S(2)}, u32[]{:S(2)}) async-start(f32[8,4,32,512]{3,2,1,0:T(8,128)} %broadcast_in_dim.48), calls=%async_computation.1 | async-start | bytes 4194304 | tf_op jit(solution)/shard_map/all_to_all | solution.py:426
  108.6 24.8 %collective-permute-start.2 = (f32[16,64,128]{2,1,0:T(8,128)S(1)}, f32[16,64,128]{2,1,0:T(8,128)}, u32[]{:S(2)}, u32[]{:S(2)}) collective-permute-start(f32[16,64,128]{2,1,0:T(8,128)S(1)} %bitcast.47), channel_id=1, source_target_pairs={{0,0},{1,16},{2,32},{3,48},{4,64},{5,80},{6,96},{7,112},{8,8},{9,2... | collective-permute-start | bytes 1572872 | tf_op jit(solution)/shard_map/ppermute | solution.py:431
  110.1 0.8 copy-start.5
  156.1 21.6 %collective-permute-start.4 = (bf16[1024,512]{1,0:T(8,128)(2,1)}, bf16[1024,512]{1,0:T(8,128)(2,1)}, u32[]{:S(2)}, u32[]{:S(2)}) collective-permute-start(bf16[1024,512]{1,0:T(8,128)(2,1)} %bitcast.51), channel_id=1, source_target_pairs={{0,8},{8,0},{16,24},{24,16},{32,40},{40,32},{48,56},{56,48},{64,72... | collective-permute-start | bytes 3145736 | tf_op jit(solution)/shard_map/ppermute | solution.py:438
  162.6 15.1 %copy-start = (f32[8,4,32,512]{3,2,1,0:T(8,128)}, f32[8,4,32,512]{3,2,1,0:T(8,128)S(1)}, u32[]{:S(2)}) copy-start(f32[8,4,32,512]{3,2,1,0:T(8,128)S(1)} %all-to-all-done.1.along_ref) | copy-start | bytes 6291460
  162.6 15.1 %all-to-all-start.4 = ((f32[16,64,128]{2,1,0:T(8,128)}), f32[16,64,128]{2,1,0:T(8,128)S(1)}, u32[]{:S(2)}, u32[]{:S(2)}) async-start(f32[16,64,128]{2,1,0:T(8,128)} %collective-permute-done.2), calls=%async_computation.4 | async-start | bytes 1048576 | tf_op jit(solution)/shard_map/all_to_all | solution.py:434
  166.8 1.6 collective-permute-start.5
  168.5 9.2 %copy-start.6 = (f32[64,512]{1,0:T(8,128)}, f32[64,512]{1,0:T(8,128)S(1)}, u32[]{:S(2)}) copy-start(f32[64,512]{1,0:T(8,128)S(1)} %collective-permute-done.5.far_white_ref) | copy-start | bytes 393220
  177.7 0.8 copy-start.2
Sparse Core Ops, SparseCore 0:
  66.9 82.6 all-gather.2

commit v5 on v4

--- a/solution.py
+++ b/solution.py
@@ -175,107 +175,127 @@
     return p0, p1
 
 
-def across_kernel(flags, across_ref, inverse_ref, l10t_ref, pc_ref, white_ref, raw, wide, wide_white):
-    blocks, parts, part = pc_ref.shape[:3]
+def piece_kernel(
+    flags, piece_ref, turned_ref, seen_ref, inverse_ref, l10t_ref, along_ref, across_ref, white_ref, raw, wide
+):
+    blocks, part = piece_ref.shape[:2]
     held = blocks * part
-    half = raw.shape[0]
-    fold = half // 2
-    steps = parts // 2
-
-    for k in range(steps):
-        two = slice(2 * k, 2 * k + 2)
-        p0, p1 = solve_rows(
-            across_ref[two, 0:held, 0:B].reshape(2 * held, B),
-            across_ref[two, 0:held, B : 2 * B].reshape(2 * held, B),
-            wide.at[k],
-            inverse_ref,
-            l10t_ref,
-        )
-        p0, p1 = p0.astype(BF16), p1.astype(BF16)
-        for h in range(2):
-            q = lax.rem(k + steps - flags[0], steps) * 2 + h
-            for b in range(blocks):
-                here = slice(h * held + b * part, h * held + (b + 1) * part)
-                level = flags[8 + flags[1] * blocks + b]
-                pc_ref[b, q, :, 0:B] = jnp.where(level > 0, p0[here], jnp.zeros_like(p0[here]))
-                pc_ref[b, q, :, B : 2 * B] = jnp.where(level > 1, p1[here], jnp.zeros_like(p1[here]))
-
+    fold = seen_ref.shape[1]
+    raw[0:held, :] = piece_ref[...].reshape(held, 2 * B)
+    raw[held : 2 * held, :] = turned_ref[...].reshape(held, 2 * B)
     for panel in range(2):
         for h in range(2):
-            for f in range(2):
-                lane = (2 * f + panel) * 128
-                raw[f * fold : (f + 1) * fold, panel * B + h * 128 : panel * B + (h + 1) * 128] = across_ref[
-                    2 * flags[6 + panel] + h, held : held + fold, lane : lane + 128
-                ]
-    w0, w1 = solve_rows(raw[:, 0:B], raw[:, B : 2 * B], wide_white, inverse_ref, l10t_ref)
-    white_ref[:, 0:B] = w0
-    white_ref[:, B : 2 * B] = w1
-
-
-def solve_across(flags, across, inverse, l10t, blocks, particles):
-    parts = across.shape[0]
-    part = B // parts
+            for parity in range(2):
+                for f in range(2):
+                    lane = (2 * f + panel) * 128
+                    top = 2 * held + (2 * parity + f) * fold
+                    raw[top : top + fold, panel * B + h * 128 : panel * B + (h + 1) * 128] = seen_ref[
+                        4 * flags[6 + panel] + 2 * h + parity, :, lane : lane + 128
+                    ]
+    for panel, p in enumerate(solve_rows(raw[:, 0:B], raw[:, B : 2 * B], wide, inverse_ref, l10t_ref)):
+        cut = slice(panel * B, (panel + 1) * B)
+        white_ref[:, cut] = p[2 * held :]
+        for b in range(blocks):
+            mine = p[b * part : (b + 1) * part].astype(BF16)
+            mine = jnp.where(flags[16 + b] > panel, mine, jnp.zeros_like(mine))
+            for q in range(along_ref.shape[0]):
+                along_ref[q, b, :, cut] = mine
+            theirs = p[held + b * part : held + (b + 1) * part].astype(BF16)
+            level = flags[8 + flags[1] * blocks + b]
+            across_ref[b, :, cut] = jnp.where(level > panel, theirs, jnp.zeros_like(theirs))
+
+
+def solve_pieces(flags, piece, turned, seen, inverse, l10t, parts):
+    held = piece.shape[0] * piece.shape[1]
+    particles = 4 * seen.shape[1]
     return pl.pallas_call(
-        across_kernel,
-        in_specs=[SMEM_SPEC] + [VMEM_SPEC] * 3,
-        out_specs=[VMEM_SPEC] * 2,
+        piece_kernel,
+        in_specs=[SMEM_SPEC] + [VMEM_SPEC] * 5,
+        out_specs=[VMEM_SPEC] * 3,
         scratch_shapes=[
-            pltpu.VMEM((particles, 2 * B), F32),
-            pltpu.VMEM((parts // 2, 2 * blocks * part, 6 * B), BF16),
-            pltpu.VMEM((particles, 6 * B), BF16),
+            pltpu.VMEM((2 * held + particles, 2 * B), F32),
+            pltpu.VMEM((2 * held + particles, 6 * B), BF16),
         ],
         out_shape=[
-            jax.ShapeDtypeStruct((blocks, parts, part, 2 * B), BF16),
+            jax.ShapeDtypeStruct((parts,) + piece.shape, BF16),
+            jax.ShapeDtypeStruct(piece.shape, BF16),
             jax.ShapeDtypeStruct((particles, 2 * B), F32),
         ],
         compiler_params=pltpu.CompilerParams(vmem_limit_bytes=VMEM_BYTES),
-        cost_estimate=pl.CostEstimate(flops=3 * 10**9, bytes_accessed=4_000_000, transcendentals=0),
-    )(flags, across, inverse, l10t)
+        cost_estimate=pl.CostEstimate(flops=10**9, bytes_accessed=4_000_000, transcendentals=0),
+    )(flags, piece, turned, seen, inverse, l10t)
 
 
 def whole(*shape):
     return pl.BlockSpec(shape, lambda i, flags: (0,) * len(shape))
 
 
+def panel_kernel(flags, first_ref, second_ref, along_ref, inverse_ref, l10t_ref, out_ref, wide):
+    level = flags[16 + pl.program_id(0)]
+    parts, _, part = along_ref.shape[:3]
+
+    @pl.when(flags[4] >= 0)
+    def _():
+        write_left(wide, first_ref[...])
+        p = dot(wide[...], inverse_ref[:, 0 : 6 * B], NT)
+        out_ref[:, 0:B] = jnp.where(level > 0, p, 0.0)
+
+    @pl.when(flags[5] >= 0)
+    def _():
+        before = along_ref[:, 0, :, 0:B].reshape(parts * part, B)
+        write_left(wide, second_ref[...] - dot(before, l10t_ref[...], NN))
+        p = dot(wide[...], inverse_ref[:, 6 * B : 12 * B], NT)
+        out_ref[:, B : 2 * B] = jnp.where(level > 1, p, 0.0)
+
+
+def solve_panels(flags, covariance, along, inverse, l10t):
+    rows = covariance.shape[0]
+    parts, blocks, part, width = along.shape
+    return pl.pallas_call(
+        panel_kernel,
+        grid_spec=pltpu.PrefetchScalarGridSpec(
+            num_scalar_prefetch=1,
+            grid=(blocks,),
+            in_specs=[
+                pl.BlockSpec((B, B), lambda i, flags: (i, jnp.maximum(flags[4], 0))),
+                pl.BlockSpec((B, B), lambda i, flags: (i, jnp.maximum(flags[5], 0))),
+                pl.BlockSpec((parts, 1, part, width), lambda i, flags: (0, i, 0, 0)),
+                whole(*inverse.shape),
+                whole(*l10t.shape),
+            ],
+            out_specs=pl.BlockSpec((B, 2 * B), lambda i, flags: (i, 0)),
+            scratch_shapes=[pltpu.VMEM((B, 6 * B), BF16)],
+        ),
+        out_shape=jax.ShapeDtypeStruct((rows, 2 * B), F32),
+        compiler_params=pltpu.CompilerParams(vmem_limit_bytes=VMEM_BYTES),
+        cost_estimate=pl.CostEstimate(flops=10**9, bytes_accessed=4_000_000, transcendentals=0),
+    )(flags, covariance, covariance, along, inverse, l10t)
+
+
 def update_kernel(
-    flags,
-    cov_ref,
-    along_ref,
-    near_ref,
-    far_ref,
-    relaid_ref,
-    near_white_ref,
-    far_white_ref,
-    inverse_ref,
-    l10t_ref,
-    lower_ref,
-    out_ref,
-    solved_ref,
-    panels,
-    rows,
-    wide,
+    flags, cov_ref, along_ref, across_ref, relaid_ref, white_ref, panel_ref, lower_ref, out_ref, solved_ref, columns
 ):
     i = pl.program_id(0)
-    parts, blocks, part = along_ref.shape[:3]
-    column_blocks = 2 * near_ref.shape[0] // B
+    parts, _, part = along_ref.shape[:3]
+    blocks = across_ref.shape[1]
+    steps = parts // 2
+    column_blocks = 2 * blocks
     half = relaid_ref.shape[1]
 
     @pl.when(i == 0)
     def _():
-        for b in range(blocks):
-            raw = along_ref[:, b].reshape(parts * part, 2 * B)
-            p0, p1 = solve_rows(raw[:, 0:B], raw[:, B : 2 * B], wide.at[b], inverse_ref, l10t_ref)
-            for panel, p in ((0, p0), (1, p1)):
-                p = jnp.where(flags[16 + b] > panel, p, 0.0)
-                panels[b, :, panel * B : (panel + 1) * B] = p
-                rows[b, :, panel * B : (panel + 1) * B] = p.astype(BF16)
+        for q in range(parts):
+            first = 4 * lax.rem(q // 2 + flags[0], steps) + 2 * (q % 2)
+            for parity in range(2):
+                for b in range(blocks):
+                    top = (parity * blocks + b) * B + q * part
+                    columns[top : top + part, :] = across_ref[first + parity, b]
 
     level = flags[16 + i]
-    own = rows[i]
-    for side, ref in ((flags[1], near_ref), (1 - flags[1], far_ref)):
-        for n in range(column_blocks // 2):
-            place = pl.ds(pl.multiple_of((side * (column_blocks // 2) + n) * B, B), B)
-            out_ref[:, place] = cov_ref[:, place] - dot(own, ref[n * B : (n + 1) * B, :], NT)
+    own = along_ref[:, 0].reshape(parts * part, 2 * B)
+    for n in range(column_blocks):
+        cut = slice(n * B, (n + 1) * B)
+        out_ref[:, cut] = cov_ref[:, cut] - dot(own, columns[cut, :], NT)
 
     for panel in range(2):
         is_row = i == flags[2 + panel]
@@ -290,28 +310,27 @@
 
         @pl.when((column >= 0) & (level > panel))
         def _():
-            out_ref[:, place] = panels[i, :, panel * B : (panel + 1) * B]
+            out_ref[:, place] = panel_ref[:, panel * B : (panel + 1) * B]
 
         @pl.when((column >= 0) & is_row)
         def _():
             out_ref[:, place] = lower_ref[:, panel * B : (panel + 1) * B]
 
-    for side, ref in ((flags[1], near_white_ref), (1 - flags[1], far_white_ref)):
-        place = pl.ds(pl.multiple_of(side * half, half), half)
-        product = dot(ref[...].astype(BF16), own, NT)
+    product = dot(white_ref[...].astype(BF16), own, NT)
+    for parity in range(2):
         for h in range(2):
-            cut = slice(h * 128, (h + 1) * 128)
-            solved_ref[place, cut] = relaid_ref[2 * h + side] - product[:, cut]
-        for panel in range(2):
-
-            @pl.when(i == flags[2 + panel])
-            def _():
-                solved_ref[place, :] = ref[:, panel * B : (panel + 1) * B]
-
-
-def update(flags, covariance, along, near, far, relaid, near_white, far_white, inverse, l10t, lower):
+            there = (slice(parity * half, (parity + 1) * half), slice(h * 128, (h + 1) * 128))
+            solved_ref[there] = relaid_ref[2 * h + parity] - product[there]
+    for panel in range(2):
+
+        @pl.when(i == flags[2 + panel])
+        def _():
+            solved_ref[...] = white_ref[:, panel * B : (panel + 1) * B]
+
+
+def update(flags, covariance, along, across, relaid, white, panels, lower):
     rows, columns = covariance.shape
-    blocks = rows // B
+    parts, blocks, part, width = along.shape
     half = relaid.shape[1]
     return pl.pallas_call(
         update_kernel,
@@ -320,30 +339,23 @@
             grid=(blocks,),
             in_specs=[
                 pl.BlockSpec((B, columns), lambda i, flags: (i, 0)),
-                whole(*along.shape),
-                whole(*near.shape),
-                whole(*far.shape),
+                pl.BlockSpec((parts, 1, part, width), lambda i, flags: (0, i, 0, 0)),
+                whole(*across.shape),
                 pl.BlockSpec((4, half, 128), lambda i, flags: (lax.rem(i + flags[0], blocks), 0, 0)),
-                whole(*near_white.shape),
-                whole(*far_white.shape),
-                whole(*inverse.shape),
-                whole(*l10t.shape),
+                whole(*white.shape),
+                pl.BlockSpec((B, width), lambda i, flags: (i, 0)),
                 whole(*lower.shape),
             ],
             out_specs=[
                 pl.BlockSpec((B, columns), lambda i, flags: (i, 0)),
                 pl.BlockSpec((2 * half, B), lambda i, flags: (0, i)),
             ],
-            scratch_shapes=[
-                pltpu.VMEM((blocks, B, 2 * B), F32),
-                pltpu.VMEM((blocks, B, 2 * B), BF16),
-                pltpu.VMEM((blocks, B, 6 * B), BF16),
-            ],
+            scratch_shapes=[pltpu.VMEM((columns, width), BF16)],
         ),
         out_shape=[jax.ShapeDtypeStruct((rows, columns), F32), jax.ShapeDtypeStruct((2 * half, rows), F32)],
         compiler_params=pltpu.CompilerParams(vmem_limit_bytes=VMEM_BYTES),
         cost_estimate=pl.CostEstimate(flops=5 * 10**9, bytes_accessed=20_000_000, transcendentals=0),
-    )(flags, covariance, along, near, far, relaid, near_white, far_white, inverse, l10t, lower)
+    )(flags, covariance, along, across, relaid, white, panels, lower)
 
 
 def per_device(covariance, innovations, block_owner, panel_index, *, n_row, n_col):
@@ -377,6 +389,11 @@
         for b in range(n_col)
     ]
 
+    fold = innovations.shape[0] // 2
+    wanted = [lax.dynamic_index_in_dim(innovations, row_root[n], 1, keepdims=False) for n in range(2)]
+    wanted = jnp.concatenate([w[h * fold : (h + 1) * fold] for h in range(2) for w in wanted], axis=1)
+    seen = lax.all_gather(lax.ppermute(wanted, ("row", "col"), across_axes), "row", axis=0)
+
     picked = pick_columns(column_slot.astype(jnp.int32), covariance, n_col)
     parts = lax.all_to_all(picked, "col", split_axis=0, concat_axis=0, tiled=True)
     part = parts.shape[2]
@@ -394,13 +411,6 @@
     kept = lax.dynamic_slice_in_dim(mine, core * half, half, 0)
     given = lax.ppermute(lax.dynamic_slice_in_dim(mine, (1 - core) * half, half, 0), "row", pairs)
     both = jnp.concatenate([jnp.where(core == 0, kept, given), jnp.where(core == 0, given, kept)], axis=0)
-
-    fold = innovations.shape[0] // 2
-    wanted = [lax.dynamic_index_in_dim(innovations, row_root[n], 1, keepdims=False) for n in range(2)]
-    wanted = jnp.concatenate([w[h * fold : (h + 1) * fold] for h in range(2) for w in wanted], axis=1)
-    payload = jnp.concatenate([piece.reshape(row_blocks * part, 2 * B), wanted], axis=0)
-    payload, both = lax.optimization_barrier((payload, both))
-    payload = lax.ppermute(payload, ("row", "col"), across_axes)
 
     spread = lax.all_to_all(
         jnp.broadcast_to(both[None], (n_row // 2,) + both.shape),
@@ -413,32 +423,25 @@
     upper = lax.dynamic_slice(spread, (row_root[0] // 2, row_root[0] % 2 * half, 0), (1, half, 2 * B))[0]
     lower = lax.dynamic_slice(spread, (row_root[1] // 2, row_root[1] % 2 * half, B), (1, half, B))[0]
     strip = jnp.concatenate([upper, lower], axis=-1)
+    strip, seen = lax.optimization_barrier((strip, seen))
     near = lax.all_to_all(
         jnp.broadcast_to(strip[None], (n_col,) + strip.shape), "col", split_axis=0, concat_axis=0, tiled=True
     )
     far = lax.ppermute(near, "row", pairs)
 
-    payload, _ = lax.optimization_barrier((payload, spread))
-    across = lax.all_gather(payload, "row", axis=0, axis_index_groups=same_core)
-
+    sent, groups, _ = lax.optimization_barrier((piece, jnp.transpose(innovations, (1, 0, 2)), near))
+    turned = lax.ppermute(sent, ("row", "col"), across_axes)
+    groups = lax.ppermute(groups, ("row", "col"), across_axes)
     inverse, l10t, lower = factor_diagonal(flags, near, far)
-
-    along = lax.all_to_all(
-        jnp.broadcast_to(piece[None], (n_col,) + piece.shape), "col", split_axis=0, concat_axis=0, tiled=True
-    )
-
-    groups, _ = lax.optimization_barrier((jnp.transpose(innovations, (1, 0, 2)), near))
-    turned = lax.ppermute(groups, ("row", "col"), across_axes)
-    across, turned = lax.optimization_barrier((across, turned))
-    turned, _ = lax.optimization_barrier((turned, along))
-    relaid = lax.all_to_all(turned, "row", split_axis=0, concat_axis=0, tiled=True)
-
-    near_rows, near_white = solve_across(flags, across, inverse, l10t, row_blocks, innovations.shape[0])
-    near_rows = near_rows.reshape(local_cols // 2, 2 * B)
-    far_rows, far_white = lax.ppermute(near_rows, "row", pairs), lax.ppermute(near_white, "row", pairs)
-    return update(
-        flags, covariance, along, near_rows, far_rows, relaid, near_white, far_white, inverse, l10t, lower
-    )
+    inverse, groups = lax.optimization_barrier((inverse, groups))
+
+    along, across, white = solve_pieces(flags, piece, turned, seen, inverse, l10t, n_col)
+    across = lax.all_gather(across, "row", axis=0)
+    along = lax.all_to_all(along, "col", split_axis=0, concat_axis=0, tiled=True)
+    groups, along = lax.optimization_barrier((groups, along))
+    relaid = lax.all_to_all(groups, "row", split_axis=0, concat_axis=0, tiled=True)
+    panels = solve_panels(flags, covariance, along, inverse, l10t)
+    return update(flags, covariance, along, across, relaid, white, panels, lower)
 
 
 def solution(mesh):

time: 202 us -> 204 us (level)
  blocking collectives: 31.7 us -> 51.5 us
  waiting for transfers between devices: 60.7 us -> 43.9 us
    all_to_all x0 -> x1, blocking collectives: none -> 33.8 us  [per_device(): lax.all_to_all(along, 'col', split_axis=0, concat_axis=0, tiled=True)]
    all_to_all x1, blocking collectives: 31.7 us -> 17.7 us  [per_device(): lax.all_to_all(jnp.broadcast_to(strip[None], (n_col,) + strip.shape), 'co...]
    all_to_all x2 -> x1, waiting for transfers between devices: 15.7 us -> 5.72 us  [per_device(): lax.all_to_all(groups, 'row', split_axis=0, concat_axis=0, tiled=True)]
    pallas_call x1, Pallas kernels: 15.7 us -> 11.8 us  [update(): pl.pallas_call(update_kernel, grid_spec=pltpu.PrefetchScalarGridSpec(num_...]
    all_gather x1 -> x2, waiting for transfers between devices: 16.2 us -> 12.9 us  [the longest x1 12.9 us: per_device(): lax.all_gather(lax.ppermute(wanted, ('row', 'col'), across_axes), 'row',...]
    pallas_call x1 -> x2, Pallas kernels: 6.57 us -> 9.8 us  [the longest x1 5.13 us: solve_panels(): pl.pallas_call(panel_kernel, grid_spec=pltpu.PrefetchScalarGridSpec(num_s...]
    all_to_all x2 -> x1, starting transfers between devices: 7.81 us -> 5.01 us  [per_device(): lax.all_to_all(groups, 'row', split_axis=0, concat_axis=0, tiled=True)]
    all_to_all x1, starting transfers between devices: 4.42 us -> 7.2 us  [per_device(): lax.all_to_all(jnp.broadcast_to(both[None], (n_row // 2,) + both.shape),...]
  transfers between devices with their start and end apart: 11 -> 10, of which waited for: 7 -> 5; matrix products, arithmetic and copies ran while one was open for 2% -> 2% of each run, Pallas kernels for 14% -> 14%
where the time goes in v5:
time: 204 us; the launch traced here: 203 us
  blocking collectives  51.5 us (25%)
  Pallas kernels  48.5 us (24%)
  waiting for transfers between devices  43.9 us (22%)
  between operations  28.5 us (14%)
  starting transfers between devices  23.3 us (11%)
  local copies, waits for them, and re-layouts  6.11 us (3%)
    all_to_all x1, blocking collectives, per_device(): lax.all_to_all(along, 'col', split_axis=0, concat_axis=0, tiled=True)  33.8 us
    pallas_call x1, Pallas kernels, factor_diagonal(): pl.pallas_call(factor_kernel, in_specs=[SMEM_SPEC] + [VMEM_SPEC] * 2, out...  22.5 us
    all_to_all x1, blocking collectives, per_device(): lax.all_to_all(jnp.broadcast_to(strip[None], (n_col,) + strip.shape), 'co...  17.7 us
    all_to_all x1, waiting for transfers between devices, per_device(): lax.all_to_all(picked, 'col', split_axis=0, concat_axis=0, tiled=True)  16.7 us
    all_gather x1, waiting for transfers between devices, per_device(): lax.all_gather(lax.ppermute(wanted, ('row', 'col'), across_axes), 'row',...  12.9 us
    pallas_call x1, Pallas kernels, update(): pl.pallas_call(update_kernel, grid_spec=pltpu.PrefetchScalarGridSpec(num_...  11.8 us
    all_to_all x1, starting transfers between devices, per_device(): lax.all_to_all(picked, 'col', split_axis=0, concat_axis=0, tiled=True)  8.16 us
    all_to_all x1, waiting for transfers between devices, per_device(): lax.all_to_all(jnp.broadcast_to(both[None], (n_row // 2,) + both.shape),...  7.4 us
  transfers between devices with their start and end apart: 10, of which 5 were waited for; matrix products, arithmetic and copies ran while one was open for 2% of the time, Pallas kernels for 14%

profile of v5, /device:TPU:0, one launch (start us, length us, event | category | flops | bytes accessed | tf_op | source)
XLA Modules:
  0.0 203.4 jit_solution(6427851167784033368)
XLA Ops:
  7.8 0.8 fusion.4
  9.2 4.5 %shard_map.59 = f32[8,4,32,512]{3,2,1,0:T(8,128)} custom-call(s32[2]{0:T(128)} %get-tuple-element.34.slots, f32[1024,2048]{1,0:T(8,128)} %cov_ref.3), custom_call_target="tpu_custom_call" | custom-call | tf_op jit(solution)/shard_map/pallas_call | solution.py:39
  13.7 8.2 %all-to-all-start = ((f32[8,4,32,512]{3,2,1,0:T(8,128)}), f32[8,4,32,512]{3,2,1,0:T(8,128)S(1)}, u32[]{:S(2)}, u32[]{:S(2)}) async-start(f32[8,4,32,512]{3,2,1,0:T(8,128)} %shard_map.59), calls=%async_computation | async-start | bytes 4194304 | tf_op jit(solution)/shard_map/all_to_all | solution.py:398
  26.6 0.7 collective-permute-start.1
  34.5 16.7 %all-to-all-done = f32[8,4,32,512]{3,2,1,0:T(8,128)S(1)} async-done(((f32[8,4,32,512]{3,2,1,0:T(8,128)}), f32[8,4,32,512]{3,2,1,0:T(8,128)S(1)}, u32[]{:S(2)}, u32[]{:S(2)}) %all-to-all-start) | async-done | bytes 2097184 | tf_op jit(solution)/shard_map/all_to_all | solution.py:398
  51.4 1.2 collective-permute-done
  52.6 0.9 broadcast_in_dim.42
  53.5 7.2 %all-to-all-start.1 = ((f32[8,32,512]{2,1,0:T(8,128)}), f32[8,32,512]{2,1,0:T(8,128)S(1)}, u32[]{:S(2)}, u32[]{:S(2)}) async-start(f32[8,32,512]{2,1,0:T(8,128)} %broadcast_in_dim.42), calls=%async_computation.1 | async-start | bytes 1048576 | tf_op jit(solution)/shard_map/all_to_all | solution.py:415
  64.6 7.4 %all-to-all-done.1 = f32[8,32,512]{2,1,0:T(8,128)S(1)} async-done(((f32[8,32,512]{2,1,0:T(8,128)}), f32[8,32,512]{2,1,0:T(8,128)S(1)}, u32[]{:S(2)}, u32[]{:S(2)}) %all-to-all-start.1) | async-done | bytes 524320 | tf_op jit(solution)/shard_map/all_to_all | solution.py:415
  72.0 12.9 %all-gather.5.cloned.1.call-done = f32[512,512]{1,0:T(8,128)} async-done(((f32[32,512]{1,0:T(8,128)}), f32[512,512]{1,0:T(8,128)}) %all-gather.5.cloned.1.call-update) | async-done | bytes 1048592 | tf_op jit(solution)/shard_map/all_gather | solution.py:395
  84.9 17.7 %all_to_all.25.near_ref = f32[8,16,768]{2,1,0:T(8,128)S(1)} all-to-all(f32[8,16,768]{2,1,0:T(8,128)S(1)} %broadcast_in_dim.43), channel_id=1, replica_groups=mesh['row'=16,'col'=8] {'col'}, dimensions={0} | all-to-all | bytes 786432 | tf_op jit(solution)/shard_map/all_to_all | solution.py:427
  102.8 0.7 concatenate.15.flags
  103.5 0.7 collective-permute-start.4
  104.2 1.5 collective-permute-start.3
  105.7 0.7 copy-done.5
  106.4 22.5 %shard_map.60 = (bf16[256,3072]{1,0:T(8,128)(2,1)}, bf16[256,256]{1,0:T(8,128)(2,1)}, f32[256,512]{1,0:T(8,128)}) custom-call(s32[20]{0:T(128)} %concatenate.15.flags, f32[8,16,768]{2,1,0:T(8,128)} %copy-done.2, f32[8,16,768]{2,1,0:T(8,128)} %copy-done.5), custom_call_target="tpu_custom_call" | custom-call | flops 20000000000 | bytes 80000000 | tf_op jit(solution)/shard_map/pallas_call | solution.py:150
  128.9 0.7 copy-done.6
  129.6 4.7 %shard_map.61 = (bf16[8,4,32,512]{3,2,1,0:T(8,128)(2,1)}, bf16[4,32,512]{2,1,0:T(8,128)(2,1)}, f32[128,512]{1,0:T(8,128)}) custom-call(s32[20]{0:T(128)} %concatenate.15.flags, f32[4,32,512]{2,1,0:T(8,128)} %copy-done.3, f32[4,32,512]{2,1,0:T(8,128)} %copy-done.6, f32[16,32,512]{2,1,0:T(8,128)} %bitcast.43, bf16[256,3072]{1,0:T(8,128)(2,1)} %get-tuple-element.22.inverse_ref, ...), custom_call_target="tpu_custom_call" | custom-call | flops 1000000000 | bytes 4000000 | tf_op jit(solution)/shard_map/pallas_call | solution.py:211
  134.3 33.8 %all_to_all.26.along_ref = bf16[8,4,32,512]{3,2,1,0:T(8,128)(2,1)} all-to-all(bf16[8,4,32,512]{3,2,1,0:T(8,128)(2,1)} %get-tuple-element.24), channel_id=1, replica_groups=mesh['row'=16,'col'=8] {'col'}, dimensions={0} | all-to-all | bytes 2097152 | tf_op jit(solution)/shard_map/all_to_all | solution.py:440
  168.1 5.0 %all-to-all-start.4 = ((f32[16,64,128]{2,1,0:T(8,128)}), f32[16,64,128]{2,1,0:T(8,128)S(1)}, u32[]{:S(2)}, u32[]{:S(2)}) async-start(f32[16,64,128]{2,1,0:T(8,128)} %collective-permute-done.3), calls=%async_computation.4 | async-start | bytes 1048576 | tf_op jit(solution)/shard_map/all_to_all | solution.py:442
  173.1 5.1 %shard_map.62.panel_ref = f32[1024,512]{1,0:T(8,128)} custom-call(s32[20]{0:T(128)} %concatenate.15.flags, f32[1024,2048]{1,0:T(8,128)} %cov_ref.3, f32[1024,2048]{1,0:T(8,128)} %cov_ref.3, bf16[8,4,32,512]{3,2,1,0:T(8,128)(2,1)} %all_to_all.26.along_ref, bf16[256,3072]{1,0:T(8,128)(2,1)} %get-tuple-element.22.inverse_ref, ...), custom_call_target="tpu_custom_call" | custom-call | flops 1000000000 | bytes 4000000 | tf_op jit(solution)/shard_map/pallas_call | solution.py:254
  178.3 5.7 %all-to-all-done.4.relaid_ref = f32[16,64,128]{2,1,0:T(8,128)S(1)} async-done(((f32[16,64,128]{2,1,0:T(8,128)}), f32[16,64,128]{2,1,0:T(8,128)S(1)}, u32[]{:S(2)}, u32[]{:S(2)}) %all-to-all-start.4) | async-done | bytes 524320 | tf_op jit(solution)/shard_map/all_to_all | solution.py:442
  184.0 0.8 copy-done.1
  184.8 11.8 %shard_map.63 = (f32[1024,2048]{1,0:T(8,128)}, f32[128,1024]{1,0:T(8,128)}) custom-call(s32[20]{0:T(128)} %concatenate.15.flags, f32[1024,2048]{1,0:T(8,128)} %cov_ref.3, bf16[8,4,32,512]{3,2,1,0:T(8,128)(2,1)} %all_to_all.26.along_ref, bf16[16,4,32,512]{3,2,1,0:T(8,128)(2,1)} %bitcast.42, f32[16,64,128]{2,1,0:T(8,128)} %copy-done.1, ...), custom_call_target="tpu_custom_call" | custom-call | flops 5000000000 | bytes 20000000 | tf_op jit(solution)/shard_map/pallas_call | solution.py:335
  (47 shorter events, 3.3 us)
Async XLA Ops:
  13.7 11.4 %copy-start = (f32[64,16,128]{2,1,0:T(8,128)S(1)}, f32[64,16,128]{2,1,0:T(8,128)}, u32[]{:S(2)}) copy-start(f32[64,16,128]{2,1,0:T(8,128)} %param.5) | copy-start | bytes 1572868
  13.7 37.6 %all-to-all-start = ((f32[8,4,32,512]{3,2,1,0:T(8,128)}), f32[8,4,32,512]{3,2,1,0:T(8,128)S(1)}, u32[]{:S(2)}, u32[]{:S(2)}) async-start(f32[8,4,32,512]{3,2,1,0:T(8,128)} %shard_map.59), calls=%async_computation | async-start | bytes 4194304 | tf_op jit(solution)/shard_map/all_to_all | solution.py:398
  21.8 63.0 %all-gather.5.cloned.1.call-start = ((), (), s32[]{:S(2)}) async-start(), calls=%async_computation.5 | async-start | bytes 1114112 | tf_op jit(solution)/shard_map/all_gather | solution.py:395
  26.6 0.7 collective-permute-start.1
  27.3 0.6 copy-start.4
  51.3 51.3 %copy-start.7 = (s32[64]{0:T(128)S(1)}, s32[64]{0:T(128)}, u32[]{:S(2)}) copy-start(s32[64]{0:T(128)} %param.6) | copy-start | bytes 772
  51.3 1.3 collective-permute-start
  53.5 18.5 %all-to-all-start.1 = ((f32[8,32,512]{2,1,0:T(8,128)}), f32[8,32,512]{2,1,0:T(8,128)S(1)}, u32[]{:S(2)}, u32[]{:S(2)}) async-start(f32[8,32,512]{2,1,0:T(8,128)} %broadcast_in_dim.42), calls=%async_computation.1 | async-start | bytes 1048576 | tf_op jit(solution)/shard_map/all_to_all | solution.py:415
  60.7 123.3 %all-gather.7.cloned.1.call-start = ((), (), s32[]{:S(2)}) async-start(), calls=%async_computation.6 | async-start | bytes 2228224 | tf_op jit(solution)/shard_map/all_gather | solution.py:439
  102.5 3.1 %copy-start.2 = (f32[8,16,768]{2,1,0:T(8,128)}, f32[8,16,768]{2,1,0:T(8,128)S(1)}, u32[]{:S(2)}) copy-start(f32[8,16,768]{2,1,0:T(8,128)S(1)} %all_to_all.25.near_ref) | copy-start | bytes 1179652
  102.5 3.1 %collective-permute-start.2 = (f32[8,16,768]{2,1,0:T(8,128)S(1)}, f32[8,16,768]{2,1,0:T(8,128)S(1)}, u32[]{:S(2)}, u32[]{:S(2)}) collective-permute-start(f32[8,16,768]{2,1,0:T(8,128)S(1)} %all_to_all.25.near_ref), channel_id=1, source_target_pairs={{0,8},{8,0},{16,24},{24,16},{32,40},{40,32},{48,56},{56,48},{64,72... | collective-permute-start | bytes 1179656 | tf_op jit(solution)/shard_map/ppermute | solution.py:430
  103.5 25.4 %copy-start.3 = (f32[4,32,512]{2,1,0:T(8,128)}, f32[4,32,512]{2,1,0:T(8,128)S(1)}, u32[]{:S(2)}) copy-start(f32[4,32,512]{2,1,0:T(8,128)S(1)} %pad_maximum_fusion.piece_ref) | copy-start | bytes 786436
  103.5 25.4 %collective-permute-start.4 = (f32[4,32,512]{2,1,0:T(8,128)S(1)}, f32[4,32,512]{2,1,0:T(8,128)S(1)}, u32[]{:S(2)}, u32[]{:S(2)}) collective-permute-start(f32[4,32,512]{2,1,0:T(8,128)S(1)} %pad_maximum_fusion.piece_ref), channel_id=1, source_target_pairs={{0,0},{1,16},{2,32},{3,48},{4,64},{5,80},{6,96},{7,112},{8,8},{9,2... | collective-permute-start | bytes 786440 | tf_op jit(solution)/shard_map/ppermute | solution.py:433
  104.2 24.7 %collective-permute-start.3 = (f32[16,64,128]{2,1,0:T(8,128)S(1)}, f32[16,64,128]{2,1,0:T(8,128)}, u32[]{:S(2)}, u32[]{:S(2)}) collective-permute-start(f32[16,64,128]{2,1,0:T(8,128)S(1)} %bitcast.39), channel_id=1, source_target_pairs={{0,0},{1,16},{2,32},{3,48},{4,64},{5,80},{6,96},{7,112},{8,8},{9,2... | collective-permute-start | bytes 1572872 | tf_op jit(solution)/shard_map/ppermute | solution.py:434
  105.6 0.7 copy-start.5
  128.9 0.7 copy-start.6
  168.1 15.9 %all-to-all-start.4 = ((f32[16,64,128]{2,1,0:T(8,128)}), f32[16,64,128]{2,1,0:T(8,128)S(1)}, u32[]{:S(2)}, u32[]{:S(2)}) async-start(f32[16,64,128]{2,1,0:T(8,128)} %collective-permute-done.3), calls=%async_computation.4 | async-start | bytes 1048576 | tf_op jit(solution)/shard_map/all_to_all | solution.py:442
  184.0 0.8 copy-start.1
Sparse Core Ops, SparseCore 0:
  28.1 56.7 all-gather.4
  134.4 39.3 all-gather.6

commit v6 on v5

--- a/solution.py
+++ b/solution.py
@@ -46,6 +46,25 @@
         ),
         out_shape=jax.ShapeDtypeStruct((parts, blocks, part, 2 * B), F32),
     )(slots, covariance)
+
+
+def tiles_kernel(where, cov_ref, out_ref):
+    for i in range(B // 8):
+        for j in range(2):
+            out_ref[i, j] = cov_ref[8 * i : 8 * i + 8, 128 * j : 128 * j + 128]
+
+
+def pick_tiles(where, covariance):
+    return pl.pallas_call(
+        tiles_kernel,
+        grid_spec=pltpu.PrefetchScalarGridSpec(
+            num_scalar_prefetch=1,
+            grid=(2,),
+            in_specs=[pl.BlockSpec((B, B), lambda j, where: (where[0], where[1 + j]))],
+            out_specs=pl.BlockSpec((B // 8, 2, 8, 128), lambda j, where: (0, j, 0, 0)),
+        ),
+        out_shape=jax.ShapeDtypeStruct((B // 8, 4, 8, 128), F32),
+    )(where, covariance)
 
 
 def lanes(tile, j):
@@ -123,11 +142,12 @@
         ref[:, start + n * B : start + (n + 1) * B] = term
 
 
-def factor_kernel(flags, near_ref, far_ref, inverse_ref, l10t_ref, lower_ref, diag_ref, work, small, inverse_small):
-    parts, part = near_ref.shape[:2]
-    for ref, first in ((near_ref, flags[1] * part), (far_ref, (1 - flags[1]) * part)):
-        for q in range(parts):
-            diag_ref[pl.ds(pl.multiple_of(q * 2 * part + first, part), part), :] = ref[q]
+def factor_kernel(tiles_ref, inverse_ref, l10t_ref, lower_ref, diag_ref, work, small, inverse_small):
+    for i in range(B // 8):
+        for j in range(4):
+            diag_ref[8 * i : 8 * i + 8, 128 * j : 128 * j + 128] = tiles_ref[4 * i + j, 0:8]
+        for j in range(2):
+            diag_ref[8 * i : 8 * i + 8, 512 + 128 * j : 640 + 128 * j] = tiles_ref[4 * i + 2 + j, 8:16]
     row = lax.broadcasted_iota(jnp.int32, (B, B), 0)
     col = lax.broadcasted_iota(jnp.int32, (B, B), 1)
     eye = jnp.where(row == col, 1.0, 0.0)
@@ -146,10 +166,10 @@
     lower_ref[:, B : 2 * B] = jnp.where(row <= col, work[:, 0:B], 0.0).T
 
 
-def factor_diagonal(flags, near, far):
+def factor_diagonal(tiles):
     return pl.pallas_call(
         factor_kernel,
-        in_specs=[SMEM_SPEC] + [VMEM_SPEC] * 2,
+        in_specs=[VMEM_SPEC],
         out_specs=[VMEM_SPEC] * 3,
         out_shape=[
             jax.ShapeDtypeStruct((B, 12 * B), BF16),
@@ -164,7 +184,7 @@
         ],
         compiler_params=pltpu.CompilerParams(vmem_limit_bytes=VMEM_BYTES),
         cost_estimate=pl.CostEstimate(flops=2 * 10**10, bytes_accessed=80_000_000, transcendentals=0),
-    )(flags, near, far)
+    )(tiles)
 
 
 def solve_rows(first, second, wide, inverse_ref, l10t_ref):
@@ -175,55 +195,32 @@
     return p0, p1
 
 
-def piece_kernel(
-    flags, piece_ref, turned_ref, seen_ref, inverse_ref, l10t_ref, along_ref, across_ref, white_ref, raw, wide
-):
+def piece_kernel(flags, piece_ref, inverse_ref, l10t_ref, along_ref, across_ref, wide):
     blocks, part = piece_ref.shape[:2]
-    held = blocks * part
-    fold = seen_ref.shape[1]
-    raw[0:held, :] = piece_ref[...].reshape(held, 2 * B)
-    raw[held : 2 * held, :] = turned_ref[...].reshape(held, 2 * B)
-    for panel in range(2):
-        for h in range(2):
-            for parity in range(2):
-                for f in range(2):
-                    lane = (2 * f + panel) * 128
-                    top = 2 * held + (2 * parity + f) * fold
-                    raw[top : top + fold, panel * B + h * 128 : panel * B + (h + 1) * 128] = seen_ref[
-                        4 * flags[6 + panel] + 2 * h + parity, :, lane : lane + 128
-                    ]
+    raw = piece_ref[...].reshape(blocks * part, 2 * B)
     for panel, p in enumerate(solve_rows(raw[:, 0:B], raw[:, B : 2 * B], wide, inverse_ref, l10t_ref)):
         cut = slice(panel * B, (panel + 1) * B)
-        white_ref[:, cut] = p[2 * held :]
         for b in range(blocks):
             mine = p[b * part : (b + 1) * part].astype(BF16)
             mine = jnp.where(flags[16 + b] > panel, mine, jnp.zeros_like(mine))
+            across_ref[b, :, cut] = mine
             for q in range(along_ref.shape[0]):
                 along_ref[q, b, :, cut] = mine
-            theirs = p[held + b * part : held + (b + 1) * part].astype(BF16)
-            level = flags[8 + flags[1] * blocks + b]
-            across_ref[b, :, cut] = jnp.where(level > panel, theirs, jnp.zeros_like(theirs))
-
-
-def solve_pieces(flags, piece, turned, seen, inverse, l10t, parts):
-    held = piece.shape[0] * piece.shape[1]
-    particles = 4 * seen.shape[1]
+
+
+def solve_piece(flags, piece, inverse, l10t, parts):
     return pl.pallas_call(
         piece_kernel,
-        in_specs=[SMEM_SPEC] + [VMEM_SPEC] * 5,
-        out_specs=[VMEM_SPEC] * 3,
-        scratch_shapes=[
-            pltpu.VMEM((2 * held + particles, 2 * B), F32),
-            pltpu.VMEM((2 * held + particles, 6 * B), BF16),
-        ],
+        in_specs=[SMEM_SPEC] + [VMEM_SPEC] * 3,
+        out_specs=[VMEM_SPEC] * 2,
+        scratch_shapes=[pltpu.VMEM((piece.shape[0] * piece.shape[1], 6 * B), BF16)],
         out_shape=[
             jax.ShapeDtypeStruct((parts,) + piece.shape, BF16),
             jax.ShapeDtypeStruct(piece.shape, BF16),
-            jax.ShapeDtypeStruct((particles, 2 * B), F32),
         ],
         compiler_params=pltpu.CompilerParams(vmem_limit_bytes=VMEM_BYTES),
         cost_estimate=pl.CostEstimate(flops=10**9, bytes_accessed=4_000_000, transcendentals=0),
-    )(flags, piece, turned, seen, inverse, l10t)
+    )(flags, piece, inverse, l10t)
 
 
 def whole(*shape):
@@ -273,14 +270,28 @@
 
 
 def update_kernel(
-    flags, cov_ref, along_ref, across_ref, relaid_ref, white_ref, panel_ref, lower_ref, out_ref, solved_ref, columns
+    flags,
+    cov_ref,
+    along_ref,
+    across_ref,
+    relaid_ref,
+    panel_ref,
+    lower_ref,
+    inverse_ref,
+    l10t_ref,
+    out_ref,
+    solved_ref,
+    columns,
+    white_ref,
+    wide,
 ):
     i = pl.program_id(0)
     parts, _, part = along_ref.shape[:3]
-    blocks = across_ref.shape[1]
+    blocks = across_ref.shape[1] - 3
     steps = parts // 2
     column_blocks = 2 * blocks
     half = relaid_ref.shape[1]
+    fold = half // 2
 
     @pl.when(i == 0)
     def _():
@@ -290,6 +301,22 @@
                 for b in range(blocks):
                     top = (parity * blocks + b) * B + q * part
                     columns[top : top + part, :] = across_ref[first + parity, b]
+        for panel in range(2):
+            for h in range(2):
+                for parity in range(2):
+                    for f in range(2):
+                        lane = (2 * f + panel) * 128
+                        terms = [
+                            across_ref[4 * flags[6 + panel] + 2 * h + parity, blocks + t, :, lane : lane + 128].astype(F32)
+                            for t in range(3)
+                        ]
+                        top = (2 * parity + f) * fold
+                        white_ref[top : top + fold, panel * B + h * 128 : panel * B + (h + 1) * 128] = (
+                            terms[0] + terms[1]
+                        ) + terms[2]
+        w0, w1 = solve_rows(white_ref[:, 0:B], white_ref[:, B : 2 * B], wide, inverse_ref, l10t_ref)
+        white_ref[:, 0:B] = w0
+        white_ref[:, B : 2 * B] = w1
 
     level = flags[16 + i]
     own = along_ref[:, 0].reshape(parts * part, 2 * B)
@@ -328,7 +355,7 @@
             solved_ref[...] = white_ref[:, panel * B : (panel + 1) * B]
 
 
-def update(flags, covariance, along, across, relaid, white, panels, lower):
+def update(flags, covariance, along, across, relaid, panels, lower, inverse, l10t):
     rows, columns = covariance.shape
     parts, blocks, part, width = along.shape
     half = relaid.shape[1]
@@ -342,20 +369,25 @@
                 pl.BlockSpec((parts, 1, part, width), lambda i, flags: (0, i, 0, 0)),
                 whole(*across.shape),
                 pl.BlockSpec((4, half, 128), lambda i, flags: (lax.rem(i + flags[0], blocks), 0, 0)),
-                whole(*white.shape),
-                pl.BlockSpec((B, width), lambda i, flags: (i, 0)),
+                pl.BlockSpec((B, width), lambda i, flags: (jnp.where((flags[4] & flags[5]) >= 0, i, 0), 0)),
                 whole(*lower.shape),
+                whole(*inverse.shape),
+                whole(*l10t.shape),
             ],
             out_specs=[
                 pl.BlockSpec((B, columns), lambda i, flags: (i, 0)),
                 pl.BlockSpec((2 * half, B), lambda i, flags: (0, i)),
             ],
-            scratch_shapes=[pltpu.VMEM((columns, width), BF16)],
+            scratch_shapes=[
+                pltpu.VMEM((columns, width), BF16),
+                pltpu.VMEM((2 * half, width), F32),
+                pltpu.VMEM((2 * half, 6 * B), BF16),
+            ],
         ),
         out_shape=[jax.ShapeDtypeStruct((rows, columns), F32), jax.ShapeDtypeStruct((2 * half, rows), F32)],
         compiler_params=pltpu.CompilerParams(vmem_limit_bytes=VMEM_BYTES),
         cost_estimate=pl.CostEstimate(flops=5 * 10**9, bytes_accessed=20_000_000, transcendentals=0),
-    )(flags, covariance, along, across, relaid, white, panels, lower)
+    )(flags, covariance, along, across, relaid, panels, lower, inverse, l10t)
 
 
 def per_device(covariance, innovations, block_owner, panel_index, *, n_row, n_col):
@@ -370,8 +402,6 @@
     levels = jnp.sum((block_owner[:, None] > targets[None, :]).astype(jnp.int32), axis=1)
     steps = n_row // 4
     shift, core = c // 2, r % 2
-    pairs = [(a, a ^ 1) for a in range(n_row)]
-    same_core = [[a for a in range(n_row) if a % 2 == k] for k in range(2)]
     flags = jnp.concatenate(
         [
             shift[None],
@@ -389,12 +419,25 @@
         for b in range(n_col)
     ]
 
-    fold = innovations.shape[0] // 2
-    wanted = [lax.dynamic_index_in_dim(innovations, row_root[n], 1, keepdims=False) for n in range(2)]
-    wanted = jnp.concatenate([w[h * fold : (h + 1) * fold] for h in range(2) for w in wanted], axis=1)
-    seen = lax.all_gather(lax.ppermute(wanted, ("row", "col"), across_axes), "row", axis=0)
+    chosen = jnp.where(r == row_root[0], row_slot[0], row_slot[1])
+    where = jnp.concatenate([chosen[None], column_slot]).astype(jnp.int32)
+    tiles = pick_tiles(where, covariance).reshape(n_row * n_col, 8, 128)
+    tiles = lax.all_to_all(tiles, ("row", "col"), split_axis=0, concat_axis=0, tiled=True)
+    source = jnp.where(c % 4 < 2, column_root[0], column_root[1])
+    tiles = jnp.concatenate(
+        [lax.dynamic_index_in_dim(tiles, row_root[n] * n_col + source, 0, keepdims=False) for n in range(2)], axis=0
+    )
+    tiles = lax.all_to_all(
+        jnp.broadcast_to(tiles[None], (n_row * n_col,) + tiles.shape),
+        ("row", "col"),
+        split_axis=0,
+        concat_axis=0,
+        tiled=True,
+    )
+    inverse, l10t, lower = factor_diagonal(tiles)
 
     picked = pick_columns(column_slot.astype(jnp.int32), covariance, n_col)
+    picked, _ = lax.optimization_barrier((picked, tiles))
     parts = lax.all_to_all(picked, "col", split_axis=0, concat_axis=0, tiled=True)
     part = parts.shape[2]
     piece = jnp.concatenate(
@@ -405,43 +448,24 @@
         axis=-1,
     )
 
-    chosen = jnp.where(r == row_root[0], row_slot[0], row_slot[1])
-    mine = lax.dynamic_index_in_dim(piece, chosen, 0, keepdims=False)
-    half = part // 2
-    kept = lax.dynamic_slice_in_dim(mine, core * half, half, 0)
-    given = lax.ppermute(lax.dynamic_slice_in_dim(mine, (1 - core) * half, half, 0), "row", pairs)
-    both = jnp.concatenate([jnp.where(core == 0, kept, given), jnp.where(core == 0, given, kept)], axis=0)
-
-    spread = lax.all_to_all(
-        jnp.broadcast_to(both[None], (n_row // 2,) + both.shape),
-        "row",
-        split_axis=0,
-        concat_axis=0,
-        tiled=True,
-        axis_index_groups=same_core,
-    )
-    upper = lax.dynamic_slice(spread, (row_root[0] // 2, row_root[0] % 2 * half, 0), (1, half, 2 * B))[0]
-    lower = lax.dynamic_slice(spread, (row_root[1] // 2, row_root[1] % 2 * half, B), (1, half, B))[0]
-    strip = jnp.concatenate([upper, lower], axis=-1)
-    strip, seen = lax.optimization_barrier((strip, seen))
-    near = lax.all_to_all(
-        jnp.broadcast_to(strip[None], (n_col,) + strip.shape), "col", split_axis=0, concat_axis=0, tiled=True
-    )
-    far = lax.ppermute(near, "row", pairs)
-
-    sent, groups, _ = lax.optimization_barrier((piece, jnp.transpose(innovations, (1, 0, 2)), near))
-    turned = lax.ppermute(sent, ("row", "col"), across_axes)
+    fold = innovations.shape[0] // 2
+    wanted = [lax.dynamic_index_in_dim(innovations, row_root[n], 1, keepdims=False) for n in range(2)]
+    wanted = jnp.concatenate([w[h * fold : (h + 1) * fold] for h in range(2) for w in wanted], axis=1)
+    high = lax.reduce_precision(wanted, 8, 7)
+    middle = lax.reduce_precision(wanted - high, 8, 7)
+    wanted = jnp.stack([high, middle, wanted - high - middle]).astype(BF16)
+
+    along, across = solve_piece(flags, piece, inverse, l10t, n_col)
+    across = lax.ppermute(jnp.concatenate([across, wanted], axis=0), ("row", "col"), across_axes)
+    across_all = lax.all_gather(across, "row", axis=0)
+    along = lax.all_to_all(along, "col", split_axis=0, concat_axis=0, tiled=True)
+
+    groups, _ = lax.optimization_barrier((jnp.transpose(innovations, (1, 0, 2)), across))
     groups = lax.ppermute(groups, ("row", "col"), across_axes)
-    inverse, l10t, lower = factor_diagonal(flags, near, far)
-    inverse, groups = lax.optimization_barrier((inverse, groups))
-
-    along, across, white = solve_pieces(flags, piece, turned, seen, inverse, l10t, n_col)
-    across = lax.all_gather(across, "row", axis=0)
-    along = lax.all_to_all(along, "col", split_axis=0, concat_axis=0, tiled=True)
-    groups, along = lax.optimization_barrier((groups, along))
+    along, groups = lax.optimization_barrier((along, groups))
     relaid = lax.all_to_all(groups, "row", split_axis=0, concat_axis=0, tiled=True)
     panels = solve_panels(flags, covariance, along, inverse, l10t)
-    return update(flags, covariance, along, across, relaid, white, panels, lower)
+    return update(flags, covariance, along, across_all, relaid, panels, lower, inverse, l10t)
 
 
 def solution(mesh):

time: 204 us -> 189 us (0.926)
  blocking collectives: 51.5 us -> 0 us
  starting transfers between devices: 23.3 us -> 45.2 us
  waiting for transfers between devices: 43.9 us -> 54.4 us
  Pallas kernels: 48.5 us -> 52.2 us
    all_to_all x2 -> x0, blocking collectives: 51.5 us -> none  [the longest x1 33.8 us: per_device(): lax.all_to_all(along, 'col', split_axis=0, concat_axis=0, tiled=True)]
    all_to_all x1 -> x3, waiting for transfers between devices: 7.4 us -> 42.5 us  [the longest x1 26 us: per_device(): lax.all_to_all(along, 'col', split_axis=0, concat_axis=0, tiled=True)]
    all_to_all x1 -> x3, starting transfers between devices: 7.2 us -> 31.7 us  [the longest x1 16 us: per_device(): lax.all_to_all(along, 'col', split_axis=0, concat_axis=0, tiled=True)]
    all_gather x2 -> x1, waiting for transfers between devices: 12.9 us -> 0.01 us  [per_device(): across_all = lax.all_gather(across, 'row', axis=0)]
    all_to_all x1, waiting for transfers between devices: 16.7 us -> 6.24 us  [per_device(): lax.all_to_all(picked, 'col', split_axis=0, concat_axis=0, tiled=True)]
    all_to_all x1, starting transfers between devices: 8.16 us -> 3.6 us  [per_device(): lax.all_to_all(picked, 'col', split_axis=0, concat_axis=0, tiled=True)]
    all_to_all x1, starting transfers between devices: 5.01 us -> 7.5 us  [per_device(): lax.all_to_all(groups, 'row', split_axis=0, concat_axis=0, tiled=True)]
    pallas_call x2 -> x3, Pallas kernels: 27.2 us -> 28.9 us  [the longest x1 22.6 us: factor_diagonal(): pl.pallas_call(factor_kernel, in_specs=[VMEM_SPEC], out_specs=[VMEM_SPEC]...]
  transfers between devices with their start and end apart: 10 -> 8, of which waited for: 5 -> 5; matrix products, arithmetic and copies ran while one was open for 2% -> 1% of each run, Pallas kernels for 14% -> 17%
where the time goes in v6:
time: 189 us; the launch traced here: 188 us
  waiting for transfers between devices  54.4 us (29%)
  Pallas kernels  52.2 us (28%)
  starting transfers between devices  45.2 us (24%)
  between operations  26.6 us (14%)
  local copies, waits for them, and re-layouts  5.87 us (3%)
  other arithmetic  3.3 us (2%)
    all_to_all x1, waiting for transfers between devices, per_device(): lax.all_to_all(along, 'col', split_axis=0, concat_axis=0, tiled=True)  26 us
    pallas_call x1, Pallas kernels, factor_diagonal(): pl.pallas_call(factor_kernel, in_specs=[VMEM_SPEC], out_specs=[VMEM_SPEC]...  22.6 us
    all_to_all x1, starting transfers between devices, per_device(): lax.all_to_all(along, 'col', split_axis=0, concat_axis=0, tiled=True)  16 us
    pallas_call x1, Pallas kernels, update(): pl.pallas_call(update_kernel, grid_spec=pltpu.PrefetchScalarGridSpec(num_...  13.5 us
    all_to_all x1, starting transfers between devices, per_device(): lax.all_to_all(tiles, ('row', 'col'), split_axis=0, concat_axis=0, tiled=...  11.1 us
    all_to_all x1, waiting for transfers between devices, per_device(): lax.all_to_all(tiles, ('row', 'col'), split_axis=0, concat_axis=0, tiled=...  10.9 us
    all_to_all x1, starting transfers between devices, per_device(): lax.all_to_all(groups, 'row', split_axis=0, concat_axis=0, tiled=True)  7.5 us
    all_to_all x1, waiting for transfers between devices, per_device(): lax.all_to_all(picked, 'col', split_axis=0, concat_axis=0, tiled=True)  6.24 us
  transfers between devices with their start and end apart: 8, of which 5 were waited for; matrix products, arithmetic and copies ran while one was open for 1% of the time, Pallas kernels for 17%

profile of v6, /device:TPU:0, one launch (start us, length us, event | category | flops | bytes accessed | tf_op | source)
XLA Modules:
  0.0 187.5 jit_solution(7055217525260311614)
XLA Ops:
  7.8 0.8 fusion.1
  12.5 2.4 %shard_map.60 = f32[32,4,8,128]{3,2,1,0:T(8,128)} custom-call(s32[3]{0:T(128)} %pad_add_fusion.where, f32[1024,2048]{1,0:T(8,128)} %cov_ref.5), custom_call_target="tpu_custom_call" | custom-call | tf_op jit(solution)/shard_map/pallas_call | solution.py:58
  14.9 11.1 %all-to-all-start = ((f32[128,8,128]{2,1,0:T(8,128)}), f32[128,8,128]{2,1,0:T(8,128)S(1)}, u32[]{:S(2)}, u32[]{:S(2)}) async-start(f32[128,8,128]{2,1,0:T(8,128)} %bitcast.31), calls=%async_computation | async-start | bytes 1048576 | tf_op jit(solution)/shard_map/all_to_all | solution.py:425
  28.5 10.9 %all-to-all-done = f32[128,8,128]{2,1,0:T(8,128)S(1)} async-done(((f32[128,8,128]{2,1,0:T(8,128)}), f32[128,8,128]{2,1,0:T(8,128)S(1)}, u32[]{:S(2)}, u32[]{:S(2)}) %all-to-all-start) | async-done | bytes 524320 | tf_op jit(solution)/shard_map/all_to_all | solution.py:425
  39.4 1.1 broadcast_in_dim.40
  40.5 4.6 %all-to-all-start.1 = ((f32[128,16,128]{2,1,0:T(8,128)}), f32[128,16,128]{2,1,0:T(8,128)S(1)}, u32[]{:S(2)}, u32[]{:S(2)}) async-start(f32[128,16,128]{2,1,0:T(8,128)} %broadcast_in_dim.40), calls=%async_computation.1 | async-start | bytes 2097152 | tf_op jit(solution)/shard_map/all_to_all | solution.py:430
  50.0 4.6 %shard_map.59 = f32[8,4,32,512]{3,2,1,0:T(8,128)} custom-call(s32[2]{0:T(128)} %copy-done.7, f32[1024,2048]{1,0:T(8,128)} %cov_ref.5), custom_call_target="tpu_custom_call" | custom-call | tf_op jit(solution)/shard_map/pallas_call | solution.py:39
  58.2 5.6 %all-to-all-done.1.tiles_ref = f32[128,16,128]{2,1,0:T(8,128)S(1)} async-done(((f32[128,16,128]{2,1,0:T(8,128)}), f32[128,16,128]{2,1,0:T(8,128)S(1)}, u32[]{:S(2)}, u32[]{:S(2)}) %all-to-all-start.1) | async-done | bytes 1048608 | tf_op jit(solution)/shard_map/all_to_all | solution.py:430
  63.9 1.0 copy-done.1
  64.9 3.6 %all-to-all-start.2 = ((f32[8,4,32,512]{3,2,1,0:T(8,128)}), f32[8,4,32,512]{3,2,1,0:T(8,128)S(1)}, u32[]{:S(2)}, u32[]{:S(2)}) async-start(f32[8,4,32,512]{3,2,1,0:T(8,128)} %shard_map.59), calls=%async_computation.2 | async-start | bytes 4194304 | tf_op jit(solution)/shard_map/all_to_all | solution.py:441
  68.7 22.6 %shard_map.61 = (bf16[256,3072]{1,0:T(8,128)(2,1)}, bf16[256,256]{1,0:T(8,128)(2,1)}, f32[256,512]{1,0:T(8,128)}) custom-call(f32[128,16,128]{2,1,0:T(8,128)} %copy-done.1), custom_call_target="tpu_custom_call" | custom-call | flops 20000000000 | bytes 80000000 | tf_op jit(solution)/shard_map/pallas_call | solution.py:170
  91.3 6.2 %all-to-all-done.2 = f32[8,4,32,512]{3,2,1,0:T(8,128)S(1)} async-done(((f32[8,4,32,512]{3,2,1,0:T(8,128)}), f32[8,4,32,512]{3,2,1,0:T(8,128)S(1)}, u32[]{:S(2)}, u32[]{:S(2)}) %all-to-all-start.2) | async-done | bytes 2097184 | tf_op jit(solution)/shard_map/all_to_all | solution.py:441
  97.6 0.7 pad_maximum_fusion.piece_ref
  98.3 3.8 %shard_map.62 = (bf16[8,4,32,512]{3,2,1,0:T(8,128)(2,1)}, bf16[4,32,512]{2,1,0:T(8,128)(2,1)}) custom-call(s32[20]{0:T(128)} %concatenate.51.flags, f32[4,32,512]{2,1,0:T(8,128)} %pad_maximum_fusion.piece_ref, bf16[256,3072]{1,0:T(8,128)(2,1)} %get-tuple-element.12.inverse_ref, bf16[256,256]{1,0:T(8,128)(2,1)} %get-tuple-element.13.l10t_ref), custom_call_target="tpu_custom_call" | custom-call | flops 1000000000 | bytes 4000000 | tf_op jit(solution)/shard_map/pallas_call | solution.py:212
  102.2 1.0 pad_maximum_fusion.1
  103.9 0.7 copy-done.6
  104.6 16.0 %all-to-all-start.3 = ((bf16[8,4,32,512]{3,2,1,0:T(8,128)(2,1)}), bf16[8,4,32,512]{3,2,1,0:T(8,128)(2,1)S(1)}, u32[]{:S(2)}, u32[]{:S(2)}) async-start(bf16[8,4,32,512]{3,2,1,0:T(8,128)(2,1)} %get-tuple-element.14), calls=%async_computation.3 | async-start | bytes 2097152 | tf_op jit(solution)/shard_map/all_to_all | solution.py:461
  120.6 1.5 collective-permute-start.1
  122.0 26.0 %all-to-all-done.3.along_ref = bf16[8,4,32,512]{3,2,1,0:T(8,128)(2,1)S(1)} async-done(((bf16[8,4,32,512]{3,2,1,0:T(8,128)(2,1)}), bf16[8,4,32,512]{3,2,1,0:T(8,128)(2,1)S(1)}, u32[]{:S(2)}, u32[]{:S(2)}) %all-to-all-start.3) | async-done | bytes 1048608 | tf_op jit(solution)/shard_map/all_to_all | solution.py:461
  148.0 7.5 %all-to-all-start.4 = ((f32[16,64,128]{2,1,0:T(8,128)}), f32[16,64,128]{2,1,0:T(8,128)S(1)}, u32[]{:S(2)}, u32[]{:S(2)}) async-start(f32[16,64,128]{2,1,0:T(8,128)} %collective-permute-done.1), calls=%async_computation.4 | async-start | bytes 1048576 | tf_op jit(solution)/shard_map/all_to_all | solution.py:466
  155.5 5.1 %shard_map.63.panel_ref = f32[1024,512]{1,0:T(8,128)} custom-call(s32[20]{0:T(128)} %concatenate.51.flags, f32[1024,2048]{1,0:T(8,128)} %cov_ref.5, f32[1024,2048]{1,0:T(8,128)} %cov_ref.5, bf16[8,4,32,512]{3,2,1,0:T(8,128)(2,1)} %copy-done, bf16[256,3072]{1,0:T(8,128)(2,1)} %get-tuple-element.12.inverse_ref, bf16[256,256]{1,0:T(8,128)(2,1)} %get-tuple-element.13.l10t_ref), custom_call_target="tpu_custom_call" | custom-call | flops 1000000000 | bytes 4000000 | tf_op jit(solution)/shard_map/pallas_call | solution.py:251
  160.7 5.7 %all-to-all-done.4.relaid_ref = f32[16,64,128]{2,1,0:T(8,128)S(1)} async-done(((f32[16,64,128]{2,1,0:T(8,128)}), f32[16,64,128]{2,1,0:T(8,128)S(1)}, u32[]{:S(2)}, u32[]{:S(2)}) %all-to-all-start.4) | async-done | bytes 524320 | tf_op jit(solution)/shard_map/all_to_all | solution.py:466
  166.4 0.8 copy-done.5
  167.2 13.5 %shard_map.64 = (f32[1024,2048]{1,0:T(8,128)}, f32[128,1024]{1,0:T(8,128)}) custom-call(s32[20]{0:T(128)} %concatenate.51.flags, f32[1024,2048]{1,0:T(8,128)} %cov_ref.5, bf16[8,4,32,512]{3,2,1,0:T(8,128)(2,1)} %copy-done, bf16[16,7,32,512]{3,2,1,0:T(8,128)(2,1)} %bitcast.33, f32[16,64,128]{2,1,0:T(8,128)} %copy-done.5, f32[1024,512]{1,0:T(8,128)} %shard_map.63.panel_ref, ...), custom_call_target="tpu_custom_call" | custom-call | flops 5000000000 | bytes 20000000 | tf_op jit(solution)/shard_map/pallas_call | solution.py:362
  (37 shorter events, 4.0 us)
Async XLA Ops:
  8.7 6.2 %copy-start.7 = (s32[2]{0:T(128)}, s32[2]{0:T(128)S(1)}, u32[]{:S(2)}) copy-start(s32[2]{0:T(128)S(1)} %get-tuple-element.24.slots) | copy-start | bytes 28
  14.9 24.5 %all-to-all-start = ((f32[128,8,128]{2,1,0:T(8,128)}), f32[128,8,128]{2,1,0:T(8,128)S(1)}, u32[]{:S(2)}, u32[]{:S(2)}) async-start(f32[128,8,128]{2,1,0:T(8,128)} %bitcast.31), calls=%async_computation | async-start | bytes 1048576 | tf_op jit(solution)/shard_map/all_to_all | solution.py:425
  40.5 23.4 %all-to-all-start.1 = ((f32[128,16,128]{2,1,0:T(8,128)}), f32[128,16,128]{2,1,0:T(8,128)S(1)}, u32[]{:S(2)}, u32[]{:S(2)}) async-start(f32[128,16,128]{2,1,0:T(8,128)} %broadcast_in_dim.40), calls=%async_computation.1 | async-start | bytes 2097152 | tf_op jit(solution)/shard_map/all_to_all | solution.py:430
  50.0 4.6 %copy-start.8 = (s32[64]{0:T(128)S(1)}, s32[64]{0:T(128)}, u32[]{:S(2)}) copy-start(s32[64]{0:T(128)} %param.6) | copy-start | bytes 772
  50.0 4.8 %copy-start.4 = (f32[64,16,128]{2,1,0:T(8,128)S(1)}, f32[64,16,128]{2,1,0:T(8,128)}, u32[]{:S(2)}) copy-start(f32[64,16,128]{2,1,0:T(8,128)} %param.5) | copy-start | bytes 1572868
  55.1 8.8 %copy-start.2 = (f32[64,16,128]{2,0,1:T(8,128)}, f32[64,16,128]{2,0,1:T(8,128)S(1)}, u32[]{:S(2)}) copy-start(f32[64,16,128]{2,0,1:T(8,128)S(1)} %copy.17) | copy-start | bytes 1572868
  63.9 1.0 copy-start.1
  64.9 32.7 %all-to-all-start.2 = ((f32[8,4,32,512]{3,2,1,0:T(8,128)}), f32[8,4,32,512]{3,2,1,0:T(8,128)S(1)}, u32[]{:S(2)}, u32[]{:S(2)}) async-start(f32[8,4,32,512]{3,2,1,0:T(8,128)} %shard_map.59), calls=%async_computation.2 | async-start | bytes 4194304 | tf_op jit(solution)/shard_map/all_to_all | solution.py:441
  68.5 97.9 %all-gather.3.cloned.1.call-start = ((), (), s32[]{:S(2)}) async-start(), calls=%async_computation.5 | async-start | bytes 3899392 | tf_op jit(solution)/shard_map/all_gather | solution.py:460
  102.2 18.4 %copy-start.3 = (f32[64,16,128]{2,0,1:T(8,128)S(1)}, f32[64,16,128]{2,0,1:T(8,128)}, u32[]{:S(2)}) copy-start(f32[64,16,128]{2,0,1:T(8,128)} %copy-done.2) | copy-start | bytes 1572868
  103.2 0.7 collective-permute-start
  103.9 0.7 copy-start.6
  104.6 43.4 %all-to-all-start.3 = ((bf16[8,4,32,512]{3,2,1,0:T(8,128)(2,1)}), bf16[8,4,32,512]{3,2,1,0:T(8,128)(2,1)S(1)}, u32[]{:S(2)}, u32[]{:S(2)}) async-start(bf16[8,4,32,512]{3,2,1,0:T(8,128)(2,1)} %get-tuple-element.14), calls=%async_computation.3 | async-start | bytes 2097152 | tf_op jit(solution)/shard_map/all_to_all | solution.py:461
  120.6 1.5 collective-permute-start.1
  148.0 7.5 %copy-start = (bf16[8,4,32,512]{3,2,1,0:T(8,128)(2,1)}, bf16[8,4,32,512]{3,2,1,0:T(8,128)(2,1)S(1)}, u32[]{:S(2)}) copy-start(bf16[8,4,32,512]{3,2,1,0:T(8,128)(2,1)S(1)} %all-to-all-done.3.along_ref) | copy-start | bytes 3145732
  148.0 18.4 %all-to-all-start.4 = ((f32[16,64,128]{2,1,0:T(8,128)}), f32[16,64,128]{2,1,0:T(8,128)S(1)}, u32[]{:S(2)}, u32[]{:S(2)}) async-start(f32[16,64,128]{2,1,0:T(8,128)} %collective-permute-done.1), calls=%async_computation.4 | async-start | bytes 1048576 | tf_op jit(solution)/shard_map/all_to_all | solution.py:466
  166.4 0.8 copy-start.5
Sparse Core Ops, SparseCore 0:
  104.7 49.4 all-gather.2

commit v7 on v6

--- a/solution.py
+++ b/solution.py
@@ -48,23 +48,40 @@
     )(slots, covariance)
 
 
-def tiles_kernel(where, cov_ref, out_ref):
-    for i in range(B // 8):
-        for j in range(2):
-            out_ref[i, j] = cov_ref[8 * i : 8 * i + 8, 128 * j : 128 * j + 128]
-
-
-def pick_tiles(where, covariance):
+def tiles_kernel(owner_ref, panel_ref, cov_ref, out_ref, held, arrived):
+    slots = [jnp.int32(0), jnp.int32(0)]
+    for place in range(owner_ref.shape[0]):
+        for n in range(2):
+            slots[n] = jnp.where(owner_ref[place] == panel_ref[0] + n, place, slots[n])
+    row_blocks, column_blocks = cov_ref.shape[0] // B, cov_ref.shape[1] // B
+    first_here = lax.div(slots[0], row_blocks) == lax.axis_index("row")
+    row = lax.rem(jnp.where(first_here, slots[0], slots[1]), row_blocks)
+    copies = []
+    for n in range(2):
+        column = lax.rem(slots[n], column_blocks)
+        copies.append(
+            pltpu.make_async_copy(
+                cov_ref.at[pl.ds(pl.multiple_of(row * B, B), B), pl.ds(pl.multiple_of(column * B, B), B)],
+                held.at[n],
+                arrived.at[n],
+            )
+        )
+        copies[n].start()
+    for n in range(2):
+        copies[n].wait()
+        for i in range(B // 8):
+            for j in range(2):
+                out_ref[i, 2 * n + j] = held[n, 8 * i : 8 * i + 8, 128 * j : 128 * j + 128]
+
+
+def pick_tiles(block_owner, panel_index, covariance):
     return pl.pallas_call(
         tiles_kernel,
-        grid_spec=pltpu.PrefetchScalarGridSpec(
-            num_scalar_prefetch=1,
-            grid=(2,),
-            in_specs=[pl.BlockSpec((B, B), lambda j, where: (where[0], where[1 + j]))],
-            out_specs=pl.BlockSpec((B // 8, 2, 8, 128), lambda j, where: (0, j, 0, 0)),
-        ),
+        in_specs=[SMEM_SPEC, SMEM_SPEC, pl.BlockSpec(memory_space=pl.ANY)],
+        out_specs=VMEM_SPEC,
         out_shape=jax.ShapeDtypeStruct((B // 8, 4, 8, 128), F32),
-    )(where, covariance)
+        scratch_shapes=[pltpu.VMEM((2, B, B), F32), pltpu.SemaphoreType.DMA((2,))],
+    )(block_owner, panel_index, covariance)
 
 
 def lanes(tile, j):
@@ -182,7 +199,7 @@
             pltpu.VMEM((S, 2 * S), F32),
             pltpu.VMEM((S, S), F32),
         ],
-        compiler_params=pltpu.CompilerParams(vmem_limit_bytes=VMEM_BYTES),
+        compiler_params=pltpu.CompilerParams(vmem_limit_bytes=VMEM_BYTES // 4),
         cost_estimate=pl.CostEstimate(flops=2 * 10**10, bytes_accessed=80_000_000, transcendentals=0),
     )(tiles)
 
@@ -195,10 +212,12 @@
     return p0, p1
 
 
-def piece_kernel(flags, piece_ref, inverse_ref, l10t_ref, along_ref, across_ref, wide):
-    blocks, part = piece_ref.shape[:2]
-    raw = piece_ref[...].reshape(blocks * part, 2 * B)
-    for panel, p in enumerate(solve_rows(raw[:, 0:B], raw[:, B : 2 * B], wide, inverse_ref, l10t_ref)):
+def piece_kernel(flags, first_ref, second_ref, inverse_ref, l10t_ref, along_ref, across_ref, wide):
+    blocks, part = first_ref.shape[1:3]
+    solved = solve_rows(
+        first_ref[0].reshape(blocks * part, B), second_ref[0].reshape(blocks * part, B), wide, inverse_ref, l10t_ref
+    )
+    for panel, p in enumerate(solved):
         cut = slice(panel * B, (panel + 1) * B)
         for b in range(blocks):
             mine = p[b * part : (b + 1) * part].astype(BF16)
@@ -208,19 +227,29 @@
                 along_ref[q, b, :, cut] = mine
 
 
-def solve_piece(flags, piece, inverse, l10t, parts):
+def solve_piece(flags, parts, inverse, l10t):
+    count, blocks, part = parts.shape[:3]
     return pl.pallas_call(
         piece_kernel,
-        in_specs=[SMEM_SPEC] + [VMEM_SPEC] * 3,
-        out_specs=[VMEM_SPEC] * 2,
-        scratch_shapes=[pltpu.VMEM((piece.shape[0] * piece.shape[1], 6 * B), BF16)],
+        grid_spec=pltpu.PrefetchScalarGridSpec(
+            num_scalar_prefetch=1,
+            grid=(1,),
+            in_specs=[
+                pl.BlockSpec((1, blocks, part, B), lambda i, flags: (flags[20], 0, 0, 0)),
+                pl.BlockSpec((1, blocks, part, B), lambda i, flags: (flags[21], 0, 0, 1)),
+                whole(*inverse.shape),
+                whole(*l10t.shape),
+            ],
+            out_specs=[whole(count, blocks, part, 2 * B), whole(blocks, part, 2 * B)],
+            scratch_shapes=[pltpu.VMEM((blocks * part, 6 * B), BF16)],
+        ),
         out_shape=[
-            jax.ShapeDtypeStruct((parts,) + piece.shape, BF16),
-            jax.ShapeDtypeStruct(piece.shape, BF16),
+            jax.ShapeDtypeStruct((count, blocks, part, 2 * B), BF16),
+            jax.ShapeDtypeStruct((blocks, part, 2 * B), BF16),
         ],
-        compiler_params=pltpu.CompilerParams(vmem_limit_bytes=VMEM_BYTES),
+        compiler_params=pltpu.CompilerParams(vmem_limit_bytes=VMEM_BYTES // 4),
         cost_estimate=pl.CostEstimate(flops=10**9, bytes_accessed=4_000_000, transcendentals=0),
-    )(flags, piece, inverse, l10t)
+    )(flags, parts, parts, inverse, l10t)
 
 
 def whole(*shape):
@@ -264,7 +293,7 @@
             scratch_shapes=[pltpu.VMEM((B, 6 * B), BF16)],
         ),
         out_shape=jax.ShapeDtypeStruct((rows, 2 * B), F32),
-        compiler_params=pltpu.CompilerParams(vmem_limit_bytes=VMEM_BYTES),
+        compiler_params=pltpu.CompilerParams(vmem_limit_bytes=VMEM_BYTES // 4),
         cost_estimate=pl.CostEstimate(flops=10**9, bytes_accessed=4_000_000, transcendentals=0),
     )(flags, covariance, covariance, along, inverse, l10t)
 
@@ -282,8 +311,10 @@
     out_ref,
     solved_ref,
     columns,
+    terms_ref,
     white_ref,
     wide,
+    arrived,
 ):
     i = pl.program_id(0)
     parts, _, part = along_ref.shape[:3]
@@ -295,20 +326,27 @@
 
     @pl.when(i == 0)
     def _():
+        copies = []
+        for panel in range(2):
+            for n in range(4):
+                source = across_ref.at[4 * flags[6 + panel] + n, pl.ds(blocks, 3)]
+                copies.append(pltpu.make_async_copy(source, terms_ref.at[panel, n], arrived.at[len(copies)]))
         for q in range(parts):
             first = 4 * lax.rem(q // 2 + flags[0], steps) + 2 * (q % 2)
             for parity in range(2):
-                for b in range(blocks):
-                    top = (parity * blocks + b) * B + q * part
-                    columns[top : top + part, :] = across_ref[first + parity, b]
+                source = across_ref.at[first + parity, pl.ds(0, blocks)]
+                copies.append(pltpu.make_async_copy(source, columns.at[parity, :, q], arrived.at[len(copies)]))
+        for copy in copies:
+            copy.start()
+        for copy in copies:
+            copy.wait()
         for panel in range(2):
             for h in range(2):
                 for parity in range(2):
                     for f in range(2):
                         lane = (2 * f + panel) * 128
                         terms = [
-                            across_ref[4 * flags[6 + panel] + 2 * h + parity, blocks + t, :, lane : lane + 128].astype(F32)
-                            for t in range(3)
+                            terms_ref[panel, 2 * h + parity, t, :, lane : lane + 128].astype(F32) for t in range(3)
                         ]
                         top = (2 * parity + f) * fold
                         white_ref[top : top + fold, panel * B + h * 128 : panel * B + (h + 1) * 128] = (
@@ -322,7 +360,7 @@
     own = along_ref[:, 0].reshape(parts * part, 2 * B)
     for n in range(column_blocks):
         cut = slice(n * B, (n + 1) * B)
-        out_ref[:, cut] = cov_ref[:, cut] - dot(own, columns[cut, :], NT)
+        out_ref[:, cut] = cov_ref[:, cut] - dot(own, columns[n // blocks, n % blocks].reshape(B, 2 * B), NT)
 
     for panel in range(2):
         is_row = i == flags[2 + panel]
@@ -367,7 +405,7 @@
             in_specs=[
                 pl.BlockSpec((B, columns), lambda i, flags: (i, 0)),
                 pl.BlockSpec((parts, 1, part, width), lambda i, flags: (0, i, 0, 0)),
-                whole(*across.shape),
+                pl.BlockSpec(memory_space=pl.ANY),
                 pl.BlockSpec((4, half, 128), lambda i, flags: (lax.rem(i + flags[0], blocks), 0, 0)),
                 pl.BlockSpec((B, width), lambda i, flags: (jnp.where((flags[4] & flags[5]) >= 0, i, 0), 0)),
                 whole(*lower.shape),
@@ -379,9 +417,11 @@
                 pl.BlockSpec((2 * half, B), lambda i, flags: (0, i)),
             ],
             scratch_shapes=[
-                pltpu.VMEM((columns, width), BF16),
+                pltpu.VMEM((2, columns // (2 * B), parts, part, width), BF16),
+                pltpu.VMEM((2, 4, 3, part, width), BF16),
                 pltpu.VMEM((2 * half, width), F32),
                 pltpu.VMEM((2 * half, 6 * B), BF16),
+                pltpu.SemaphoreType.DMA((2 * parts + 8,)),
             ],
         ),
         out_shape=[jax.ShapeDtypeStruct((rows, columns), F32), jax.ShapeDtypeStruct((2 * half, rows), F32)],
@@ -411,6 +451,7 @@
             (row_slot + shift) % steps,
             lax.dynamic_slice_in_dim(levels, c * column_blocks, column_blocks),
             lax.dynamic_slice_in_dim(levels, r * row_blocks, row_blocks),
+            column_root,
         ]
     ).astype(jnp.int32)
     across_axes = [
@@ -419,14 +460,15 @@
         for b in range(n_col)
     ]
 
-    chosen = jnp.where(r == row_root[0], row_slot[0], row_slot[1])
-    where = jnp.concatenate([chosen[None], column_slot]).astype(jnp.int32)
-    tiles = pick_tiles(where, covariance).reshape(n_row * n_col, 8, 128)
+    groups = lax.ppermute(jnp.transpose(innovations, (1, 0, 2)), ("row", "col"), across_axes)
+
+    tiles = pick_tiles(block_owner, panel_index, covariance).reshape(n_row * n_col, 8, 128)
     tiles = lax.all_to_all(tiles, ("row", "col"), split_axis=0, concat_axis=0, tiled=True)
     source = jnp.where(c % 4 < 2, column_root[0], column_root[1])
     tiles = jnp.concatenate(
         [lax.dynamic_index_in_dim(tiles, row_root[n] * n_col + source, 0, keepdims=False) for n in range(2)], axis=0
     )
+    tiles, groups = lax.optimization_barrier((tiles, groups))
     tiles = lax.all_to_all(
         jnp.broadcast_to(tiles[None], (n_row * n_col,) + tiles.shape),
         ("row", "col"),
@@ -439,33 +481,22 @@
     picked = pick_columns(column_slot.astype(jnp.int32), covariance, n_col)
     picked, _ = lax.optimization_barrier((picked, tiles))
     parts = lax.all_to_all(picked, "col", split_axis=0, concat_axis=0, tiled=True)
-    part = parts.shape[2]
-    piece = jnp.concatenate(
-        [
-            lax.dynamic_slice(parts, (column_root[n], 0, 0, n * B), (1, row_blocks, part, B))[0]
-            for n in range(2)
-        ],
-        axis=-1,
-    )
 
     fold = innovations.shape[0] // 2
-    wanted = [lax.dynamic_index_in_dim(innovations, row_root[n], 1, keepdims=False) for n in range(2)]
+    wanted = [lax.dynamic_index_in_dim(groups, row_root[n], 0, keepdims=False) for n in range(2)]
     wanted = jnp.concatenate([w[h * fold : (h + 1) * fold] for h in range(2) for w in wanted], axis=1)
     high = lax.reduce_precision(wanted, 8, 7)
     middle = lax.reduce_precision(wanted - high, 8, 7)
     wanted = jnp.stack([high, middle, wanted - high - middle]).astype(BF16)
 
-    along, across = solve_piece(flags, piece, inverse, l10t, n_col)
-    across = lax.ppermute(jnp.concatenate([across, wanted], axis=0), ("row", "col"), across_axes)
-    across_all = lax.all_gather(across, "row", axis=0)
+    along, across = solve_piece(flags, parts, inverse, l10t)
+    across = lax.ppermute(across, ("row", "col"), across_axes)
+    across = lax.all_gather(jnp.concatenate([across, wanted], axis=0), "row", axis=0)
     along = lax.all_to_all(along, "col", split_axis=0, concat_axis=0, tiled=True)
-
-    groups, _ = lax.optimization_barrier((jnp.transpose(innovations, (1, 0, 2)), across))
-    groups = lax.ppermute(groups, ("row", "col"), across_axes)
     along, groups = lax.optimization_barrier((along, groups))
     relaid = lax.all_to_all(groups, "row", split_axis=0, concat_axis=0, tiled=True)
     panels = solve_panels(flags, covariance, along, inverse, l10t)
-    return update(flags, covariance, along, across_all, relaid, panels, lower, inverse, l10t)
+    return update(flags, covariance, along, across, relaid, panels, lower, inverse, l10t)
 
 
 def solution(mesh):

time: 189 us -> 187 us (0.989)
  blocking collectives: 0 us -> 40.8 us
  waiting for transfers between devices: 54.4 us -> 29.9 us
  starting transfers between devices: 45.2 us -> 34.9 us
  local copies, waits for them, and re-layouts: 5.87 us -> 13.5 us
  Pallas kernels: 52.2 us -> 44.7 us
  between operations: 26.6 us -> 21.2 us
    all_to_all x0 -> x1, blocking collectives: none -> 40.8 us  [per_device(): lax.all_to_all(along, 'col', split_axis=0, concat_axis=0, tiled=True)]
    all_to_all x1 -> x0, waiting for transfers between devices: 26 us -> none  [per_device(): lax.all_to_all(along, 'col', split_axis=0, concat_axis=0, tiled=True)]
    all_to_all x1 -> x0, starting transfers between devices: 16 us -> none  [per_device(): lax.all_to_all(along, 'col', split_axis=0, concat_axis=0, tiled=True)]
    all_to_all x1, starting transfers between devices: 4.64 us -> 14.9 us  [per_device(): lax.all_to_all(jnp.broadcast_to(tiles[None], (n_row * n_col,) + tiles.sha...]
    unnamed x19 -> x29, local copies, waits for them, and re-layouts: 2.69 us -> 10.1 us
    all_to_all x1, waiting for transfers between devices: 5.63 us -> 10.2 us  [per_device(): lax.all_to_all(jnp.broadcast_to(tiles[None], (n_row * n_col,) + tiles.sha...]
    pallas_call x1, Pallas kernels: 5.14 us -> 0.99 us  [solve_panels(): pl.pallas_call(panel_kernel, grid_spec=pltpu.PrefetchScalarGridSpec(num_s...]
    all_to_all x1, starting transfers between devices: 7.5 us -> 3.57 us  [per_device(): lax.all_to_all(groups, 'row', split_axis=0, concat_axis=0, tiled=True)]
  transfers between devices with their start and end apart: 8 -> 7, of which waited for: 5 -> 4; matrix products, arithmetic and copies ran while one was open for 1% -> 2% of each run, Pallas kernels for 17% -> 14%
where the time goes in v7:
time: 187 us
  Pallas kernels  44.7 us (24%)
  blocking collectives  40.8 us (22%)
  starting transfers between devices  34.9 us (19%)
  waiting for transfers between devices  29.9 us (16%)
  between operations  21.2 us (11%)
  local copies, waits for them, and re-layouts  13.5 us (7%)
    all_to_all x1, blocking collectives, per_device(): lax.all_to_all(along, 'col', split_axis=0, concat_axis=0, tiled=True)  40.8 us
    pallas_call x1, Pallas kernels, factor_diagonal(): pl.pallas_call(factor_kernel, in_specs=[VMEM_SPEC], out_specs=[VMEM_SPEC]...  20.1 us
    all_to_all x1, starting transfers between devices, per_device(): lax.all_to_all(jnp.broadcast_to(tiles[None], (n_row * n_col,) + tiles.sha...  14.9 us
    pallas_call x1, Pallas kernels, update(): pl.pallas_call(update_kernel, grid_spec=pltpu.PrefetchScalarGridSpec(num_...  14.4 us
    all_to_all x1, starting transfers between devices, per_device(): lax.all_to_all(tiles, ('row', 'col'), split_axis=0, concat_axis=0, tiled=...  11.1 us
    all_to_all x1, waiting for transfers between devices, per_device(): lax.all_to_all(jnp.broadcast_to(tiles[None], (n_row * n_col,) + tiles.sha...  10.2 us
    unnamed x29, local copies, waits for them, and re-layouts  10.1 us
    all_to_all x1, waiting for transfers between devices, per_device(): lax.all_to_all(tiles, ('row', 'col'), split_axis=0, concat_axis=0, tiled=...  7.87 us
  transfers between devices with their start and end apart: 7, of which 4 were waited for; matrix products, arithmetic and copies ran while one was open for 2% of the time, Pallas kernels for 14%

profile of v7, /device:TPU:0, one launch (start us, length us, event | category | flops | bytes accessed | tf_op | source)
XLA Modules:
  0.0 186.5 jit_solution(11082898588422943256)
XLA Ops:
  7.8 2.8 %shard_map.60 = f32[32,4,8,128]{3,2,1,0:T(8,128)} custom-call(s32[64]{0:T(128)} %owner_ref.1, s32[1]{0:T(128)} %copy.11.panel_ref, f32[1024,2048]{1,0:T(8,128)} %cov_ref.5), custom_call_target="tpu_custom_call" | custom-call | tf_op jit(solution)/shard_map/pallas_call | solution.py:78
  10.6 11.1 %all-to-all-start = ((f32[128,8,128]{2,1,0:T(8,128)}), f32[128,8,128]{2,1,0:T(8,128)S(1)}, u32[]{:S(2)}, u32[]{:S(2)}) async-start(f32[128,8,128]{2,1,0:T(8,128)} %bitcast.17), calls=%async_computation | async-start | bytes 1048576 | tf_op jit(solution)/shard_map/all_to_all | solution.py:466
  27.2 7.9 %all-to-all-done = f32[128,8,128]{2,1,0:T(8,128)S(1)} async-done(((f32[128,8,128]{2,1,0:T(8,128)}), f32[128,8,128]{2,1,0:T(8,128)S(1)}, u32[]{:S(2)}, u32[]{:S(2)}) %all-to-all-start) | async-done | bytes 524320 | tf_op jit(solution)/shard_map/all_to_all | solution.py:466
  35.1 1.2 broadcast_in_dim.36
  36.2 14.9 %all-to-all-start.1 = ((f32[128,16,128]{2,1,0:T(8,128)}), f32[128,16,128]{2,1,0:T(8,128)S(1)}, u32[]{:S(2)}, u32[]{:S(2)}) async-start(f32[128,16,128]{2,1,0:T(8,128)} %broadcast_in_dim.36), calls=%async_computation.1 | async-start | bytes 2097152 | tf_op jit(solution)/shard_map/all_to_all | solution.py:472
  53.9 4.5 %shard_map.59 = f32[8,4,32,512]{3,2,1,0:T(8,128)} custom-call(s32[2]{0:T(128)} %get-tuple-element.26.slots, f32[1024,2048]{1,0:T(8,128)} %cov_ref.5), custom_call_target="tpu_custom_call" | custom-call | tf_op jit(solution)/shard_map/pallas_call | solution.py:39
  59.7 10.2 %all-to-all-done.1.tiles_ref = f32[128,16,128]{2,1,0:T(8,128)S(1)} async-done(((f32[128,16,128]{2,1,0:T(8,128)}), f32[128,16,128]{2,1,0:T(8,128)S(1)}, u32[]{:S(2)}, u32[]{:S(2)}) %all-to-all-start.1) | async-done | bytes 1048608 | tf_op jit(solution)/shard_map/all_to_all | solution.py:472
  69.8 3.6 %all-to-all-start.2 = ((f32[8,4,32,512]{3,2,1,0:T(8,128)}), f32[8,4,32,512]{3,2,1,0:T(8,128)S(1)}, u32[]{:S(2)}, u32[]{:S(2)}) async-start(f32[8,4,32,512]{3,2,1,0:T(8,128)} %shard_map.59), calls=%async_computation.2 | async-start | bytes 4194304 | tf_op jit(solution)/shard_map/all_to_all | solution.py:483
  73.7 20.1 %shard_map.61 = (bf16[256,3072]{1,0:T(8,128)(2,1)S(1)}, bf16[256,256]{1,0:T(8,128)(2,1)S(1)}, f32[256,512]{1,0:T(8,128)S(1)}) custom-call(f32[128,16,128]{2,1,0:T(8,128)S(1)} %all-to-all-done.1.tiles_ref), custom_call_target="tpu_custom_call" | custom-call | flops 20000000000 | bytes 80000000 | tf_op jit(solution)/shard_map/pallas_call | solution.py:187
  93.8 1.1 copy-done.1
  94.9 0.9 copy-done.9
  95.8 6.7 %all-to-all-done.2.first_ref.second_ref = f32[8,4,32,512]{3,2,1,0:T(8,128)S(1)} async-done(((f32[8,4,32,512]{3,2,1,0:T(8,128)}), f32[8,4,32,512]{3,2,1,0:T(8,128)S(1)}, u32[]{:S(2)}, u32[]{:S(2)}) %all-to-all-start.2) | async-done | bytes 2097184 | tf_op jit(solution)/shard_map/all_to_all | solution.py:483
  102.6 1.4 copy-done.2
  104.0 1.9 %shard_map.62 = (bf16[8,4,32,512]{3,2,1,0:T(8,128)(2,1)S(1)}, bf16[4,32,512]{2,1,0:T(8,128)(2,1)S(1)}) custom-call(s32[22]{0:T(128)S(1)} %concatenate.37.flags, f32[8,4,32,512]{3,2,1,0:T(8,128)S(1)} %all-to-all-done.2.first_ref.second_ref, f32[8,4,32,512]{3,2,1,0:T(8,128)S(1)} %all-to-all-done.2.first_ref.second_ref, bf16[256,3072]{1,0:T(8,128)(2,1)S(1)} %copy-done.2, ...), custom_call_target="tpu_custom_call" | custom-call | flops 1000000000 | bytes 4000000 | tf_op jit(solution)/shard_map/pallas_call | solution.py:232
  105.9 1.0 copy-done.6
  106.9 0.8 collective-permute-start.1
  109.2 40.8 %all_to_all.25.along_ref = bf16[8,4,32,512]{3,2,1,0:T(8,128)(2,1)S(1)} all-to-all(bf16[8,4,32,512]{3,2,1,0:T(8,128)(2,1)} %copy-done.6), channel_id=1, replica_groups=mesh['row'=16,'col'=8] {'col'}, dimensions={0} | all-to-all | bytes 2097152 | tf_op jit(solution)/shard_map/all_to_all | solution.py:495
  150.0 3.6 %all-to-all-start.4 = ((f32[16,64,128]{2,1,0:T(8,128)}), f32[16,64,128]{2,1,0:T(8,128)S(1)}, u32[]{:S(2)}, u32[]{:S(2)}) async-start(f32[16,64,128]{2,1,0:T(8,128)} %copy-done.10), calls=%async_computation.4 | async-start | bytes 1048576 | tf_op jit(solution)/shard_map/all_to_all | solution.py:497
  153.6 3.4 %copy-done = f32[1024,2048]{1,0:T(8,128)S(1)} copy-done((f32[1024,2048]{1,0:T(8,128)S(1)}, f32[1024,2048]{1,0:T(8,128)}, u32[]{:S(2)}) %copy-start) | copy-done | bytes 8388632
  157.0 1.0 shard_map.63.panel_ref
  158.1 1.3 copy-done.5
  159.4 5.0 %all-to-all-done.4.relaid_ref = f32[16,64,128]{2,1,0:T(8,128)S(1)} async-done(((f32[16,64,128]{2,1,0:T(8,128)}), f32[16,64,128]{2,1,0:T(8,128)S(1)}, u32[]{:S(2)}, u32[]{:S(2)}) %all-to-all-start.4) | async-done | bytes 524320 | tf_op jit(solution)/shard_map/all_to_all | solution.py:497
  164.4 0.8 copy-done.12
  165.2 14.4 %shard_map.64 = (f32[1024,2048]{1,0:T(8,128)}, f32[128,1024]{1,0:T(8,128)}) custom-call(s32[22]{0:T(128)} %copy-done.8, f32[1024,2048]{1,0:T(8,128)} %cov_ref.5, bf16[8,4,32,512]{3,2,1,0:T(8,128)(2,1)} %copy-done.4, bf16[16,7,32,512]{3,2,1,0:T(8,128)(2,1)} %bitcast.19, f32[16,64,128]{2,1,0:T(8,128)} %copy-done.12, f32[1024,512]{1,0:T(8,128)} %copy-done.5, ...), custom_call_target="tpu_custom_call" | custom-call | flops 5000000000 | bytes 20000000 | tf_op jit(solution)/shard_map/pallas_call | solution.py:400
  (43 shorter events, 5.0 us)
Async XLA Ops:
  7.8 13.9 %copy-start.11 = (f32[64,16,128]{2,1,0:T(8,128)S(1)}, f32[64,16,128]{2,1,0:T(8,128)}, u32[]{:S(2)}) copy-start(f32[64,16,128]{2,1,0:T(8,128)} %param.5) | copy-start | bytes 1572868
  10.6 12.1 %copy-start.13 = (s32[64]{0:T(128)S(1)}, s32[64]{0:T(128)}, u32[]{:S(2)}) copy-start(s32[64]{0:T(128)} %owner_ref.1) | copy-start | bytes 772
  10.6 24.5 %all-to-all-start = ((f32[128,8,128]{2,1,0:T(8,128)}), f32[128,8,128]{2,1,0:T(8,128)S(1)}, u32[]{:S(2)}, u32[]{:S(2)}) async-start(f32[128,8,128]{2,1,0:T(8,128)} %bitcast.17), calls=%async_computation | async-start | bytes 1048576 | tf_op jit(solution)/shard_map/all_to_all | solution.py:466
  21.9 13.1 %collective-permute-start = (f32[16,64,128]{2,1,0:T(8,128)S(1)}, f32[16,64,128]{2,1,0:T(8,128)S(1)}, u32[]{:S(2)}, u32[]{:S(2)}) collective-permute-start(f32[16,64,128]{2,1,0:T(8,128)S(1)} %bitcast.18), channel_id=1, source_target_pairs={{0,0},{1,16},{2,32},{3,48},{4,64},{5,80},{6,96},{7,112},{8,8},{9,2... | collective-permute-start | bytes 1572872 | tf_op jit(solution)/shard_map/ppermute | solution.py:463
  35.1 1.2 copy-start.10
  36.2 33.6 %all-to-all-start.1 = ((f32[128,16,128]{2,1,0:T(8,128)}), f32[128,16,128]{2,1,0:T(8,128)S(1)}, u32[]{:S(2)}, u32[]{:S(2)}) async-start(f32[128,16,128]{2,1,0:T(8,128)} %broadcast_in_dim.36), calls=%async_computation.1 | async-start | bytes 2097152 | tf_op jit(solution)/shard_map/all_to_all | solution.py:472
  59.6 94.0 %copy-start.8 = (s32[22]{0:T(128)}, s32[22]{0:T(128)S(1)}, u32[]{:S(2)}) copy-start(s32[22]{0:T(128)S(1)} %concatenate.37.flags) | copy-start | bytes 268
  69.8 32.7 %all-to-all-start.2 = ((f32[8,4,32,512]{3,2,1,0:T(8,128)}), f32[8,4,32,512]{3,2,1,0:T(8,128)S(1)}, u32[]{:S(2)}, u32[]{:S(2)}) async-start(f32[8,4,32,512]{3,2,1,0:T(8,128)} %shard_map.59), calls=%async_computation.2 | async-start | bytes 4194304 | tf_op jit(solution)/shard_map/all_to_all | solution.py:483
  73.5 91.0 %all-gather.3.cloned.1.call-start = ((), (), s32[]{:S(2)}) async-start(), calls=%async_computation.5 | async-start | bytes 3899392 | tf_op jit(solution)/shard_map/all_gather | solution.py:494
  93.8 1.2 copy-start.1
  94.9 0.9 copy-start.9
  95.8 57.8 %copy-start.7 = (bf16[256,256]{1,0:T(8,128)(2,1)}, bf16[256,256]{1,0:T(8,128)(2,1)S(1)}, u32[]{:S(2)}) copy-start(bf16[256,256]{1,0:T(8,128)(2,1)S(1)} %get-tuple-element.15.l10t_ref) | copy-start | bytes 393220
  102.6 1.4 copy-start.2
  105.9 1.0 copy-start.6
  106.9 46.8 %copy-start.3 = (bf16[256,3072]{1,0:T(8,128)(2,1)S(1)}, bf16[256,3072]{1,0:T(8,128)(2,1)}, u32[]{:S(2)}) copy-start(bf16[256,3072]{1,0:T(8,128)(2,1)} %copy-done.1) | copy-start | bytes 4718596
  106.9 1.6 collective-permute-start.1
  150.0 8.0 %copy-start.4 = (bf16[8,4,32,512]{3,2,1,0:T(8,128)(2,1)}, bf16[8,4,32,512]{3,2,1,0:T(8,128)(2,1)S(1)}, u32[]{:S(2)}) copy-start(bf16[8,4,32,512]{3,2,1,0:T(8,128)(2,1)S(1)} %all_to_all.25.along_ref) | copy-start | bytes 3145732
  150.0 14.4 %all-to-all-start.4 = ((f32[16,64,128]{2,1,0:T(8,128)}), f32[16,64,128]{2,1,0:T(8,128)S(1)}, u32[]{:S(2)}, u32[]{:S(2)}) async-start(f32[16,64,128]{2,1,0:T(8,128)} %copy-done.10), calls=%async_computation.4 | async-start | bytes 1048576 | tf_op jit(solution)/shard_map/all_to_all | solution.py:497
  153.6 3.4 %copy-start = (f32[1024,2048]{1,0:T(8,128)S(1)}, f32[1024,2048]{1,0:T(8,128)}, u32[]{:S(2)}) copy-start(f32[1024,2048]{1,0:T(8,128)} %cov_ref.5) | copy-start | bytes 25165828
  158.0 1.3 copy-start.5
  164.4 0.8 copy-start.12
Sparse Core Ops, SparseCore 0:
  109.4 46.4 all-gather.2

commit v8 on v7

--- a/solution.py
+++ b/solution.py
@@ -199,7 +199,7 @@
             pltpu.VMEM((S, 2 * S), F32),
             pltpu.VMEM((S, S), F32),
         ],
-        compiler_params=pltpu.CompilerParams(vmem_limit_bytes=VMEM_BYTES // 4),
+        compiler_params=pltpu.CompilerParams(vmem_limit_bytes=VMEM_BYTES),
         cost_estimate=pl.CostEstimate(flops=2 * 10**10, bytes_accessed=80_000_000, transcendentals=0),
     )(tiles)
 
@@ -247,7 +247,7 @@
             jax.ShapeDtypeStruct((count, blocks, part, 2 * B), BF16),
             jax.ShapeDtypeStruct((blocks, part, 2 * B), BF16),
         ],
-        compiler_params=pltpu.CompilerParams(vmem_limit_bytes=VMEM_BYTES // 4),
+        compiler_params=pltpu.CompilerParams(vmem_limit_bytes=VMEM_BYTES),
         cost_estimate=pl.CostEstimate(flops=10**9, bytes_accessed=4_000_000, transcendentals=0),
     )(flags, parts, parts, inverse, l10t)
 
@@ -293,9 +293,39 @@
             scratch_shapes=[pltpu.VMEM((B, 6 * B), BF16)],
         ),
         out_shape=jax.ShapeDtypeStruct((rows, 2 * B), F32),
-        compiler_params=pltpu.CompilerParams(vmem_limit_bytes=VMEM_BYTES // 4),
+        compiler_params=pltpu.CompilerParams(vmem_limit_bytes=VMEM_BYTES),
         cost_estimate=pl.CostEstimate(flops=10**9, bytes_accessed=4_000_000, transcendentals=0),
     )(flags, covariance, covariance, along, inverse, l10t)
+
+
+def white_kernel(flags, exchanged_ref, inverse_ref, l10t_ref, white_ref, wide):
+    half = white_ref.shape[0] // 2
+    for panel in range(2):
+        for h in range(2):
+            for parity in range(2):
+                there = (
+                    slice(parity * half, (parity + 1) * half),
+                    slice(panel * B + h * 128, panel * B + (h + 1) * 128),
+                )
+                white_ref[there] = exchanged_ref[
+                    4 * flags[6 + panel] + 2 * h + parity, (1 + panel) * half : (2 + panel) * half, :
+                ]
+    w0, w1 = solve_rows(white_ref[:, 0:B], white_ref[:, B : 2 * B], wide, inverse_ref, l10t_ref)
+    white_ref[:, 0:B] = w0
+    white_ref[:, B : 2 * B] = w1
+
+
+def solve_white(flags, exchanged, inverse, l10t):
+    particles = exchanged.shape[1] // 3 * 2
+    return pl.pallas_call(
+        white_kernel,
+        in_specs=[SMEM_SPEC] + [VMEM_SPEC] * 3,
+        out_specs=VMEM_SPEC,
+        out_shape=jax.ShapeDtypeStruct((particles, 2 * B), F32),
+        scratch_shapes=[pltpu.VMEM((particles, 6 * B), BF16)],
+        compiler_params=pltpu.CompilerParams(vmem_limit_bytes=VMEM_BYTES),
+        cost_estimate=pl.CostEstimate(flops=10**9, bytes_accessed=4_000_000, transcendentals=0),
+    )(flags, exchanged, inverse, l10t)
 
 
 def update_kernel(
@@ -306,55 +336,31 @@
     relaid_ref,
     panel_ref,
     lower_ref,
-    inverse_ref,
-    l10t_ref,
+    white_ref,
     out_ref,
     solved_ref,
     columns,
-    terms_ref,
-    white_ref,
-    wide,
     arrived,
 ):
     i = pl.program_id(0)
     parts, _, part = along_ref.shape[:3]
-    blocks = across_ref.shape[1] - 3
+    blocks = across_ref.shape[1]
     steps = parts // 2
     column_blocks = 2 * blocks
     half = relaid_ref.shape[1]
-    fold = half // 2
 
     @pl.when(i == 0)
     def _():
         copies = []
-        for panel in range(2):
-            for n in range(4):
-                source = across_ref.at[4 * flags[6 + panel] + n, pl.ds(blocks, 3)]
-                copies.append(pltpu.make_async_copy(source, terms_ref.at[panel, n], arrived.at[len(copies)]))
         for q in range(parts):
             first = 4 * lax.rem(q // 2 + flags[0], steps) + 2 * (q % 2)
             for parity in range(2):
-                source = across_ref.at[first + parity, pl.ds(0, blocks)]
+                source = across_ref.at[first + parity]
                 copies.append(pltpu.make_async_copy(source, columns.at[parity, :, q], arrived.at[len(copies)]))
         for copy in copies:
             copy.start()
         for copy in copies:
             copy.wait()
-        for panel in range(2):
-            for h in range(2):
-                for parity in range(2):
-                    for f in range(2):
-                        lane = (2 * f + panel) * 128
-                        terms = [
-                            terms_ref[panel, 2 * h + parity, t, :, lane : lane + 128].astype(F32) for t in range(3)
-                        ]
-                        top = (2 * parity + f) * fold
-                        white_ref[top : top + fold, panel * B + h * 128 : panel * B + (h + 1) * 128] = (
-                            terms[0] + terms[1]
-                        ) + terms[2]
-        w0, w1 = solve_rows(white_ref[:, 0:B], white_ref[:, B : 2 * B], wide, inverse_ref, l10t_ref)
-        white_ref[:, 0:B] = w0
-        white_ref[:, B : 2 * B] = w1
 
     level = flags[16 + i]
     own = along_ref[:, 0].reshape(parts * part, 2 * B)
@@ -393,10 +399,10 @@
             solved_ref[...] = white_ref[:, panel * B : (panel + 1) * B]
 
 
-def update(flags, covariance, along, across, relaid, panels, lower, inverse, l10t):
+def update(flags, covariance, along, across, exchanged, panels, lower, white):
     rows, columns = covariance.shape
     parts, blocks, part, width = along.shape
-    half = relaid.shape[1]
+    half = white.shape[0] // 2
     return pl.pallas_call(
         update_kernel,
         grid_spec=pltpu.PrefetchScalarGridSpec(
@@ -409,8 +415,7 @@
                 pl.BlockSpec((4, half, 128), lambda i, flags: (lax.rem(i + flags[0], blocks), 0, 0)),
                 pl.BlockSpec((B, width), lambda i, flags: (jnp.where((flags[4] & flags[5]) >= 0, i, 0), 0)),
                 whole(*lower.shape),
-                whole(*inverse.shape),
-                whole(*l10t.shape),
+                whole(*white.shape),
             ],
             out_specs=[
                 pl.BlockSpec((B, columns), lambda i, flags: (i, 0)),
@@ -418,16 +423,13 @@
             ],
             scratch_shapes=[
                 pltpu.VMEM((2, columns // (2 * B), parts, part, width), BF16),
-                pltpu.VMEM((2, 4, 3, part, width), BF16),
-                pltpu.VMEM((2 * half, width), F32),
-                pltpu.VMEM((2 * half, 6 * B), BF16),
-                pltpu.SemaphoreType.DMA((2 * parts + 8,)),
+                pltpu.SemaphoreType.DMA((2 * parts,)),
             ],
         ),
         out_shape=[jax.ShapeDtypeStruct((rows, columns), F32), jax.ShapeDtypeStruct((2 * half, rows), F32)],
         compiler_params=pltpu.CompilerParams(vmem_limit_bytes=VMEM_BYTES),
         cost_estimate=pl.CostEstimate(flops=5 * 10**9, bytes_accessed=20_000_000, transcendentals=0),
-    )(flags, covariance, along, across, relaid, panels, lower, inverse, l10t)
+    )(flags, covariance, along, across, exchanged, panels, lower, white)
 
 
 def per_device(covariance, innovations, block_owner, panel_index, *, n_row, n_col):
@@ -468,7 +470,6 @@
     tiles = jnp.concatenate(
         [lax.dynamic_index_in_dim(tiles, row_root[n] * n_col + source, 0, keepdims=False) for n in range(2)], axis=0
     )
-    tiles, groups = lax.optimization_barrier((tiles, groups))
     tiles = lax.all_to_all(
         jnp.broadcast_to(tiles[None], (n_row * n_col,) + tiles.shape),
         ("row", "col"),
@@ -476,27 +477,28 @@
         concat_axis=0,
         tiled=True,
     )
+    tiles, groups = lax.optimization_barrier((tiles, groups))
     inverse, l10t, lower = factor_diagonal(tiles)
 
     picked = pick_columns(column_slot.astype(jnp.int32), covariance, n_col)
     picked, _ = lax.optimization_barrier((picked, tiles))
     parts = lax.all_to_all(picked, "col", split_axis=0, concat_axis=0, tiled=True)
 
-    fold = innovations.shape[0] // 2
+    along, across = solve_piece(flags, parts, inverse, l10t)
+    turned = lax.ppermute(across, ("row", "col"), across_axes)
+    gathered = lax.all_gather(turned, "row", axis=0)
+
     wanted = [lax.dynamic_index_in_dim(groups, row_root[n], 0, keepdims=False) for n in range(2)]
-    wanted = jnp.concatenate([w[h * fold : (h + 1) * fold] for h in range(2) for w in wanted], axis=1)
-    high = lax.reduce_precision(wanted, 8, 7)
-    middle = lax.reduce_precision(wanted - high, 8, 7)
-    wanted = jnp.stack([high, middle, wanted - high - middle]).astype(BF16)
-
-    along, across = solve_piece(flags, parts, inverse, l10t)
-    across = lax.ppermute(across, ("row", "col"), across_axes)
-    across = lax.all_gather(jnp.concatenate([across, wanted], axis=0), "row", axis=0)
+    wanted = jnp.concatenate(wanted, axis=0)
+    sent = jnp.concatenate([groups, jnp.broadcast_to(wanted[None], (n_row,) + wanted.shape)], axis=1)
+    sent, _ = lax.optimization_barrier((sent, across))
+    exchanged = lax.all_to_all(sent, "row", split_axis=0, concat_axis=0, tiled=True)
+    along, exchanged = lax.optimization_barrier((along, exchanged))
     along = lax.all_to_all(along, "col", split_axis=0, concat_axis=0, tiled=True)
-    along, groups = lax.optimization_barrier((along, groups))
-    relaid = lax.all_to_all(groups, "row", split_axis=0, concat_axis=0, tiled=True)
+
+    white = solve_white(flags, exchanged, inverse, l10t)
     panels = solve_panels(flags, covariance, along, inverse, l10t)
-    return update(flags, covariance, along, across, relaid, panels, lower, inverse, l10t)
+    return update(flags, covariance, along, gathered, exchanged, panels, lower, white)
 
 
 def solution(mesh):

time: 187 us -> 204 us (1.091)
  Pallas kernels: 44.7 us -> 57.2 us
  waiting for transfers between devices: 29.9 us -> 40.5 us
  local copies, waits for them, and re-layouts: 13.5 us -> 6.47 us
    all_to_all x1, starting transfers between devices: 3.61 us -> 14.6 us  [per_device(): lax.all_to_all(picked, 'col', split_axis=0, concat_axis=0, tiled=True)]
    all_to_all x1, starting transfers between devices: 14.9 us -> 4.64 us  [per_device(): lax.all_to_all(jnp.broadcast_to(tiles[None], (n_row * n_col,) + tiles.sha...]
    all_to_all x1, waiting for transfers between devices: 5.05 us -> 13.9 us  [per_device(): lax.all_to_all(along, 'col', split_axis=0, concat_axis=0, tiled=True)]
    unnamed x29 -> x17, local copies, waits for them, and re-layouts: 10.1 us -> 3.22 us
    pallas_call x1, Pallas kernels: 0.99 us -> 5.97 us  [solve_panels(): pl.pallas_call(panel_kernel, grid_spec=pltpu.PrefetchScalarGridSpec(num_s...]
    pallas_call x0 -> x1, Pallas kernels: none -> 3.78 us  [solve_white(): pl.pallas_call(white_kernel, in_specs=[SMEM_SPEC] + [VMEM_SPEC] * 3, out_...]
    pallas_call x1, Pallas kernels: 1.91 us -> 4.75 us  [solve_piece(): pl.pallas_call(piece_kernel, grid_spec=pltpu.PrefetchScalarGridSpec(num_s...]
    pallas_call x1, Pallas kernels: 20.1 us -> 22.7 us  [factor_diagonal(): pl.pallas_call(factor_kernel, in_specs=[VMEM_SPEC], out_specs=[VMEM_SPEC]...]
  transfers between devices with their start and end apart: 7 -> 7, of which waited for: 4 -> 4; matrix products, arithmetic and copies ran while one was open for 2% -> 2% of each run, Pallas kernels for 14% -> 18%
where the time goes in v8:
time: 204 us; the launch traced here: 203 us
  Pallas kernels  57.2 us (28%)
  waiting for transfers between devices  40.5 us (20%)
  blocking collectives  40.3 us (20%)
  starting transfers between devices  36.4 us (18%)
  between operations  21.4 us (10%)
  local copies, waits for them, and re-layouts  6.47 us (3%)
    all_to_all x1, blocking collectives, per_device(): lax.all_to_all(sent, 'row', split_axis=0, concat_axis=0, tiled=True)  40.3 us
    pallas_call x1, Pallas kernels, factor_diagonal(): pl.pallas_call(factor_kernel, in_specs=[VMEM_SPEC], out_specs=[VMEM_SPEC]...  22.7 us
    all_to_all x1, starting transfers between devices, per_device(): lax.all_to_all(picked, 'col', split_axis=0, concat_axis=0, tiled=True)  14.6 us
    all_to_all x1, waiting for transfers between devices, per_device(): lax.all_to_all(along, 'col', split_axis=0, concat_axis=0, tiled=True)  13.9 us
    pallas_call x1, Pallas kernels, update(): pl.pallas_call(update_kernel, grid_spec=pltpu.PrefetchScalarGridSpec(num_...  12.8 us
    all_to_all x1, waiting for transfers between devices, per_device(): lax.all_to_all(jnp.broadcast_to(tiles[None], (n_row * n_col,) + tiles.sha...  12.4 us
    all_to_all x1, starting transfers between devices, per_device(): lax.all_to_all(tiles, ('row', 'col'), split_axis=0, concat_axis=0, tiled=...  11.1 us
    all_to_all x1, waiting for transfers between devices, per_device(): lax.all_to_all(tiles, ('row', 'col'), split_axis=0, concat_axis=0, tiled=...  8.71 us
  transfers between devices with their start and end apart: 7, of which 4 were waited for; matrix products, arithmetic and copies ran while one was open for 2% of the time, Pallas kernels for 18%

profile of v8, /device:TPU:0, one launch (start us, length us, event | category | flops | bytes accessed | tf_op | source)
XLA Modules:
  0.0 203.3 jit_solution(752162129514877574)
XLA Ops:
  7.8 2.7 %shard_map.60 = f32[32,4,8,128]{3,2,1,0:T(8,128)} custom-call(s32[64]{0:T(128)} %owner_ref.1, s32[1]{0:T(128)} %copy.11.panel_ref, f32[1024,2048]{1,0:T(8,128)} %cov_ref.5), custom_call_target="tpu_custom_call" | custom-call | tf_op jit(solution)/shard_map/pallas_call | solution.py:78
  10.6 11.1 %all-to-all-start = ((f32[128,8,128]{2,1,0:T(8,128)}), f32[128,8,128]{2,1,0:T(8,128)S(1)}, u32[]{:S(2)}, u32[]{:S(2)}) async-start(f32[128,8,128]{2,1,0:T(8,128)} %bitcast.21), calls=%async_computation | async-start | bytes 1048576 | tf_op jit(solution)/shard_map/all_to_all | solution.py:468
  22.5 0.7 fusion.3
  26.4 8.7 %all-to-all-done = f32[128,8,128]{2,1,0:T(8,128)S(1)} async-done(((f32[128,8,128]{2,1,0:T(8,128)}), f32[128,8,128]{2,1,0:T(8,128)S(1)}, u32[]{:S(2)}, u32[]{:S(2)}) %all-to-all-start) | async-done | bytes 524320 | tf_op jit(solution)/shard_map/all_to_all | solution.py:468
  35.1 1.1 broadcast_in_dim.42
  36.1 4.6 %all-to-all-start.1 = ((f32[128,16,128]{2,1,0:T(8,128)}), f32[128,16,128]{2,1,0:T(8,128)S(1)}, u32[]{:S(2)}, u32[]{:S(2)}) async-start(f32[128,16,128]{2,1,0:T(8,128)} %broadcast_in_dim.42), calls=%async_computation.1 | async-start | bytes 2097152 | tf_op jit(solution)/shard_map/all_to_all | solution.py:473
  41.0 0.7 collective-permute-start
  41.9 4.5 %shard_map.59 = f32[8,4,32,512]{3,2,1,0:T(8,128)} custom-call(s32[2]{0:T(128)} %get-tuple-element.28.slots, f32[1024,2048]{1,0:T(8,128)} %cov_ref.5), custom_call_target="tpu_custom_call" | custom-call | tf_op jit(solution)/shard_map/pallas_call | solution.py:39
  46.4 0.7 concatenate.12.flags
  47.1 12.4 %all-to-all-done.1.tiles_ref = f32[128,16,128]{2,1,0:T(8,128)S(1)} async-done(((f32[128,16,128]{2,1,0:T(8,128)}), f32[128,16,128]{2,1,0:T(8,128)S(1)}, u32[]{:S(2)}, u32[]{:S(2)}) %all-to-all-start.1) | async-done | bytes 1048608 | tf_op jit(solution)/shard_map/all_to_all | solution.py:473
  59.5 14.6 %all-to-all-start.2 = ((f32[8,4,32,512]{3,2,1,0:T(8,128)}), f32[8,4,32,512]{3,2,1,0:T(8,128)S(1)}, u32[]{:S(2)}, u32[]{:S(2)}) async-start(f32[8,4,32,512]{3,2,1,0:T(8,128)} %shard_map.59), calls=%async_computation.2 | async-start | bytes 4194304 | tf_op jit(solution)/shard_map/all_to_all | solution.py:485
  74.4 22.7 %shard_map.61 = (bf16[256,3072]{1,0:T(8,128)(2,1)}, bf16[256,256]{1,0:T(8,128)(2,1)}, f32[256,512]{1,0:T(8,128)}) custom-call(f32[128,16,128]{2,1,0:T(8,128)} %copy-done.2), custom_call_target="tpu_custom_call" | custom-call | flops 20000000000 | bytes 80000000 | tf_op jit(solution)/shard_map/pallas_call | solution.py:187
  97.0 5.4 %all-to-all-done.2.first_ref.second_ref = f32[8,4,32,512]{3,2,1,0:T(8,128)S(1)} async-done(((f32[8,4,32,512]{3,2,1,0:T(8,128)}), f32[8,4,32,512]{3,2,1,0:T(8,128)S(1)}, u32[]{:S(2)}, u32[]{:S(2)}) %all-to-all-start.2) | async-done | bytes 2097184 | tf_op jit(solution)/shard_map/all_to_all | solution.py:485
  102.5 1.3 copy-done
  103.8 4.7 %shard_map.62 = (bf16[8,4,32,512]{3,2,1,0:T(8,128)(2,1)}, bf16[4,32,512]{2,1,0:T(8,128)(2,1)}) custom-call(s32[22]{0:T(128)} %concatenate.12.flags, f32[8,4,32,512]{3,2,1,0:T(8,128)} %copy-done, f32[8,4,32,512]{3,2,1,0:T(8,128)} %copy-done, bf16[256,3072]{1,0:T(8,128)(2,1)} %get-tuple-element.15.inverse_ref, bf16[256,256]{1,0:T(8,128)(2,1)} %get-tuple-element.16.l10t_ref), custom_call_target="tpu_custom_call" | custom-call | flops 1000000000 | bytes 4000000 | tf_op jit(solution)/shard_map/pallas_call | solution.py:232
  108.6 1.6 collective-permute-start.1
  110.1 0.7 copy-done.6
  115.0 40.3 %all_to_all.25.exchanged_ref.relaid_ref = f32[16,192,128]{2,1,0:T(8,128)} all-to-all(f32[16,192,128]{2,1,0:T(8,128)S(1)} %pad_maximum_fusion), channel_id=1, replica_groups=mesh['row'=16,'col'=8] {'row'}, dimensions={0} | all-to-all | bytes 3145728 | tf_op jit(solution)/shard_map/all_to_all | solution.py:495
  155.3 3.6 %all-to-all-start.4 = ((bf16[8,4,32,512]{3,2,1,0:T(8,128)(2,1)}), bf16[8,4,32,512]{3,2,1,0:T(8,128)(2,1)S(1)}, u32[]{:S(2)}, u32[]{:S(2)}) async-start(bf16[8,4,32,512]{3,2,1,0:T(8,128)(2,1)} %get-tuple-element.21), calls=%async_computation.4 | async-start | bytes 2097152 | tf_op jit(solution)/shard_map/all_to_all | solution.py:497
  158.9 3.8 %shard_map.64.white_ref = f32[128,512]{1,0:T(8,128)} custom-call(s32[22]{0:T(128)} %concatenate.12.flags, f32[16,192,128]{2,1,0:T(8,128)} %all_to_all.25.exchanged_ref.relaid_ref, bf16[256,3072]{1,0:T(8,128)(2,1)} %get-tuple-element.15.inverse_ref, bf16[256,256]{1,0:T(8,128)(2,1)} %get-tuple-element.16.l10t_ref), custom_call_target="tpu_custom_call" | custom-call | flops 1000000000 | bytes 4000000 | tf_op jit(solution)/shard_map/pallas_call | solution.py:320
  162.7 13.9 %all-to-all-done.4.along_ref = bf16[8,4,32,512]{3,2,1,0:T(8,128)(2,1)S(1)} async-done(((bf16[8,4,32,512]{3,2,1,0:T(8,128)(2,1)}), bf16[8,4,32,512]{3,2,1,0:T(8,128)(2,1)S(1)}, u32[]{:S(2)}, u32[]{:S(2)}) %all-to-all-start.4) | async-done | bytes 1048608 | tf_op jit(solution)/shard_map/all_to_all | solution.py:497
  176.6 1.1 copy-done.1
  177.6 6.0 %shard_map.63.panel_ref = f32[1024,512]{1,0:T(8,128)} custom-call(s32[22]{0:T(128)} %concatenate.12.flags, f32[1024,2048]{1,0:T(8,128)} %cov_ref.5, f32[1024,2048]{1,0:T(8,128)} %cov_ref.5, bf16[8,4,32,512]{3,2,1,0:T(8,128)(2,1)} %copy-done.1, bf16[256,3072]{1,0:T(8,128)(2,1)} %get-tuple-element.15.inverse_ref, bf16[256,256]{1,0:T(8,128)(2,1)} %get-tuple-element.16.l10t_ref), custom_call_target="tpu_custom_call" | custom-call | flops 1000000000 | bytes 4000000 | tf_op jit(solution)/shard_map/pallas_call | solution.py:280
  183.6 12.8 %shard_map.65 = (f32[1024,2048]{1,0:T(8,128)}, f32[128,1024]{1,0:T(8,128)}) custom-call(s32[22]{0:T(128)} %concatenate.12.flags, f32[1024,2048]{1,0:T(8,128)} %cov_ref.5, bf16[8,4,32,512]{3,2,1,0:T(8,128)(2,1)} %copy-done.1, bf16[16,4,32,512]{3,2,1,0:T(8,128)(2,1)} %bitcast.23, f32[16,192,128]{2,1,0:T(8,128)} %all_to_all.25.exchanged_ref.relaid_ref, ...), custom_call_target="tpu_custom_call" | custom-call | flops 5000000000 | bytes 20000000 | tf_op jit(solution)/shard_map/pallas_call | solution.py:406
  (33 shorter events, 2.2 us)
Async XLA Ops:
  7.8 14.0 %copy-start.7 = (s32[64]{0:T(128)S(1)}, s32[64]{0:T(128)}, u32[]{:S(2)}) copy-start(s32[64]{0:T(128)} %owner_ref.1) | copy-start | bytes 772
  10.6 30.2 %copy-start.5 = (f32[64,16,128]{2,1,0:T(8,128)S(1)}, f32[64,16,128]{2,1,0:T(8,128)}, u32[]{:S(2)}) copy-start(f32[64,16,128]{2,1,0:T(8,128)} %param.5) | copy-start | bytes 1572868
  10.6 24.5 %all-to-all-start = ((f32[128,8,128]{2,1,0:T(8,128)}), f32[128,8,128]{2,1,0:T(8,128)S(1)}, u32[]{:S(2)}, u32[]{:S(2)}) async-start(f32[128,8,128]{2,1,0:T(8,128)} %bitcast.21), calls=%async_computation | async-start | bytes 1048576 | tf_op jit(solution)/shard_map/all_to_all | solution.py:468
  36.1 23.4 %all-to-all-start.1 = ((f32[128,16,128]{2,1,0:T(8,128)}), f32[128,16,128]{2,1,0:T(8,128)S(1)}, u32[]{:S(2)}, u32[]{:S(2)}) async-start(f32[128,16,128]{2,1,0:T(8,128)} %broadcast_in_dim.42), calls=%async_computation.1 | async-start | bytes 2097152 | tf_op jit(solution)/shard_map/all_to_all | solution.py:473
  41.0 6.1 %collective-permute-start = (f32[16,64,128]{2,1,0:T(8,128)S(1)}, f32[16,64,128]{2,1,0:T(8,128)S(1)}, u32[]{:S(2)}, u32[]{:S(2)}) collective-permute-start(f32[16,64,128]{2,1,0:T(8,128)S(1)} %bitcast.22), channel_id=1, source_target_pairs={{0,0},{1,16},{2,32},{3,48},{4,64},{5,80},{6,96},{7,112},{8,8},{9,2... | collective-permute-start | bytes 1572872 | tf_op jit(solution)/shard_map/ppermute | solution.py:465
  47.1 12.4 %copy-start.3 = (f32[16,64,128]{2,1,0:T(8,128)}, f32[16,64,128]{2,1,0:T(8,128)S(1)}, u32[]{:S(2)}) copy-start(f32[16,64,128]{2,1,0:T(8,128)S(1)} %collective-permute-done) | copy-start | bytes 1572868
  59.5 14.9 %copy-start.2 = (f32[128,16,128]{2,1,0:T(8,128)}, f32[128,16,128]{2,1,0:T(8,128)S(1)}, u32[]{:S(2)}) copy-start(f32[128,16,128]{2,1,0:T(8,128)S(1)} %all-to-all-done.1.tiles_ref) | copy-start | bytes 3145732
  59.5 43.0 %all-to-all-start.2 = ((f32[8,4,32,512]{3,2,1,0:T(8,128)}), f32[8,4,32,512]{3,2,1,0:T(8,128)S(1)}, u32[]{:S(2)}, u32[]{:S(2)}) async-start(f32[8,4,32,512]{3,2,1,0:T(8,128)} %shard_map.59), calls=%async_computation.2 | async-start | bytes 4194304 | tf_op jit(solution)/shard_map/all_to_all | solution.py:485
  74.1 109.4 %all-gather.3.cloned.1.call-start = ((), (), s32[]{:S(2)}) async-start(), calls=%async_computation.5 | async-start | bytes 2228224 | tf_op jit(solution)/shard_map/all_gather | solution.py:489
  102.5 1.3 copy-start
  103.8 10.9 %copy-start.4 = (f32[16,64,128]{2,1,0:T(8,128)S(1)}, f32[16,64,128]{2,1,0:T(8,128)}, u32[]{:S(2)}) copy-start(f32[16,64,128]{2,1,0:T(8,128)} %copy-done.3) | copy-start | bytes 1572868
  108.6 1.6 collective-permute-start.1
  110.1 0.7 copy-start.6
  155.3 21.2 %all-to-all-start.4 = ((bf16[8,4,32,512]{3,2,1,0:T(8,128)(2,1)}), bf16[8,4,32,512]{3,2,1,0:T(8,128)(2,1)S(1)}, u32[]{:S(2)}, u32[]{:S(2)}) async-start(bf16[8,4,32,512]{3,2,1,0:T(8,128)(2,1)} %get-tuple-element.21), calls=%async_computation.4 | async-start | bytes 2097152 | tf_op jit(solution)/shard_map/all_to_all | solution.py:497
  176.6 1.1 copy-start.1
Sparse Core Ops, SparseCore 0:
  110.9 50.2 all-gather.2

commit v9 on v3

--- a/solution.py
+++ b/solution.py
@@ -123,7 +123,11 @@
         ref[:, start + n * B : start + (n + 1) * B] = term
 
 
-def factor_kernel(diag_ref, inverse_ref, l10t_ref, lower_ref, work, small, inverse_small):
+def factor_kernel(flags, near_ref, far_ref, inverse_ref, l10t_ref, lower_ref, diag_ref, work, small, inverse_small):
+    parts, part = near_ref.shape[:2]
+    for ref, first in ((near_ref, flags[1] * part), (far_ref, (1 - flags[1]) * part)):
+        for q in range(parts):
+            diag_ref[pl.ds(pl.multiple_of(q * 2 * part + first, part), part), :] = ref[q]
     row = lax.broadcasted_iota(jnp.int32, (B, B), 0)
     col = lax.broadcasted_iota(jnp.int32, (B, B), 1)
     eye = jnp.where(row == col, 1.0, 0.0)
@@ -142,20 +146,25 @@
     lower_ref[:, B : 2 * B] = jnp.where(row <= col, work[:, 0:B], 0.0).T
 
 
-def factor_diagonal(diag):
+def factor_diagonal(flags, near, far):
     return pl.pallas_call(
         factor_kernel,
-        in_specs=[VMEM_SPEC],
+        in_specs=[SMEM_SPEC] + [VMEM_SPEC] * 2,
         out_specs=[VMEM_SPEC] * 3,
         out_shape=[
             jax.ShapeDtypeStruct((B, 12 * B), BF16),
             jax.ShapeDtypeStruct((B, B), BF16),
             jax.ShapeDtypeStruct((B, 2 * B), F32),
         ],
-        scratch_shapes=[pltpu.VMEM((B, 2 * B), F32), pltpu.VMEM((S, 2 * S), F32), pltpu.VMEM((S, S), F32)],
+        scratch_shapes=[
+            pltpu.VMEM((B, 3 * B), F32),
+            pltpu.VMEM((B, 2 * B), F32),
+            pltpu.VMEM((S, 2 * S), F32),
+            pltpu.VMEM((S, S), F32),
+        ],
         compiler_params=pltpu.CompilerParams(vmem_limit_bytes=VMEM_BYTES),
         cost_estimate=pl.CostEstimate(flops=2 * 10**10, bytes_accessed=80_000_000, transcendentals=0),
-    )(diag)
+    )(flags, near, far)
 
 
 def solve_rows(first, second, wide, inverse_ref, l10t_ref):
@@ -248,25 +257,56 @@
     )(flags, across, inverse, l10t)
 
 
+def rows_kernel(flags, along_ref, inverse_ref, l10t_ref, panel_ref, rows_ref, wide):
+    level = flags[16 + pl.program_id(0)]
+    parts, _, part = along_ref.shape[:3]
+    raw = along_ref[:, 0].reshape(parts * part, 2 * B)
+    for panel, p in enumerate(solve_rows(raw[:, 0:B], raw[:, B : 2 * B], wide, inverse_ref, l10t_ref)):
+        cut = slice(panel * B, (panel + 1) * B)
+        p = jnp.where(level > panel, p, 0.0)
+        panel_ref[:, cut] = p
+        rows_ref[:, cut] = p.astype(BF16)
+
+
+def solve_own(flags, along, inverse, l10t):
+    parts, blocks, part, width = along.shape
+    here = pl.BlockSpec((B, width), lambda i, flags: (i, 0))
+    return pl.pallas_call(
+        rows_kernel,
+        grid_spec=pltpu.PrefetchScalarGridSpec(
+            num_scalar_prefetch=1,
+            grid=(blocks,),
+            in_specs=[
+                pl.BlockSpec((parts, 1, part, width), lambda i, flags: (0, i, 0, 0)),
+                whole(*inverse.shape),
+                whole(*l10t.shape),
+            ],
+            out_specs=[here, here],
+            scratch_shapes=[pltpu.VMEM((B, 6 * B), BF16)],
+        ),
+        out_shape=[
+            jax.ShapeDtypeStruct((blocks * B, width), F32),
+            jax.ShapeDtypeStruct((blocks * B, width), BF16),
+        ],
+        compiler_params=pltpu.CompilerParams(vmem_limit_bytes=VMEM_BYTES),
+        cost_estimate=pl.CostEstimate(flops=2 * 10**9, bytes_accessed=4_000_000, transcendentals=0),
+    )(flags, along, inverse, l10t)
+
+
 def update_kernel(
-    flags, cov_ref, along_ref, pc_ref, relaid_ref, white_ref, inverse_ref, l10t_ref, lower_ref, out_ref, solved_ref, wide
+    flags, cov_ref, rows_ref, columns_ref, relaid_ref, white_ref, panel_ref, lower_ref, out_ref, solved_ref
 ):
     i = pl.program_id(0)
-    parts, part = along_ref.shape[0], along_ref.shape[2]
-    column_blocks = pc_ref.shape[0] // B
-    fold = relaid_ref.shape[1]
+    column_blocks = columns_ref.shape[0] // B
+    half = relaid_ref.shape[1]
 
     level = flags[16 + i]
-    raw = along_ref[:, 0].reshape(parts * part, 2 * B)
-    p0, p1 = solve_rows(raw[:, 0:B], raw[:, B : 2 * B], wide, inverse_ref, l10t_ref)
-    p0 = jnp.where(level > 0, p0, 0.0)
-    p1 = jnp.where(level > 1, p1, 0.0)
-    rows = jnp.concatenate([p0.astype(BF16), p1.astype(BF16)], axis=1)
+    own = rows_ref[...]
     for n in range(column_blocks):
         cut = slice(n * B, (n + 1) * B)
-        out_ref[:, cut] = cov_ref[:, cut] - dot(rows, pc_ref[cut, :], NT)
-
-    for panel, solved in ((0, p0), (1, p1)):
+        out_ref[:, cut] = cov_ref[:, cut] - dot(own, columns_ref[cut, :], NT)
+
+    for panel in range(2):
         is_row = i == flags[2 + panel]
         for n in range(column_blocks):
 
@@ -279,19 +319,17 @@
 
         @pl.when((column >= 0) & (level > panel))
         def _():
-            out_ref[:, place] = solved
+            out_ref[:, place] = panel_ref[:, panel * B : (panel + 1) * B]
 
         @pl.when((column >= 0) & is_row)
         def _():
             out_ref[:, place] = lower_ref[:, panel * B : (panel + 1) * B]
 
-    product = dot(white_ref[...].astype(BF16), rows, NT)
-    for n in range(4):
-        h, parity = n // 2, n % 2
-        for f in range(4):
-            top = parity * 4 * fold + f * fold
-            there = (slice(top, top + fold), slice(h * 128, (h + 1) * 128))
-            solved_ref[there] = relaid_ref[n, :, f * 128 : (f + 1) * 128] - product[there]
+    product = dot(white_ref[...].astype(BF16), own, NT)
+    for parity in range(2):
+        for h in range(2):
+            there = (slice(parity * half, (parity + 1) * half), slice(h * 128, (h + 1) * 128))
+            solved_ref[there] = relaid_ref[2 * h + parity] - product[there]
     for panel in range(2):
 
         @pl.when(i == flags[2 + panel])
@@ -299,14 +337,11 @@
             solved_ref[...] = white_ref[:, panel * B : (panel + 1) * B]
 
 
-def update(flags, covariance, along, pc, exchanged, white, inverse, l10t, lower):
+def update(flags, covariance, own, across, relaid, white, panels, lower):
     rows, columns = covariance.shape
+    width = own.shape[1]
     blocks = rows // B
-    parts = along.shape[0]
-    part = B // parts
-    particles = white.shape[0]
-    fold = particles // 8
-    below = exchanged.shape[1] // fold - 1
+    half = relaid.shape[1]
     return pl.pallas_call(
         update_kernel,
         grid_spec=pltpu.PrefetchScalarGridSpec(
@@ -314,24 +349,22 @@
             grid=(blocks,),
             in_specs=[
                 pl.BlockSpec((B, columns), lambda i, flags: (i, 0)),
-                pl.BlockSpec((parts, 1, part, 2 * B), lambda i, flags: (0, i, 0, 0)),
-                whole(*pc.shape),
-                pl.BlockSpec((4, fold, 2 * B), lambda i, flags: (lax.rem(i + flags[0], blocks), below, 0)),
+                pl.BlockSpec((B, width), lambda i, flags: (i, 0)),
+                whole(*across.shape),
+                pl.BlockSpec((4, half, 128), lambda i, flags: (lax.rem(i + flags[0], blocks), 0, 0)),
                 whole(*white.shape),
-                whole(*inverse.shape),
-                whole(*l10t.shape),
+                pl.BlockSpec((B, width), lambda i, flags: (jnp.where((flags[4] & flags[5]) >= 0, i, 0), 0)),
                 whole(*lower.shape),
             ],
             out_specs=[
                 pl.BlockSpec((B, columns), lambda i, flags: (i, 0)),
-                pl.BlockSpec((particles, B), lambda i, flags: (0, i)),
-            ],
-            scratch_shapes=[pltpu.VMEM((B, 6 * B), BF16)],
+                pl.BlockSpec((2 * half, B), lambda i, flags: (0, i)),
+            ],
         ),
-        out_shape=[jax.ShapeDtypeStruct((rows, columns), F32), jax.ShapeDtypeStruct((particles, rows), F32)],
+        out_shape=[jax.ShapeDtypeStruct((rows, columns), F32), jax.ShapeDtypeStruct((2 * half, rows), F32)],
         compiler_params=pltpu.CompilerParams(vmem_limit_bytes=VMEM_BYTES),
         cost_estimate=pl.CostEstimate(flops=5 * 10**9, bytes_accessed=20_000_000, transcendentals=0),
-    )(flags, covariance, along, pc, exchanged, white, inverse, l10t, lower)
+    )(flags, covariance, own, across, relaid, white, panels, lower)
 
 
 def per_device(covariance, innovations, block_owner, panel_index, *, n_row, n_col):
@@ -345,10 +378,13 @@
     row_slot, column_slot = slot % row_blocks, slot % column_blocks
     levels = jnp.sum((block_owner[:, None] > targets[None, :]).astype(jnp.int32), axis=1)
     steps = n_row // 4
-    shift = c // 2
+    shift, core = c // 2, r % 2
+    pairs = [(a, a ^ 1) for a in range(n_row)]
+    same_core = [[a for a in range(n_row) if a % 2 == k] for k in range(2)]
     flags = jnp.concatenate(
         [
-            jnp.full((2,), shift, jnp.int32),
+            shift[None],
+            core[None],
             jnp.where(row_root == r, row_slot, -1),
             jnp.where(column_root == c, column_slot, -1),
             (row_slot + shift) % steps,
@@ -362,8 +398,6 @@
         for b in range(n_col)
     ]
 
-    turned = lax.ppermute(jnp.transpose(innovations, (1, 0, 2)), ("row", "col"), across_axes)
-
     picked = pick_columns(column_slot.astype(jnp.int32), covariance, n_col)
     parts = lax.all_to_all(picked, "col", split_axis=0, concat_axis=0, tiled=True)
     part = parts.shape[2]
@@ -377,34 +411,53 @@
 
     chosen = jnp.where(r == row_root[0], row_slot[0], row_slot[1])
     mine = lax.dynamic_index_in_dim(piece, chosen, 0, keepdims=False)
-    fold = turned.shape[1] // 4
-    groups = jnp.concatenate([turned[:, f * fold : (f + 1) * fold] for f in range(4)], axis=2)
-    sent = jnp.concatenate([jnp.broadcast_to(mine[None], (n_row,) + mine.shape), groups], axis=1)
-    exchanged = lax.all_to_all(sent, "row", split_axis=0, concat_axis=0, tiled=True)
-    upper = lax.dynamic_slice(exchanged, (row_root[0], 0, 0), (1, part, 2 * B))[0]
-    lower = lax.dynamic_slice(exchanged, (row_root[1], 0, B), (1, part, B))[0]
+    half = part // 2
+    kept = lax.dynamic_slice_in_dim(mine, core * half, half, 0)
+    given = lax.ppermute(lax.dynamic_slice_in_dim(mine, (1 - core) * half, half, 0), "row", pairs)
+    both = jnp.concatenate([jnp.where(core == 0, kept, given), jnp.where(core == 0, given, kept)], axis=0)
+
+    fold = innovations.shape[0] // 2
+    wanted = [lax.dynamic_index_in_dim(innovations, row_root[n], 1, keepdims=False) for n in range(2)]
+    wanted = jnp.concatenate([w[h * fold : (h + 1) * fold] for h in range(2) for w in wanted], axis=1)
+    payload = jnp.concatenate([piece.reshape(row_blocks * part, 2 * B), wanted], axis=0)
+    payload, both = lax.optimization_barrier((payload, both))
+    payload = lax.ppermute(payload, ("row", "col"), across_axes)
+
+    spread = lax.all_to_all(
+        jnp.broadcast_to(both[None], (n_row // 2,) + both.shape),
+        "row",
+        split_axis=0,
+        concat_axis=0,
+        tiled=True,
+        axis_index_groups=same_core,
+    )
+    upper = lax.dynamic_slice(spread, (row_root[0] // 2, row_root[0] % 2 * half, 0), (1, half, 2 * B))[0]
+    lower = lax.dynamic_slice(spread, (row_root[1] // 2, row_root[1] % 2 * half, B), (1, half, B))[0]
     strip = jnp.concatenate([upper, lower], axis=-1)
-    diag = lax.all_to_all(
+    near = lax.all_to_all(
         jnp.broadcast_to(strip[None], (n_col,) + strip.shape), "col", split_axis=0, concat_axis=0, tiled=True
-    ).reshape(B, 3 * B)
-
-    tiled = lax.ppermute(piece.reshape(row_blocks * part, 2 * B), ("row", "col"), across_axes)
-    wanted = [lax.dynamic_index_in_dim(turned, row_root[n], 0, keepdims=False) for n in range(2)]
-    wanted = jnp.concatenate(
-        [w[h * 2 * fold : (h + 1) * 2 * fold] for h in range(2) for w in wanted], axis=1
-    )
-    payload, _ = lax.optimization_barrier((jnp.concatenate([tiled, wanted], axis=0), exchanged))
+    )
+    far = lax.ppermute(near, "row", pairs)
+
+    payload, _ = lax.optimization_barrier((payload, near))
     across = lax.all_gather(payload, "row", axis=0)
 
-    inverse, l10t, lower = factor_diagonal(diag)
+    inverse, l10t, lower = factor_diagonal(flags, near, far)
 
     along = lax.all_to_all(
         jnp.broadcast_to(piece[None], (n_col,) + piece.shape), "col", split_axis=0, concat_axis=0, tiled=True
     )
 
-    pc, white = solve_across(flags, across, inverse, l10t, row_blocks, n_col, 2 * turned.shape[1])
+    groups, _ = lax.optimization_barrier((jnp.transpose(innovations, (1, 0, 2)), near))
+    turned = lax.ppermute(groups, ("row", "col"), across_axes)
+    inverse, turned = lax.optimization_barrier((inverse, turned))
+    turned, _ = lax.optimization_barrier((turned, along))
+    relaid = lax.all_to_all(turned, "row", split_axis=0, concat_axis=0, tiled=True)
+
+    panels, own = solve_own(flags, along, inverse, l10t)
+    columns, white = solve_across(flags, across, inverse, l10t, row_blocks, n_col, 2 * innovations.shape[0])
     return update(
-        flags, covariance, along, pc.reshape(local_cols, 2 * B), exchanged, white, inverse, l10t, lower
+        flags, covariance, own, columns.reshape(local_cols, 2 * B), relaid, white, panels, lower
     )
 
 

time: 194 us -> 194 us (level)
  Pallas kernels: 53.8 us -> 59.1 us
  waiting for transfers between devices: 65.5 us -> 60.4 us
  between operations: 24.5 us -> 28.3 us
  starting transfers between devices: 38.6 us -> 35.3 us
  other arithmetic: 3.58 us -> 1.56 us
    all_to_all x1, waiting for transfers between devices: 0.01 us -> 26.7 us  [per_device(): lax.all_to_all(jnp.broadcast_to(piece[None], (n_col,) + piece.shape), 'co...]
    all_to_all x1, waiting for transfers between devices: 21.7 us -> 9.11 us  [per_device(): lax.all_to_all(jnp.broadcast_to(strip[None], (n_col,) + strip.shape), 'co...]
    all_to_all x1, starting transfers between devices: 15.9 us -> 3.45 us  [per_device(): lax.all_to_all(jnp.broadcast_to(strip[None], (n_col,) + strip.shape), 'co...]
    all_to_all x1 -> x2, waiting for transfers between devices: 16.6 us -> 5.97 us  [the longest x1 5.96 us: per_device(): lax.all_to_all(jnp.broadcast_to(both[None], (n_row // 2,) + both.shape),...]
    all_to_all x1, waiting for transfers between devices: 27.1 us -> 17.4 us  [per_device(): lax.all_to_all(picked, 'col', split_axis=0, concat_axis=0, tiled=True)]
    all_to_all x1, starting transfers between devices: 3.79 us -> 12.7 us  [per_device(): lax.all_to_all(jnp.broadcast_to(piece[None], (n_col,) + piece.shape), 'co...]
    pallas_call x1 -> x2, Pallas kernels: 22.5 us -> 30.6 us  [the longest x1 22.6 us: factor_diagonal(): pl.pallas_call(factor_kernel, in_specs=[SMEM_SPEC] + [VMEM_SPEC] * 2, out...]
    pallas_call x1, Pallas kernels: 14.1 us -> 11.5 us  [update(): pl.pallas_call(update_kernel, grid_spec=pltpu.PrefetchScalarGridSpec(num_...]
  transfers between devices with their start and end apart: 7 -> 10, of which waited for: 3 -> 5; matrix products, arithmetic and copies ran while one was open for 3% -> 2% of each run, Pallas kernels for 18% -> 22%
where the time goes in v9:
time: 194 us; the launch traced here: 192 us
  waiting for transfers between devices  60.4 us (31%)
  Pallas kernels  59.1 us (30%)
  starting transfers between devices  35.3 us (18%)
  between operations  28.3 us (15%)
  local copies, waits for them, and re-layouts  7.08 us (4%)
    all_to_all x1, waiting for transfers between devices, per_device(): lax.all_to_all(jnp.broadcast_to(piece[None], (n_col,) + piece.shape), 'co...  26.7 us
    pallas_call x1, Pallas kernels, factor_diagonal(): pl.pallas_call(factor_kernel, in_specs=[SMEM_SPEC] + [VMEM_SPEC] * 2, out...  22.6 us
    all_to_all x1, waiting for transfers between devices, per_device(): lax.all_to_all(picked, 'col', split_axis=0, concat_axis=0, tiled=True)  17.4 us
    all_to_all x1, starting transfers between devices, per_device(): lax.all_to_all(jnp.broadcast_to(piece[None], (n_col,) + piece.shape), 'co...  12.7 us
    pallas_call x1, Pallas kernels, solve_across(): pl.pallas_call(across_kernel, grid_spec=pltpu.PrefetchScalarGridSpec(num_...  12.5 us
    pallas_call x1, Pallas kernels, update(): pl.pallas_call(update_kernel, grid_spec=pltpu.PrefetchScalarGridSpec(num_...  11.5 us
    all_to_all x1, waiting for transfers between devices, per_device(): lax.all_to_all(jnp.broadcast_to(strip[None], (n_col,) + strip.shape), 'co...  9.11 us
    all_to_all x1, starting transfers between devices, per_device(): lax.all_to_all(picked, 'col', split_axis=0, concat_axis=0, tiled=True)  8.16 us
  transfers between devices with their start and end apart: 10, of which 5 were waited for; matrix products, arithmetic and copies ran while one was open for 2% of the time, Pallas kernels for 22%

profile of v9, /device:TPU:0, one launch (start us, length us, event | category | flops | bytes accessed | tf_op | source)
XLA Modules:
  0.0 191.7 jit_solution(9927229402966172252)
XLA Ops:
  7.8 0.8 fusion.4
  9.2 4.5 %shard_map.59 = f32[8,4,32,512]{3,2,1,0:T(8,128)} custom-call(s32[2]{0:T(128)} %get-tuple-element.34.slots, f32[1024,2048]{1,0:T(8,128)} %cov_ref.3), custom_call_target="tpu_custom_call" | custom-call | tf_op jit(solution)/shard_map/pallas_call | solution.py:39
  13.7 8.2 %all-to-all-start = ((f32[8,4,32,512]{3,2,1,0:T(8,128)}), f32[8,4,32,512]{3,2,1,0:T(8,128)S(1)}, u32[]{:S(2)}, u32[]{:S(2)}) async-start(f32[8,4,32,512]{3,2,1,0:T(8,128)} %shard_map.59), calls=%async_computation | async-start | bytes 4194304 | tf_op jit(solution)/shard_map/all_to_all | solution.py:402
  32.9 17.4 %all-to-all-done = f32[8,4,32,512]{3,2,1,0:T(8,128)S(1)} async-done(((f32[8,4,32,512]{3,2,1,0:T(8,128)}), f32[8,4,32,512]{3,2,1,0:T(8,128)S(1)}, u32[]{:S(2)}, u32[]{:S(2)}) %all-to-all-start) | async-done | bytes 2097184 | tf_op jit(solution)/shard_map/all_to_all | solution.py:402
  50.5 1.1 collective-permute-done
  51.7 0.9 broadcast_in_dim.49
  52.5 4.4 %all-to-all-start.2 = ((f32[8,32,512]{2,1,0:T(8,128)}), f32[8,32,512]{2,1,0:T(8,128)S(1)}, u32[]{:S(2)}, u32[]{:S(2)}) async-start(f32[8,32,512]{2,1,0:T(8,128)} %broadcast_in_dim.49), calls=%async_computation.2 | async-start | bytes 1048576 | tf_op jit(solution)/shard_map/all_to_all | solution.py:426
  60.8 6.0 %all-to-all-done.2 = f32[8,32,512]{2,1,0:T(8,128)S(1)} async-done(((f32[8,32,512]{2,1,0:T(8,128)}), f32[8,32,512]{2,1,0:T(8,128)S(1)}, u32[]{:S(2)}, u32[]{:S(2)}) %all-to-all-start.2) | async-done | bytes 524320 | tf_op jit(solution)/shard_map/all_to_all | solution.py:426
  66.8 0.8 broadcast_in_dim.50
  67.5 3.5 %all-to-all-start.3 = ((f32[8,16,768]{2,1,0:T(8,128)}), f32[8,16,768]{2,1,0:T(8,128)S(1)}, u32[]{:S(2)}, u32[]{:S(2)}) async-start(f32[8,16,768]{2,1,0:T(8,128)} %broadcast_in_dim.50), calls=%async_computation.3 | async-start | bytes 786432 | tf_op jit(solution)/shard_map/all_to_all | solution.py:437
  71.0 0.7 collective-permute-start.3
  71.8 9.1 %all-to-all-done.3.near_ref = f32[8,16,768]{2,1,0:T(8,128)S(1)} async-done(((f32[8,16,768]{2,1,0:T(8,128)}), f32[8,16,768]{2,1,0:T(8,128)S(1)}, u32[]{:S(2)}, u32[]{:S(2)}) %all-to-all-start.3) | async-done | bytes 393248 | tf_op jit(solution)/shard_map/all_to_all | solution.py:437
  81.2 0.7 concatenate.25.flags
  81.9 1.6 broadcast_in_dim.48
  83.5 12.7 %all-to-all-start.1 = ((f32[8,4,32,512]{3,2,1,0:T(8,128)}), f32[8,4,32,512]{3,2,1,0:T(8,128)S(1)}, u32[]{:S(2)}, u32[]{:S(2)}) async-start(f32[8,4,32,512]{3,2,1,0:T(8,128)} %broadcast_in_dim.48), calls=%async_computation.1 | async-start | bytes 4194304 | tf_op jit(solution)/shard_map/all_to_all | solution.py:447
  96.3 1.5 collective-permute-start.2
  97.7 0.8 copy-done.5
  98.5 22.6 %shard_map.60 = (bf16[256,3072]{1,0:T(8,128)(2,1)}, bf16[256,256]{1,0:T(8,128)(2,1)}, f32[256,512]{1,0:T(8,128)}) custom-call(s32[20]{0:T(128)} %concatenate.25.flags, f32[8,16,768]{2,1,0:T(8,128)} %copy-done.3, f32[8,16,768]{2,1,0:T(8,128)} %copy-done.5), custom_call_target="tpu_custom_call" | custom-call | flops 20000000000 | bytes 80000000 | tf_op jit(solution)/shard_map/pallas_call | solution.py:150
  121.1 26.7 %all-to-all-done.1.along_ref = f32[8,4,32,512]{3,2,1,0:T(8,128)S(1)} async-done(((f32[8,4,32,512]{3,2,1,0:T(8,128)}), f32[8,4,32,512]{3,2,1,0:T(8,128)S(1)}, u32[]{:S(2)}, u32[]{:S(2)}) %all-to-all-start.1) | async-done | bytes 2097184 | tf_op jit(solution)/shard_map/all_to_all | solution.py:447
  147.8 4.2 %all-to-all-start.4 = ((f32[16,64,128]{2,1,0:T(8,128)}), f32[16,64,128]{2,1,0:T(8,128)S(1)}, u32[]{:S(2)}, u32[]{:S(2)}) async-start(f32[16,64,128]{2,1,0:T(8,128)} %collective-permute-done.2), calls=%async_computation.4 | async-start | bytes 1048576 | tf_op jit(solution)/shard_map/all_to_all | solution.py:455
  152.0 8.0 %shard_map.61 = (f32[1024,512]{1,0:T(8,128)}, bf16[1024,512]{1,0:T(8,128)(2,1)}) custom-call(s32[20]{0:T(128)} %concatenate.25.flags, f32[8,4,32,512]{3,2,1,0:T(8,128)} %copy-done, bf16[256,3072]{1,0:T(8,128)(2,1)} %get-tuple-element.19.inverse_ref, bf16[256,256]{1,0:T(8,128)(2,1)} %get-tuple-element.20.l10t_ref), custom_call_target="tpu_custom_call" | custom-call | flops 2000000000 | bytes 4000000 | tf_op jit(solution)/shard_map/pallas_call | solution.py:274
  160.0 12.5 %shard_map.62 = (bf16[2,4,8,32,512]{4,3,2,1,0:T(8,128)(2,1)}, f32[128,512]{1,0:T(8,128)}) custom-call(s32[20]{0:T(128)} %concatenate.25.flags, f32[16,160,512]{2,1,0:T(8,128)} %bitcast.50, bf16[256,3072]{1,0:T(8,128)(2,1)} %get-tuple-element.19.inverse_ref, bf16[256,256]{1,0:T(8,128)(2,1)} %get-tuple-element.20.l10t_ref), custom_call_target="tpu_custom_call" | custom-call | flops 6000000000 | bytes 8000000 | tf_op jit(solution)/shard_map/pallas_call | solution.py:229
  172.5 0.8 copy-done.2
  173.3 11.5 %shard_map.63 = (f32[1024,2048]{1,0:T(8,128)}, f32[128,1024]{1,0:T(8,128)}) custom-call(s32[20]{0:T(128)} %concatenate.25.flags, f32[1024,2048]{1,0:T(8,128)} %cov_ref.3, bf16[1024,512]{1,0:T(8,128)(2,1)} %get-tuple-element.21.rows_ref, bf16[2048,512]{1,0:T(8,128)(2,1)} %bitcast.51, f32[16,64,128]{2,1,0:T(8,128)} %copy-done.2, ...), custom_call_target="tpu_custom_call" | custom-call | flops 5000000000 | bytes 20000000 | tf_op jit(solution)/shard_map/pallas_call | solution.py:345
  (43 shorter events, 2.6 us)
Async XLA Ops:
  13.7 16.4 %copy-start.1 = (f32[64,16,128]{2,1,0:T(8,128)S(1)}, f32[64,16,128]{2,1,0:T(8,128)}, u32[]{:S(2)}) copy-start(f32[64,16,128]{2,1,0:T(8,128)} %param.5) | copy-start | bytes 1572868
  13.7 36.6 %all-to-all-start = ((f32[8,4,32,512]{3,2,1,0:T(8,128)}), f32[8,4,32,512]{3,2,1,0:T(8,128)S(1)}, u32[]{:S(2)}, u32[]{:S(2)}) async-start(f32[8,4,32,512]{3,2,1,0:T(8,128)} %shard_map.59), calls=%async_computation | async-start | bytes 4194304 | tf_op jit(solution)/shard_map/all_to_all | solution.py:402
  50.4 1.3 collective-permute-start
  50.5 30.5 %copy-start.6 = (s32[64]{0:T(128)S(1)}, s32[64]{0:T(128)}, u32[]{:S(2)}) copy-start(s32[64]{0:T(128)} %param.6) | copy-start | bytes 772
  52.5 14.2 %all-to-all-start.2 = ((f32[8,32,512]{2,1,0:T(8,128)}), f32[8,32,512]{2,1,0:T(8,128)S(1)}, u32[]{:S(2)}, u32[]{:S(2)}) async-start(f32[8,32,512]{2,1,0:T(8,128)} %broadcast_in_dim.49), calls=%async_computation.2 | async-start | bytes 1048576 | tf_op jit(solution)/shard_map/all_to_all | solution.py:426
  67.5 13.3 %all-to-all-start.3 = ((f32[8,16,768]{2,1,0:T(8,128)}), f32[8,16,768]{2,1,0:T(8,128)S(1)}, u32[]{:S(2)}, u32[]{:S(2)}) async-start(f32[8,16,768]{2,1,0:T(8,128)} %broadcast_in_dim.50), calls=%async_computation.3 | async-start | bytes 786432 | tf_op jit(solution)/shard_map/all_to_all | solution.py:437
  71.0 89.0 %all-gather.3.cloned.1.call-start = ((), (), s32[]{:S(2)}) async-start(), calls=%async_computation.5 | async-start | bytes 5570560 | tf_op jit(solution)/shard_map/all_gather | solution.py:443
  71.0 0.7 collective-permute-start.3
  71.7 9.1 %copy-start.4 = (f32[160,512]{1,0:T(8,128)}, f32[160,512]{1,0:T(8,128)S(1)}, u32[]{:S(2)}) copy-start(f32[160,512]{1,0:T(8,128)S(1)} %collective-permute-done.3) | copy-start | bytes 983044
  80.9 2.6 %copy-start.3 = (f32[8,16,768]{2,1,0:T(8,128)}, f32[8,16,768]{2,1,0:T(8,128)S(1)}, u32[]{:S(2)}) copy-start(f32[8,16,768]{2,1,0:T(8,128)S(1)} %all-to-all-done.3.near_ref) | copy-start | bytes 1179652
  80.9 16.8 %collective-permute-start.1 = (f32[8,16,768]{2,1,0:T(8,128)S(1)}, f32[8,16,768]{2,1,0:T(8,128)S(1)}, u32[]{:S(2)}, u32[]{:S(2)}) collective-permute-start(f32[8,16,768]{2,1,0:T(8,128)S(1)} %all-to-all-done.3.near_ref), channel_id=1, source_target_pairs={{0,8},{8,0},{16,24},{24,16},{32,40},{40,32},{48,56},{56,48},{64,72... | collective-permute-start | bytes 1179656 | tf_op jit(solution)/shard_map/ppermute | solution.py:440
  83.5 64.3 %all-to-all-start.1 = ((f32[8,4,32,512]{3,2,1,0:T(8,128)}), f32[8,4,32,512]{3,2,1,0:T(8,128)S(1)}, u32[]{:S(2)}, u32[]{:S(2)}) async-start(f32[8,4,32,512]{3,2,1,0:T(8,128)} %broadcast_in_dim.48), calls=%async_computation.1 | async-start | bytes 4194304 | tf_op jit(solution)/shard_map/all_to_all | solution.py:447
  96.3 24.8 %collective-permute-start.2 = (f32[16,64,128]{2,1,0:T(8,128)S(1)}, f32[16,64,128]{2,1,0:T(8,128)}, u32[]{:S(2)}, u32[]{:S(2)}) collective-permute-start(f32[16,64,128]{2,1,0:T(8,128)S(1)} %bitcast.47), channel_id=1, source_target_pairs={{0,0},{1,16},{2,32},{3,48},{4,64},{5,80},{6,96},{7,112},{8,8},{9,2... | collective-permute-start | bytes 1572872 | tf_op jit(solution)/shard_map/ppermute | solution.py:452
  97.7 0.8 copy-start.5
  147.8 4.2 %copy-start = (f32[8,4,32,512]{3,2,1,0:T(8,128)}, f32[8,4,32,512]{3,2,1,0:T(8,128)S(1)}, u32[]{:S(2)}) copy-start(f32[8,4,32,512]{3,2,1,0:T(8,128)S(1)} %all-to-all-done.1.along_ref) | copy-start | bytes 6291460
  147.8 24.7 %all-to-all-start.4 = ((f32[16,64,128]{2,1,0:T(8,128)}), f32[16,64,128]{2,1,0:T(8,128)S(1)}, u32[]{:S(2)}, u32[]{:S(2)}) async-start(f32[16,64,128]{2,1,0:T(8,128)} %collective-permute-done.2), calls=%async_computation.4 | async-start | bytes 1048576 | tf_op jit(solution)/shard_map/all_to_all | solution.py:455
  172.5 0.8 copy-start.2
Sparse Core Ops, SparseCore 0:
  81.0 64.4 all-gather.2

commit v10 on v7

--- a/solution.py
+++ b/solution.py
@@ -199,7 +199,7 @@
             pltpu.VMEM((S, 2 * S), F32),
             pltpu.VMEM((S, S), F32),
         ],
-        compiler_params=pltpu.CompilerParams(vmem_limit_bytes=VMEM_BYTES // 4),
+        compiler_params=pltpu.CompilerParams(vmem_limit_bytes=VMEM_BYTES),
         cost_estimate=pl.CostEstimate(flops=2 * 10**10, bytes_accessed=80_000_000, transcendentals=0),
     )(tiles)
 
@@ -247,7 +247,7 @@
             jax.ShapeDtypeStruct((count, blocks, part, 2 * B), BF16),
             jax.ShapeDtypeStruct((blocks, part, 2 * B), BF16),
         ],
-        compiler_params=pltpu.CompilerParams(vmem_limit_bytes=VMEM_BYTES // 4),
+        compiler_params=pltpu.CompilerParams(vmem_limit_bytes=VMEM_BYTES),
         cost_estimate=pl.CostEstimate(flops=10**9, bytes_accessed=4_000_000, transcendentals=0),
     )(flags, parts, parts, inverse, l10t)
 
@@ -293,7 +293,7 @@
             scratch_shapes=[pltpu.VMEM((B, 6 * B), BF16)],
         ),
         out_shape=jax.ShapeDtypeStruct((rows, 2 * B), F32),
-        compiler_params=pltpu.CompilerParams(vmem_limit_bytes=VMEM_BYTES // 4),
+        compiler_params=pltpu.CompilerParams(vmem_limit_bytes=VMEM_BYTES),
         cost_estimate=pl.CostEstimate(flops=10**9, bytes_accessed=4_000_000, transcendentals=0),
     )(flags, covariance, covariance, along, inverse, l10t)
 
@@ -406,7 +406,7 @@
                 pl.BlockSpec((B, columns), lambda i, flags: (i, 0)),
                 pl.BlockSpec((parts, 1, part, width), lambda i, flags: (0, i, 0, 0)),
                 pl.BlockSpec(memory_space=pl.ANY),
-                pl.BlockSpec((4, half, 128), lambda i, flags: (lax.rem(i + flags[0], blocks), 0, 0)),
+                pl.BlockSpec((4, half, 128), lambda i, flags: (i, 0, 0)),
                 pl.BlockSpec((B, width), lambda i, flags: (jnp.where((flags[4] & flags[5]) >= 0, i, 0), 0)),
                 whole(*lower.shape),
                 whole(*inverse.shape),
@@ -460,7 +460,10 @@
         for b in range(n_col)
     ]
 
-    groups = lax.ppermute(jnp.transpose(innovations, (1, 0, 2)), ("row", "col"), across_axes)
+    fold = innovations.shape[0] // 2
+    wanted = [lax.dynamic_index_in_dim(innovations, row_root[n], 1, keepdims=False) for n in range(2)]
+    wanted = jnp.concatenate([w[h * fold : (h + 1) * fold] for h in range(2) for w in wanted], axis=1)
+    wanted = lax.ppermute(wanted, ("row", "col"), across_axes)
 
     tiles = pick_tiles(block_owner, panel_index, covariance).reshape(n_row * n_col, 8, 128)
     tiles = lax.all_to_all(tiles, ("row", "col"), split_axis=0, concat_axis=0, tiled=True)
@@ -468,7 +471,6 @@
     tiles = jnp.concatenate(
         [lax.dynamic_index_in_dim(tiles, row_root[n] * n_col + source, 0, keepdims=False) for n in range(2)], axis=0
     )
-    tiles, groups = lax.optimization_barrier((tiles, groups))
     tiles = lax.all_to_all(
         jnp.broadcast_to(tiles[None], (n_row * n_col,) + tiles.shape),
         ("row", "col"),
@@ -476,25 +478,28 @@
         concat_axis=0,
         tiled=True,
     )
+    tiles, wanted = lax.optimization_barrier((tiles, wanted))
     inverse, l10t, lower = factor_diagonal(tiles)
 
     picked = pick_columns(column_slot.astype(jnp.int32), covariance, n_col)
     picked, _ = lax.optimization_barrier((picked, tiles))
     parts = lax.all_to_all(picked, "col", split_axis=0, concat_axis=0, tiled=True)
 
-    fold = innovations.shape[0] // 2
-    wanted = [lax.dynamic_index_in_dim(groups, row_root[n], 0, keepdims=False) for n in range(2)]
-    wanted = jnp.concatenate([w[h * fold : (h + 1) * fold] for h in range(2) for w in wanted], axis=1)
     high = lax.reduce_precision(wanted, 8, 7)
     middle = lax.reduce_precision(wanted - high, 8, 7)
     wanted = jnp.stack([high, middle, wanted - high - middle]).astype(BF16)
 
+    groups, _ = lax.optimization_barrier((jnp.transpose(innovations, (1, 0, 2)), parts))
+    groups = lax.all_to_all(groups, "row", split_axis=0, concat_axis=0, tiled=True)
+
     along, across = solve_piece(flags, parts, inverse, l10t)
     across = lax.ppermute(across, ("row", "col"), across_axes)
+    across, groups = lax.optimization_barrier((across, groups))
     across = lax.all_gather(jnp.concatenate([across, wanted], axis=0), "row", axis=0)
+    along, groups = lax.optimization_barrier((along, groups))
     along = lax.all_to_all(along, "col", split_axis=0, concat_axis=0, tiled=True)
     along, groups = lax.optimization_barrier((along, groups))
-    relaid = lax.all_to_all(groups, "row", split_axis=0, concat_axis=0, tiled=True)
+    relaid = lax.all_to_all(groups, "col", split_axis=0, concat_axis=0, tiled=True)
     panels = solve_panels(flags, covariance, along, inverse, l10t)
     return update(flags, covariance, along, across, relaid, panels, lower, inverse, l10t)
 

time: 187 us -> 207 us (1.11); the launches traced: 187 us -> 204 us
  waiting for transfers between devices: 29.9 us -> 52 us
  Pallas kernels: 44.7 us -> 54.1 us
  local copies, waits for them, and re-layouts: 13.5 us -> 6.58 us
  starting transfers between devices: 34.9 us -> 30.2 us
  blocking collectives: 40.8 us -> 38.6 us
    all_to_all x1, waiting for transfers between devices: 6.73 us -> 27.9 us  [per_device(): lax.all_to_all(picked, 'col', split_axis=0, concat_axis=0, tiled=True)]
    all_to_all x1, starting transfers between devices: 14.9 us -> 4.64 us  [per_device(): lax.all_to_all(jnp.broadcast_to(tiles[None], (n_row * n_col,) + tiles.sha...]
    all_to_all x0 -> x1, waiting for transfers between devices: none -> 7.36 us  [per_device(): lax.all_to_all(groups, 'col', split_axis=0, concat_axis=0, tiled=True)]
    unnamed x29 -> x11, local copies, waits for them, and re-layouts: 10.1 us -> 2.76 us
    all_to_all x1, waiting for transfers between devices: 5.05 us -> 0.01 us  [per_device(): lax.all_to_all(groups, 'row', split_axis=0, concat_axis=0, tiled=True)]
    pallas_call x1, Pallas kernels: 0.99 us -> 5.18 us  [solve_panels(): pl.pallas_call(panel_kernel, grid_spec=pltpu.PrefetchScalarGridSpec(num_s...]
    all_to_all x0 -> x1, starting transfers between devices: none -> 3.49 us  [per_device(): lax.all_to_all(groups, 'col', split_axis=0, concat_axis=0, tiled=True)]
    pallas_call x1, Pallas kernels: 1.91 us -> 4.62 us  [solve_piece(): pl.pallas_call(piece_kernel, grid_spec=pltpu.PrefetchScalarGridSpec(num_s...]
  transfers between devices with their start and end apart: 7 -> 8, of which waited for: 4 -> 4; matrix products, arithmetic and copies ran while one was open for 2% -> 2% of each run, Pallas kernels for 14% -> 18%
where the time goes in v10:
time: 207 us; the launch traced here: 204 us
  Pallas kernels  54.1 us (26%)
  waiting for transfers between devices  52 us (25%)
  blocking collectives  38.6 us (19%)
  starting transfers between devices  30.2 us (15%)
  between operations  21.2 us (10%)
  local copies, waits for them, and re-layouts  6.58 us (3%)
    all_to_all x1, blocking collectives, per_device(): lax.all_to_all(along, 'col', split_axis=0, concat_axis=0, tiled=True)  38.6 us
    all_to_all x1, waiting for transfers between devices, per_device(): lax.all_to_all(picked, 'col', split_axis=0, concat_axis=0, tiled=True)  27.9 us
    pallas_call x1, Pallas kernels, factor_diagonal(): pl.pallas_call(factor_kernel, in_specs=[VMEM_SPEC], out_specs=[VMEM_SPEC]...  22.6 us
    pallas_call x1, Pallas kernels, update(): pl.pallas_call(update_kernel, grid_spec=pltpu.PrefetchScalarGridSpec(num_...  14.4 us
    all_to_all x1, starting transfers between devices, per_device(): lax.all_to_all(tiles, ('row', 'col'), split_axis=0, concat_axis=0, tiled=...  11.1 us
    all_to_all x1, waiting for transfers between devices, per_device(): lax.all_to_all(tiles, ('row', 'col'), split_axis=0, concat_axis=0, tiled=...  8.71 us
    all_to_all x1, waiting for transfers between devices, per_device(): lax.all_to_all(jnp.broadcast_to(tiles[None], (n_row * n_col,) + tiles.sha...  8.01 us
    all_to_all x1, waiting for transfers between devices, per_device(): lax.all_to_all(groups, 'col', split_axis=0, concat_axis=0, tiled=True)  7.36 us
  transfers between devices with their start and end apart: 8, of which 4 were waited for; matrix products, arithmetic and copies ran while one was open for 2% of the time, Pallas kernels for 18%

profile of v10, /device:TPU:0, one launch (start us, length us, event | category | flops | bytes accessed | tf_op | source)
XLA Modules:
  0.0 204.2 jit_solution(15635640740296366100)
XLA Ops:
  7.8 2.8 %shard_map.60 = f32[32,4,8,128]{3,2,1,0:T(8,128)} custom-call(s32[64]{0:T(128)} %owner_ref.1, s32[1]{0:T(128)} %copy.18.panel_ref, f32[1024,2048]{1,0:T(8,128)} %cov_ref.5), custom_call_target="tpu_custom_call" | custom-call | tf_op jit(solution)/shard_map/pallas_call | solution.py:78
  10.6 11.1 %all-to-all-start = ((f32[128,8,128]{2,1,0:T(8,128)}), f32[128,8,128]{2,1,0:T(8,128)S(1)}, u32[]{:S(2)}, u32[]{:S(2)}) async-start(f32[128,8,128]{2,1,0:T(8,128)} %bitcast.31), calls=%async_computation | async-start | bytes 1048576 | tf_op jit(solution)/shard_map/all_to_all | solution.py:469
  26.4 8.7 %all-to-all-done = f32[128,8,128]{2,1,0:T(8,128)S(1)} async-done(((f32[128,8,128]{2,1,0:T(8,128)}), f32[128,8,128]{2,1,0:T(8,128)S(1)}, u32[]{:S(2)}, u32[]{:S(2)}) %all-to-all-start) | async-done | bytes 524320 | tf_op jit(solution)/shard_map/all_to_all | solution.py:469
  35.1 1.1 broadcast_in_dim.36
  36.1 4.6 %all-to-all-start.1 = ((f32[128,16,128]{2,1,0:T(8,128)}), f32[128,16,128]{2,1,0:T(8,128)S(1)}, u32[]{:S(2)}, u32[]{:S(2)}) async-start(f32[128,16,128]{2,1,0:T(8,128)} %broadcast_in_dim.36), calls=%async_computation.1 | async-start | bytes 2097152 | tf_op jit(solution)/shard_map/all_to_all | solution.py:474
  43.3 1.0 copy.17
  45.6 0.8 dynamic-slice_bitcast_fusion.3
  46.4 0.7 collective-permute-start
  47.0 4.5 %shard_map.59 = f32[8,4,32,512]{3,2,1,0:T(8,128)} custom-call(s32[2]{0:T(128)} %get-tuple-element.36.slots, f32[1024,2048]{1,0:T(8,128)} %cov_ref.5), custom_call_target="tpu_custom_call" | custom-call | tf_op jit(solution)/shard_map/pallas_call | solution.py:39
  51.5 8.0 %all-to-all-done.1.tiles_ref = f32[128,16,128]{2,1,0:T(8,128)S(1)} async-done(((f32[128,16,128]{2,1,0:T(8,128)}), f32[128,16,128]{2,1,0:T(8,128)S(1)}, u32[]{:S(2)}, u32[]{:S(2)}) %all-to-all-start.1) | async-done | bytes 1048608 | tf_op jit(solution)/shard_map/all_to_all | solution.py:474
  59.5 1.0 copy-done.1
  60.5 4.2 %all-to-all-start.2 = ((f32[8,4,32,512]{3,2,1,0:T(8,128)}), f32[8,4,32,512]{3,2,1,0:T(8,128)S(1)}, u32[]{:S(2)}, u32[]{:S(2)}) async-start(f32[8,4,32,512]{3,2,1,0:T(8,128)} %shard_map.59), calls=%async_computation.2 | async-start | bytes 4194304 | tf_op jit(solution)/shard_map/all_to_all | solution.py:486
  65.5 27.9 %all-to-all-done.2.first_ref.second_ref = f32[8,4,32,512]{3,2,1,0:T(8,128)S(1)} async-done(((f32[8,4,32,512]{3,2,1,0:T(8,128)}), f32[8,4,32,512]{3,2,1,0:T(8,128)S(1)}, u32[]{:S(2)}, u32[]{:S(2)}) %all-to-all-start.2) | async-done | bytes 2097184 | tf_op jit(solution)/shard_map/all_to_all | solution.py:486
  93.4 4.2 %all-to-all-start.3 = ((f32[16,64,128]{2,1,0:T(8,128)}), f32[16,64,128]{2,1,0:T(8,128)}, u32[]{:S(2)}, u32[]{:S(2)}) async-start(f32[16,64,128]{2,1,0:T(8,128)} %bitcast.29), calls=%async_computation.3 | async-start | bytes 1048576 | tf_op jit(solution)/shard_map/all_to_all | solution.py:493
  97.9 22.6 %shard_map.61 = (bf16[256,3072]{1,0:T(8,128)(2,1)}, bf16[256,256]{1,0:T(8,128)(2,1)}, f32[256,512]{1,0:T(8,128)}) custom-call(f32[128,16,128]{2,1,0:T(8,128)} %copy-done.1), custom_call_target="tpu_custom_call" | custom-call | flops 20000000000 | bytes 80000000 | tf_op jit(solution)/shard_map/pallas_call | solution.py:187
  120.5 4.6 %shard_map.62 = (bf16[8,4,32,512]{3,2,1,0:T(8,128)(2,1)}, bf16[4,32,512]{2,1,0:T(8,128)(2,1)}) custom-call(s32[22]{0:T(128)} %concatenate.13.flags, f32[8,4,32,512]{3,2,1,0:T(8,128)} %copy-done, f32[8,4,32,512]{3,2,1,0:T(8,128)} %copy-done, bf16[256,3072]{1,0:T(8,128)(2,1)} %get-tuple-element.19.inverse_ref, bf16[256,256]{1,0:T(8,128)(2,1)} %get-tuple-element.20.l10t_ref), custom_call_target="tpu_custom_call" | custom-call | flops 1000000000 | bytes 4000000 | tf_op jit(solution)/shard_map/pallas_call | solution.py:232
  125.2 1.6 collective-permute-start.1
  126.7 0.7 pad_maximum_fusion
  127.5 38.6 %all_to_all.30.along_ref = bf16[8,4,32,512]{3,2,1,0:T(8,128)(2,1)} all-to-all(bf16[8,4,32,512]{3,2,1,0:T(8,128)(2,1)} %get-tuple-element.25), channel_id=1, replica_groups=mesh['row'=16,'col'=8] {'col'}, dimensions={0} | all-to-all | bytes 2097152 | tf_op jit(solution)/shard_map/all_to_all | solution.py:500
  166.1 3.5 %all-to-all-start.5 = ((f32[16,64,128]{2,1,0:T(8,128)}), f32[16,64,128]{2,1,0:T(8,128)S(1)}, u32[]{:S(2)}, u32[]{:S(2)}) async-start(f32[16,64,128]{2,1,0:T(8,128)} %all-to-all-done.3), calls=%async_computation.5 | async-start | bytes 1048576 | tf_op jit(solution)/shard_map/all_to_all | solution.py:502
  169.6 5.2 %shard_map.63.panel_ref = f32[1024,512]{1,0:T(8,128)} custom-call(s32[22]{0:T(128)} %concatenate.13.flags, f32[1024,2048]{1,0:T(8,128)} %cov_ref.5, f32[1024,2048]{1,0:T(8,128)} %cov_ref.5, bf16[8,4,32,512]{3,2,1,0:T(8,128)(2,1)} %all_to_all.30.along_ref, bf16[256,3072]{1,0:T(8,128)(2,1)} %get-tuple-element.19.inverse_ref, ...), custom_call_target="tpu_custom_call" | custom-call | flops 1000000000 | bytes 4000000 | tf_op jit(solution)/shard_map/pallas_call | solution.py:280
  174.7 7.4 %all-to-all-done.5.relaid_ref = f32[16,64,128]{2,1,0:T(8,128)S(1)} async-done(((f32[16,64,128]{2,1,0:T(8,128)}), f32[16,64,128]{2,1,0:T(8,128)S(1)}, u32[]{:S(2)}, u32[]{:S(2)}) %all-to-all-start.5) | async-done | bytes 524320 | tf_op jit(solution)/shard_map/all_to_all | solution.py:502
  182.1 0.8 copy-done.3
  182.9 14.4 %shard_map.64 = (f32[1024,2048]{1,0:T(8,128)}, f32[128,1024]{1,0:T(8,128)}) custom-call(s32[22]{0:T(128)} %concatenate.13.flags, f32[1024,2048]{1,0:T(8,128)} %cov_ref.5, bf16[8,4,32,512]{3,2,1,0:T(8,128)(2,1)} %all_to_all.30.along_ref, bf16[16,7,32,512]{3,2,1,0:T(8,128)(2,1)} %bitcast.32, f32[16,64,128]{2,1,0:T(8,128)} %copy-done.3, ...), custom_call_target="tpu_custom_call" | custom-call | flops 5000000000 | bytes 20000000 | tf_op jit(solution)/shard_map/pallas_call | solution.py:400
  (28 shorter events, 3.1 us)
Async XLA Ops:
  7.8 14.0 %copy-start.4 = (s32[64]{0:T(128)S(1)}, s32[64]{0:T(128)}, u32[]{:S(2)}) copy-start(s32[64]{0:T(128)} %owner_ref.1) | copy-start | bytes 772
  10.6 32.7 %copy-start.2 = (f32[64,16,128]{2,1,0:T(8,128)S(1)}, f32[64,16,128]{2,1,0:T(8,128)}, u32[]{:S(2)}) copy-start(f32[64,16,128]{2,1,0:T(8,128)} %param.5) | copy-start | bytes 1572868
  10.6 24.5 %all-to-all-start = ((f32[128,8,128]{2,1,0:T(8,128)}), f32[128,8,128]{2,1,0:T(8,128)S(1)}, u32[]{:S(2)}, u32[]{:S(2)}) async-start(f32[128,8,128]{2,1,0:T(8,128)} %bitcast.31), calls=%async_computation | async-start | bytes 1048576 | tf_op jit(solution)/shard_map/all_to_all | solution.py:469
  36.1 23.4 %all-to-all-start.1 = ((f32[128,16,128]{2,1,0:T(8,128)}), f32[128,16,128]{2,1,0:T(8,128)S(1)}, u32[]{:S(2)}, u32[]{:S(2)}) async-start(f32[128,16,128]{2,1,0:T(8,128)} %broadcast_in_dim.36), calls=%async_computation.1 | async-start | bytes 2097152 | tf_op jit(solution)/shard_map/all_to_all | solution.py:474
  46.4 5.1 %collective-permute-start = (f32[32,512]{1,0:T(8,128)S(1)}, f32[32,512]{1,0:T(8,128)S(1)}, u32[]{:S(2)}, u32[]{:S(2)}) collective-permute-start(f32[32,512]{1,0:T(8,128)S(1)} %pad_maximum_fusion.1), channel_id=1, source_target_pairs={{0,0},{1,16},{2,32},{3,48},{4,64},{5,80},{6,96},{7,112},{8,8},{9,2... | collective-permute-start | bytes 196616 | tf_op jit(solution)/shard_map/ppermute | solution.py:466
  59.5 1.0 copy-start.1
  60.5 32.9 %all-to-all-start.2 = ((f32[8,4,32,512]{3,2,1,0:T(8,128)}), f32[8,4,32,512]{3,2,1,0:T(8,128)S(1)}, u32[]{:S(2)}, u32[]{:S(2)}) async-start(f32[8,4,32,512]{3,2,1,0:T(8,128)} %shard_map.59), calls=%async_computation.2 | async-start | bytes 4194304 | tf_op jit(solution)/shard_map/all_to_all | solution.py:486
  93.4 27.1 %copy-start = (f32[8,4,32,512]{3,2,1,0:T(8,128)}, f32[8,4,32,512]{3,2,1,0:T(8,128)S(1)}, u32[]{:S(2)}) copy-start(f32[8,4,32,512]{3,2,1,0:T(8,128)S(1)} %all-to-all-done.2.first_ref.second_ref) | copy-start | bytes 6291460
  93.4 33.3 %all-to-all-start.3 = ((f32[16,64,128]{2,1,0:T(8,128)}), f32[16,64,128]{2,1,0:T(8,128)}, u32[]{:S(2)}, u32[]{:S(2)}) async-start(f32[16,64,128]{2,1,0:T(8,128)} %bitcast.29), calls=%async_computation.3 | async-start | bytes 1048576 | tf_op jit(solution)/shard_map/all_to_all | solution.py:493
  97.7 84.4 %all-gather.3.cloned.1.call-start = ((), (), s32[]{:S(2)}) async-start(), calls=%async_computation.6 | async-start | bytes 3899392 | tf_op jit(solution)/shard_map/all_gather | solution.py:498
  125.2 1.6 collective-permute-start.1
  166.1 16.0 %all-to-all-start.5 = ((f32[16,64,128]{2,1,0:T(8,128)}), f32[16,64,128]{2,1,0:T(8,128)S(1)}, u32[]{:S(2)}, u32[]{:S(2)}) async-start(f32[16,64,128]{2,1,0:T(8,128)} %all-to-all-done.3), calls=%async_computation.5 | async-start | bytes 1048576 | tf_op jit(solution)/shard_map/all_to_all | solution.py:502
  182.1 0.8 copy-start.3
Sparse Core Ops, SparseCore 0:
  127.6 50.3 all-gather.2

commit v11 on v10

--- a/solution.py
+++ b/solution.py
@@ -489,7 +489,7 @@
     middle = lax.reduce_precision(wanted - high, 8, 7)
     wanted = jnp.stack([high, middle, wanted - high - middle]).astype(BF16)
 
-    groups, _ = lax.optimization_barrier((jnp.transpose(innovations, (1, 0, 2)), parts))
+    groups, _, _ = lax.optimization_barrier((jnp.transpose(innovations, (1, 0, 2)), parts, l10t))
     groups = lax.all_to_all(groups, "row", split_axis=0, concat_axis=0, tiled=True)
 
     along, across = solve_piece(flags, parts, inverse, l10t)

time: 207 us -> 185 us (0.89)
  waiting for transfers between devices: 52 us -> 33.9 us
  blocking collectives: 38.6 us -> 34.7 us
    all_to_all x1, waiting for transfers between devices: 27.9 us -> 6.03 us  [per_device(): lax.all_to_all(picked, 'col', split_axis=0, concat_axis=0, tiled=True)]
    all_to_all x1, waiting for transfers between devices: 0.01 us -> 4 us  [per_device(): lax.all_to_all(groups, 'row', split_axis=0, concat_axis=0, tiled=True)]
    all_to_all x1, blocking collectives: 38.6 us -> 34.7 us  [per_device(): lax.all_to_all(along, 'col', split_axis=0, concat_axis=0, tiled=True)]
  transfers between devices with their start and end apart: 8 -> 8, of which waited for: 4 -> 5; matrix products, arithmetic and copies ran while one was open for 2% -> 3% of each run, Pallas kernels for 18% -> 20%
where the time goes in v11:
time: 185 us; the launch traced here: 182 us
  Pallas kernels  53.9 us (29%)
  blocking collectives  34.7 us (19%)
  waiting for transfers between devices  33.9 us (18%)
  starting transfers between devices  30.3 us (16%)
  between operations  21.2 us (11%)
  local copies, waits for them, and re-layouts  6.63 us (4%)
    all_to_all x1, blocking collectives, per_device(): lax.all_to_all(along, 'col', split_axis=0, concat_axis=0, tiled=True)  34.7 us
    pallas_call x1, Pallas kernels, factor_diagonal(): pl.pallas_call(factor_kernel, in_specs=[VMEM_SPEC], out_specs=[VMEM_SPEC]...  22.6 us
    pallas_call x1, Pallas kernels, update(): pl.pallas_call(update_kernel, grid_spec=pltpu.PrefetchScalarGridSpec(num_...  14.4 us
    all_to_all x1, starting transfers between devices, per_device(): lax.all_to_all(tiles, ('row', 'col'), split_axis=0, concat_axis=0, tiled=...  11.1 us
    all_to_all x1, waiting for transfers between devices, per_device(): lax.all_to_all(tiles, ('row', 'col'), split_axis=0, concat_axis=0, tiled=...  8.69 us
    all_to_all x1, waiting for transfers between devices, per_device(): lax.all_to_all(jnp.broadcast_to(tiles[None], (n_row * n_col,) + tiles.sha...  7.96 us
    all_to_all x1, waiting for transfers between devices, per_device(): lax.all_to_all(groups, 'col', split_axis=0, concat_axis=0, tiled=True)  7.17 us
    all_to_all x1, waiting for transfers between devices, per_device(): lax.all_to_all(picked, 'col', split_axis=0, concat_axis=0, tiled=True)  6.03 us
  transfers between devices with their start and end apart: 8, of which 5 were waited for; matrix products, arithmetic and copies ran while one was open for 3% of the time, Pallas kernels for 20%

profile of v11, /device:TPU:0, one launch (start us, length us, event | category | flops | bytes accessed | tf_op | source)
XLA Modules:
  0.0 182.2 jit_solution(17258153297326961027)
XLA Ops:
  7.8 2.7 %shard_map.60 = f32[32,4,8,128]{3,2,1,0:T(8,128)} custom-call(s32[64]{0:T(128)} %owner_ref.1, s32[1]{0:T(128)} %copy.18.panel_ref, f32[1024,2048]{1,0:T(8,128)} %cov_ref.5), custom_call_target="tpu_custom_call" | custom-call | tf_op jit(solution)/shard_map/pallas_call | solution.py:78
  10.6 11.1 %all-to-all-start = ((f32[128,8,128]{2,1,0:T(8,128)}), f32[128,8,128]{2,1,0:T(8,128)S(1)}, u32[]{:S(2)}, u32[]{:S(2)}) async-start(f32[128,8,128]{2,1,0:T(8,128)} %bitcast.31), calls=%async_computation | async-start | bytes 1048576 | tf_op jit(solution)/shard_map/all_to_all | solution.py:469
  26.4 8.7 %all-to-all-done = f32[128,8,128]{2,1,0:T(8,128)S(1)} async-done(((f32[128,8,128]{2,1,0:T(8,128)}), f32[128,8,128]{2,1,0:T(8,128)S(1)}, u32[]{:S(2)}, u32[]{:S(2)}) %all-to-all-start) | async-done | bytes 524320 | tf_op jit(solution)/shard_map/all_to_all | solution.py:469
  35.1 1.1 broadcast_in_dim.36
  36.1 4.6 %all-to-all-start.1 = ((f32[128,16,128]{2,1,0:T(8,128)}), f32[128,16,128]{2,1,0:T(8,128)S(1)}, u32[]{:S(2)}, u32[]{:S(2)}) async-start(f32[128,16,128]{2,1,0:T(8,128)} %broadcast_in_dim.36), calls=%async_computation.1 | async-start | bytes 2097152 | tf_op jit(solution)/shard_map/all_to_all | solution.py:474
  43.4 1.0 copy.17
  45.6 0.8 dynamic-slice_bitcast_fusion.3
  47.1 4.5 %shard_map.59 = f32[8,4,32,512]{3,2,1,0:T(8,128)} custom-call(s32[2]{0:T(128)} %get-tuple-element.36.slots, f32[1024,2048]{1,0:T(8,128)} %cov_ref.5), custom_call_target="tpu_custom_call" | custom-call | tf_op jit(solution)/shard_map/pallas_call | solution.py:39
  51.5 8.0 %all-to-all-done.1.tiles_ref = f32[128,16,128]{2,1,0:T(8,128)S(1)} async-done(((f32[128,16,128]{2,1,0:T(8,128)}), f32[128,16,128]{2,1,0:T(8,128)S(1)}, u32[]{:S(2)}, u32[]{:S(2)}) %all-to-all-start.1) | async-done | bytes 1048608 | tf_op jit(solution)/shard_map/all_to_all | solution.py:474
  59.5 1.0 copy-done.1
  60.5 4.3 %all-to-all-start.2 = ((f32[8,4,32,512]{3,2,1,0:T(8,128)}), f32[8,4,32,512]{3,2,1,0:T(8,128)S(1)}, u32[]{:S(2)}, u32[]{:S(2)}) async-start(f32[8,4,32,512]{3,2,1,0:T(8,128)} %shard_map.59), calls=%async_computation.2 | async-start | bytes 4194304 | tf_op jit(solution)/shard_map/all_to_all | solution.py:486
  64.8 22.6 %shard_map.61 = (bf16[256,3072]{1,0:T(8,128)(2,1)}, bf16[256,256]{1,0:T(8,128)(2,1)}, f32[256,512]{1,0:T(8,128)}) custom-call(f32[128,16,128]{2,1,0:T(8,128)} %copy-done.1), custom_call_target="tpu_custom_call" | custom-call | flops 20000000000 | bytes 80000000 | tf_op jit(solution)/shard_map/pallas_call | solution.py:187
  87.4 6.0 %all-to-all-done.2.first_ref.second_ref = f32[8,4,32,512]{3,2,1,0:T(8,128)S(1)} async-done(((f32[8,4,32,512]{3,2,1,0:T(8,128)}), f32[8,4,32,512]{3,2,1,0:T(8,128)S(1)}, u32[]{:S(2)}, u32[]{:S(2)}) %all-to-all-start.2) | async-done | bytes 2097184 | tf_op jit(solution)/shard_map/all_to_all | solution.py:486
  93.4 4.5 %all-to-all-start.3 = ((f32[16,64,128]{2,1,0:T(8,128)}), f32[16,64,128]{2,1,0:T(8,128)}, u32[]{:S(2)}, u32[]{:S(2)}) async-start(f32[16,64,128]{2,1,0:T(8,128)} %bitcast.29), calls=%async_computation.3 | async-start | bytes 1048576 | tf_op jit(solution)/shard_map/all_to_all | solution.py:493
  98.8 4.4 %shard_map.62 = (bf16[8,4,32,512]{3,2,1,0:T(8,128)(2,1)}, bf16[4,32,512]{2,1,0:T(8,128)(2,1)}) custom-call(s32[22]{0:T(128)} %concatenate.13.flags, f32[8,4,32,512]{3,2,1,0:T(8,128)} %copy-done, f32[8,4,32,512]{3,2,1,0:T(8,128)} %copy-done, bf16[256,3072]{1,0:T(8,128)(2,1)} %get-tuple-element.19.inverse_ref, bf16[256,256]{1,0:T(8,128)(2,1)} %get-tuple-element.20.l10t_ref), custom_call_target="tpu_custom_call" | custom-call | flops 1000000000 | bytes 4000000 | tf_op jit(solution)/shard_map/pallas_call | solution.py:232
  103.2 1.6 collective-permute-start.1
  104.8 4.0 %all-to-all-done.3 = f32[16,64,128]{2,1,0:T(8,128)} async-done(((f32[16,64,128]{2,1,0:T(8,128)}), f32[16,64,128]{2,1,0:T(8,128)}, u32[]{:S(2)}, u32[]{:S(2)}) %all-to-all-start.3) | async-done | bytes 524320 | tf_op jit(solution)/shard_map/all_to_all | solution.py:493
  108.8 0.7 pad_maximum_fusion
  109.5 34.7 %all_to_all.30.along_ref = bf16[8,4,32,512]{3,2,1,0:T(8,128)(2,1)} all-to-all(bf16[8,4,32,512]{3,2,1,0:T(8,128)(2,1)} %get-tuple-element.25), channel_id=1, replica_groups=mesh['row'=16,'col'=8] {'col'}, dimensions={0} | all-to-all | bytes 2097152 | tf_op jit(solution)/shard_map/all_to_all | solution.py:500
  144.2 3.5 %all-to-all-start.5 = ((f32[16,64,128]{2,1,0:T(8,128)}), f32[16,64,128]{2,1,0:T(8,128)S(1)}, u32[]{:S(2)}, u32[]{:S(2)}) async-start(f32[16,64,128]{2,1,0:T(8,128)} %all-to-all-done.3), calls=%async_computation.5 | async-start | bytes 1048576 | tf_op jit(solution)/shard_map/all_to_all | solution.py:502
  147.7 5.2 %shard_map.63.panel_ref = f32[1024,512]{1,0:T(8,128)} custom-call(s32[22]{0:T(128)} %concatenate.13.flags, f32[1024,2048]{1,0:T(8,128)} %cov_ref.5, f32[1024,2048]{1,0:T(8,128)} %cov_ref.5, bf16[8,4,32,512]{3,2,1,0:T(8,128)(2,1)} %all_to_all.30.along_ref, bf16[256,3072]{1,0:T(8,128)(2,1)} %get-tuple-element.19.inverse_ref, ...), custom_call_target="tpu_custom_call" | custom-call | flops 1000000000 | bytes 4000000 | tf_op jit(solution)/shard_map/pallas_call | solution.py:280
  152.9 7.2 %all-to-all-done.5.relaid_ref = f32[16,64,128]{2,1,0:T(8,128)S(1)} async-done(((f32[16,64,128]{2,1,0:T(8,128)}), f32[16,64,128]{2,1,0:T(8,128)S(1)}, u32[]{:S(2)}, u32[]{:S(2)}) %all-to-all-start.5) | async-done | bytes 524320 | tf_op jit(solution)/shard_map/all_to_all | solution.py:502
  160.1 0.8 copy-done.3
  160.9 14.4 %shard_map.64 = (f32[1024,2048]{1,0:T(8,128)}, f32[128,1024]{1,0:T(8,128)}) custom-call(s32[22]{0:T(128)} %concatenate.13.flags, f32[1024,2048]{1,0:T(8,128)} %cov_ref.5, bf16[8,4,32,512]{3,2,1,0:T(8,128)(2,1)} %all_to_all.30.along_ref, bf16[16,7,32,512]{3,2,1,0:T(8,128)(2,1)} %bitcast.32, f32[16,64,128]{2,1,0:T(8,128)} %copy-done.3, ...), custom_call_target="tpu_custom_call" | custom-call | flops 5000000000 | bytes 20000000 | tf_op jit(solution)/shard_map/pallas_call | solution.py:400
  (28 shorter events, 3.6 us)
Async XLA Ops:
  7.8 14.0 %copy-start.4 = (s32[64]{0:T(128)S(1)}, s32[64]{0:T(128)}, u32[]{:S(2)}) copy-start(s32[64]{0:T(128)} %owner_ref.1) | copy-start | bytes 772
  10.6 32.8 %copy-start.2 = (f32[64,16,128]{2,1,0:T(8,128)S(1)}, f32[64,16,128]{2,1,0:T(8,128)}, u32[]{:S(2)}) copy-start(f32[64,16,128]{2,1,0:T(8,128)} %param.5) | copy-start | bytes 1572868
  10.6 24.5 %all-to-all-start = ((f32[128,8,128]{2,1,0:T(8,128)}), f32[128,8,128]{2,1,0:T(8,128)S(1)}, u32[]{:S(2)}, u32[]{:S(2)}) async-start(f32[128,8,128]{2,1,0:T(8,128)} %bitcast.31), calls=%async_computation | async-start | bytes 1048576 | tf_op jit(solution)/shard_map/all_to_all | solution.py:469
  36.1 23.4 %all-to-all-start.1 = ((f32[128,16,128]{2,1,0:T(8,128)}), f32[128,16,128]{2,1,0:T(8,128)S(1)}, u32[]{:S(2)}, u32[]{:S(2)}) async-start(f32[128,16,128]{2,1,0:T(8,128)} %broadcast_in_dim.36), calls=%async_computation.1 | async-start | bytes 2097152 | tf_op jit(solution)/shard_map/all_to_all | solution.py:474
  46.4 5.1 %collective-permute-start = (f32[32,512]{1,0:T(8,128)S(1)}, f32[32,512]{1,0:T(8,128)S(1)}, u32[]{:S(2)}, u32[]{:S(2)}) collective-permute-start(f32[32,512]{1,0:T(8,128)S(1)} %pad_maximum_fusion.1), channel_id=1, source_target_pairs={{0,0},{1,16},{2,32},{3,48},{4,64},{5,80},{6,96},{7,112},{8,8},{9,2... | collective-permute-start | bytes 196616 | tf_op jit(solution)/shard_map/ppermute | solution.py:466
  59.5 1.0 copy-start.1
  60.5 32.9 %all-to-all-start.2 = ((f32[8,4,32,512]{3,2,1,0:T(8,128)}), f32[8,4,32,512]{3,2,1,0:T(8,128)S(1)}, u32[]{:S(2)}, u32[]{:S(2)}) async-start(f32[8,4,32,512]{3,2,1,0:T(8,128)} %shard_map.59), calls=%async_computation.2 | async-start | bytes 4194304 | tf_op jit(solution)/shard_map/all_to_all | solution.py:486
  93.4 5.3 %copy-start = (f32[8,4,32,512]{3,2,1,0:T(8,128)}, f32[8,4,32,512]{3,2,1,0:T(8,128)S(1)}, u32[]{:S(2)}) copy-start(f32[8,4,32,512]{3,2,1,0:T(8,128)S(1)} %all-to-all-done.2.first_ref.second_ref) | copy-start | bytes 6291460
  93.4 15.3 %all-to-all-start.3 = ((f32[16,64,128]{2,1,0:T(8,128)}), f32[16,64,128]{2,1,0:T(8,128)}, u32[]{:S(2)}, u32[]{:S(2)}) async-start(f32[16,64,128]{2,1,0:T(8,128)} %bitcast.29), calls=%async_computation.3 | async-start | bytes 1048576 | tf_op jit(solution)/shard_map/all_to_all | solution.py:493
  97.9 62.2 %all-gather.3.cloned.1.call-start = ((), (), s32[]{:S(2)}) async-start(), calls=%async_computation.6 | async-start | bytes 3899392 | tf_op jit(solution)/shard_map/all_gather | solution.py:498
  103.2 1.6 collective-permute-start.1
  144.2 15.9 %all-to-all-start.5 = ((f32[16,64,128]{2,1,0:T(8,128)}), f32[16,64,128]{2,1,0:T(8,128)S(1)}, u32[]{:S(2)}, u32[]{:S(2)}) async-start(f32[16,64,128]{2,1,0:T(8,128)} %all-to-all-done.3), calls=%async_computation.5 | async-start | bytes 1048576 | tf_op jit(solution)/shard_map/all_to_all | solution.py:502
  160.1 0.8 copy-start.3
Sparse Core Ops, SparseCore 0:
  109.6 46.3 all-gather.2

commit v12 on v11

--- a/solution.py
+++ b/solution.py
@@ -277,19 +277,20 @@
 def solve_panels(flags, covariance, along, inverse, l10t):
     rows = covariance.shape[0]
     parts, blocks, part, width = along.shape
+    turn = lambda i, flags: jnp.where((flags[4] & flags[5]) >= 0, i, 0)
     return pl.pallas_call(
         panel_kernel,
         grid_spec=pltpu.PrefetchScalarGridSpec(
             num_scalar_prefetch=1,
             grid=(blocks,),
             in_specs=[
-                pl.BlockSpec((B, B), lambda i, flags: (i, jnp.maximum(flags[4], 0))),
-                pl.BlockSpec((B, B), lambda i, flags: (i, jnp.maximum(flags[5], 0))),
-                pl.BlockSpec((parts, 1, part, width), lambda i, flags: (0, i, 0, 0)),
+                pl.BlockSpec((B, B), lambda i, flags: (turn(i, flags), jnp.maximum(flags[4], 0))),
+                pl.BlockSpec((B, B), lambda i, flags: (turn(i, flags), jnp.maximum(flags[5], 0))),
+                pl.BlockSpec((parts, 1, part, width), lambda i, flags: (0, turn(i, flags), 0, 0)),
                 whole(*inverse.shape),
                 whole(*l10t.shape),
             ],
-            out_specs=pl.BlockSpec((B, 2 * B), lambda i, flags: (i, 0)),
+            out_specs=pl.BlockSpec((B, 2 * B), lambda i, flags: (turn(i, flags), 0)),
             scratch_shapes=[pltpu.VMEM((B, 6 * B), BF16)],
         ),
         out_shape=jax.ShapeDtypeStruct((rows, 2 * B), F32),
@@ -338,7 +339,7 @@
                 copies.append(pltpu.make_async_copy(source, columns.at[parity, :, q], arrived.at[len(copies)]))
         for copy in copies:
             copy.start()
-        for copy in copies:
+        for copy in copies[:8]:
             copy.wait()
         for panel in range(2):
             for h in range(2):
@@ -355,6 +356,8 @@
         w0, w1 = solve_rows(white_ref[:, 0:B], white_ref[:, B : 2 * B], wide, inverse_ref, l10t_ref)
         white_ref[:, 0:B] = w0
         white_ref[:, B : 2 * B] = w1
+        for copy in copies[8:]:
+            copy.wait()
 
     level = flags[16 + i]
     own = along_ref[:, 0].reshape(parts * part, 2 * B)

time: 185 us -> 184 us (level)
  Pallas kernels: 53.9 us -> 51.3 us
  waiting for transfers between devices: 33.9 us -> 35.9 us
    all_to_all x1, waiting for transfers between devices: 7.17 us -> 9.14 us  [per_device(): lax.all_to_all(groups, 'col', split_axis=0, concat_axis=0, tiled=True)]
    pallas_call x1, Pallas kernels: 5.19 us -> 3.21 us  [solve_panels(): pl.pallas_call(panel_kernel, grid_spec=pltpu.PrefetchScalarGridSpec(num_s...]
  transfers between devices with their start and end apart: 8 -> 8, of which waited for: 5 -> 5; matrix products, arithmetic and copies ran while one was open for 3% -> 3% of each run, Pallas kernels for 20% -> 19%
where the time goes in v12:
time: 184 us; the launch traced here: 182 us
  Pallas kernels  51.3 us (28%)
  waiting for transfers between devices  35.9 us (20%)
  blocking collectives  34.7 us (19%)
  starting transfers between devices  30.3 us (16%)
  between operations  21.2 us (12%)
  local copies, waits for them, and re-layouts  6.63 us (4%)
    all_to_all x1, blocking collectives, per_device(): lax.all_to_all(along, 'col', split_axis=0, concat_axis=0, tiled=True)  34.7 us
    pallas_call x1, Pallas kernels, factor_diagonal(): pl.pallas_call(factor_kernel, in_specs=[VMEM_SPEC], out_specs=[VMEM_SPEC]...  22.6 us
    pallas_call x1, Pallas kernels, update(): pl.pallas_call(update_kernel, grid_spec=pltpu.PrefetchScalarGridSpec(num_...  13.8 us
    all_to_all x1, starting transfers between devices, per_device(): lax.all_to_all(tiles, ('row', 'col'), split_axis=0, concat_axis=0, tiled=...  11.1 us
    all_to_all x1, waiting for transfers between devices, per_device(): lax.all_to_all(groups, 'col', split_axis=0, concat_axis=0, tiled=True)  9.14 us
    all_to_all x1, waiting for transfers between devices, per_device(): lax.all_to_all(tiles, ('row', 'col'), split_axis=0, concat_axis=0, tiled=...  8.69 us
    all_to_all x1, waiting for transfers between devices, per_device(): lax.all_to_all(jnp.broadcast_to(tiles[None], (n_row * n_col,) + tiles.sha...  7.96 us
    all_to_all x1, waiting for transfers between devices, per_device(): lax.all_to_all(picked, 'col', split_axis=0, concat_axis=0, tiled=True)  6.03 us
  transfers between devices with their start and end apart: 8, of which 5 were waited for; matrix products, arithmetic and copies ran while one was open for 3% of the time, Pallas kernels for 19%

profile of v12, /device:TPU:0, one launch (start us, length us, event | category | flops | bytes accessed | tf_op | source)
XLA Modules:
  0.0 181.6 jit_solution(11145837121977492178)
XLA Ops:
  7.8 2.7 %shard_map.60 = f32[32,4,8,128]{3,2,1,0:T(8,128)} custom-call(s32[64]{0:T(128)} %owner_ref.1, s32[1]{0:T(128)} %copy.18.panel_ref, f32[1024,2048]{1,0:T(8,128)} %cov_ref.5), custom_call_target="tpu_custom_call" | custom-call | tf_op jit(solution)/shard_map/pallas_call | solution.py:78
  10.6 11.1 %all-to-all-start = ((f32[128,8,128]{2,1,0:T(8,128)}), f32[128,8,128]{2,1,0:T(8,128)S(1)}, u32[]{:S(2)}, u32[]{:S(2)}) async-start(f32[128,8,128]{2,1,0:T(8,128)} %bitcast.31), calls=%async_computation | async-start | bytes 1048576 | tf_op jit(solution)/shard_map/all_to_all | solution.py:472
  26.4 8.7 %all-to-all-done = f32[128,8,128]{2,1,0:T(8,128)S(1)} async-done(((f32[128,8,128]{2,1,0:T(8,128)}), f32[128,8,128]{2,1,0:T(8,128)S(1)}, u32[]{:S(2)}, u32[]{:S(2)}) %all-to-all-start) | async-done | bytes 524320 | tf_op jit(solution)/shard_map/all_to_all | solution.py:472
  35.1 1.1 broadcast_in_dim.36
  36.1 4.6 %all-to-all-start.1 = ((f32[128,16,128]{2,1,0:T(8,128)}), f32[128,16,128]{2,1,0:T(8,128)S(1)}, u32[]{:S(2)}, u32[]{:S(2)}) async-start(f32[128,16,128]{2,1,0:T(8,128)} %broadcast_in_dim.36), calls=%async_computation.1 | async-start | bytes 2097152 | tf_op jit(solution)/shard_map/all_to_all | solution.py:477
  43.4 1.0 copy.17
  45.6 0.8 dynamic-slice_bitcast_fusion.3
  47.1 4.5 %shard_map.59 = f32[8,4,32,512]{3,2,1,0:T(8,128)} custom-call(s32[2]{0:T(128)} %get-tuple-element.36.slots, f32[1024,2048]{1,0:T(8,128)} %cov_ref.5), custom_call_target="tpu_custom_call" | custom-call | tf_op jit(solution)/shard_map/pallas_call | solution.py:39
  51.5 8.0 %all-to-all-done.1.tiles_ref = f32[128,16,128]{2,1,0:T(8,128)S(1)} async-done(((f32[128,16,128]{2,1,0:T(8,128)}), f32[128,16,128]{2,1,0:T(8,128)S(1)}, u32[]{:S(2)}, u32[]{:S(2)}) %all-to-all-start.1) | async-done | bytes 1048608 | tf_op jit(solution)/shard_map/all_to_all | solution.py:477
  59.5 1.0 copy-done.1
  60.5 4.3 %all-to-all-start.2 = ((f32[8,4,32,512]{3,2,1,0:T(8,128)}), f32[8,4,32,512]{3,2,1,0:T(8,128)S(1)}, u32[]{:S(2)}, u32[]{:S(2)}) async-start(f32[8,4,32,512]{3,2,1,0:T(8,128)} %shard_map.59), calls=%async_computation.2 | async-start | bytes 4194304 | tf_op jit(solution)/shard_map/all_to_all | solution.py:489
  64.8 22.6 %shard_map.61 = (bf16[256,3072]{1,0:T(8,128)(2,1)}, bf16[256,256]{1,0:T(8,128)(2,1)}, f32[256,512]{1,0:T(8,128)}) custom-call(f32[128,16,128]{2,1,0:T(8,128)} %copy-done.1), custom_call_target="tpu_custom_call" | custom-call | flops 20000000000 | bytes 80000000 | tf_op jit(solution)/shard_map/pallas_call | solution.py:187
  87.4 6.0 %all-to-all-done.2.first_ref.second_ref = f32[8,4,32,512]{3,2,1,0:T(8,128)S(1)} async-done(((f32[8,4,32,512]{3,2,1,0:T(8,128)}), f32[8,4,32,512]{3,2,1,0:T(8,128)S(1)}, u32[]{:S(2)}, u32[]{:S(2)}) %all-to-all-start.2) | async-done | bytes 2097184 | tf_op jit(solution)/shard_map/all_to_all | solution.py:489
  93.4 4.5 %all-to-all-start.3 = ((f32[16,64,128]{2,1,0:T(8,128)}), f32[16,64,128]{2,1,0:T(8,128)}, u32[]{:S(2)}, u32[]{:S(2)}) async-start(f32[16,64,128]{2,1,0:T(8,128)} %bitcast.29), calls=%async_computation.3 | async-start | bytes 1048576 | tf_op jit(solution)/shard_map/all_to_all | solution.py:496
  98.8 4.4 %shard_map.62 = (bf16[8,4,32,512]{3,2,1,0:T(8,128)(2,1)}, bf16[4,32,512]{2,1,0:T(8,128)(2,1)}) custom-call(s32[22]{0:T(128)} %concatenate.13.flags, f32[8,4,32,512]{3,2,1,0:T(8,128)} %copy-done, f32[8,4,32,512]{3,2,1,0:T(8,128)} %copy-done, bf16[256,3072]{1,0:T(8,128)(2,1)} %get-tuple-element.19.inverse_ref, bf16[256,256]{1,0:T(8,128)(2,1)} %get-tuple-element.20.l10t_ref), custom_call_target="tpu_custom_call" | custom-call | flops 1000000000 | bytes 4000000 | tf_op jit(solution)/shard_map/pallas_call | solution.py:232
  103.2 1.6 collective-permute-start.1
  104.8 4.0 %all-to-all-done.3 = f32[16,64,128]{2,1,0:T(8,128)} async-done(((f32[16,64,128]{2,1,0:T(8,128)}), f32[16,64,128]{2,1,0:T(8,128)}, u32[]{:S(2)}, u32[]{:S(2)}) %all-to-all-start.3) | async-done | bytes 524320 | tf_op jit(solution)/shard_map/all_to_all | solution.py:496
  108.8 0.7 pad_maximum_fusion
  109.5 34.7 %all_to_all.30.along_ref = bf16[8,4,32,512]{3,2,1,0:T(8,128)(2,1)} all-to-all(bf16[8,4,32,512]{3,2,1,0:T(8,128)(2,1)} %get-tuple-element.25), channel_id=1, replica_groups=mesh['row'=16,'col'=8] {'col'}, dimensions={0} | all-to-all | bytes 2097152 | tf_op jit(solution)/shard_map/all_to_all | solution.py:503
  144.2 3.5 %all-to-all-start.5 = ((f32[16,64,128]{2,1,0:T(8,128)}), f32[16,64,128]{2,1,0:T(8,128)S(1)}, u32[]{:S(2)}, u32[]{:S(2)}) async-start(f32[16,64,128]{2,1,0:T(8,128)} %all-to-all-done.3), calls=%async_computation.5 | async-start | bytes 1048576 | tf_op jit(solution)/shard_map/all_to_all | solution.py:505
  147.7 3.2 %shard_map.63.panel_ref = f32[1024,512]{1,0:T(8,128)} custom-call(s32[22]{0:T(128)} %concatenate.13.flags, f32[1024,2048]{1,0:T(8,128)} %cov_ref.5, f32[1024,2048]{1,0:T(8,128)} %cov_ref.5, bf16[8,4,32,512]{3,2,1,0:T(8,128)(2,1)} %all_to_all.30.along_ref, bf16[256,3072]{1,0:T(8,128)(2,1)} %get-tuple-element.19.inverse_ref, ...), custom_call_target="tpu_custom_call" | custom-call | flops 1000000000 | bytes 4000000 | tf_op jit(solution)/shard_map/pallas_call | solution.py:281
  150.9 9.1 %all-to-all-done.5.relaid_ref = f32[16,64,128]{2,1,0:T(8,128)S(1)} async-done(((f32[16,64,128]{2,1,0:T(8,128)}), f32[16,64,128]{2,1,0:T(8,128)S(1)}, u32[]{:S(2)}, u32[]{:S(2)}) %all-to-all-start.5) | async-done | bytes 524320 | tf_op jit(solution)/shard_map/all_to_all | solution.py:505
  160.1 0.8 copy-done.3
  160.9 13.8 %shard_map.64 = (f32[1024,2048]{1,0:T(8,128)}, f32[128,1024]{1,0:T(8,128)}) custom-call(s32[22]{0:T(128)} %concatenate.13.flags, f32[1024,2048]{1,0:T(8,128)} %cov_ref.5, bf16[8,4,32,512]{3,2,1,0:T(8,128)(2,1)} %all_to_all.30.along_ref, bf16[16,7,32,512]{3,2,1,0:T(8,128)(2,1)} %bitcast.32, f32[16,64,128]{2,1,0:T(8,128)} %copy-done.3, ...), custom_call_target="tpu_custom_call" | custom-call | flops 5000000000 | bytes 20000000 | tf_op jit(solution)/shard_map/pallas_call | solution.py:403
  (28 shorter events, 3.6 us)
Async XLA Ops:
  7.8 14.0 %copy-start.4 = (s32[64]{0:T(128)S(1)}, s32[64]{0:T(128)}, u32[]{:S(2)}) copy-start(s32[64]{0:T(128)} %owner_ref.1) | copy-start | bytes 772
  10.6 32.8 %copy-start.2 = (f32[64,16,128]{2,1,0:T(8,128)S(1)}, f32[64,16,128]{2,1,0:T(8,128)}, u32[]{:S(2)}) copy-start(f32[64,16,128]{2,1,0:T(8,128)} %param.5) | copy-start | bytes 1572868
  10.6 24.5 %all-to-all-start = ((f32[128,8,128]{2,1,0:T(8,128)}), f32[128,8,128]{2,1,0:T(8,128)S(1)}, u32[]{:S(2)}, u32[]{:S(2)}) async-start(f32[128,8,128]{2,1,0:T(8,128)} %bitcast.31), calls=%async_computation | async-start | bytes 1048576 | tf_op jit(solution)/shard_map/all_to_all | solution.py:472
  36.1 23.4 %all-to-all-start.1 = ((f32[128,16,128]{2,1,0:T(8,128)}), f32[128,16,128]{2,1,0:T(8,128)S(1)}, u32[]{:S(2)}, u32[]{:S(2)}) async-start(f32[128,16,128]{2,1,0:T(8,128)} %broadcast_in_dim.36), calls=%async_computation.1 | async-start | bytes 2097152 | tf_op jit(solution)/shard_map/all_to_all | solution.py:477
  46.4 5.1 %collective-permute-start = (f32[32,512]{1,0:T(8,128)S(1)}, f32[32,512]{1,0:T(8,128)S(1)}, u32[]{:S(2)}, u32[]{:S(2)}) collective-permute-start(f32[32,512]{1,0:T(8,128)S(1)} %pad_maximum_fusion.1), channel_id=1, source_target_pairs={{0,0},{1,16},{2,32},{3,48},{4,64},{5,80},{6,96},{7,112},{8,8},{9,2... | collective-permute-start | bytes 196616 | tf_op jit(solution)/shard_map/ppermute | solution.py:469
  59.5 1.0 copy-start.1
  60.5 32.9 %all-to-all-start.2 = ((f32[8,4,32,512]{3,2,1,0:T(8,128)}), f32[8,4,32,512]{3,2,1,0:T(8,128)S(1)}, u32[]{:S(2)}, u32[]{:S(2)}) async-start(f32[8,4,32,512]{3,2,1,0:T(8,128)} %shard_map.59), calls=%async_computation.2 | async-start | bytes 4194304 | tf_op jit(solution)/shard_map/all_to_all | solution.py:489
  93.4 5.3 %copy-start = (f32[8,4,32,512]{3,2,1,0:T(8,128)}, f32[8,4,32,512]{3,2,1,0:T(8,128)S(1)}, u32[]{:S(2)}) copy-start(f32[8,4,32,512]{3,2,1,0:T(8,128)S(1)} %all-to-all-done.2.first_ref.second_ref) | copy-start | bytes 6291460
  93.4 15.3 %all-to-all-start.3 = ((f32[16,64,128]{2,1,0:T(8,128)}), f32[16,64,128]{2,1,0:T(8,128)}, u32[]{:S(2)}, u32[]{:S(2)}) async-start(f32[16,64,128]{2,1,0:T(8,128)} %bitcast.29), calls=%async_computation.3 | async-start | bytes 1048576 | tf_op jit(solution)/shard_map/all_to_all | solution.py:496
  97.9 62.2 %all-gather.3.cloned.1.call-start = ((), (), s32[]{:S(2)}) async-start(), calls=%async_computation.6 | async-start | bytes 3899392 | tf_op jit(solution)/shard_map/all_gather | solution.py:501
  103.2 1.6 collective-permute-start.1
  144.2 15.9 %all-to-all-start.5 = ((f32[16,64,128]{2,1,0:T(8,128)}), f32[16,64,128]{2,1,0:T(8,128)S(1)}, u32[]{:S(2)}, u32[]{:S(2)}) async-start(f32[16,64,128]{2,1,0:T(8,128)} %all-to-all-done.3), calls=%async_computation.5 | async-start | bytes 1048576 | tf_op jit(solution)/shard_map/all_to_all | solution.py:505
  160.1 0.8 copy-start.3
Sparse Core Ops, SparseCore 0:
  109.6 46.3 all-gather.2

commit v13 on v12

--- a/solution.py
+++ b/solution.py
@@ -276,7 +276,8 @@
 
 def solve_panels(flags, covariance, along, inverse, l10t):
     rows = covariance.shape[0]
-    parts, blocks, part, width = along.shape
+    parts, _, part, width = along.shape
+    blocks = rows // B
     turn = lambda i, flags: jnp.where((flags[4] & flags[5]) >= 0, i, 0)
     return pl.pallas_call(
         panel_kernel,
@@ -304,7 +305,9 @@
     cov_ref,
     along_ref,
     across_ref,
-    relaid_ref,
+    high_ref,
+    middle_ref,
+    low_ref,
     panel_ref,
     lower_ref,
     inverse_ref,
@@ -322,8 +325,8 @@
     blocks = across_ref.shape[1] - 3
     steps = parts // 2
     column_blocks = 2 * blocks
-    half = relaid_ref.shape[1]
-    fold = half // 2
+    fold = high_ref.shape[2]
+    half = 2 * fold
 
     @pl.when(i == 0)
     def _():
@@ -387,8 +390,12 @@
     product = dot(white_ref[...].astype(BF16), own, NT)
     for parity in range(2):
         for h in range(2):
-            there = (slice(parity * half, (parity + 1) * half), slice(h * 128, (h + 1) * 128))
-            solved_ref[there] = relaid_ref[2 * h + parity] - product[there]
+            for f in range(2):
+                top, lane = parity * half + f * fold, (2 * parity + f) * 128
+                there = (slice(top, top + fold), slice(h * 128, (h + 1) * 128))
+                cut = (h, 0, slice(None), slice(lane, lane + 128))
+                held = (high_ref[cut].astype(F32) + middle_ref[cut].astype(F32)) + low_ref[cut].astype(F32)
+                solved_ref[there] = held - product[there]
     for panel in range(2):
 
         @pl.when(i == flags[2 + panel])
@@ -396,10 +403,11 @@
             solved_ref[...] = white_ref[:, panel * B : (panel + 1) * B]
 
 
-def update(flags, covariance, along, across, relaid, panels, lower, inverse, l10t):
+def update(flags, covariance, along, across, panels, lower, inverse, l10t):
     rows, columns = covariance.shape
-    parts, blocks, part, width = along.shape
-    half = relaid.shape[1]
+    parts, _, part, width = along.shape
+    blocks = rows // B
+    half = 2 * part
     return pl.pallas_call(
         update_kernel,
         grid_spec=pltpu.PrefetchScalarGridSpec(
@@ -409,7 +417,9 @@
                 pl.BlockSpec((B, columns), lambda i, flags: (i, 0)),
                 pl.BlockSpec((parts, 1, part, width), lambda i, flags: (0, i, 0, 0)),
                 pl.BlockSpec(memory_space=pl.ANY),
-                pl.BlockSpec((4, half, 128), lambda i, flags: (i, 0, 0)),
+                pl.BlockSpec((2, 1, part, width), lambda i, flags: (i, blocks, 0, 0)),
+                pl.BlockSpec((2, 1, part, width), lambda i, flags: (i, blocks + 1, 0, 0)),
+                pl.BlockSpec((2, 1, part, width), lambda i, flags: (i, blocks + 2, 0, 0)),
                 pl.BlockSpec((B, width), lambda i, flags: (jnp.where((flags[4] & flags[5]) >= 0, i, 0), 0)),
                 whole(*lower.shape),
                 whole(*inverse.shape),
@@ -430,7 +440,7 @@
         out_shape=[jax.ShapeDtypeStruct((rows, columns), F32), jax.ShapeDtypeStruct((2 * half, rows), F32)],
         compiler_params=pltpu.CompilerParams(vmem_limit_bytes=VMEM_BYTES),
         cost_estimate=pl.CostEstimate(flops=5 * 10**9, bytes_accessed=20_000_000, transcendentals=0),
-    )(flags, covariance, along, across, relaid, panels, lower, inverse, l10t)
+    )(flags, covariance, along, across, along, along, along, panels, lower, inverse, l10t)
 
 
 def per_device(covariance, innovations, block_owner, panel_index, *, n_row, n_col):
@@ -499,12 +509,17 @@
     across = lax.ppermute(across, ("row", "col"), across_axes)
     across, groups = lax.optimization_barrier((across, groups))
     across = lax.all_gather(jnp.concatenate([across, wanted], axis=0), "row", axis=0)
-    along, groups = lax.optimization_barrier((along, groups))
+    groups = groups.reshape(n_col, 2, 2 * fold, 128)
+    groups = jnp.concatenate(
+        [groups[:, parity, f * fold : (f + 1) * fold] for parity in range(2) for f in range(2)], axis=2
+    )
+    high = lax.reduce_precision(groups, 8, 7)
+    middle = lax.reduce_precision(groups - high, 8, 7)
+    terms = jnp.stack([high, middle, groups - high - middle], axis=1).astype(BF16)
+    along = jnp.concatenate([along, terms], axis=1)
     along = lax.all_to_all(along, "col", split_axis=0, concat_axis=0, tiled=True)
-    along, groups = lax.optimization_barrier((along, groups))
-    relaid = lax.all_to_all(groups, "col", split_axis=0, concat_axis=0, tiled=True)
     panels = solve_panels(flags, covariance, along, inverse, l10t)
-    return update(flags, covariance, along, across, relaid, panels, lower, inverse, l10t)
+    return update(flags, covariance, along, across, panels, lower, inverse, l10t)
 
 
 def solution(mesh):

time: 184 us -> 187 us (1.016)
  blocking collectives: 34.7 us -> 51.9 us
  waiting for transfers between devices: 35.9 us -> 26.5 us
  starting transfers between devices: 30.3 us -> 26.2 us
    all_to_all x1, blocking collectives: 34.7 us -> 51.9 us  [per_device(): lax.all_to_all(along, 'col', split_axis=0, concat_axis=0, tiled=True)]
    all_to_all x1 -> x0, waiting for transfers between devices: 9.14 us -> none  [per_device(): lax.all_to_all(groups, 'col', split_axis=0, concat_axis=0, tiled=True)]
    all_to_all x1 -> x0, starting transfers between devices: 3.49 us -> none  [per_device(): lax.all_to_all(groups, 'col', split_axis=0, concat_axis=0, tiled=True)]
  transfers between devices with their start and end apart: 8 -> 7, of which waited for: 5 -> 4; matrix products, arithmetic and copies ran while one was open for 3% -> 3% of each run, Pallas kernels for 19% -> 19%
where the time goes in v13:
time: 187 us; the launch traced here: 185 us
  blocking collectives  51.9 us (28%)
  Pallas kernels  51.3 us (27%)
  waiting for transfers between devices  26.5 us (14%)
  starting transfers between devices  26.2 us (14%)
  between operations  21.2 us (11%)
  local copies, waits for them, and re-layouts  5.92 us (3%)
  other arithmetic  2.01 us (1%)
    all_to_all x1, blocking collectives, per_device(): lax.all_to_all(along, 'col', split_axis=0, concat_axis=0, tiled=True)  51.9 us
    pallas_call x1, Pallas kernels, factor_diagonal(): pl.pallas_call(factor_kernel, in_specs=[VMEM_SPEC], out_specs=[VMEM_SPEC]...  22.7 us
    pallas_call x1, Pallas kernels, update(): pl.pallas_call(update_kernel, grid_spec=pltpu.PrefetchScalarGridSpec(num_...  13.8 us
    all_to_all x1, starting transfers between devices, per_device(): lax.all_to_all(tiles, ('row', 'col'), split_axis=0, concat_axis=0, tiled=...  11.1 us
    all_to_all x1, waiting for transfers between devices, per_device(): lax.all_to_all(tiles, ('row', 'col'), split_axis=0, concat_axis=0, tiled=...  8.7 us
    all_to_all x1, waiting for transfers between devices, per_device(): lax.all_to_all(jnp.broadcast_to(tiles[None], (n_row * n_col,) + tiles.sha...  8.01 us
    all_to_all x1, waiting for transfers between devices, per_device(): lax.all_to_all(picked, 'col', split_axis=0, concat_axis=0, tiled=True)  6.03 us
    all_to_all x1, starting transfers between devices, per_device(): lax.all_to_all(jnp.broadcast_to(tiles[None], (n_row * n_col,) + tiles.sha...  4.64 us
  transfers between devices with their start and end apart: 7, of which 4 were waited for; matrix products, arithmetic and copies ran while one was open for 3% of the time, Pallas kernels for 19%

profile of v13, /device:TPU:0, one launch (start us, length us, event | category | flops | bytes accessed | tf_op | source)
XLA Modules:
  0.0 185.0 jit_solution(14728847077027775105)
XLA Ops:
  7.8 2.7 %shard_map.60 = f32[32,4,8,128]{3,2,1,0:T(8,128)} custom-call(s32[64]{0:T(128)} %owner_ref.1, s32[1]{0:T(128)} %copy.18.panel_ref, f32[1024,2048]{1,0:T(8,128)} %cov_ref.5), custom_call_target="tpu_custom_call" | custom-call | tf_op jit(solution)/shard_map/pallas_call | solution.py:78
  10.6 11.1 %all-to-all-start = ((f32[128,8,128]{2,1,0:T(8,128)}), f32[128,8,128]{2,1,0:T(8,128)S(1)}, u32[]{:S(2)}, u32[]{:S(2)}) async-start(f32[128,8,128]{2,1,0:T(8,128)} %bitcast.33), calls=%async_computation | async-start | bytes 1048576 | tf_op jit(solution)/shard_map/all_to_all | solution.py:482
  23.8 0.6 fusion.10
  26.3 8.7 %all-to-all-done = f32[128,8,128]{2,1,0:T(8,128)S(1)} async-done(((f32[128,8,128]{2,1,0:T(8,128)}), f32[128,8,128]{2,1,0:T(8,128)S(1)}, u32[]{:S(2)}, u32[]{:S(2)}) %all-to-all-start) | async-done | bytes 524320 | tf_op jit(solution)/shard_map/all_to_all | solution.py:482
  35.1 1.1 broadcast_in_dim.36
  36.1 4.6 %all-to-all-start.1 = ((f32[128,16,128]{2,1,0:T(8,128)}), f32[128,16,128]{2,1,0:T(8,128)S(1)}, u32[]{:S(2)}, u32[]{:S(2)}) async-start(f32[128,16,128]{2,1,0:T(8,128)} %broadcast_in_dim.36), calls=%async_computation.1 | async-start | bytes 2097152 | tf_op jit(solution)/shard_map/all_to_all | solution.py:487
  43.3 1.0 copy.17
  45.5 0.8 dynamic-slice_bitcast_fusion.3
  46.3 0.7 collective-permute-start
  47.0 4.5 %shard_map.59 = f32[8,4,32,512]{3,2,1,0:T(8,128)} custom-call(s32[2]{0:T(128)} %get-tuple-element.28.slots, f32[1024,2048]{1,0:T(8,128)} %cov_ref.5), custom_call_target="tpu_custom_call" | custom-call | tf_op jit(solution)/shard_map/pallas_call | solution.py:39
  51.5 8.0 %all-to-all-done.1.tiles_ref = f32[128,16,128]{2,1,0:T(8,128)S(1)} async-done(((f32[128,16,128]{2,1,0:T(8,128)}), f32[128,16,128]{2,1,0:T(8,128)S(1)}, u32[]{:S(2)}, u32[]{:S(2)}) %all-to-all-start.1) | async-done | bytes 1048608 | tf_op jit(solution)/shard_map/all_to_all | solution.py:487
  59.5 1.0 copy-done.2
  60.5 4.2 %all-to-all-start.2 = ((f32[8,4,32,512]{3,2,1,0:T(8,128)}), f32[8,4,32,512]{3,2,1,0:T(8,128)S(1)}, u32[]{:S(2)}, u32[]{:S(2)}) async-start(f32[8,4,32,512]{3,2,1,0:T(8,128)} %shard_map.59), calls=%async_computation.2 | async-start | bytes 4194304 | tf_op jit(solution)/shard_map/all_to_all | solution.py:499
  64.7 22.7 %shard_map.61 = (bf16[256,3072]{1,0:T(8,128)(2,1)}, bf16[256,256]{1,0:T(8,128)(2,1)}, f32[256,512]{1,0:T(8,128)}) custom-call(f32[128,16,128]{2,1,0:T(8,128)} %copy-done.2), custom_call_target="tpu_custom_call" | custom-call | flops 20000000000 | bytes 80000000 | tf_op jit(solution)/shard_map/pallas_call | solution.py:187
  87.4 6.0 %all-to-all-done.2.first_ref.second_ref = f32[8,4,32,512]{3,2,1,0:T(8,128)S(1)} async-done(((f32[8,4,32,512]{3,2,1,0:T(8,128)}), f32[8,4,32,512]{3,2,1,0:T(8,128)S(1)}, u32[]{:S(2)}, u32[]{:S(2)}) %all-to-all-start.2) | async-done | bytes 2097184 | tf_op jit(solution)/shard_map/all_to_all | solution.py:499
  93.4 3.8 %all-to-all-start.3 = ((f32[16,64,128]{2,1,0:T(8,128)}), f32[16,64,128]{2,1,0:T(8,128)S(1)}, u32[]{:S(2)}, u32[]{:S(2)}) async-start(f32[16,64,128]{2,1,0:T(8,128)} %bitcast.30), calls=%async_computation.3 | async-start | bytes 1048576 | tf_op jit(solution)/shard_map/all_to_all | solution.py:506
  97.5 0.7 concatenate.44.flags
  98.2 4.4 %shard_map.62 = (bf16[8,4,32,512]{3,2,1,0:T(8,128)(2,1)}, bf16[4,32,512]{2,1,0:T(8,128)(2,1)}) custom-call(s32[22]{0:T(128)} %concatenate.44.flags, f32[8,4,32,512]{3,2,1,0:T(8,128)} %copy-done, f32[8,4,32,512]{3,2,1,0:T(8,128)} %copy-done, bf16[256,3072]{1,0:T(8,128)(2,1)} %get-tuple-element.15.inverse_ref, bf16[256,256]{1,0:T(8,128)(2,1)} %get-tuple-element.16.l10t_ref), custom_call_target="tpu_custom_call" | custom-call | flops 1000000000 | bytes 4000000 | tf_op jit(solution)/shard_map/pallas_call | solution.py:232
  102.6 1.7 collective-permute-start.1
  104.3 3.7 %all-to-all-done.3 = f32[16,64,128]{2,1,0:T(8,128)S(1)} async-done(((f32[16,64,128]{2,1,0:T(8,128)}), f32[16,64,128]{2,1,0:T(8,128)S(1)}, u32[]{:S(2)}, u32[]{:S(2)}) %all-to-all-start.3) | async-done | bytes 524320 | tf_op jit(solution)/shard_map/all_to_all | solution.py:506
  108.0 0.7 pad_maximum_fusion.2
  109.3 51.9 %all_to_all.25.along_ref.high_ref.middle_ref.low_ref = bf16[8,7,32,512]{3,2,1,0:T(8,128)(2,1)} all-to-all(bf16[8,7,32,512]{3,2,1,0:T(8,128)(2,1)S(1)} %pad_maximum_fusion), channel_id=1, replica_groups=mesh['row'=16,'col'=8] {'col'}, dimensions={0} | all-to-all | bytes 3670016 | tf_op jit(solution)/shard_map/all_to_all | solution.py:520
  161.1 3.2 %shard_map.63.panel_ref = f32[1024,512]{1,0:T(8,128)} custom-call(s32[22]{0:T(128)} %concatenate.44.flags, f32[1024,2048]{1,0:T(8,128)} %cov_ref.5, f32[1024,2048]{1,0:T(8,128)} %cov_ref.5, bf16[8,7,32,512]{3,2,1,0:T(8,128)(2,1)} %all_to_all.25.along_ref.high_ref.middle_ref.low_ref, bf16[256,3072]{1,0:T(8,128)(2,1)} %get-tuple-element.15.inverse_ref, ...), custom_call_target="tpu_custom_call" | custom-call | flops 1000000000 | bytes 4000000 | tf_op jit(solution)/shard_map/pallas_call | solution.py:282
  164.3 13.8 %shard_map.64 = (f32[1024,2048]{1,0:T(8,128)}, f32[128,1024]{1,0:T(8,128)}) custom-call(s32[22]{0:T(128)} %concatenate.44.flags, f32[1024,2048]{1,0:T(8,128)} %cov_ref.5, bf16[8,7,32,512]{3,2,1,0:T(8,128)(2,1)} %all_to_all.25.along_ref.high_ref.middle_ref.low_ref, bf16[16,7,32,512]{3,2,1,0:T(8,128)(2,1)} %bitcast.32, ...), custom_call_target="tpu_custom_call" | custom-call | flops 5000000000 | bytes 20000000 | tf_op jit(solution)/shard_map/pallas_call | solution.py:411
  (29 shorter events, 2.2 us)
Async XLA Ops:
  7.8 14.0 %copy-start.4 = (s32[64]{0:T(128)S(1)}, s32[64]{0:T(128)}, u32[]{:S(2)}) copy-start(s32[64]{0:T(128)} %owner_ref.1) | copy-start | bytes 772
  10.6 24.5 %all-to-all-start = ((f32[128,8,128]{2,1,0:T(8,128)}), f32[128,8,128]{2,1,0:T(8,128)S(1)}, u32[]{:S(2)}, u32[]{:S(2)}) async-start(f32[128,8,128]{2,1,0:T(8,128)} %bitcast.33), calls=%async_computation | async-start | bytes 1048576 | tf_op jit(solution)/shard_map/all_to_all | solution.py:482
  21.7 21.6 %copy-start.3 = (f32[64,16,128]{2,1,0:T(8,128)S(1)}, f32[64,16,128]{2,1,0:T(8,128)}, u32[]{:S(2)}) copy-start(f32[64,16,128]{2,1,0:T(8,128)} %param.5) | copy-start | bytes 1572868
  36.1 23.4 %all-to-all-start.1 = ((f32[128,16,128]{2,1,0:T(8,128)}), f32[128,16,128]{2,1,0:T(8,128)S(1)}, u32[]{:S(2)}, u32[]{:S(2)}) async-start(f32[128,16,128]{2,1,0:T(8,128)} %broadcast_in_dim.36), calls=%async_computation.1 | async-start | bytes 2097152 | tf_op jit(solution)/shard_map/all_to_all | solution.py:487
  46.3 5.1 %collective-permute-start = (f32[32,512]{1,0:T(8,128)S(1)}, f32[32,512]{1,0:T(8,128)S(1)}, u32[]{:S(2)}, u32[]{:S(2)}) collective-permute-start(f32[32,512]{1,0:T(8,128)S(1)} %pad_maximum_fusion.3), channel_id=1, source_target_pairs={{0,0},{1,16},{2,32},{3,48},{4,64},{5,80},{6,96},{7,112},{8,8},{9,2... | collective-permute-start | bytes 196616 | tf_op jit(solution)/shard_map/ppermute | solution.py:479
  59.5 1.0 copy-start.2
  60.5 32.9 %all-to-all-start.2 = ((f32[8,4,32,512]{3,2,1,0:T(8,128)}), f32[8,4,32,512]{3,2,1,0:T(8,128)S(1)}, u32[]{:S(2)}, u32[]{:S(2)}) async-start(f32[8,4,32,512]{3,2,1,0:T(8,128)} %shard_map.59), calls=%async_computation.2 | async-start | bytes 4194304 | tf_op jit(solution)/shard_map/all_to_all | solution.py:499
  93.4 4.8 %copy-start = (f32[8,4,32,512]{3,2,1,0:T(8,128)}, f32[8,4,32,512]{3,2,1,0:T(8,128)S(1)}, u32[]{:S(2)}) copy-start(f32[8,4,32,512]{3,2,1,0:T(8,128)S(1)} %all-to-all-done.2.first_ref.second_ref) | copy-start | bytes 6291460
  93.4 14.6 %all-to-all-start.3 = ((f32[16,64,128]{2,1,0:T(8,128)}), f32[16,64,128]{2,1,0:T(8,128)S(1)}, u32[]{:S(2)}, u32[]{:S(2)}) async-start(f32[16,64,128]{2,1,0:T(8,128)} %bitcast.30), calls=%async_computation.3 | async-start | bytes 1048576 | tf_op jit(solution)/shard_map/all_to_all | solution.py:506
  97.2 67.1 %all-gather.3.cloned.1.call-start = ((), (), s32[]{:S(2)}) async-start(), calls=%async_computation.5 | async-start | bytes 3899392 | tf_op jit(solution)/shard_map/all_gather | solution.py:511
  102.6 6.4 %copy-start.1 = (bf16[8,4,32,512]{3,2,1,0:T(8,128)(2,1)S(1)}, bf16[8,4,32,512]{3,2,1,0:T(8,128)(2,1)}, u32[]{:S(2)}) copy-start(bf16[8,4,32,512]{3,2,1,0:T(8,128)(2,1)} %get-tuple-element.17) | copy-start | bytes 3145732
  102.6 1.7 collective-permute-start.1
Sparse Core Ops, SparseCore 0:
  108.9 50.0 all-gather.2

commit v14 on v12

--- a/solution.py
+++ b/solution.py
@@ -492,12 +492,10 @@
     middle = lax.reduce_precision(wanted - high, 8, 7)
     wanted = jnp.stack([high, middle, wanted - high - middle]).astype(BF16)
 
-    groups, _, _ = lax.optimization_barrier((jnp.transpose(innovations, (1, 0, 2)), parts, l10t))
+    along, across = solve_piece(flags, parts, inverse, l10t)
+    groups, _ = lax.optimization_barrier((jnp.transpose(innovations, (1, 0, 2)), across))
     groups = lax.all_to_all(groups, "row", split_axis=0, concat_axis=0, tiled=True)
-
-    along, across = solve_piece(flags, parts, inverse, l10t)
     across = lax.ppermute(across, ("row", "col"), across_axes)
-    across, groups = lax.optimization_barrier((across, groups))
     across = lax.all_gather(jnp.concatenate([across, wanted], axis=0), "row", axis=0)
     along, groups = lax.optimization_barrier((along, groups))
     along = lax.all_to_all(along, "col", split_axis=0, concat_axis=0, tiled=True)

time: 184 us -> 194 us (1.054)
  blocking collectives: 34.7 us -> 54.3 us
  waiting for transfers between devices: 35.9 us -> 29.3 us
  starting transfers between devices: 30.3 us -> 25.9 us
  Pallas kernels: 51.3 us -> 54.7 us
    all_to_all x0 -> x1, blocking collectives: none -> 26.1 us  [per_device(): lax.all_to_all(groups, 'row', split_axis=0, concat_axis=0, tiled=True)]
    all_to_all x1, blocking collectives: 34.7 us -> 28.2 us  [per_device(): lax.all_to_all(along, 'col', split_axis=0, concat_axis=0, tiled=True)]
    all_to_all x1 -> x0, starting transfers between devices: 4.46 us -> none  [per_device(): lax.all_to_all(groups, 'row', split_axis=0, concat_axis=0, tiled=True)]
    all_to_all x1 -> x0, waiting for transfers between devices: 4 us -> none  [per_device(): lax.all_to_all(groups, 'row', split_axis=0, concat_axis=0, tiled=True)]
    all_to_all x1, waiting for transfers between devices: 9.14 us -> 5.88 us  [per_device(): lax.all_to_all(groups, 'col', split_axis=0, concat_axis=0, tiled=True)]
    pallas_call x1, Pallas kernels: 3.21 us -> 6.2 us  [solve_panels(): pl.pallas_call(panel_kernel, grid_spec=pltpu.PrefetchScalarGridSpec(num_s...]
  transfers between devices with their start and end apart: 8 -> 7, of which waited for: 5 -> 4; matrix products, arithmetic and copies ran while one was open for 3% -> 2% of each run, Pallas kernels for 19% -> 17%
where the time goes in v14:
time: 194 us; the launch traced here: 193 us
  Pallas kernels  54.7 us (28%)
  blocking collectives  54.3 us (28%)
  waiting for transfers between devices  29.3 us (15%)
  starting transfers between devices  25.9 us (13%)
  between operations  21.2 us (11%)
  local copies, waits for them, and re-layouts  6.44 us (3%)
    all_to_all x1, blocking collectives, per_device(): lax.all_to_all(along, 'col', split_axis=0, concat_axis=0, tiled=True)  28.2 us
    all_to_all x1, blocking collectives, per_device(): lax.all_to_all(groups, 'row', split_axis=0, concat_axis=0, tiled=True)  26.1 us
    pallas_call x1, Pallas kernels, factor_diagonal(): pl.pallas_call(factor_kernel, in_specs=[VMEM_SPEC], out_specs=[VMEM_SPEC]...  22.6 us
    pallas_call x1, Pallas kernels, update(): pl.pallas_call(update_kernel, grid_spec=pltpu.PrefetchScalarGridSpec(num_...  14.1 us
    all_to_all x1, starting transfers between devices, per_device(): lax.all_to_all(tiles, ('row', 'col'), split_axis=0, concat_axis=0, tiled=...  11.1 us
    all_to_all x1, waiting for transfers between devices, per_device(): lax.all_to_all(tiles, ('row', 'col'), split_axis=0, concat_axis=0, tiled=...  8.72 us
    all_to_all x1, waiting for transfers between devices, per_device(): lax.all_to_all(jnp.broadcast_to(tiles[None], (n_row * n_col,) + tiles.sha...  8.62 us
    pallas_call x1, Pallas kernels, solve_panels(): pl.pallas_call(panel_kernel, grid_spec=pltpu.PrefetchScalarGridSpec(num_s...  6.2 us
  transfers between devices with their start and end apart: 7, of which 4 were waited for; matrix products, arithmetic and copies ran while one was open for 2% of the time, Pallas kernels for 17%

profile of v14, /device:TPU:0, one launch (start us, length us, event | category | flops | bytes accessed | tf_op | source)
XLA Modules:
  0.0 193.5 jit_solution(1089481343775762774)
XLA Ops:
  7.8 2.7 %shard_map.60 = f32[32,4,8,128]{3,2,1,0:T(8,128)} custom-call(s32[64]{0:T(128)} %owner_ref.1, s32[1]{0:T(128)} %copy.18.panel_ref, f32[1024,2048]{1,0:T(8,128)} %cov_ref.5), custom_call_target="tpu_custom_call" | custom-call | tf_op jit(solution)/shard_map/pallas_call | solution.py:78
  10.6 11.1 %all-to-all-start = ((f32[128,8,128]{2,1,0:T(8,128)}), f32[128,8,128]{2,1,0:T(8,128)S(1)}, u32[]{:S(2)}, u32[]{:S(2)}) async-start(f32[128,8,128]{2,1,0:T(8,128)} %bitcast.32), calls=%async_computation | async-start | bytes 1048576 | tf_op jit(solution)/shard_map/all_to_all | solution.py:472
  22.5 0.6 fusion.7
  26.3 8.7 %all-to-all-done = f32[128,8,128]{2,1,0:T(8,128)S(1)} async-done(((f32[128,8,128]{2,1,0:T(8,128)}), f32[128,8,128]{2,1,0:T(8,128)S(1)}, u32[]{:S(2)}, u32[]{:S(2)}) %all-to-all-start) | async-done | bytes 524320 | tf_op jit(solution)/shard_map/all_to_all | solution.py:472
  35.1 1.1 broadcast_in_dim.36
  36.1 4.6 %all-to-all-start.1 = ((f32[128,16,128]{2,1,0:T(8,128)}), f32[128,16,128]{2,1,0:T(8,128)S(1)}, u32[]{:S(2)}, u32[]{:S(2)}) async-start(f32[128,16,128]{2,1,0:T(8,128)} %broadcast_in_dim.36), calls=%async_computation.1 | async-start | bytes 2097152 | tf_op jit(solution)/shard_map/all_to_all | solution.py:477
  44.9 0.7 collective-permute-start
  45.8 4.5 %shard_map.59 = f32[8,4,32,512]{3,2,1,0:T(8,128)} custom-call(s32[2]{0:T(128)} %get-tuple-element.32.slots, f32[1024,2048]{1,0:T(8,128)} %cov_ref.5), custom_call_target="tpu_custom_call" | custom-call | tf_op jit(solution)/shard_map/pallas_call | solution.py:39
  50.9 8.6 %all-to-all-done.1.tiles_ref = f32[128,16,128]{2,1,0:T(8,128)S(1)} async-done(((f32[128,16,128]{2,1,0:T(8,128)}), f32[128,16,128]{2,1,0:T(8,128)S(1)}, u32[]{:S(2)}, u32[]{:S(2)}) %all-to-all-start.1) | async-done | bytes 1048608 | tf_op jit(solution)/shard_map/all_to_all | solution.py:477
  59.5 1.0 copy-done.1
  60.5 4.0 %all-to-all-start.2 = ((f32[8,4,32,512]{3,2,1,0:T(8,128)}), f32[8,4,32,512]{3,2,1,0:T(8,128)S(1)}, u32[]{:S(2)}, u32[]{:S(2)}) async-start(f32[8,4,32,512]{3,2,1,0:T(8,128)} %shard_map.59), calls=%async_computation.2 | async-start | bytes 4194304 | tf_op jit(solution)/shard_map/all_to_all | solution.py:489
  64.7 22.6 %shard_map.61 = (bf16[256,3072]{1,0:T(8,128)(2,1)}, bf16[256,256]{1,0:T(8,128)(2,1)}, f32[256,512]{1,0:T(8,128)}) custom-call(f32[128,16,128]{2,1,0:T(8,128)} %copy-done.1), custom_call_target="tpu_custom_call" | custom-call | flops 20000000000 | bytes 80000000 | tf_op jit(solution)/shard_map/pallas_call | solution.py:187
  87.4 6.1 %all-to-all-done.2.first_ref.second_ref = f32[8,4,32,512]{3,2,1,0:T(8,128)S(1)} async-done(((f32[8,4,32,512]{3,2,1,0:T(8,128)}), f32[8,4,32,512]{3,2,1,0:T(8,128)S(1)}, u32[]{:S(2)}, u32[]{:S(2)}) %all-to-all-start.2) | async-done | bytes 2097184 | tf_op jit(solution)/shard_map/all_to_all | solution.py:489
  93.4 1.3 copy-done
  94.8 4.6 %shard_map.62 = (bf16[8,4,32,512]{3,2,1,0:T(8,128)(2,1)}, bf16[4,32,512]{2,1,0:T(8,128)(2,1)}) custom-call(s32[22]{0:T(128)} %concatenate.13.flags, f32[8,4,32,512]{3,2,1,0:T(8,128)} %copy-done, f32[8,4,32,512]{3,2,1,0:T(8,128)} %copy-done, bf16[256,3072]{1,0:T(8,128)(2,1)} %get-tuple-element.17.inverse_ref, bf16[256,256]{1,0:T(8,128)(2,1)} %get-tuple-element.18.l10t_ref), custom_call_target="tpu_custom_call" | custom-call | flops 1000000000 | bytes 4000000 | tf_op jit(solution)/shard_map/pallas_call | solution.py:232
  99.4 1.7 collective-permute-start.1
  101.1 0.7 pad_maximum_fusion
  101.8 26.1 %all_to_all.30 = f32[16,64,128]{2,1,0:T(8,128)} all-to-all(f32[16,64,128]{2,1,0:T(8,128)S(1)} %bitcast.31), channel_id=1, replica_groups=mesh['row'=16,'col'=8] {'row'}, dimensions={0} | all-to-all | bytes 1048576 | tf_op jit(solution)/shard_map/all_to_all | solution.py:497
  127.9 28.2 %all_to_all.31.along_ref = bf16[8,4,32,512]{3,2,1,0:T(8,128)(2,1)} all-to-all(bf16[8,4,32,512]{3,2,1,0:T(8,128)(2,1)S(1)} %copy-done.2), channel_id=1, replica_groups=mesh['row'=16,'col'=8] {'col'}, dimensions={0} | all-to-all | bytes 2097152 | tf_op jit(solution)/shard_map/all_to_all | solution.py:501
  156.2 3.5 %all-to-all-start.5 = ((f32[16,64,128]{2,1,0:T(8,128)}), f32[16,64,128]{2,1,0:T(8,128)S(1)}, u32[]{:S(2)}, u32[]{:S(2)}) async-start(f32[16,64,128]{2,1,0:T(8,128)} %all_to_all.30), calls=%async_computation.5 | async-start | bytes 1048576 | tf_op jit(solution)/shard_map/all_to_all | solution.py:503
  159.7 6.2 %shard_map.63.panel_ref = f32[1024,512]{1,0:T(8,128)} custom-call(s32[22]{0:T(128)} %concatenate.13.flags, f32[1024,2048]{1,0:T(8,128)} %cov_ref.5, f32[1024,2048]{1,0:T(8,128)} %cov_ref.5, bf16[8,4,32,512]{3,2,1,0:T(8,128)(2,1)} %all_to_all.31.along_ref, bf16[256,3072]{1,0:T(8,128)(2,1)} %get-tuple-element.17.inverse_ref, ...), custom_call_target="tpu_custom_call" | custom-call | flops 1000000000 | bytes 4000000 | tf_op jit(solution)/shard_map/pallas_call | solution.py:281
  165.9 5.9 %all-to-all-done.5.relaid_ref = f32[16,64,128]{2,1,0:T(8,128)S(1)} async-done(((f32[16,64,128]{2,1,0:T(8,128)}), f32[16,64,128]{2,1,0:T(8,128)S(1)}, u32[]{:S(2)}, u32[]{:S(2)}) %all-to-all-start.5) | async-done | bytes 524320 | tf_op jit(solution)/shard_map/all_to_all | solution.py:503
  171.8 0.8 copy-done.4
  172.6 14.1 %shard_map.64 = (f32[1024,2048]{1,0:T(8,128)}, f32[128,1024]{1,0:T(8,128)}) custom-call(s32[22]{0:T(128)} %concatenate.13.flags, f32[1024,2048]{1,0:T(8,128)} %cov_ref.5, bf16[8,4,32,512]{3,2,1,0:T(8,128)(2,1)} %all_to_all.31.along_ref, bf16[16,7,32,512]{3,2,1,0:T(8,128)(2,1)} %bitcast.33, f32[16,64,128]{2,1,0:T(8,128)} %copy-done.4, ...), custom_call_target="tpu_custom_call" | custom-call | flops 5000000000 | bytes 20000000 | tf_op jit(solution)/shard_map/pallas_call | solution.py:403
  (29 shorter events, 2.7 us)
Async XLA Ops:
  7.8 14.0 %copy-start.5 = (s32[64]{0:T(128)S(1)}, s32[64]{0:T(128)}, u32[]{:S(2)}) copy-start(s32[64]{0:T(128)} %owner_ref.1) | copy-start | bytes 772
  10.6 32.8 %copy-start.3 = (f32[64,16,128]{2,1,0:T(8,128)S(1)}, f32[64,16,128]{2,1,0:T(8,128)}, u32[]{:S(2)}) copy-start(f32[64,16,128]{2,1,0:T(8,128)} %param.5) | copy-start | bytes 1572868
  10.6 24.5 %all-to-all-start = ((f32[128,8,128]{2,1,0:T(8,128)}), f32[128,8,128]{2,1,0:T(8,128)S(1)}, u32[]{:S(2)}, u32[]{:S(2)}) async-start(f32[128,8,128]{2,1,0:T(8,128)} %bitcast.32), calls=%async_computation | async-start | bytes 1048576 | tf_op jit(solution)/shard_map/all_to_all | solution.py:472
  36.1 23.4 %all-to-all-start.1 = ((f32[128,16,128]{2,1,0:T(8,128)}), f32[128,16,128]{2,1,0:T(8,128)S(1)}, u32[]{:S(2)}, u32[]{:S(2)}) async-start(f32[128,16,128]{2,1,0:T(8,128)} %broadcast_in_dim.36), calls=%async_computation.1 | async-start | bytes 2097152 | tf_op jit(solution)/shard_map/all_to_all | solution.py:477
  44.9 6.0 %collective-permute-start = (f32[32,512]{1,0:T(8,128)S(1)}, f32[32,512]{1,0:T(8,128)S(1)}, u32[]{:S(2)}, u32[]{:S(2)}) collective-permute-start(f32[32,512]{1,0:T(8,128)S(1)} %pad_maximum_fusion.1), channel_id=1, source_target_pairs={{0,0},{1,16},{2,32},{3,48},{4,64},{5,80},{6,96},{7,112},{8,8},{9,2... | collective-permute-start | bytes 196616 | tf_op jit(solution)/shard_map/ppermute | solution.py:469
  59.5 1.0 copy-start.1
  60.5 32.9 %all-to-all-start.2 = ((f32[8,4,32,512]{3,2,1,0:T(8,128)}), f32[8,4,32,512]{3,2,1,0:T(8,128)S(1)}, u32[]{:S(2)}, u32[]{:S(2)}) async-start(f32[8,4,32,512]{3,2,1,0:T(8,128)} %shard_map.59), calls=%async_computation.2 | async-start | bytes 4194304 | tf_op jit(solution)/shard_map/all_to_all | solution.py:489
  64.5 107.2 %all-gather.3.cloned.1.call-start = ((), (), s32[]{:S(2)}) async-start(), calls=%async_computation.6 | async-start | bytes 3899392 | tf_op jit(solution)/shard_map/all_gather | solution.py:499
  93.4 1.3 copy-start
  99.4 28.6 %copy-start.2 = (bf16[8,4,32,512]{3,2,1,0:T(8,128)(2,1)S(1)}, bf16[8,4,32,512]{3,2,1,0:T(8,128)(2,1)}, u32[]{:S(2)}) copy-start(bf16[8,4,32,512]{3,2,1,0:T(8,128)(2,1)} %get-tuple-element.22) | copy-start | bytes 3145732
  99.4 1.7 collective-permute-start.1
  156.2 15.6 %all-to-all-start.5 = ((f32[16,64,128]{2,1,0:T(8,128)}), f32[16,64,128]{2,1,0:T(8,128)S(1)}, u32[]{:S(2)}, u32[]{:S(2)}) async-start(f32[16,64,128]{2,1,0:T(8,128)} %all_to_all.30), calls=%async_computation.5 | async-start | bytes 1048576 | tf_op jit(solution)/shard_map/all_to_all | solution.py:503
  171.7 0.8 copy-start.4
Sparse Core Ops, SparseCore 0:
  102.0 50.4 all-gather.2
